TPU v7x, 32 devices: a whole 2x2x4 slice. The times are simulated.
32 devices in a mesh: groups: 2 (over y), expert: 4 (over z), tensor: 4 (over x, core).
Axes of the slice: x: 2, y: 2, z: 4, core: 2. Of those that a mesh axis runs over, the one named last changes fastest.
Arguments:
- tokens: bfloat16 [512, 3072], P(('groups', 'expert'), 'tensor'), parts along dimension 0, may hold values from -6 to 6
- expert_ids: int32 [512, 2], P(('groups', 'expert')), parts along dimension 0, may hold values from 0 to 3, all different within a row; in each aligned block of 64 rows (0 to 63, 64 to 127, ...) at most 34 rows name the same one
- gate_probs: float32 [512, 2], P(('groups', 'expert')), parts along dimension 0, may hold values from 0.2 to 1
- out_grad: bfloat16 [512, 3072], P(('groups', 'expert'), 'tensor'), parts along dimension 0, may hold values from -1.5 to 1.5
- gate_weight: bfloat16 [4, 3072, 8192], P('expert', None, 'tensor'), may hold values from -0.109375 to 0.109375
- up_weight: bfloat16 [4, 3072, 8192], P('expert', None, 'tensor'), may hold values from -0.109375 to 0.109375
- down_weight: bfloat16 [4, 8192, 3072], P('expert', None, 'tensor'), may hold values from -0.0625 to 0.0625
Outputs:
- mixed: bfloat16 [512, 3072], P(('groups', 'expert'), 'tensor'), parts along dimension 0
- gate_grad: float32 [512, 2], P(('groups', 'expert')), parts along dimension 0
There are 2 independent parts, one for each index of `groups`. A program takes and returns all parts, laid end to end along the dimension named above; an argument that names none is the same for every part. Nothing has to cross between parts.
Inputs may be any that keep to these rules, and one draw needn't show every extreme that they name: `expert_ids`: each token names 2 different experts; among the 64 rows of one device no expert is named by more than 34 rows.
All inputs are finite; a program needn't handle non-finite values.
Results may differ from a plain program's by a relative error of at most 0.005.
Values may be sent and summed in bfloat16 or wider, within the bound.
No kernel may reach another device: no remote copies, remote signals or barrier semaphores. Data moves between devices by JAX's collectives and lax.ppermute only.
A program may use at most 128 MiB of HBM per device.

v0:
```python
import jax
import jax.numpy as jnp
from jax import lax
from jax.sharding import PartitionSpec as P

EXPERTS = 4
MOST = 34


def per_device(tokens, expert_ids, gate_probs, out_grad, gate_weight, up_weight, down_weight):
    devices_expert = lax.axis_size("expert")
    span_count = devices_expert // EXPERTS
    slot_count = MOST
    part_width = tokens.shape[1]
    w_gate = gate_weight[0]
    w_up = up_weight[0]
    w_down = down_weight[0]
    hit_table = expert_ids[:, :, None] == jnp.arange(EXPERTS, dtype=jnp.int32)[None, None, :]
    hit_float = hit_table.astype(jnp.float32)
    member = jnp.sum(hit_table.astype(jnp.int32), axis=1)
    position = jnp.cumsum(member, axis=0) - member
    placed = (position[None, :, :] == jnp.arange(slot_count, dtype=jnp.int32)[:, None, None]) & (
        member[None, :, :] == 1
    )
    select = jnp.transpose(placed, (2, 0, 1)).astype(jnp.float32)
    select_half = select.astype(jnp.bfloat16)
    route_weight = jnp.sum(hit_float * gate_probs[:, :, None], axis=1)
    grad_float = out_grad.astype(jnp.float32)
    token_rows = jnp.einsum(
        "est,td->esd", select_half, tokens, preferred_element_type=jnp.float32
    ).astype(jnp.bfloat16)
    token_send = jnp.repeat(token_rows, span_count, axis=0)
    arrived = lax.all_to_all(token_send, "expert", split_axis=0, concat_axis=0, tiled=True)
    piece = lax.all_gather(arrived, "tensor", axis=2, tiled=True)
    gate_pre = jnp.einsum("smd,df->smf", piece, w_gate, preferred_element_type=jnp.float32)
    up_pre = jnp.einsum("smd,df->smf", piece, w_up, preferred_element_type=jnp.float32)
    sigmoid_gate = jax.nn.sigmoid(gate_pre)
    hidden = (gate_pre * sigmoid_gate * up_pre).astype(jnp.bfloat16)
    partial_out = jnp.einsum(
        "smf,fd->smd",
        lax.all_gather(hidden, "tensor", axis=2, tiled=True),
        w_down,
        preferred_element_type=jnp.float32,
    )
    returned = lax.all_to_all(partial_out, "expert", split_axis=0, concat_axis=0, tiled=True)
    expert_out = jnp.sum(returned.reshape(EXPERTS, span_count, slot_count, part_width), axis=1)
    token_out = jnp.einsum("est,esd->ted", select, expert_out, precision=lax.Precision.HIGHEST)
    mixed = jnp.sum(route_weight[:, :, None] * token_out, axis=1).astype(jnp.bfloat16)
    local_dots = jnp.sum(grad_float[:, None, :] * token_out, axis=2)
    dots = lax.psum(local_dots, "tensor")
    gate_grad = jnp.sum(hit_float * dots[:, None, :], axis=2)
    return (mixed, gate_grad)


def solution(mesh):
    in_specs = (
        P(("groups", "expert"), "tensor"),
        P(("groups", "expert"), None),
        P(("groups", "expert"), None),
        P(("groups", "expert"), "tensor"),
        P("expert", None, "tensor"),
        P("expert", None, "tensor"),
        P("expert", None, "tensor"),
    )
    out_specs = (P(("groups", "expert"), "tensor"), P(("groups", "expert"), None))
    return jax.shard_map(
        per_device, mesh=mesh, in_specs=in_specs, out_specs=out_specs, check_vma=False
    )
```

profile of v0, /device:TPU:0, one launch (start us, length us, event | category | flops | bytes accessed | tf_op | source)
XLA Modules:
  0.0 110.2 jit_solution(12110065346913813669)
XLA Ops:
  7.2 0.0 copy-start
  7.2 0.0 all-gather.2.cloned.1.call-start
  7.2 0.7 convert_reduce_fusion
  7.9 0.1 copy.18
  8.0 0.1 reduce_window_sum.11
  8.1 0.1 copy.20
  8.2 0.0 copy-done
  8.2 0.2 convolution_convert_fusion
  8.4 14.6 %all_to_all.10 = bf16[4,34,768]{2,1,0:T(8,128)(2,1)S(1)} all-to-all(bf16[4,34,768]{2,1,0:T(8,128)(2,1)S(1)} %convolution_convert_fusion), channel_id=1, replica_groups=mesh['groups'=2,'expert'=4,'tensor'=4] {'expert'}, dimensions={0} | all-to-all | bytes 417792 | tf_op jit(solution)/shard_map/all_to_all | solution.py:33
  23.1 9.7 %all_gather.6 = bf16[4,34,3072]{2,1,0:T(8,128)(2,1)S(1)} all-gather(bf16[4,34,768]{2,1,0:T(8,128)(2,1)S(1)} %all_to_all.10), channel_id=1, replica_groups=mesh['groups'=2,'expert'=4,'tensor'=4] {'tensor'}, dimensions={2}, use_global_device_ids=true | all-gather | bytes 1044480 | tf_op jit(solution)/shard_map/all_gather | solution.py:34
  32.7 0.0 copy-start.4
  32.7 7.0 %fusion.4 = f32[4,34,2048]{2,1,0:T(8,128)S(1)} fusion(bf16[4,34,3072]{2,1,0:T(8,128)(2,1)S(1)} %all_gather.6, bf16[1,3072,2048]{2,1,0:T(8,128)(2,1)} %param.11), kind=kOutput, calls=%fused_computation.4 | convolution fusion | flops 1711276032 | bytes 14532608 | tf_op jit(solution)/shard_map/smd,df->smf/dot_general | solution.py:35
  39.7 1.2 %copy-done.4 = bf16[1,3072,2048]{2,1,0:T(8,128)(2,1)S(1)} copy-done((bf16[1,3072,2048]{2,1,0:T(8,128)(2,1)S(1)}, bf16[1,3072,2048]{2,1,0:T(8,128)(2,1)}, u32[]{:S(2)}) %copy-start.4) | copy-done | bytes 12582936
  40.9 3.5 %fusion.9 = bf16[4,34,2048]{2,1,0:T(8,128)(2,1)} fusion(bf16[4,34,3072]{2,1,0:T(8,128)(2,1)S(1)} %all_gather.6, bf16[1,3072,2048]{2,1,0:T(8,128)(2,1)S(1)} %copy-done.4, f32[4,34,2048]{2,1,0:T(8,128)S(1)} %fusion.4), kind=kOutput, calls=%fused_computation.7 | convolution fusion | flops 1712947200 | bytes 15089664 | tf_op jit(solution)/shard_map/smd,df->smf/dot_general | solution.py:36
  44.3 0.0 all-gather.2.cloned.1.call-update
  44.4 0.0 copy-start.1
  44.4 0.0 copy-start.2
  44.4 0.0 copy-start.3
  44.4 24.0 %all-gather.2.cloned.1.call-done = bf16[4,34,8192]{2,1,0:T(8,128)(2,1)} async-done(((bf16[4,34,2048]{2,1,0:T(8,128)(2,1)}), bf16[4,34,8192]{2,1,0:T(8,128)(2,1)}) %all-gather.2.cloned.1.call-update) | async-done | bytes 2228240 | tf_op jit(solution)/shard_map/all_gather | solution.py:41
  68.4 8.5 %fusion = f32[4,34,768]{2,1,0:T(8,128)} fusion(bf16[4,34,8192]{2,1,0:T(8,128)(2,1)} %all-gather.2.cloned.1.call-done, bf16[1,8192,768]{2,1,0:T(8,128)(2,1)} %param.13), kind=kOutput, calls=%fused_computation | convolution fusion | flops 1711276032 | bytes 15228928 | tf_op jit(solution)/shard_map/smf,fd->smd/dot_general | solution.py:39
  76.9 4.6 %all-to-all-start.1 = ((f32[4,34,768]{2,1,0:T(8,128)}), f32[4,34,768]{2,1,0:T(8,128)S(1)}, u32[]{:S(2)}, u32[]{:S(2)}) async-start(f32[4,34,768]{2,1,0:T(8,128)} %fusion), calls=%async_computation.1 | async-start | bytes 983040 | tf_op jit(solution)/shard_map/all_to_all | solution.py:45
  81.5 0.0 copy-done.1
  81.5 0.0 copy-done.2
  81.5 0.0 copy-done.3
  81.6 14.1 %all-to-all-done.1 = f32[4,34,768]{2,1,0:T(8,128)S(1)} async-done(((f32[4,34,768]{2,1,0:T(8,128)}), f32[4,34,768]{2,1,0:T(8,128)S(1)}, u32[]{:S(2)}, u32[]{:S(2)}) %all-to-all-start.1) | async-done | bytes 417824 | tf_op jit(solution)/shard_map/all_to_all | solution.py:45
  95.7 1.2 %multiply_reduce_fusion = (f32[64,4]{0,1:T(4,128)S(1)}, bf16[64,768]{1,0:T(8,128)(2,1)}) fusion(f32[64,768]{1,0:T(8,128)S(1)} %convert_element_type.28, f32[64,4]{0,1:T(4,128)S(1)} %select_reduce_fusion.1, f32[4,34,768]{2,1,0:T(8,128)S(1)} %all-to-all-done.1, s32[4,64]{1,0:T(4,128)S(1)} %copy.20, pred[4,64]{1,0:T(4,128)(4,1)S(1)} %compare_bitcast_fusion), kind=kOutput, calls=%fused_computation.10 | convolution fusion | flops 80970496 | bytes 716032 | tf_op jit(solution)/shard_map/est,esd->ted/dot_general | solution.py:47
  96.9 5.9 %psum.7 = f32[64,4]{0,1:T(4,128)S(1)} all-reduce(f32[64,4]{0,1:T(4,128)S(1)} %get-tuple-element.2), channel_id=1, replica_groups=mesh['groups'=2,'expert'=4,'tensor'=4] {'tensor'}, use_global_device_ids=true, to_apply=%region_5.6 | all-reduce | flops 256 | bytes 2048 | tf_op jit(solution)/shard_map/psum | solution.py:50
  102.8 0.6 select_reduce_fusion
  (4 shorter events, 0.0 us)
Async XLA Ops:
  7.2 1.0 copy-start
  7.2 61.2 %all-gather.2.cloned.1.call-start = ((), (), s32[]{:S(2)}) async-start(), calls=%async_computation.2 | async-start | bytes 3276800 | tf_op jit(solution)/shard_map/all_gather | solution.py:41
  32.7 8.2 %copy-start.4 = (bf16[1,3072,2048]{2,1,0:T(8,128)(2,1)S(1)}, bf16[1,3072,2048]{2,1,0:T(8,128)(2,1)}, u32[]{:S(2)}) copy-start(bf16[1,3072,2048]{2,1,0:T(8,128)(2,1)} %param.12) | copy-start | bytes 37748740
  44.4 37.1 %copy-start.1 = (bf16[64,768]{1,0:T(8,128)(2,1)S(1)}, bf16[64,768]{1,0:T(8,128)(2,1)}, u32[]{:S(2)}) copy-start(bf16[64,768]{1,0:T(8,128)(2,1)} %param.10) | copy-start | bytes 294916
  44.4 37.2 %copy-start.2 = (s32[64,2]{0,1:T(2,128)S(1)}, s32[64,2]{0,1:T(2,128)}, u32[]{:S(2)}) copy-start(s32[64,2]{0,1:T(2,128)} %param.8) | copy-start | bytes 1540
  44.4 37.2 %copy-start.3 = (f32[64,2]{0,1:T(2,128)S(1)}, f32[64,2]{0,1:T(2,128)}, u32[]{:S(2)}) copy-start(f32[64,2]{0,1:T(2,128)} %param.9) | copy-start | bytes 1540
  76.9 18.8 %all-to-all-start.1 = ((f32[4,34,768]{2,1,0:T(8,128)}), f32[4,34,768]{2,1,0:T(8,128)S(1)}, u32[]{:S(2)}, u32[]{:S(2)}) async-start(f32[4,34,768]{2,1,0:T(8,128)} %fusion), calls=%async_computation.1 | async-start | bytes 983040 | tf_op jit(solution)/shard_map/all_to_all | solution.py:45
Sparse Core Ops, SparseCore 0:
  44.5 23.8 all-gather.1
where the time goes:
time: 111 us; the launch traced here: 110 us
  waiting for transfers between devices  38.1 us (34%)
  blocking collectives  30.2 us (27%)
  matrix products  20.4 us (18%)
  between operations  14.1 us (13%)
  starting transfers between devices  4.64 us (4%)
  other arithmetic  1.41 us (1%)
  local copies, waits for them, and re-layouts  1.39 us (1%)
    all_gather x1, waiting for transfers between devices, per_device(): lax.all_gather(hidden, 'tensor', axis=2, tiled=True)  24 us
    all_to_all x1, blocking collectives, per_device(): lax.all_to_all(token_send, 'expert', split_axis=0, concat_axis=0, tiled=T...  14.6 us
    all_to_all x1, waiting for transfers between devices, per_device(): lax.all_to_all(partial_out, 'expert', split_axis=0, concat_axis=0, tiled=...  14.1 us
    all_gather x1, blocking collectives, per_device(): piece = lax.all_gather(arrived, 'tensor', axis=2, tiled=True)  9.65 us
    dot_general x1, matrix products, per_device(): jnp.einsum('smf,fd->smd', lax.all_gather(hidden, 'tensor', axis=2, tiled=...  8.51 us
    dot_general x1, matrix products, per_device(): jnp.einsum('smd,df->smf', piece, w_gate, preferred_element_type=jnp.float32)  6.96 us
    psum x1, blocking collectives, per_device(): dots = lax.psum(local_dots, 'tensor')  5.9 us
    all_to_all x1, starting transfers between devices, per_device(): lax.all_to_all(partial_out, 'expert', split_axis=0, concat_axis=0, tiled=...  4.6 us
  transfers between devices with their start and end apart: 2, of which 2 were waited for; matrix products, arithmetic and copies ran while one was open for 0% of the time, Pallas kernels for 0%

commit v1 on v0

v1 whole, which is shorter than its diff:
```python
import functools

import jax
import jax.numpy as jnp
from jax import lax
from jax.experimental import pallas as pl
from jax.experimental.pallas import tpu as pltpu
from jax.sharding import PartitionSpec as P

EXPERTS = 4
MOST = 34
BF = jnp.bfloat16
F32 = jnp.float32
VMEM_LIMIT = 24 * 1024 * 1024
FF_TILE = 256
K_TILE = 512


def swap(value, axis, bit):
    size = lax.axis_size(axis)
    return lax.ppermute(value, axis, [(i, i ^ bit) for i in range(size)])


def select_kernel(me_ref, ids_ref, tokens_ref, *out_refs):
    rows = tokens_ref.shape[0]
    upper = (
        lax.broadcasted_iota(jnp.int32, (rows, rows), 0)
        < lax.broadcasted_iota(jnp.int32, (rows, rows), 1)
    ).astype(BF)
    slot = lax.broadcasted_iota(jnp.int32, (MOST, rows), 0)
    for step, out_ref in enumerate(out_refs):
        expert = me_ref[0] ^ step
        member = jnp.max((ids_ref[...] == expert).astype(jnp.int32), axis=0, keepdims=True)
        before = jnp.dot(
            jnp.broadcast_to(member.astype(F32), (16, rows)).astype(BF), upper, preferred_element_type=F32
        )[:1]
        place = jnp.where(member > 0, before.astype(jnp.int32), -1)
        pick = (slot == place).astype(F32).astype(BF)
        out_ref[...] = jnp.dot(pick, tokens_ref[...], preferred_element_type=F32).astype(BF)


def select_rows(me, ids_t, tokens):
    width = tokens.shape[1]
    vmem = pl.BlockSpec(memory_space=pltpu.VMEM)
    return pl.pallas_call(
        select_kernel,
        out_shape=[jax.ShapeDtypeStruct((MOST, width), BF)] * EXPERTS,
        in_specs=[pl.BlockSpec(memory_space=pltpu.SMEM), vmem, vmem],
        out_specs=[vmem] * EXPERTS,
        name="select_rows",
    )(me, ids_t, tokens)


def hidden_kernel(parts, t_ref, *refs):
    x_refs = refs[:parts]
    gate_ref, up_ref, out_ref = refs[parts:]
    depth = x_refs[0].shape[1]
    gate = up = None
    for j in range(parts):
        at = pl.ds(pl.multiple_of((t_ref[0] ^ j) * depth, depth), depth)
        x = x_refs[j][...]
        g = jnp.dot(x, gate_ref[0, at, :], preferred_element_type=F32)
        u = jnp.dot(x, up_ref[0, at, :], preferred_element_type=F32)
        gate = g if gate is None else gate + g
        up = u if up is None else up + u
    out_ref[...] = (gate * jax.nn.sigmoid(gate) * up).astype(BF)


def hidden_part(t, xs, gate_weight, up_weight, start, size):
    rows = xs[0].shape[0]
    depth = gate_weight.shape[1]
    first = start // FF_TILE
    whole = lambda x: pl.BlockSpec(x.shape, lambda i, t_ref: (0, 0))
    weight = pl.BlockSpec((1, depth, FF_TILE), lambda i, t_ref: (0, 0, first + i))
    return pl.pallas_call(
        functools.partial(hidden_kernel, len(xs)),
        out_shape=jax.ShapeDtypeStruct((rows, size), BF),
        grid_spec=pltpu.PrefetchScalarGridSpec(
            num_scalar_prefetch=1,
            grid=(size // FF_TILE,),
            in_specs=[whole(x) for x in xs] + [weight, weight],
            out_specs=pl.BlockSpec((rows, FF_TILE), lambda i, t_ref: (0, i)),
        ),
        compiler_params=pltpu.CompilerParams(vmem_limit_bytes=VMEM_LIMIT),
        cost_estimate=pl.CostEstimate(
            flops=4 * rows * depth * size, bytes_accessed=4 * depth * size, transcendentals=rows * size
        ),
        name="hidden_part",
    )(t, *xs, gate_weight, up_weight)


def down_kernel(count, steps, has_sum, last, where_ref, *refs):
    pieces = refs[:count]
    weight_ref = refs[count]
    rest = refs[count + 1:]
    sum_ref = rest[0] if has_sum else None
    outs = rest[1:-1] if has_sum else rest[:-1]
    total = rest[-1]
    here = pl.program_id(0)
    for number, (piece, start) in enumerate(steps):
        @pl.when(here == number)
        def _():
            term = jnp.dot(
                pieces[piece][:, start:start + K_TILE], weight_ref[0], preferred_element_type=F32
            )
            if number > 0:
                total[...] += term
            elif has_sum:
                total[...] = sum_ref[...] + term
            else:
                total[...] = term
            if number == len(steps) - 1:
                if last:
                    value = total[...]
                    for k, out in enumerate(outs):
                        out[...] = value[k * MOST:(k + 1) * MOST].astype(BF)
                else:
                    outs[0][...] = total[...]


def down_part(pieces, where, weight, running, last):
    rows = pieces[0].shape[0]
    width = weight.shape[2]
    steps = [(n, s) for n, p in enumerate(pieces) for s in range(0, p.shape[1], K_TILE)]
    whole = lambda x: pl.BlockSpec(x.shape, lambda i, w: (0, 0))
    has_sum = running is not None
    if last:
        out_shape = [jax.ShapeDtypeStruct((MOST, width), BF)] * EXPERTS
    else:
        out_shape = [jax.ShapeDtypeStruct((rows, width), F32)]
    return pl.pallas_call(
        functools.partial(down_kernel, len(pieces), steps, has_sum, last),
        out_shape=out_shape,
        grid_spec=pltpu.PrefetchScalarGridSpec(
            num_scalar_prefetch=1,
            grid=(len(steps),),
            in_specs=[whole(p) for p in pieces]
            + [pl.BlockSpec((1, K_TILE, width), lambda i, w: (0, w[i], 0))]
            + ([whole(running)] if has_sum else []),
            out_specs=[whole(o) for o in out_shape],
            scratch_shapes=[pltpu.VMEM((rows, width), F32)],
        ),
        compiler_params=pltpu.CompilerParams(vmem_limit_bytes=VMEM_LIMIT),
        cost_estimate=pl.CostEstimate(
            flops=2 * rows * width * K_TILE * len(steps),
            bytes_accessed=2 * width * K_TILE * len(steps),
            transcendentals=0,
        ),
        name="down_part",
    )(jnp.stack(where).astype(jnp.int32), *pieces, weight, *([running] if has_sum else []))


def combine_kernel(place_ref, route_ref, grad_ref, *refs):
    back_refs = refs[:EXPERTS]
    mixed_ref, dots_ref = refs[EXPERTS:]
    rows = grad_ref.shape[0]
    grad = grad_ref[...].astype(F32)
    slot = lax.broadcasted_iota(jnp.int32, (rows, MOST), 1)
    column = lax.broadcasted_iota(jnp.int32, (rows, EXPERTS), 1)
    mixed = None
    dots = jnp.zeros((rows, EXPERTS), F32)
    for k in range(EXPERTS):
        pick = (place_ref[:, k:k + 1] == slot).astype(F32).astype(BF)
        out = jnp.dot(pick, back_refs[k][...], preferred_element_type=F32)
        term = route_ref[:, k:k + 1] * out
        mixed = term if mixed is None else mixed + term
        dots = jnp.where(column == k, jnp.sum(grad * out, axis=1, keepdims=True), dots)
    mixed_ref[...] = mixed.astype(BF)
    dots_ref[...] = dots


def combine(place, route, out_grad, back):
    vmem = pl.BlockSpec(memory_space=pltpu.VMEM)
    rows = out_grad.shape[0]
    return pl.pallas_call(
        combine_kernel,
        out_shape=[
            jax.ShapeDtypeStruct(out_grad.shape, BF),
            jax.ShapeDtypeStruct((rows, EXPERTS), F32),
        ],
        in_specs=[vmem] * (3 + EXPERTS),
        out_specs=[vmem] * 2,
        name="combine",
    )(place, route, out_grad, *back)


CHUNKS = (512, 512, 512, 512)


def per_device(tokens, expert_ids, gate_probs, out_grad, gate_weight, up_weight, down_weight):
    me = lax.axis_index("expert")
    t = lax.axis_index("tensor")
    t_index = t.astype(jnp.int32).reshape(1)
    slab = gate_weight.shape[2]

    rows = select_rows(me.astype(jnp.int32).reshape(1), expert_ids.T, tokens)
    arrived = [rows[0]] + [swap(rows[k], "expert", k) for k in (1, 2, 3)]
    own = jnp.concatenate(arrived, axis=0)
    across = swap(own, "tensor", 2)
    xs = [own, swap(own, "tensor", 1), across, swap(across, "tensor", 1)]

    order = me ^ jnp.arange(EXPERTS, dtype=jnp.int32)
    hits = expert_ids[:, :, None] == order[None, None, :]
    member = jnp.sum(hits.astype(jnp.int32), axis=1)
    place = jnp.where(member > 0, jnp.cumsum(member, axis=0) - member, -1)
    route = jnp.sum(hits.astype(F32) * gate_probs[:, :, None], axis=1)

    starts = [sum(CHUNKS[:i]) for i in range(len(CHUNKS))]
    piece = {}
    for start, size in zip(starts, CHUNKS):
        h = hidden_part(t_index, xs, gate_weight, up_weight, start, size)
        far = swap(h, "tensor", 2)
        piece[start] = [h, swap(h, "tensor", 1), far, swap(far, "tensor", 1)]

    def rows_of(start, size, j):
        return [((t ^ j) * slab + start) // K_TILE + i for i in range(size // K_TILE)]

    near, near_at = [], []
    for start, size in zip(starts, CHUNKS):
        for j in (0, 1):
            near.append(piece[start][j])
            near_at += rows_of(start, size, j)
    running = down_part(near, near_at, down_weight, None, False)[0]
    for start, size in zip(starts, CHUNKS):
        last = start == starts[-1]
        result = down_part(
            piece[start][2:], rows_of(start, size, 2) + rows_of(start, size, 3), down_weight, running, last
        )
        running = result[0]
    back = [result[0]] + [swap(result[k], "expert", k) for k in (1, 2, 3)]
    mixed, dots = combine(place, route, out_grad, back)
    dots = dots + swap(dots, "tensor", 2)
    dots = dots + swap(dots, "tensor", 1)
    gate_grad = jnp.sum(hits.astype(F32) * dots[:, None, :], axis=2)
    return mixed, gate_grad


def per_device_any(tokens, expert_ids, gate_probs, out_grad, gate_weight, up_weight, down_weight):
    span_count = lax.axis_size("expert") // EXPERTS
    hits = expert_ids[:, :, None] == jnp.arange(EXPERTS, dtype=jnp.int32)[None, None, :]
    hit_float = hits.astype(F32)
    member = jnp.sum(hits.astype(jnp.int32), axis=1)
    place = jnp.cumsum(member, axis=0) - member
    placed = (place[None, :, :] == jnp.arange(MOST, dtype=jnp.int32)[:, None, None]) & (member[None, :, :] == 1)
    select = jnp.transpose(placed, (2, 0, 1)).astype(F32)
    route = jnp.sum(hit_float * gate_probs[:, :, None], axis=1)
    rows = jnp.einsum("est,td->esd", select.astype(BF), tokens, preferred_element_type=F32).astype(BF)
    arrived = lax.all_to_all(
        jnp.repeat(rows, span_count, axis=0), "expert", split_axis=0, concat_axis=0, tiled=True
    )
    full = lax.all_gather(arrived, "tensor", axis=2, tiled=True)
    gate = jnp.einsum("smd,df->smf", full, gate_weight[0], preferred_element_type=F32)
    up = jnp.einsum("smd,df->smf", full, up_weight[0], preferred_element_type=F32)
    hidden = (gate * jax.nn.sigmoid(gate) * up).astype(BF)
    partial_out = jnp.einsum(
        "smf,fd->smd",
        lax.all_gather(hidden, "tensor", axis=2, tiled=True),
        down_weight[0],
        preferred_element_type=F32,
    )
    back = lax.all_to_all(partial_out, "expert", split_axis=0, concat_axis=0, tiled=True)
    expert_out = jnp.sum(back.reshape(EXPERTS, span_count, MOST, tokens.shape[1]), axis=1)
    token_out = jnp.einsum("est,esd->ted", select, expert_out, precision=lax.Precision.HIGHEST)
    mixed = jnp.sum(route[:, :, None] * token_out, axis=1).astype(BF)
    dots = lax.psum(jnp.sum(out_grad.astype(F32)[:, None, :] * token_out, axis=2), "tensor")
    return mixed, jnp.sum(hit_float * dots[:, None, :], axis=2)


def solution(mesh):
    in_specs = (
        P(("groups", "expert"), "tensor"),
        P(("groups", "expert"), None),
        P(("groups", "expert"), None),
        P(("groups", "expert"), "tensor"),
        P("expert", None, "tensor"),
        P("expert", None, "tensor"),
        P("expert", None, "tensor"),
    )
    out_specs = (P(("groups", "expert"), "tensor"), P(("groups", "expert"), None))
    direct = mesh.shape["expert"] == EXPERTS and mesh.shape["tensor"] == 4
    return jax.shard_map(
        per_device if direct else per_device_any,
        mesh=mesh, in_specs=in_specs, out_specs=out_specs, check_vma=False,
    )
```

time: 111 us -> 90.6 us (0.82)
  blocking collectives: 30.2 us -> 0 us
  Pallas kernels: 0 us -> 21.2 us
  matrix products: 20.4 us -> 0 us
  local copies, waits for them, and re-layouts: 1.39 us -> 20.6 us
  starting transfers between devices: 4.64 us -> 18.3 us
  waiting for transfers between devices: 38.1 us -> 24.9 us
  between operations: 14.1 us -> 0.98 us
  other arithmetic: 1.41 us -> 4.16 us
    ppermute x0 -> x23, waiting for transfers between devices: none -> 24.9 us  [swap(): return lax.ppermute(value, axis, [(i, i ^ bit) for i in range(size)])]
    all_gather x1 -> x0, waiting for transfers between devices: 24 us -> none  [per_device(): lax.all_gather(hidden, 'tensor', axis=2, tiled=True)]
    pallas_call x0 -> x11, Pallas kernels: none -> 21.2 us  [the longest x4 9.02 us: hidden_part(): pl.pallas_call(functools.partial(hidden_kernel, len(xs)), out_shape=jax.S...]
    dot_general x5 -> x0, matrix products: 20.4 us -> none  [the longest x1 8.51 us: per_device(): jnp.einsum('smf,fd->smd', lax.all_gather(hidden, 'tensor', axis=2, tiled=...]
    unnamed x10 -> x20, local copies, waits for them, and re-layouts: 1.22 us -> 19.6 us
    ppermute x0 -> x23, starting transfers between devices: none -> 18.3 us  [swap(): return lax.ppermute(value, axis, [(i, i ^ bit) for i in range(size)])]
    all_to_all x1 -> x0, blocking collectives: 14.6 us -> none  [per_device(): lax.all_to_all(token_send, 'expert', split_axis=0, concat_axis=0, tiled=T...]
    all_to_all x1 -> x0, waiting for transfers between devices: 14.1 us -> none  [per_device(): lax.all_to_all(partial_out, 'expert', split_axis=0, concat_axis=0, tiled=...]
  transfers between devices with their start and end apart: 2 -> 23, of which waited for: 2 -> 11; matrix products, arithmetic and copies ran while one was open for 0% -> 3% of each run, Pallas kernels for 0% -> 15%
where the time goes in v1:
time: 90.6 us; the launch traced here: 90.1 us
  waiting for transfers between devices  24.9 us (27%)
  Pallas kernels  21.2 us (23%)
  local copies, waits for them, and re-layouts  20.6 us (23%)
  starting transfers between devices  18.3 us (20%)
  other arithmetic  4.16 us (5%)
  between operations  0.98 us (1%)
    ppermute x23, waiting for transfers between devices, swap(): return lax.ppermute(value, axis, [(i, i ^ bit) for i in range(size)])  24.9 us
    unnamed x20, local copies, waits for them, and re-layouts  19.6 us
    ppermute x23, starting transfers between devices, swap(): return lax.ppermute(value, axis, [(i, i ^ bit) for i in range(size)])  18.3 us
    pallas_call x4, Pallas kernels, hidden_part(): pl.pallas_call(functools.partial(hidden_kernel, len(xs)), out_shape=jax.S...  9.02 us
    pallas_call x5, Pallas kernels, down_part(): pl.pallas_call(functools.partial(down_kernel, len(pieces), steps, has_sum...  7.85 us
    pallas_call x1, Pallas kernels, select_rows(): pl.pallas_call(select_kernel, out_shape=[jax.ShapeDtypeStruct((MOST, widt...  2.26 us
    pallas_call x1, Pallas kernels, combine(): pl.pallas_call(combine_kernel, out_shape=[jax.ShapeDtypeStruct(out_grad.s...  2.05 us
  transfers between devices with their start and end apart: 23, of which 11 were waited for; matrix products, arithmetic and copies ran while one was open for 3% of the time, Pallas kernels for 15%

profile of v1, /device:TPU:0, one launch (start us, length us, event | category | flops | bytes accessed | tf_op | source)
XLA Modules:
  0.0 90.1 jit_solution(16061765516969430890)
XLA Ops:
  0.6 2.3 %select_rows.1 = (bf16[34,768]{1,0:T(8,128)(2,1)}, bf16[34,768]{1,0:T(8,128)(2,1)}, bf16[34,768]{1,0:T(8,128)(2,1)}, bf16[34,768]{1,0:T(8,128)(2,1)}) custom-call(s32[1]{0:T(128)} %bitcast.3.me_ref, s32[2,64]{1,0:T(2,128)} %bitcast.19, bf16[64,768]{1,0:T(8,128)(2,1)} %tokens_ref.1), custom_call_target="tpu_custom_call" | custom-call | tf_op jit(solution)/shard_map/select_rows/pallas_call | solution.py:45
  2.9 3.0 %collective-permute-start = (bf16[34,768]{1,0:T(8,128)(2,1)}, bf16[34,768]{1,0:T(8,128)(2,1)S(1)}, u32[]{:S(2)}, u32[]{:S(2)}) collective-permute-start(bf16[34,768]{1,0:T(8,128)(2,1)} %get-tuple-element.13), channel_id=1, source_target_pairs={{0,4},{4,0},{8,12},{12,8},{1,5},{5,1},{9,13},{13,9},{2,6},{6,2},{1... | collective-permute-start | bytes 156680 | tf_op jit(solution)/shard_map/ppermute | solution.py:21
  5.9 2.6 %collective-permute-start.1 = (bf16[34,768]{1,0:T(8,128)(2,1)}, bf16[34,768]{1,0:T(8,128)(2,1)S(1)}, u32[]{:S(2)}, u32[]{:S(2)}) collective-permute-start(bf16[34,768]{1,0:T(8,128)(2,1)} %get-tuple-element.14), channel_id=1, source_target_pairs={{0,8},{4,12},{8,0},{12,4},{1,9},{5,13},{9,1},{13,5},{2,10},{6,14},... | collective-permute-start | bytes 156680 | tf_op jit(solution)/shard_map/ppermute | solution.py:21
  8.5 0.8 fusion
  9.3 3.2 %collective-permute-done.1 = bf16[34,768]{1,0:T(8,128)(2,1)S(1)} collective-permute-done((bf16[34,768]{1,0:T(8,128)(2,1)}, bf16[34,768]{1,0:T(8,128)(2,1)S(1)}, u32[]{:S(2)}, u32[]{:S(2)}) %collective-permute-start.1) | collective-permute-done | bytes 52256 | tf_op jit(solution)/shard_map/ppermute | solution.py:21
  12.5 2.3 %collective-permute-done.2 = bf16[34,768]{1,0:T(8,128)(2,1)S(1)} collective-permute-done((bf16[34,768]{1,0:T(8,128)(2,1)}, bf16[34,768]{1,0:T(8,128)(2,1)S(1)}, u32[]{:S(2)}, u32[]{:S(2)}) %collective-permute-start.2) | collective-permute-done | bytes 52256 | tf_op jit(solution)/shard_map/ppermute | solution.py:21
  14.7 0.9 pad_maximum_fusion.refs_0_
  15.6 1.6 %collective-permute-start.4 = (bf16[136,768]{1,0:T(8,128)(2,1)S(1)}, bf16[136,768]{1,0:T(8,128)(2,1)S(1)}, u32[]{:S(2)}, u32[]{:S(2)}) collective-permute-start(bf16[136,768]{1,0:T(8,128)(2,1)S(1)} %pad_maximum_fusion.refs_0_), channel_id=1, source_target_pairs={{0,2},{1,3},{2,0},{3,1},{4,6},{5,7},{6,4},{7,5},{8,10},{9,11},{10,... | collective-permute-start | bytes 626696 | tf_op jit(solution)/shard_map/ppermute | solution.py:21
  17.2 0.1 copy.17
  17.3 0.1 reduce_window_sum.11
  17.4 0.1 copy.19
  17.6 0.1 pad_add_fusion.3.where_ref
  17.7 0.0 collective-permute-start.3
  17.7 3.8 %collective-permute-done.4.refs_2_ = bf16[136,768]{1,0:T(8,128)(2,1)S(1)} collective-permute-done((bf16[136,768]{1,0:T(8,128)(2,1)S(1)}, bf16[136,768]{1,0:T(8,128)(2,1)S(1)}, u32[]{:S(2)}, u32[]{:S(2)}) %collective-permute-start.4) | collective-permute-done | bytes 208928 | tf_op jit(solution)/shard_map/ppermute | solution.py:21
  21.5 0.6 subtract_select_fusion.place_ref
  22.1 0.8 collective-permute-done.5.refs_3_
  23.0 4.6 %copy-done.2 = bf16[1,3072,2048]{2,1,0:T(8,128)(2,1)S(1)} copy-done((bf16[1,3072,2048]{2,1,0:T(8,128)(2,1)S(1)}, bf16[1,3072,2048]{2,1,0:T(8,128)(2,1)}, u32[]{:S(2)}) %copy-start.2) | copy-done | bytes 12582936
  27.5 4.6 %copy-done.3 = bf16[1,3072,2048]{2,1,0:T(8,128)(2,1)S(1)} copy-done((bf16[1,3072,2048]{2,1,0:T(8,128)(2,1)S(1)}, bf16[1,3072,2048]{2,1,0:T(8,128)(2,1)}, u32[]{:S(2)}) %copy-start.3) | copy-done | bytes 12582936
  32.1 2.2 %hidden_part.7.refs_0_ = bf16[136,512]{1,0:T(8,128)(2,1)S(1)} custom-call(s32[1]{0:T(128)} %bitcast.2.t_ref, bf16[136,768]{1,0:T(8,128)(2,1)S(1)} %pad_maximum_fusion.refs_0_, bf16[136,768]{1,0:T(8,128)(2,1)S(1)} %collective-permute-done.3.refs_1_, bf16[136,768]{1,0:T(8,128)(2,1)S(1)} %collective-permute-done.4.refs_2_, ...), custom_call_target="tpu_custom_call" | custom-call | flops 855638016 | bytes 6291456 | tf_op jit(solution)/shard_map/hidden_part/pallas_call | solution.py:75
  34.4 0.2 collective-permute-start.14
  34.6 2.3 %hidden_part.6.refs_2_ = bf16[136,512]{1,0:T(8,128)(2,1)S(1)} custom-call(s32[1]{0:T(128)} %bitcast.2.t_ref, bf16[136,768]{1,0:T(8,128)(2,1)S(1)} %pad_maximum_fusion.refs_0_, bf16[136,768]{1,0:T(8,128)(2,1)S(1)} %collective-permute-done.3.refs_1_, bf16[136,768]{1,0:T(8,128)(2,1)S(1)} %collective-permute-done.4.refs_2_, ...), custom_call_target="tpu_custom_call" | custom-call | flops 855638016 | bytes 6291456 | tf_op jit(solution)/shard_map/hidden_part/pallas_call | solution.py:75
  36.8 0.4 collective-permute-start.15
  37.3 2.3 %hidden_part.5.refs_4_ = bf16[136,512]{1,0:T(8,128)(2,1)S(1)} custom-call(s32[1]{0:T(128)} %bitcast.2.t_ref, bf16[136,768]{1,0:T(8,128)(2,1)S(1)} %pad_maximum_fusion.refs_0_, bf16[136,768]{1,0:T(8,128)(2,1)S(1)} %collective-permute-done.3.refs_1_, bf16[136,768]{1,0:T(8,128)(2,1)S(1)} %collective-permute-done.4.refs_2_, ...), custom_call_target="tpu_custom_call" | custom-call | flops 855638016 | bytes 6291456 | tf_op jit(solution)/shard_map/hidden_part/pallas_call | solution.py:75
  39.5 0.2 collective-permute-start.16
  39.7 0.1 pad_add_fusion.2.where_ref
  39.8 1.5 %collective-permute-start.12 = (bf16[136,512]{1,0:T(8,128)(2,1)S(1)}, bf16[136,512]{1,0:T(8,128)(2,1)S(1)}, u32[]{:S(2)}, u32[]{:S(2)}) collective-permute-start(bf16[136,512]{1,0:T(8,128)(2,1)S(1)} %hidden_part.7.refs_0_), channel_id=1, source_target_pairs={{0,2},{1,3},{2,0},{3,1},{4,6},{5,7},{6,4},{7,5},{8,10},{9,11},{10,... | collective-permute-start | bytes 417800 | tf_op jit(solution)/shard_map/ppermute | solution.py:21
  41.3 0.5 collective-permute-start.10
  41.9 1.5 %collective-permute-start.8 = (bf16[136,512]{1,0:T(8,128)(2,1)S(1)}, bf16[136,512]{1,0:T(8,128)(2,1)S(1)}, u32[]{:S(2)}, u32[]{:S(2)}) collective-permute-start(bf16[136,512]{1,0:T(8,128)(2,1)S(1)} %hidden_part.5.refs_4_), channel_id=1, source_target_pairs={{0,2},{1,3},{2,0},{3,1},{4,6},{5,7},{6,4},{7,5},{8,10},{9,11},{10,... | collective-permute-start | bytes 417800 | tf_op jit(solution)/shard_map/ppermute | solution.py:21
  43.3 2.3 %hidden_part.4.refs_6_ = bf16[136,512]{1,0:T(8,128)(2,1)S(1)} custom-call(s32[1]{0:T(128)} %bitcast.2.t_ref, bf16[136,768]{1,0:T(8,128)(2,1)S(1)} %pad_maximum_fusion.refs_0_, bf16[136,768]{1,0:T(8,128)(2,1)S(1)} %collective-permute-done.3.refs_1_, bf16[136,768]{1,0:T(8,128)(2,1)S(1)} %collective-permute-done.4.refs_2_, ...), custom_call_target="tpu_custom_call" | custom-call | flops 855638016 | bytes 6291456 | tf_op jit(solution)/shard_map/hidden_part/pallas_call | solution.py:75
  45.6 0.1 collective-permute-start.17
  45.7 0.6 collective-permute-start.6
  46.3 0.1 pad_add_fusion.1.where_ref
  46.4 0.2 collective-permute-start.13
  46.5 2.7 %collective-permute-done.10.refs_0_ = bf16[136,512]{1,0:T(8,128)(2,1)S(1)} collective-permute-done((bf16[136,512]{1,0:T(8,128)(2,1)S(1)}, bf16[136,512]{1,0:T(8,128)(2,1)S(1)}, u32[]{:S(2)}, u32[]{:S(2)}) %collective-permute-start.10) | collective-permute-done | bytes 139296 | tf_op jit(solution)/shard_map/ppermute | solution.py:21
  49.3 3.0 %collective-permute-done.8.refs_0_ = bf16[136,512]{1,0:T(8,128)(2,1)S(1)} collective-permute-done((bf16[136,512]{1,0:T(8,128)(2,1)S(1)}, bf16[136,512]{1,0:T(8,128)(2,1)S(1)}, u32[]{:S(2)}, u32[]{:S(2)}) %collective-permute-start.8) | collective-permute-done | bytes 139296 | tf_op jit(solution)/shard_map/ppermute | solution.py:21
  52.3 0.1 pad_add_fusion.where_ref
  52.4 0.1 stack.83.where_ref
  52.5 2.2 %collective-permute-done.6.refs_0_ = bf16[136,512]{1,0:T(8,128)(2,1)S(1)} collective-permute-done((bf16[136,512]{1,0:T(8,128)(2,1)S(1)}, bf16[136,512]{1,0:T(8,128)(2,1)S(1)}, u32[]{:S(2)}, u32[]{:S(2)}) %collective-permute-start.6) | collective-permute-done | bytes 139296 | tf_op jit(solution)/shard_map/ppermute | solution.py:21
  54.7 4.6 %copy-done = bf16[1,8192,768]{2,1,0:T(8,128)(2,1)S(1)} copy-done((bf16[1,8192,768]{2,1,0:T(8,128)(2,1)S(1)}, bf16[1,8192,768]{2,1,0:T(8,128)(2,1)}, u32[]{:S(2)}) %copy-start) | copy-done | bytes 12582936
  59.3 3.2 %down_part.5.refs_3_ = f32[136,768]{1,0:T(8,128)S(1)} custom-call(s32[8]{0:T(128)S(1)} %stack.83.where_ref, bf16[136,512]{1,0:T(8,128)(2,1)S(1)} %hidden_part.7.refs_0_, bf16[136,512]{1,0:T(8,128)(2,1)S(1)} %collective-permute-done.14.refs_1_, bf16[136,512]{1,0:T(8,128)(2,1)S(1)} %hidden_part.6.refs_2_, ...), custom_call_target="tpu_custom_call" | custom-call | flops 855638016 | bytes 6291456 | tf_op jit(solution)/shard_map/down_part/pallas_call | solution.py:131
  62.5 0.0 copy-start.1
  62.5 4.6 %copy-done.1 = bf16[1,8192,768]{2,1,0:T(8,128)(2,1)S(1)} copy-done((bf16[1,8192,768]{2,1,0:T(8,128)(2,1)S(1)}, bf16[1,8192,768]{2,1,0:T(8,128)(2,1)}, u32[]{:S(2)}) %copy-start.1) | copy-done | bytes 12582936
  67.1 1.2 %down_part.6.refs_3_ = f32[136,768]{1,0:T(8,128)S(1)} custom-call(s32[2]{0:T(128)S(1)} %pad_add_fusion.3.where_ref, bf16[136,512]{1,0:T(8,128)(2,1)S(1)} %collective-permute-done.12.refs_0_, bf16[136,512]{1,0:T(8,128)(2,1)S(1)} %collective-permute-done.13.refs_1_, bf16[1,8192,768]{2,1,0:T(8,128)(2,1)S(1)} %copy-done.1, f32[136,768]{1,0:T(8,128)S(1)} %down_part.5.refs_3_), custom_call_target="tpu_custom_call" | custom-call | flops 213909504 | bytes 1572864 | tf_op jit(solution)/shard_map/down_part/pallas_call | solution.py:131
  68.3 1.2 %down_part.7.refs_3_ = f32[136,768]{1,0:T(8,128)S(1)} custom-call(s32[2]{0:T(128)S(1)} %pad_add_fusion.2.where_ref, bf16[136,512]{1,0:T(8,128)(2,1)S(1)} %collective-permute-done.10.refs_0_, bf16[136,512]{1,0:T(8,128)(2,1)S(1)} %collective-permute-done.11.refs_1_, bf16[1,8192,768]{2,1,0:T(8,128)(2,1)S(1)} %copy-done.1, f32[136,768]{1,0:T(8,128)S(1)} %down_part.6.refs_3_), custom_call_target="tpu_custom_call" | custom-call | flops 213909504 | bytes 1572864 | tf_op jit(solution)/shard_map/down_part/pallas_call | solution.py:131
  69.4 0.0 copy-start.8
  69.5 0.0 copy-start.9
  69.5 1.2 %down_part.8.refs_3_ = f32[136,768]{1,0:T(8,128)S(1)} custom-call(s32[2]{0:T(128)S(1)} %pad_add_fusion.1.where_ref, bf16[136,512]{1,0:T(8,128)(2,1)S(1)} %collective-permute-done.8.refs_0_, bf16[136,512]{1,0:T(8,128)(2,1)S(1)} %collective-permute-done.9.refs_1_, bf16[1,8192,768]{2,1,0:T(8,128)(2,1)S(1)} %copy-done.1, f32[136,768]{1,0:T(8,128)S(1)} %down_part.7.refs_3_), custom_call_target="tpu_custom_call" | custom-call | flops 213909504 | bytes 1572864 | tf_op jit(solution)/shard_map/down_part/pallas_call | solution.py:131
  70.7 1.2 %down_part.9 = (bf16[34,768]{1,0:T(8,128)(2,1)S(1)}, bf16[34,768]{1,0:T(8,128)(2,1)S(1)}, bf16[34,768]{1,0:T(8,128)(2,1)S(1)}, bf16[34,768]{1,0:T(8,128)(2,1)S(1)}) custom-call(s32[2]{0:T(128)S(1)} %pad_add_fusion.where_ref, bf16[136,512]{1,0:T(8,128)(2,1)S(1)} %collective-permute-done.6.refs_0_, bf16[136,512]{1,0:T(8,128)(2,1)S(1)} %collective-permute-done.7.refs_1_, ...), custom_call_target="tpu_custom_call" | custom-call | flops 213909504 | bytes 1572864 | tf_op jit(solution)/shard_map/down_part/pallas_call | solution.py:131
  71.8 0.6 copy-done.4
  72.5 2.1 %collective-permute-start.19 = (bf16[34,768]{1,0:T(8,128)(2,1)S(1)}, bf16[34,768]{1,0:T(8,128)(2,1)S(1)}, u32[]{:S(2)}, u32[]{:S(2)}) collective-permute-start(bf16[34,768]{1,0:T(8,128)(2,1)S(1)} %get-tuple-element.18), channel_id=1, source_target_pairs={{0,8},{4,12},{8,0},{12,4},{1,9},{5,13},{9,1},{13,5},{2,10},{6,14},... | collective-permute-start | bytes 156680 | tf_op jit(solution)/shard_map/ppermute | solution.py:21
  74.5 2.3 %collective-permute-start.20 = (bf16[34,768]{1,0:T(8,128)(2,1)S(1)}, bf16[34,768]{1,0:T(8,128)(2,1)S(1)}, u32[]{:S(2)}, u32[]{:S(2)}) collective-permute-start(bf16[34,768]{1,0:T(8,128)(2,1)S(1)} %get-tuple-element.19), channel_id=1, source_target_pairs={{0,12},{4,8},{8,4},{12,0},{1,13},{5,9},{9,5},{13,1},{2,14},{6,10},... | collective-permute-start | bytes 156680 | tf_op jit(solution)/shard_map/ppermute | solution.py:21
  76.9 0.1 fusion.1
  76.9 0.7 copy.20.route_ref
  77.6 0.5 collective-permute-done.18.refs_1_
  78.1 2.4 %collective-permute-done.19.refs_2_ = bf16[34,768]{1,0:T(8,128)(2,1)S(1)} collective-permute-done((bf16[34,768]{1,0:T(8,128)(2,1)S(1)}, bf16[34,768]{1,0:T(8,128)(2,1)S(1)}, u32[]{:S(2)}, u32[]{:S(2)}) %collective-permute-start.19) | collective-permute-done | bytes 52256 | tf_op jit(solution)/shard_map/ppermute | solution.py:21
  80.6 0.6 copy-done.6
  81.2 0.0 copy-done.7
  81.2 2.1 %combine.1 = (bf16[64,768]{1,0:T(8,128)(2,1)}, f32[64,4]{1,0:T(8,128)}) custom-call(s32[64,4]{1,0:T(8,128)} %subtract_select_fusion.place_ref, f32[64,4]{1,0:T(8,128)} %copy.20.route_ref, bf16[64,768]{1,0:T(8,128)(2,1)} %grad_ref.1, bf16[34,768]{1,0:T(8,128)(2,1)} %copy-done.4, bf16[34,768]{1,0:T(8,128)(2,1)} %copy-done.5, bf16[34,768]{1,0:T(8,128)(2,1)} %copy-done.6, ...), custom_call_target="tpu_custom_call" | custom-call | tf_op jit(solution)/shard_map/combine/pallas_call | solution.py:175
  83.3 1.5 %collective-permute-start.21 = (f32[64,4]{1,0:T(8,128)}, f32[64,4]{1,0:T(8,128)S(1)}, u32[]{:S(2)}, u32[]{:S(2)}) collective-permute-start(f32[64,4]{1,0:T(8,128)} %get-tuple-element.21), channel_id=1, source_target_pairs={{0,2},{1,3},{2,0},{3,1},{4,6},{5,7},{6,4},{7,5},{8,10},{9,11},{10,... | collective-permute-start | bytes 3080 | tf_op jit(solution)/shard_map/ppermute | solution.py:21
  84.8 2.6 %collective-permute-done.21 = f32[64,4]{1,0:T(8,128)S(1)} collective-permute-done((f32[64,4]{1,0:T(8,128)}, f32[64,4]{1,0:T(8,128)S(1)}, u32[]{:S(2)}, u32[]{:S(2)}) %collective-permute-start.21) | collective-permute-done | bytes 1056 | tf_op jit(solution)/shard_map/ppermute | solution.py:21
  87.4 0.8 add.70
  88.2 1.2 %collective-permute-done.22 = f32[64,4]{1,0:T(8,128)S(1)} collective-permute-done((f32[64,4]{1,0:T(8,128)S(1)}, f32[64,4]{1,0:T(8,128)S(1)}, u32[]{:S(2)}, u32[]{:S(2)}) %collective-permute-start.22) | collective-permute-done | bytes 1056 | tf_op jit(solution)/shard_map/ppermute | solution.py:21
  89.4 0.1 copy.21
  89.4 0.7 fusion.2
  (32 shorter events, 0.1 us)
Async XLA Ops:
  2.9 6.4 %collective-permute-start = (bf16[34,768]{1,0:T(8,128)(2,1)}, bf16[34,768]{1,0:T(8,128)(2,1)S(1)}, u32[]{:S(2)}, u32[]{:S(2)}) collective-permute-start(bf16[34,768]{1,0:T(8,128)(2,1)} %get-tuple-element.13), channel_id=1, source_target_pairs={{0,4},{4,0},{8,12},{12,8},{1,5},{5,1},{9,13},{13,9},{2,6},{6,2},{1... | collective-permute-start | bytes 156680 | tf_op jit(solution)/shard_map/ppermute | solution.py:21
  5.9 6.6 %collective-permute-start.1 = (bf16[34,768]{1,0:T(8,128)(2,1)}, bf16[34,768]{1,0:T(8,128)(2,1)S(1)}, u32[]{:S(2)}, u32[]{:S(2)}) collective-permute-start(bf16[34,768]{1,0:T(8,128)(2,1)} %get-tuple-element.14), channel_id=1, source_target_pairs={{0,8},{4,12},{8,0},{12,4},{1,9},{5,13},{9,1},{13,5},{2,10},{6,14},... | collective-permute-start | bytes 156680 | tf_op jit(solution)/shard_map/ppermute | solution.py:21
  8.5 6.2 %collective-permute-start.2 = (bf16[34,768]{1,0:T(8,128)(2,1)}, bf16[34,768]{1,0:T(8,128)(2,1)S(1)}, u32[]{:S(2)}, u32[]{:S(2)}) collective-permute-start(bf16[34,768]{1,0:T(8,128)(2,1)} %get-tuple-element.15), channel_id=1, source_target_pairs={{0,12},{4,8},{8,4},{12,0},{1,13},{5,9},{9,5},{13,1},{2,14},{6,10},... | collective-permute-start | bytes 156680 | tf_op jit(solution)/shard_map/ppermute | solution.py:21
  15.6 5.9 %collective-permute-start.4 = (bf16[136,768]{1,0:T(8,128)(2,1)S(1)}, bf16[136,768]{1,0:T(8,128)(2,1)S(1)}, u32[]{:S(2)}, u32[]{:S(2)}) collective-permute-start(bf16[136,768]{1,0:T(8,128)(2,1)S(1)} %pad_maximum_fusion.refs_0_), channel_id=1, source_target_pairs={{0,2},{1,3},{2,0},{3,1},{4,6},{5,7},{6,4},{7,5},{8,10},{9,11},{10,... | collective-permute-start | bytes 626696 | tf_op jit(solution)/shard_map/ppermute | solution.py:21
  17.7 4.4 %collective-permute-start.3 = (bf16[136,768]{1,0:T(8,128)(2,1)S(1)}, bf16[136,768]{1,0:T(8,128)(2,1)S(1)}, u32[]{:S(2)}, u32[]{:S(2)}) collective-permute-start(bf16[136,768]{1,0:T(8,128)(2,1)S(1)} %pad_maximum_fusion.refs_0_), channel_id=1, source_target_pairs={{0,1},{1,0},{2,3},{3,2},{4,5},{5,4},{6,7},{7,6},{8,9},{9,8},{10,11... | collective-permute-start | bytes 626696 | tf_op jit(solution)/shard_map/ppermute | solution.py:21
  21.5 1.5 %collective-permute-start.5 = (bf16[136,768]{1,0:T(8,128)(2,1)S(1)}, bf16[136,768]{1,0:T(8,128)(2,1)S(1)}, u32[]{:S(2)}, u32[]{:S(2)}) collective-permute-start(bf16[136,768]{1,0:T(8,128)(2,1)S(1)} %collective-permute-done.4.refs_2_), channel_id=1, source_target_pairs={{0,1},{1,0},{2,3},{3,2},{4,5},{5,4},{6,7},{7,6},{8,9},{9,8},{10,11... | collective-permute-start | bytes 626696 | tf_op jit(solution)/shard_map/ppermute | solution.py:21
  23.0 4.6 %copy-start.2 = (bf16[1,3072,2048]{2,1,0:T(8,128)(2,1)S(1)}, bf16[1,3072,2048]{2,1,0:T(8,128)(2,1)}, u32[]{:S(2)}) copy-start(bf16[1,3072,2048]{2,1,0:T(8,128)(2,1)} %refs_4_.7) | copy-start | bytes 37748740
  27.5 4.6 %copy-start.3 = (bf16[1,3072,2048]{2,1,0:T(8,128)(2,1)S(1)}, bf16[1,3072,2048]{2,1,0:T(8,128)(2,1)}, u32[]{:S(2)}) copy-start(bf16[1,3072,2048]{2,1,0:T(8,128)(2,1)} %refs_5_.7) | copy-start | bytes 37748740
  34.4 7.5 %collective-permute-start.14 = (bf16[136,512]{1,0:T(8,128)(2,1)S(1)}, bf16[136,512]{1,0:T(8,128)(2,1)S(1)}, u32[]{:S(2)}, u32[]{:S(2)}) collective-permute-start(bf16[136,512]{1,0:T(8,128)(2,1)S(1)} %hidden_part.7.refs_0_), channel_id=1, source_target_pairs={{0,1},{1,0},{2,3},{3,2},{4,5},{5,4},{6,7},{7,6},{8,9},{9,8},{10,11... | collective-permute-start | bytes 417800 | tf_op jit(solution)/shard_map/ppermute | solution.py:21
  36.8 8.8 %collective-permute-start.15 = (bf16[136,512]{1,0:T(8,128)(2,1)S(1)}, bf16[136,512]{1,0:T(8,128)(2,1)S(1)}, u32[]{:S(2)}, u32[]{:S(2)}) collective-permute-start(bf16[136,512]{1,0:T(8,128)(2,1)S(1)} %hidden_part.6.refs_2_), channel_id=1, source_target_pairs={{0,1},{1,0},{2,3},{3,2},{4,5},{5,4},{6,7},{7,6},{8,9},{9,8},{10,11... | collective-permute-start | bytes 417800 | tf_op jit(solution)/shard_map/ppermute | solution.py:21
  39.5 6.2 %collective-permute-start.16 = (bf16[136,512]{1,0:T(8,128)(2,1)S(1)}, bf16[136,512]{1,0:T(8,128)(2,1)S(1)}, u32[]{:S(2)}, u32[]{:S(2)}) collective-permute-start(bf16[136,512]{1,0:T(8,128)(2,1)S(1)} %hidden_part.5.refs_4_), channel_id=1, source_target_pairs={{0,1},{1,0},{2,3},{3,2},{4,5},{5,4},{6,7},{7,6},{8,9},{9,8},{10,11... | collective-permute-start | bytes 417800 | tf_op jit(solution)/shard_map/ppermute | solution.py:21
  39.8 6.6 %collective-permute-start.12 = (bf16[136,512]{1,0:T(8,128)(2,1)S(1)}, bf16[136,512]{1,0:T(8,128)(2,1)S(1)}, u32[]{:S(2)}, u32[]{:S(2)}) collective-permute-start(bf16[136,512]{1,0:T(8,128)(2,1)S(1)} %hidden_part.7.refs_0_), channel_id=1, source_target_pairs={{0,2},{1,3},{2,0},{3,1},{4,6},{5,7},{6,4},{7,5},{8,10},{9,11},{10,... | collective-permute-start | bytes 417800 | tf_op jit(solution)/shard_map/ppermute | solution.py:21
  41.3 8.0 %collective-permute-start.10 = (bf16[136,512]{1,0:T(8,128)(2,1)S(1)}, bf16[136,512]{1,0:T(8,128)(2,1)S(1)}, u32[]{:S(2)}, u32[]{:S(2)}) collective-permute-start(bf16[136,512]{1,0:T(8,128)(2,1)S(1)} %hidden_part.6.refs_2_), channel_id=1, source_target_pairs={{0,2},{1,3},{2,0},{3,1},{4,6},{5,7},{6,4},{7,5},{8,10},{9,11},{10,... | collective-permute-start | bytes 417800 | tf_op jit(solution)/shard_map/ppermute | solution.py:21
  41.9 10.4 %collective-permute-start.8 = (bf16[136,512]{1,0:T(8,128)(2,1)S(1)}, bf16[136,512]{1,0:T(8,128)(2,1)S(1)}, u32[]{:S(2)}, u32[]{:S(2)}) collective-permute-start(bf16[136,512]{1,0:T(8,128)(2,1)S(1)} %hidden_part.5.refs_4_), channel_id=1, source_target_pairs={{0,2},{1,3},{2,0},{3,1},{4,6},{5,7},{6,4},{7,5},{8,10},{9,11},{10,... | collective-permute-start | bytes 417800 | tf_op jit(solution)/shard_map/ppermute | solution.py:21
  45.6 9.1 %collective-permute-start.17 = (bf16[136,512]{1,0:T(8,128)(2,1)S(1)}, bf16[136,512]{1,0:T(8,128)(2,1)S(1)}, u32[]{:S(2)}, u32[]{:S(2)}) collective-permute-start(bf16[136,512]{1,0:T(8,128)(2,1)S(1)} %hidden_part.4.refs_6_), channel_id=1, source_target_pairs={{0,1},{1,0},{2,3},{3,2},{4,5},{5,4},{6,7},{7,6},{8,9},{9,8},{10,11... | collective-permute-start | bytes 417800 | tf_op jit(solution)/shard_map/ppermute | solution.py:21
  45.7 9.0 %collective-permute-start.6 = (bf16[136,512]{1,0:T(8,128)(2,1)S(1)}, bf16[136,512]{1,0:T(8,128)(2,1)S(1)}, u32[]{:S(2)}, u32[]{:S(2)}) collective-permute-start(bf16[136,512]{1,0:T(8,128)(2,1)S(1)} %hidden_part.4.refs_6_), channel_id=1, source_target_pairs={{0,2},{1,3},{2,0},{3,1},{4,6},{5,7},{6,4},{7,5},{8,10},{9,11},{10,... | collective-permute-start | bytes 417800 | tf_op jit(solution)/shard_map/ppermute | solution.py:21
  46.4 16.1 %collective-permute-start.13 = (bf16[136,512]{1,0:T(8,128)(2,1)S(1)}, bf16[136,512]{1,0:T(8,128)(2,1)S(1)}, u32[]{:S(2)}, u32[]{:S(2)}) collective-permute-start(bf16[136,512]{1,0:T(8,128)(2,1)S(1)} %collective-permute-done.12.refs_0_), channel_id=1, source_target_pairs={{0,1},{1,0},{2,3},{3,2},{4,5},{5,4},{6,7},{7,6},{8,9},{9,8},{10,11... | collective-permute-start | bytes 417800 | tf_op jit(solution)/shard_map/ppermute | solution.py:21
  49.3 19.0 %collective-permute-start.11 = (bf16[136,512]{1,0:T(8,128)(2,1)S(1)}, bf16[136,512]{1,0:T(8,128)(2,1)S(1)}, u32[]{:S(2)}, u32[]{:S(2)}) collective-permute-start(bf16[136,512]{1,0:T(8,128)(2,1)S(1)} %collective-permute-done.10.refs_0_), channel_id=1, source_target_pairs={{0,1},{1,0},{2,3},{3,2},{4,5},{5,4},{6,7},{7,6},{8,9},{9,8},{10,11... | collective-permute-start | bytes 417800 | tf_op jit(solution)/shard_map/ppermute | solution.py:21
  52.3 17.2 %collective-permute-start.9 = (bf16[136,512]{1,0:T(8,128)(2,1)S(1)}, bf16[136,512]{1,0:T(8,128)(2,1)S(1)}, u32[]{:S(2)}, u32[]{:S(2)}) collective-permute-start(bf16[136,512]{1,0:T(8,128)(2,1)S(1)} %collective-permute-done.8.refs_0_), channel_id=1, source_target_pairs={{0,1},{1,0},{2,3},{3,2},{4,5},{5,4},{6,7},{7,6},{8,9},{9,8},{10,11... | collective-permute-start | bytes 417800 | tf_op jit(solution)/shard_map/ppermute | solution.py:21
  54.7 15.9 %collective-permute-start.7 = (bf16[136,512]{1,0:T(8,128)(2,1)S(1)}, bf16[136,512]{1,0:T(8,128)(2,1)S(1)}, u32[]{:S(2)}, u32[]{:S(2)}) collective-permute-start(bf16[136,512]{1,0:T(8,128)(2,1)S(1)} %collective-permute-done.6.refs_0_), channel_id=1, source_target_pairs={{0,1},{1,0},{2,3},{3,2},{4,5},{5,4},{6,7},{7,6},{8,9},{9,8},{10,11... | collective-permute-start | bytes 417800 | tf_op jit(solution)/shard_map/ppermute | solution.py:21
  54.7 4.6 %copy-start = (bf16[1,8192,768]{2,1,0:T(8,128)(2,1)S(1)}, bf16[1,8192,768]{2,1,0:T(8,128)(2,1)}, u32[]{:S(2)}) copy-start(bf16[1,8192,768]{2,1,0:T(8,128)(2,1)} %refs_2_.7) | copy-start | bytes 37748740
  62.5 4.6 %copy-start.1 = (bf16[1,8192,768]{2,1,0:T(8,128)(2,1)S(1)}, bf16[1,8192,768]{2,1,0:T(8,128)(2,1)}, u32[]{:S(2)}) copy-start(bf16[1,8192,768]{2,1,0:T(8,128)(2,1)} %refs_2_.7) | copy-start | bytes 37748740
  69.4 7.4 %copy-start.8 = (s32[64,2]{0,1:T(2,128)S(1)}, s32[64,2]{0,1:T(2,128)}, u32[]{:S(2)}) copy-start(s32[64,2]{0,1:T(2,128)} %param.8) | copy-start | bytes 1540
  69.5 7.4 %copy-start.9 = (f32[64,2]{0,1:T(2,128)S(1)}, f32[64,2]{0,1:T(2,128)}, u32[]{:S(2)}) copy-start(f32[64,2]{0,1:T(2,128)} %param.9) | copy-start | bytes 1540
  71.8 0.6 copy-start.4
  72.5 5.6 %collective-permute-start.18 = (bf16[34,768]{1,0:T(8,128)(2,1)S(1)}, bf16[34,768]{1,0:T(8,128)(2,1)S(1)}, u32[]{:S(2)}, u32[]{:S(2)}) collective-permute-start(bf16[34,768]{1,0:T(8,128)(2,1)S(1)} %get-tuple-element.17), channel_id=1, source_target_pairs={{0,4},{4,0},{8,12},{12,8},{1,5},{5,1},{9,13},{13,9},{2,6},{6,2},{1... | collective-permute-start | bytes 156680 | tf_op jit(solution)/shard_map/ppermute | solution.py:21
  72.5 8.1 %collective-permute-start.19 = (bf16[34,768]{1,0:T(8,128)(2,1)S(1)}, bf16[34,768]{1,0:T(8,128)(2,1)S(1)}, u32[]{:S(2)}, u32[]{:S(2)}) collective-permute-start(bf16[34,768]{1,0:T(8,128)(2,1)S(1)} %get-tuple-element.18), channel_id=1, source_target_pairs={{0,8},{4,12},{8,0},{12,4},{1,9},{5,13},{9,1},{13,5},{2,10},{6,14},... | collective-permute-start | bytes 156680 | tf_op jit(solution)/shard_map/ppermute | solution.py:21
  74.5 6.0 %collective-permute-start.20 = (bf16[34,768]{1,0:T(8,128)(2,1)S(1)}, bf16[34,768]{1,0:T(8,128)(2,1)S(1)}, u32[]{:S(2)}, u32[]{:S(2)}) collective-permute-start(bf16[34,768]{1,0:T(8,128)(2,1)S(1)} %get-tuple-element.19), channel_id=1, source_target_pairs={{0,12},{4,8},{8,4},{12,0},{1,13},{5,9},{9,5},{13,1},{2,14},{6,10},... | collective-permute-start | bytes 156680 | tf_op jit(solution)/shard_map/ppermute | solution.py:21
  78.1 2.5 %copy-start.5 = (bf16[34,768]{1,0:T(8,128)(2,1)}, bf16[34,768]{1,0:T(8,128)(2,1)S(1)}, u32[]{:S(2)}) copy-start(bf16[34,768]{1,0:T(8,128)(2,1)S(1)} %collective-permute-done.18.refs_1_) | copy-start | bytes 156676
  80.6 0.6 copy-start.6
  80.6 0.6 copy-start.7
  83.3 4.1 %collective-permute-start.21 = (f32[64,4]{1,0:T(8,128)}, f32[64,4]{1,0:T(8,128)S(1)}, u32[]{:S(2)}, u32[]{:S(2)}) collective-permute-start(f32[64,4]{1,0:T(8,128)} %get-tuple-element.21), channel_id=1, source_target_pairs={{0,2},{1,3},{2,0},{3,1},{4,6},{5,7},{6,4},{7,5},{8,10},{9,11},{10,... | collective-permute-start | bytes 3080 | tf_op jit(solution)/shard_map/ppermute | solution.py:21
  88.2 1.2 %collective-permute-start.22 = (f32[64,4]{1,0:T(8,128)S(1)}, f32[64,4]{1,0:T(8,128)S(1)}, u32[]{:S(2)}, u32[]{:S(2)}) collective-permute-start(f32[64,4]{1,0:T(8,128)S(1)} %add.70), channel_id=1, source_target_pairs={{0,1},{1,0},{2,3},{3,2},{4,5},{5,4},{6,7},{7,6},{8,9},{9,8},{10,11... | collective-permute-start | bytes 3080 | tf_op jit(solution)/shard_map/ppermute | solution.py:21

commit v2 on v1

--- a/solution.py
+++ b/solution.py
@@ -12,6 +12,7 @@
 BF = jnp.bfloat16
 F32 = jnp.float32
 VMEM_LIMIT = 24 * 1024 * 1024
+SMALL_LIMIT = 4 * 1024 * 1024
 FF_TILE = 256
 K_TILE = 512
 
@@ -47,13 +48,16 @@
         out_shape=[jax.ShapeDtypeStruct((MOST, width), BF)] * EXPERTS,
         in_specs=[pl.BlockSpec(memory_space=pltpu.SMEM), vmem, vmem],
         out_specs=[vmem] * EXPERTS,
+        compiler_params=pltpu.CompilerParams(vmem_limit_bytes=SMALL_LIMIT),
+        cost_estimate=pl.CostEstimate(flops=1000, bytes_accessed=1000, transcendentals=0),
         name="select_rows",
     )(me, ids_t, tokens)
 
 
 def hidden_kernel(parts, t_ref, *refs):
     x_refs = refs[:parts]
-    gate_ref, up_ref, out_ref = refs[parts:]
+    gate_ref, up_ref = refs[parts:parts + 2]
+    out_ref = refs[-1]
     depth = x_refs[0].shape[1]
     gate = up = None
     for j in range(parts):
@@ -66,7 +70,7 @@
     out_ref[...] = (gate * jax.nn.sigmoid(gate) * up).astype(BF)
 
 
-def hidden_part(t, xs, gate_weight, up_weight, start, size):
+def hidden_part(t, xs, gate_weight, up_weight, start, size, after=()):
     rows = xs[0].shape[0]
     depth = gate_weight.shape[1]
     first = start // FF_TILE
@@ -78,15 +82,13 @@
         grid_spec=pltpu.PrefetchScalarGridSpec(
             num_scalar_prefetch=1,
             grid=(size // FF_TILE,),
-            in_specs=[whole(x) for x in xs] + [weight, weight],
+            in_specs=[whole(x) for x in xs] + [weight, weight] + [pl.BlockSpec(memory_space=pl.ANY)] * len(after),
             out_specs=pl.BlockSpec((rows, FF_TILE), lambda i, t_ref: (0, i)),
         ),
         compiler_params=pltpu.CompilerParams(vmem_limit_bytes=VMEM_LIMIT),
-        cost_estimate=pl.CostEstimate(
-            flops=4 * rows * depth * size, bytes_accessed=4 * depth * size, transcendentals=rows * size
-        ),
+        cost_estimate=pl.CostEstimate(flops=1000, bytes_accessed=1000, transcendentals=0),
         name="hidden_part",
-    )(t, *xs, gate_weight, up_weight)
+    )(t, *xs, gate_weight, up_weight, *after)
 
 
 def down_kernel(count, steps, has_sum, last, where_ref, *refs):
@@ -118,10 +120,18 @@
                     outs[0][...] = total[...]
 
 
-def down_part(pieces, where, weight, running, last):
+def down_part(t, slab, pieces, where, weight, running, last):
     rows = pieces[0].shape[0]
     width = weight.shape[2]
     steps = [(n, s) for n, p in enumerate(pieces) for s in range(0, p.shape[1], K_TILE)]
+    at = [(where[n][0], (where[n][1] + s) // K_TILE) for n, s in steps]
+
+    def weight_row(i, t_ref):
+        row = jnp.int32(0)
+        for number, (j, tile) in enumerate(at):
+            row = jnp.where(i == number, (t_ref[0] ^ j) * (slab // K_TILE) + tile, row)
+        return 0, row, 0
+
     whole = lambda x: pl.BlockSpec(x.shape, lambda i, w: (0, 0))
     has_sum = running is not None
     if last:
@@ -135,19 +145,19 @@
             num_scalar_prefetch=1,
             grid=(len(steps),),
             in_specs=[whole(p) for p in pieces]
-            + [pl.BlockSpec((1, K_TILE, width), lambda i, w: (0, w[i], 0))]
+            + [pl.BlockSpec((1, K_TILE, width), weight_row)]
             + ([whole(running)] if has_sum else []),
             out_specs=[whole(o) for o in out_shape],
             scratch_shapes=[pltpu.VMEM((rows, width), F32)],
         ),
         compiler_params=pltpu.CompilerParams(vmem_limit_bytes=VMEM_LIMIT),
         cost_estimate=pl.CostEstimate(
-            flops=2 * rows * width * K_TILE * len(steps),
-            bytes_accessed=2 * width * K_TILE * len(steps),
+            flops=4 * rows * width * K_TILE * len(steps),
+            bytes_accessed=4 * width * K_TILE * len(steps),
             transcendentals=0,
         ),
         name="down_part",
-    )(jnp.stack(where).astype(jnp.int32), *pieces, weight, *([running] if has_sum else []))
+    )(t, *pieces, weight, *([running] if has_sum else []))
 
 
 def combine_kernel(place_ref, route_ref, grad_ref, *refs):
@@ -180,6 +190,8 @@
         ],
         in_specs=[vmem] * (3 + EXPERTS),
         out_specs=[vmem] * 2,
+        compiler_params=pltpu.CompilerParams(vmem_limit_bytes=SMALL_LIMIT),
+        cost_estimate=pl.CostEstimate(flops=1000, bytes_accessed=1000, transcendentals=0),
         name="combine",
     )(place, route, out_grad, *back)
 
@@ -192,6 +204,9 @@
     t = lax.axis_index("tensor")
     t_index = t.astype(jnp.int32).reshape(1)
     slab = gate_weight.shape[2]
+    gate_weight, up_weight, down_weight = (
+        pltpu.with_memory_space_constraint(w, pltpu.HBM) for w in (gate_weight, up_weight, down_weight)
+    )
 
     rows = select_rows(me.astype(jnp.int32).reshape(1), expert_ids.T, tokens)
     arrived = [rows[0]] + [swap(rows[k], "expert", k) for k in (1, 2, 3)]
@@ -206,25 +221,22 @@
     route = jnp.sum(hits.astype(F32) * gate_probs[:, :, None], axis=1)
 
     starts = [sum(CHUNKS[:i]) for i in range(len(CHUNKS))]
-    piece = {}
-    for start, size in zip(starts, CHUNKS):
-        h = hidden_part(t_index, xs, gate_weight, up_weight, start, size)
+    pieces = []
+    for i, (start, size) in enumerate(zip(starts, CHUNKS)):
+        after = [pieces[i - 2][2]] if i >= 2 else []
+        h = hidden_part(t_index, xs, gate_weight, up_weight, start, size, after)
         far = swap(h, "tensor", 2)
-        piece[start] = [h, swap(h, "tensor", 1), far, swap(far, "tensor", 1)]
-
-    def rows_of(start, size, j):
-        return [((t ^ j) * slab + start) // K_TILE + i for i in range(size // K_TILE)]
-
-    near, near_at = [], []
-    for start, size in zip(starts, CHUNKS):
-        for j in (0, 1):
-            near.append(piece[start][j])
-            near_at += rows_of(start, size, j)
-    running = down_part(near, near_at, down_weight, None, False)[0]
-    for start, size in zip(starts, CHUNKS):
-        last = start == starts[-1]
+        pieces.append([h, swap(h, "tensor", 1), far, swap(far, "tensor", 1)])
+    running = None
+    for i, start in enumerate(starts):
+        use = [(i, 2), (i, 3)]
+        if i == 0:
+            use = [(0, 0), (0, 1)] + use
+        if i + 1 < len(starts):
+            use += [(i + 1, 0), (i + 1, 1)]
         result = down_part(
-            piece[start][2:], rows_of(start, size, 2) + rows_of(start, size, 3), down_weight, running, last
+            t_index, slab, [pieces[n][j] for n, j in use], [(j, starts[n]) for n, j in use], down_weight, running,
+            i + 1 == len(starts),
         )
         running = result[0]
     back = [result[0]] + [swap(result[k], "expert", k) for k in (1, 2, 3)]

time: 90.6 us -> 75.6 us (0.83)
  local copies, waits for them, and re-layouts: 20.6 us -> 1.97 us
  Pallas kernels: 21.2 us -> 29.2 us
  other arithmetic: 4.16 us -> 1.67 us
  waiting for transfers between devices: 24.9 us -> 23.4 us
    unnamed x20 -> x10, local copies, waits for them, and re-layouts: 19.6 us -> 1.58 us
    pallas_call x5 -> x4, Pallas kernels: 7.85 us -> 13.2 us  [down_part(): pl.pallas_call(functools.partial(down_kernel, len(pieces), steps, has_sum...]
    pallas_call x4, Pallas kernels: 9.02 us -> 14.2 us  [hidden_part(): pl.pallas_call(functools.partial(hidden_kernel, len(xs)), out_shape=jax.S...]
    pallas_call x1, Pallas kernels: 2.26 us -> 0.69 us  [select_rows(): pl.pallas_call(select_kernel, out_shape=[jax.ShapeDtypeStruct((MOST, widt...]
    ppermute x23, waiting for transfers between devices: 24.9 us -> 23.4 us  [swap(): return lax.ppermute(value, axis, [(i, i ^ bit) for i in range(size)])]
    pallas_call x1, Pallas kernels: 2.05 us -> 1.04 us  [combine(): pl.pallas_call(combine_kernel, out_shape=[jax.ShapeDtypeStruct(out_grad.s...]
  transfers between devices with their start and end apart: 23 -> 23, of which waited for: 11 -> 10; matrix products, arithmetic and copies ran while one was open for 3% -> 2% of each run, Pallas kernels for 15% -> 29%
where the time goes in v2:
time: 75.6 us; the launch traced here: 75.2 us
  Pallas kernels  29.2 us (39%)
  waiting for transfers between devices  23.4 us (31%)
  starting transfers between devices  18.1 us (24%)
  local copies, waits for them, and re-layouts  1.97 us (3%)
  other arithmetic  1.67 us (2%)
  between operations  0.83 us (1%)
    ppermute x23, waiting for transfers between devices, swap(): return lax.ppermute(value, axis, [(i, i ^ bit) for i in range(size)])  23.4 us
    ppermute x23, starting transfers between devices, swap(): return lax.ppermute(value, axis, [(i, i ^ bit) for i in range(size)])  18.1 us
    pallas_call x4, Pallas kernels, hidden_part(): pl.pallas_call(functools.partial(hidden_kernel, len(xs)), out_shape=jax.S...  14.2 us
    pallas_call x4, Pallas kernels, down_part(): pl.pallas_call(functools.partial(down_kernel, len(pieces), steps, has_sum...  13.2 us
    unnamed x10, local copies, waits for them, and re-layouts  1.58 us
  transfers between devices with their start and end apart: 23, of which 10 were waited for; matrix products, arithmetic and copies ran while one was open for 2% of the time, Pallas kernels for 29%

profile of v2, /device:TPU:0, one launch (start us, length us, event | category | flops | bytes accessed | tf_op | source)
XLA Modules:
  0.0 75.2 jit_solution(8149940284573961812)
XLA Ops:
  0.6 0.9 %copy-done = bf16[64,768]{1,0:T(8,128)(2,1)S(1)} copy-done((bf16[64,768]{1,0:T(8,128)(2,1)S(1)}, bf16[64,768]{1,0:T(8,128)(2,1)}, u32[]{:S(2)}) %copy-start) | copy-done | bytes 98328
  1.5 0.7 copy-done.2
  2.2 0.7 select_rows.1
  2.9 3.1 %collective-permute-start = (bf16[34,768]{1,0:T(8,128)(2,1)S(1)}, bf16[34,768]{1,0:T(8,128)(2,1)S(1)}, u32[]{:S(2)}, u32[]{:S(2)}) collective-permute-start(bf16[34,768]{1,0:T(8,128)(2,1)S(1)} %get-tuple-element.13), channel_id=1, source_target_pairs={{0,4},{4,0},{8,12},{12,8},{1,5},{5,1},{9,13},{13,9},{2,6},{6,2},{1... | collective-permute-start | bytes 156680 | tf_op jit(solution)/shard_map/ppermute | solution.py:22
  6.0 2.6 %collective-permute-start.1 = (bf16[34,768]{1,0:T(8,128)(2,1)S(1)}, bf16[34,768]{1,0:T(8,128)(2,1)S(1)}, u32[]{:S(2)}, u32[]{:S(2)}) collective-permute-start(bf16[34,768]{1,0:T(8,128)(2,1)S(1)} %get-tuple-element.14), channel_id=1, source_target_pairs={{0,8},{4,12},{8,0},{12,4},{1,9},{5,13},{9,1},{13,5},{2,10},{6,14},... | collective-permute-start | bytes 156680 | tf_op jit(solution)/shard_map/ppermute | solution.py:22
  8.6 0.0 collective-permute-start.2
  8.6 0.0 collective-permute-done
  8.6 3.8 %collective-permute-done.1 = bf16[34,768]{1,0:T(8,128)(2,1)S(1)} collective-permute-done((bf16[34,768]{1,0:T(8,128)(2,1)S(1)}, bf16[34,768]{1,0:T(8,128)(2,1)S(1)}, u32[]{:S(2)}, u32[]{:S(2)}) %collective-permute-start.1) | collective-permute-done | bytes 52256 | tf_op jit(solution)/shard_map/ppermute | solution.py:22
  12.3 2.3 %collective-permute-done.2 = bf16[34,768]{1,0:T(8,128)(2,1)S(1)} collective-permute-done((bf16[34,768]{1,0:T(8,128)(2,1)S(1)}, bf16[34,768]{1,0:T(8,128)(2,1)S(1)}, u32[]{:S(2)}, u32[]{:S(2)}) %collective-permute-start.2) | collective-permute-done | bytes 52256 | tf_op jit(solution)/shard_map/ppermute | solution.py:22
  14.6 0.1 pad_maximum_fusion.refs_0_
  14.7 1.6 %collective-permute-start.4 = (bf16[136,768]{1,0:T(8,128)(2,1)S(1)}, bf16[136,768]{1,0:T(8,128)(2,1)S(1)}, u32[]{:S(2)}, u32[]{:S(2)}) collective-permute-start(bf16[136,768]{1,0:T(8,128)(2,1)S(1)} %pad_maximum_fusion.refs_0_), channel_id=1, source_target_pairs={{0,2},{1,3},{2,0},{3,1},{4,6},{5,7},{6,4},{7,5},{8,10},{9,11},{10,... | collective-permute-start | bytes 626696 | tf_op jit(solution)/shard_map/ppermute | solution.py:22
  16.2 0.0 collective-permute-start.3
  16.2 4.3 %collective-permute-done.4.refs_2_ = bf16[136,768]{1,0:T(8,128)(2,1)S(1)} collective-permute-done((bf16[136,768]{1,0:T(8,128)(2,1)S(1)}, bf16[136,768]{1,0:T(8,128)(2,1)S(1)}, u32[]{:S(2)}, u32[]{:S(2)}) %collective-permute-start.4) | collective-permute-done | bytes 208928 | tf_op jit(solution)/shard_map/ppermute | solution.py:22
  20.5 0.0 collective-permute-start.5
  20.5 0.8 %fusion = s32[64,4]{0,1:T(4,128)S(1)} fusion(s32[64,2]{0,1:T(2,128)} %param.8, s32[4]{0:T(128)S(1)} %iota_xor_fusion), kind=kLoop, calls=%fused_computation.5 | loop fusion | flops 1280 | bytes 1552 | tf_op jit(solution)/shard_map/reduce_sum | solution.py:219
  21.3 0.1 copy.17
  21.4 0.0 collective-permute-done.3.refs_1_
  21.4 0.6 collective-permute-done.5.refs_3_
  22.0 3.5 %hidden_part.6.refs_0_ = bf16[136,512]{1,0:T(8,128)(2,1)S(1)} custom-call(s32[1]{0:T(128)} %bitcast.t_ref.where_ref, bf16[136,768]{1,0:T(8,128)(2,1)S(1)} %pad_maximum_fusion.refs_0_, bf16[136,768]{1,0:T(8,128)(2,1)S(1)} %collective-permute-done.3.refs_1_, bf16[136,768]{1,0:T(8,128)(2,1)S(1)} %collective-permute-done.4.refs_2_, ...), custom_call_target="tpu_custom_call" | custom-call | flops 1000 | bytes 1000 | tf_op jit(solution)/shard_map/hidden_part/pallas_call | solution.py:79
  25.5 1.6 %collective-permute-start.9 = (bf16[136,512]{1,0:T(8,128)(2,1)S(1)}, bf16[136,512]{1,0:T(8,128)(2,1)S(1)}, u32[]{:S(2)}, u32[]{:S(2)}) collective-permute-start(bf16[136,512]{1,0:T(8,128)(2,1)S(1)} %hidden_part.6.refs_0_), channel_id=1, source_target_pairs={{0,2},{1,3},{2,0},{3,1},{4,6},{5,7},{6,4},{7,5},{8,10},{9,11},{10,... | collective-permute-start | bytes 417800 | tf_op jit(solution)/shard_map/ppermute | solution.py:22
  27.1 0.0 collective-permute-start.15
  27.1 3.6 %hidden_part.4.refs_4_ = bf16[136,512]{1,0:T(8,128)(2,1)S(1)} custom-call(s32[1]{0:T(128)} %bitcast.t_ref.where_ref, bf16[136,768]{1,0:T(8,128)(2,1)S(1)} %pad_maximum_fusion.refs_0_, bf16[136,768]{1,0:T(8,128)(2,1)S(1)} %collective-permute-done.3.refs_1_, bf16[136,768]{1,0:T(8,128)(2,1)S(1)} %collective-permute-done.4.refs_2_, ...), custom_call_target="tpu_custom_call" | custom-call | flops 1000 | bytes 1000 | tf_op jit(solution)/shard_map/hidden_part/pallas_call | solution.py:79
  30.7 0.6 collective-permute-start.17
  31.2 0.5 collective-permute-start.6
  31.8 0.1 copy.19
  31.9 0.1 reduce_window_sum.11
  32.0 0.0 collective-permute-done.9.refs_6_.refs_2_
  32.0 3.6 %hidden_part.7.refs_2_ = bf16[136,512]{1,0:T(8,128)(2,1)S(1)} custom-call(s32[1]{0:T(128)} %bitcast.t_ref.where_ref, bf16[136,768]{1,0:T(8,128)(2,1)S(1)} %pad_maximum_fusion.refs_0_, bf16[136,768]{1,0:T(8,128)(2,1)S(1)} %collective-permute-done.3.refs_1_, bf16[136,768]{1,0:T(8,128)(2,1)S(1)} %collective-permute-done.4.refs_2_, ...), custom_call_target="tpu_custom_call" | custom-call | flops 1000 | bytes 1000 | tf_op jit(solution)/shard_map/hidden_part/pallas_call | solution.py:79
  35.6 0.1 collective-permute-start.14
  35.7 1.6 %collective-permute-start.10 = (bf16[136,512]{1,0:T(8,128)(2,1)S(1)}, bf16[136,512]{1,0:T(8,128)(2,1)S(1)}, u32[]{:S(2)}, u32[]{:S(2)}) collective-permute-start(bf16[136,512]{1,0:T(8,128)(2,1)S(1)} %hidden_part.7.refs_2_), channel_id=1, source_target_pairs={{0,2},{1,3},{2,0},{3,1},{4,6},{5,7},{6,4},{7,5},{8,10},{9,11},{10,... | collective-permute-start | bytes 417800 | tf_op jit(solution)/shard_map/ppermute | solution.py:22
  37.2 0.0 collective-permute-done.6.refs_6_.refs_0_
  37.2 3.6 %hidden_part.5.refs_2_ = bf16[136,512]{1,0:T(8,128)(2,1)S(1)} custom-call(s32[1]{0:T(128)} %bitcast.t_ref.where_ref, bf16[136,768]{1,0:T(8,128)(2,1)S(1)} %pad_maximum_fusion.refs_0_, bf16[136,768]{1,0:T(8,128)(2,1)S(1)} %collective-permute-done.3.refs_1_, bf16[136,768]{1,0:T(8,128)(2,1)S(1)} %collective-permute-done.4.refs_2_, ...), custom_call_target="tpu_custom_call" | custom-call | flops 1000 | bytes 1000 | tf_op jit(solution)/shard_map/hidden_part/pallas_call | solution.py:79
  40.8 0.6 collective-permute-start.7
  41.4 0.5 collective-permute-start.13
  41.9 0.8 %collective-permute-done.16.refs_3_ = bf16[136,512]{1,0:T(8,128)(2,1)S(1)} collective-permute-done((bf16[136,512]{1,0:T(8,128)(2,1)S(1)}, bf16[136,512]{1,0:T(8,128)(2,1)S(1)}, u32[]{:S(2)}, u32[]{:S(2)}) %collective-permute-start.16) | collective-permute-done | bytes 139296 | tf_op jit(solution)/shard_map/ppermute | solution.py:22
  42.8 0.1 collective-permute-start.12
  42.9 0.0 collective-permute-done.10.refs_0_
  42.9 0.4 collective-permute-start.11
  43.3 3.3 %collective-permute-done.7.refs_0_ = bf16[136,512]{1,0:T(8,128)(2,1)S(1)} collective-permute-done((bf16[136,512]{1,0:T(8,128)(2,1)S(1)}, bf16[136,512]{1,0:T(8,128)(2,1)S(1)}, u32[]{:S(2)}, u32[]{:S(2)}) %collective-permute-start.7) | collective-permute-done | bytes 139296 | tf_op jit(solution)/shard_map/ppermute | solution.py:22
  46.6 4.8 %down_part.4.refs_5_ = f32[136,768]{1,0:T(8,128)S(1)} custom-call(s32[1]{0:T(128)} %bitcast.t_ref.where_ref, bf16[136,512]{1,0:T(8,128)(2,1)S(1)} %hidden_part.6.refs_0_, bf16[136,512]{1,0:T(8,128)(2,1)S(1)} %collective-permute-done.15.refs_1_, bf16[136,512]{1,0:T(8,128)(2,1)S(1)} %collective-permute-done.9.refs_6_.refs_2_, ...), custom_call_target="tpu_custom_call" | custom-call | flops 1283457024 | bytes 9437184 | tf_op jit(solution)/shard_map/down_part/pallas_call | solution.py:141
  51.4 0.0 collective-permute-done.13.refs_1_
  51.4 3.3 %down_part.5.refs_5_ = f32[136,768]{1,0:T(8,128)S(1)} custom-call(s32[1]{0:T(128)} %bitcast.t_ref.where_ref, bf16[136,512]{1,0:T(8,128)(2,1)S(1)} %collective-permute-done.6.refs_6_.refs_0_, bf16[136,512]{1,0:T(8,128)(2,1)S(1)} %collective-permute-done.13.refs_1_, bf16[136,512]{1,0:T(8,128)(2,1)S(1)} %hidden_part.7.refs_2_, ...), custom_call_target="tpu_custom_call" | custom-call | flops 855638016 | bytes 6291456 | tf_op jit(solution)/shard_map/down_part/pallas_call | solution.py:141
  54.7 0.0 copy-start.3
  54.8 0.0 copy-start.4
  54.8 0.0 copy-start.1
  54.8 0.0 collective-permute-done.12.refs_3_
  54.8 0.0 collective-permute-done.11.refs_1_
  54.8 3.3 %down_part.6.refs_3_ = f32[136,768]{1,0:T(8,128)S(1)} custom-call(s32[1]{0:T(128)} %bitcast.t_ref.where_ref, bf16[136,512]{1,0:T(8,128)(2,1)S(1)} %collective-permute-done.10.refs_0_, bf16[136,512]{1,0:T(8,128)(2,1)S(1)} %collective-permute-done.11.refs_1_, bf16[136,512]{1,0:T(8,128)(2,1)S(1)} %hidden_part.5.refs_2_, ...), custom_call_target="tpu_custom_call" | custom-call | flops 855638016 | bytes 6291456 | tf_op jit(solution)/shard_map/down_part/pallas_call | solution.py:141
  58.1 0.0 collective-permute-done.8.refs_1_
  58.2 1.8 %down_part.7 = (bf16[34,768]{1,0:T(8,128)(2,1)S(1)}, bf16[34,768]{1,0:T(8,128)(2,1)S(1)}, bf16[34,768]{1,0:T(8,128)(2,1)S(1)}, bf16[34,768]{1,0:T(8,128)(2,1)S(1)}) custom-call(s32[1]{0:T(128)} %bitcast.t_ref.where_ref, bf16[136,512]{1,0:T(8,128)(2,1)S(1)} %collective-permute-done.7.refs_0_, bf16[136,512]{1,0:T(8,128)(2,1)S(1)} %collective-permute-done.8.refs_1_, ...), custom_call_target="tpu_custom_call" | custom-call | flops 427819008 | bytes 3145728 | tf_op jit(solution)/shard_map/down_part/pallas_call | solution.py:141
  59.9 0.1 collective-permute-start.18
  60.0 2.1 %collective-permute-start.19 = (bf16[34,768]{1,0:T(8,128)(2,1)S(1)}, bf16[34,768]{1,0:T(8,128)(2,1)S(1)}, u32[]{:S(2)}, u32[]{:S(2)}) collective-permute-start(bf16[34,768]{1,0:T(8,128)(2,1)S(1)} %get-tuple-element.18), channel_id=1, source_target_pairs={{0,8},{4,12},{8,0},{12,4},{1,9},{5,13},{9,1},{13,5},{2,10},{6,14},... | collective-permute-start | bytes 156680 | tf_op jit(solution)/shard_map/ppermute | solution.py:22
  62.1 2.3 %collective-permute-start.20 = (bf16[34,768]{1,0:T(8,128)(2,1)S(1)}, bf16[34,768]{1,0:T(8,128)(2,1)S(1)}, u32[]{:S(2)}, u32[]{:S(2)}) collective-permute-start(bf16[34,768]{1,0:T(8,128)(2,1)S(1)} %get-tuple-element.19), channel_id=1, source_target_pairs={{0,12},{4,8},{8,4},{12,0},{1,13},{5,9},{9,5},{13,1},{2,14},{6,10},... | collective-permute-start | bytes 156680 | tf_op jit(solution)/shard_map/ppermute | solution.py:22
  64.4 0.1 fusion.1
  64.5 0.1 copy.20.route_ref
  64.6 1.0 %collective-permute-done.18.refs_1_ = bf16[34,768]{1,0:T(8,128)(2,1)S(1)} collective-permute-done((bf16[34,768]{1,0:T(8,128)(2,1)S(1)}, bf16[34,768]{1,0:T(8,128)(2,1)S(1)}, u32[]{:S(2)}, u32[]{:S(2)}) %collective-permute-start.18) | collective-permute-done | bytes 52256 | tf_op jit(solution)/shard_map/ppermute | solution.py:22
  65.6 2.7 %collective-permute-done.19.refs_2_ = bf16[34,768]{1,0:T(8,128)(2,1)S(1)} collective-permute-done((bf16[34,768]{1,0:T(8,128)(2,1)S(1)}, bf16[34,768]{1,0:T(8,128)(2,1)S(1)}, u32[]{:S(2)}, u32[]{:S(2)}) %collective-permute-start.19) | collective-permute-done | bytes 52256 | tf_op jit(solution)/shard_map/ppermute | solution.py:22
  68.3 0.0 collective-permute-done.20.refs_3_
  68.3 1.0 %combine.1 = (bf16[64,768]{1,0:T(8,128)(2,1)}, f32[64,4]{1,0:T(8,128)S(1)}) custom-call(s32[64,4]{1,0:T(8,128)S(1)} %subtract_select_fusion.place_ref, f32[64,4]{1,0:T(8,128)S(1)} %copy.20.route_ref, bf16[64,768]{1,0:T(8,128)(2,1)S(1)} %copy-done.1, bf16[34,768]{1,0:T(8,128)(2,1)S(1)} %get-tuple-element.16.refs_0_, ...), custom_call_target="tpu_custom_call" | custom-call | flops 1000 | bytes 1000 | tf_op jit(solution)/shard_map/combine/pallas_call | solution.py:185
  69.3 0.5 collective-permute-start.21
  69.9 3.4 %collective-permute-done.21 = f32[64,4]{1,0:T(8,128)S(1)} collective-permute-done((f32[64,4]{1,0:T(8,128)S(1)}, f32[64,4]{1,0:T(8,128)S(1)}, u32[]{:S(2)}, u32[]{:S(2)}) %collective-permute-start.21) | collective-permute-done | bytes 1056 | tf_op jit(solution)/shard_map/ppermute | solution.py:22
  73.3 1.2 %collective-permute-done.22 = f32[64,4]{1,0:T(8,128)S(1)} collective-permute-done((f32[64,4]{1,0:T(8,128)S(1)}, f32[64,4]{1,0:T(8,128)S(1)}, u32[]{:S(2)}, u32[]{:S(2)}) %collective-permute-start.22) | collective-permute-done | bytes 1056 | tf_op jit(solution)/shard_map/ppermute | solution.py:22
  74.5 0.1 copy.21
  74.5 0.7 fusion.2
  (16 shorter events, 0.1 us)
Async XLA Ops:
  0.6 0.9 %copy-start = (bf16[64,768]{1,0:T(8,128)(2,1)S(1)}, bf16[64,768]{1,0:T(8,128)(2,1)}, u32[]{:S(2)}) copy-start(bf16[64,768]{1,0:T(8,128)(2,1)} %tokens_ref.1) | copy-start | bytes 294916
  1.5 0.7 copy-start.2
  2.9 5.7 %collective-permute-start = (bf16[34,768]{1,0:T(8,128)(2,1)S(1)}, bf16[34,768]{1,0:T(8,128)(2,1)S(1)}, u32[]{:S(2)}, u32[]{:S(2)}) collective-permute-start(bf16[34,768]{1,0:T(8,128)(2,1)S(1)} %get-tuple-element.13), channel_id=1, source_target_pairs={{0,4},{4,0},{8,12},{12,8},{1,5},{5,1},{9,13},{13,9},{2,6},{6,2},{1... | collective-permute-start | bytes 156680 | tf_op jit(solution)/shard_map/ppermute | solution.py:22
  6.0 6.4 %collective-permute-start.1 = (bf16[34,768]{1,0:T(8,128)(2,1)S(1)}, bf16[34,768]{1,0:T(8,128)(2,1)S(1)}, u32[]{:S(2)}, u32[]{:S(2)}) collective-permute-start(bf16[34,768]{1,0:T(8,128)(2,1)S(1)} %get-tuple-element.14), channel_id=1, source_target_pairs={{0,8},{4,12},{8,0},{12,4},{1,9},{5,13},{9,1},{13,5},{2,10},{6,14},... | collective-permute-start | bytes 156680 | tf_op jit(solution)/shard_map/ppermute | solution.py:22
  8.6 6.0 %collective-permute-start.2 = (bf16[34,768]{1,0:T(8,128)(2,1)S(1)}, bf16[34,768]{1,0:T(8,128)(2,1)S(1)}, u32[]{:S(2)}, u32[]{:S(2)}) collective-permute-start(bf16[34,768]{1,0:T(8,128)(2,1)S(1)} %get-tuple-element.15), channel_id=1, source_target_pairs={{0,12},{4,8},{8,4},{12,0},{1,13},{5,9},{9,5},{13,1},{2,14},{6,10},... | collective-permute-start | bytes 156680 | tf_op jit(solution)/shard_map/ppermute | solution.py:22
  14.7 5.9 %collective-permute-start.4 = (bf16[136,768]{1,0:T(8,128)(2,1)S(1)}, bf16[136,768]{1,0:T(8,128)(2,1)S(1)}, u32[]{:S(2)}, u32[]{:S(2)}) collective-permute-start(bf16[136,768]{1,0:T(8,128)(2,1)S(1)} %pad_maximum_fusion.refs_0_), channel_id=1, source_target_pairs={{0,2},{1,3},{2,0},{3,1},{4,6},{5,7},{6,4},{7,5},{8,10},{9,11},{10,... | collective-permute-start | bytes 626696 | tf_op jit(solution)/shard_map/ppermute | solution.py:22
  16.2 5.2 %collective-permute-start.3 = (bf16[136,768]{1,0:T(8,128)(2,1)S(1)}, bf16[136,768]{1,0:T(8,128)(2,1)S(1)}, u32[]{:S(2)}, u32[]{:S(2)}) collective-permute-start(bf16[136,768]{1,0:T(8,128)(2,1)S(1)} %pad_maximum_fusion.refs_0_), channel_id=1, source_target_pairs={{0,1},{1,0},{2,3},{3,2},{4,5},{5,4},{6,7},{7,6},{8,9},{9,8},{10,11... | collective-permute-start | bytes 626696 | tf_op jit(solution)/shard_map/ppermute | solution.py:22
  20.5 1.5 %collective-permute-start.5 = (bf16[136,768]{1,0:T(8,128)(2,1)S(1)}, bf16[136,768]{1,0:T(8,128)(2,1)S(1)}, u32[]{:S(2)}, u32[]{:S(2)}) collective-permute-start(bf16[136,768]{1,0:T(8,128)(2,1)S(1)} %collective-permute-done.4.refs_2_), channel_id=1, source_target_pairs={{0,1},{1,0},{2,3},{3,2},{4,5},{5,4},{6,7},{7,6},{8,9},{9,8},{10,11... | collective-permute-start | bytes 626696 | tf_op jit(solution)/shard_map/ppermute | solution.py:22
  25.5 6.5 %collective-permute-start.9 = (bf16[136,512]{1,0:T(8,128)(2,1)S(1)}, bf16[136,512]{1,0:T(8,128)(2,1)S(1)}, u32[]{:S(2)}, u32[]{:S(2)}) collective-permute-start(bf16[136,512]{1,0:T(8,128)(2,1)S(1)} %hidden_part.6.refs_0_), channel_id=1, source_target_pairs={{0,2},{1,3},{2,0},{3,1},{4,6},{5,7},{6,4},{7,5},{8,10},{9,11},{10,... | collective-permute-start | bytes 417800 | tf_op jit(solution)/shard_map/ppermute | solution.py:22
  27.1 14.3 %collective-permute-start.15 = (bf16[136,512]{1,0:T(8,128)(2,1)S(1)}, bf16[136,512]{1,0:T(8,128)(2,1)S(1)}, u32[]{:S(2)}, u32[]{:S(2)}) collective-permute-start(bf16[136,512]{1,0:T(8,128)(2,1)S(1)} %hidden_part.6.refs_0_), channel_id=1, source_target_pairs={{0,1},{1,0},{2,3},{3,2},{4,5},{5,4},{6,7},{7,6},{8,9},{9,8},{10,11... | collective-permute-start | bytes 417800 | tf_op jit(solution)/shard_map/ppermute | solution.py:22
  30.7 10.7 %collective-permute-start.17 = (bf16[136,512]{1,0:T(8,128)(2,1)S(1)}, bf16[136,512]{1,0:T(8,128)(2,1)S(1)}, u32[]{:S(2)}, u32[]{:S(2)}) collective-permute-start(bf16[136,512]{1,0:T(8,128)(2,1)S(1)} %hidden_part.4.refs_4_), channel_id=1, source_target_pairs={{0,1},{1,0},{2,3},{3,2},{4,5},{5,4},{6,7},{7,6},{8,9},{9,8},{10,11... | collective-permute-start | bytes 417800 | tf_op jit(solution)/shard_map/ppermute | solution.py:22
  31.2 6.0 %collective-permute-start.6 = (bf16[136,512]{1,0:T(8,128)(2,1)S(1)}, bf16[136,512]{1,0:T(8,128)(2,1)S(1)}, u32[]{:S(2)}, u32[]{:S(2)}) collective-permute-start(bf16[136,512]{1,0:T(8,128)(2,1)S(1)} %hidden_part.4.refs_4_), channel_id=1, source_target_pairs={{0,2},{1,3},{2,0},{3,1},{4,6},{5,7},{6,4},{7,5},{8,10},{9,11},{10,... | collective-permute-start | bytes 417800 | tf_op jit(solution)/shard_map/ppermute | solution.py:22
  35.6 15.8 %collective-permute-start.14 = (bf16[136,512]{1,0:T(8,128)(2,1)S(1)}, bf16[136,512]{1,0:T(8,128)(2,1)S(1)}, u32[]{:S(2)}, u32[]{:S(2)}) collective-permute-start(bf16[136,512]{1,0:T(8,128)(2,1)S(1)} %hidden_part.7.refs_2_), channel_id=1, source_target_pairs={{0,1},{1,0},{2,3},{3,2},{4,5},{5,4},{6,7},{7,6},{8,9},{9,8},{10,11... | collective-permute-start | bytes 417800 | tf_op jit(solution)/shard_map/ppermute | solution.py:22
  35.7 7.2 %collective-permute-start.10 = (bf16[136,512]{1,0:T(8,128)(2,1)S(1)}, bf16[136,512]{1,0:T(8,128)(2,1)S(1)}, u32[]{:S(2)}, u32[]{:S(2)}) collective-permute-start(bf16[136,512]{1,0:T(8,128)(2,1)S(1)} %hidden_part.7.refs_2_), channel_id=1, source_target_pairs={{0,2},{1,3},{2,0},{3,1},{4,6},{5,7},{6,4},{7,5},{8,10},{9,11},{10,... | collective-permute-start | bytes 417800 | tf_op jit(solution)/shard_map/ppermute | solution.py:22
  40.8 5.8 %collective-permute-start.7 = (bf16[136,512]{1,0:T(8,128)(2,1)S(1)}, bf16[136,512]{1,0:T(8,128)(2,1)S(1)}, u32[]{:S(2)}, u32[]{:S(2)}) collective-permute-start(bf16[136,512]{1,0:T(8,128)(2,1)S(1)} %hidden_part.5.refs_2_), channel_id=1, source_target_pairs={{0,2},{1,3},{2,0},{3,1},{4,6},{5,7},{6,4},{7,5},{8,10},{9,11},{10,... | collective-permute-start | bytes 417800 | tf_op jit(solution)/shard_map/ppermute | solution.py:22
  41.4 1.4 %collective-permute-start.16 = (bf16[136,512]{1,0:T(8,128)(2,1)S(1)}, bf16[136,512]{1,0:T(8,128)(2,1)S(1)}, u32[]{:S(2)}, u32[]{:S(2)}) collective-permute-start(bf16[136,512]{1,0:T(8,128)(2,1)S(1)} %collective-permute-done.9.refs_6_.refs_2_), channel_id=1, source_target_pairs={{0,1},{1,0},{2,3},{3,2},{4,5},{5,4},{6,7},{7,6},{8,9},{9,8},{10,11... | collective-permute-start | bytes 417800 | tf_op jit(solution)/shard_map/ppermute | solution.py:22
  41.4 10.0 %collective-permute-start.13 = (bf16[136,512]{1,0:T(8,128)(2,1)S(1)}, bf16[136,512]{1,0:T(8,128)(2,1)S(1)}, u32[]{:S(2)}, u32[]{:S(2)}) collective-permute-start(bf16[136,512]{1,0:T(8,128)(2,1)S(1)} %collective-permute-done.6.refs_6_.refs_0_), channel_id=1, source_target_pairs={{0,1},{1,0},{2,3},{3,2},{4,5},{5,4},{6,7},{7,6},{8,9},{9,8},{10,11... | collective-permute-start | bytes 417800 | tf_op jit(solution)/shard_map/ppermute | solution.py:22
  42.8 12.0 %collective-permute-start.12 = (bf16[136,512]{1,0:T(8,128)(2,1)S(1)}, bf16[136,512]{1,0:T(8,128)(2,1)S(1)}, u32[]{:S(2)}, u32[]{:S(2)}) collective-permute-start(bf16[136,512]{1,0:T(8,128)(2,1)S(1)} %hidden_part.5.refs_2_), channel_id=1, source_target_pairs={{0,1},{1,0},{2,3},{3,2},{4,5},{5,4},{6,7},{7,6},{8,9},{9,8},{10,11... | collective-permute-start | bytes 417800 | tf_op jit(solution)/shard_map/ppermute | solution.py:22
  42.9 11.9 %collective-permute-start.11 = (bf16[136,512]{1,0:T(8,128)(2,1)S(1)}, bf16[136,512]{1,0:T(8,128)(2,1)S(1)}, u32[]{:S(2)}, u32[]{:S(2)}) collective-permute-start(bf16[136,512]{1,0:T(8,128)(2,1)S(1)} %collective-permute-done.10.refs_0_), channel_id=1, source_target_pairs={{0,1},{1,0},{2,3},{3,2},{4,5},{5,4},{6,7},{7,6},{8,9},{9,8},{10,11... | collective-permute-start | bytes 417800 | tf_op jit(solution)/shard_map/ppermute | solution.py:22
  46.6 11.5 %collective-permute-start.8 = (bf16[136,512]{1,0:T(8,128)(2,1)S(1)}, bf16[136,512]{1,0:T(8,128)(2,1)S(1)}, u32[]{:S(2)}, u32[]{:S(2)}) collective-permute-start(bf16[136,512]{1,0:T(8,128)(2,1)S(1)} %collective-permute-done.7.refs_0_), channel_id=1, source_target_pairs={{0,1},{1,0},{2,3},{3,2},{4,5},{5,4},{6,7},{7,6},{8,9},{9,8},{10,11... | collective-permute-start | bytes 417800 | tf_op jit(solution)/shard_map/ppermute | solution.py:22
  54.7 9.6 %copy-start.3 = (s32[64,2]{0,1:T(2,128)S(1)}, s32[64,2]{0,1:T(2,128)}, u32[]{:S(2)}) copy-start(s32[64,2]{0,1:T(2,128)} %param.8) | copy-start | bytes 1540
  54.8 9.6 %copy-start.4 = (f32[64,2]{0,1:T(2,128)S(1)}, f32[64,2]{0,1:T(2,128)}, u32[]{:S(2)}) copy-start(f32[64,2]{0,1:T(2,128)} %param.9) | copy-start | bytes 1540
  54.8 13.5 %copy-start.1 = (bf16[64,768]{1,0:T(8,128)(2,1)S(1)}, bf16[64,768]{1,0:T(8,128)(2,1)}, u32[]{:S(2)}) copy-start(bf16[64,768]{1,0:T(8,128)(2,1)} %grad_ref.1) | copy-start | bytes 294916
  59.9 5.6 %collective-permute-start.18 = (bf16[34,768]{1,0:T(8,128)(2,1)S(1)}, bf16[34,768]{1,0:T(8,128)(2,1)S(1)}, u32[]{:S(2)}, u32[]{:S(2)}) collective-permute-start(bf16[34,768]{1,0:T(8,128)(2,1)S(1)} %get-tuple-element.17), channel_id=1, source_target_pairs={{0,4},{4,0},{8,12},{12,8},{1,5},{5,1},{9,13},{13,9},{2,6},{6,2},{1... | collective-permute-start | bytes 156680 | tf_op jit(solution)/shard_map/ppermute | solution.py:22
  60.0 8.3 %collective-permute-start.19 = (bf16[34,768]{1,0:T(8,128)(2,1)S(1)}, bf16[34,768]{1,0:T(8,128)(2,1)S(1)}, u32[]{:S(2)}, u32[]{:S(2)}) collective-permute-start(bf16[34,768]{1,0:T(8,128)(2,1)S(1)} %get-tuple-element.18), channel_id=1, source_target_pairs={{0,8},{4,12},{8,0},{12,4},{1,9},{5,13},{9,1},{13,5},{2,10},{6,14},... | collective-permute-start | bytes 156680 | tf_op jit(solution)/shard_map/ppermute | solution.py:22
  62.1 6.2 %collective-permute-start.20 = (bf16[34,768]{1,0:T(8,128)(2,1)S(1)}, bf16[34,768]{1,0:T(8,128)(2,1)S(1)}, u32[]{:S(2)}, u32[]{:S(2)}) collective-permute-start(bf16[34,768]{1,0:T(8,128)(2,1)S(1)} %get-tuple-element.19), channel_id=1, source_target_pairs={{0,12},{4,8},{8,4},{12,0},{1,13},{5,9},{9,5},{13,1},{2,14},{6,10},... | collective-permute-start | bytes 156680 | tf_op jit(solution)/shard_map/ppermute | solution.py:22
  69.3 3.9 %collective-permute-start.21 = (f32[64,4]{1,0:T(8,128)S(1)}, f32[64,4]{1,0:T(8,128)S(1)}, u32[]{:S(2)}, u32[]{:S(2)}) collective-permute-start(f32[64,4]{1,0:T(8,128)S(1)} %get-tuple-element.21), channel_id=1, source_target_pairs={{0,2},{1,3},{2,0},{3,1},{4,6},{5,7},{6,4},{7,5},{8,10},{9,11},{10,... | collective-permute-start | bytes 3080 | tf_op jit(solution)/shard_map/ppermute | solution.py:22
  73.3 1.2 %collective-permute-start.22 = (f32[64,4]{1,0:T(8,128)S(1)}, f32[64,4]{1,0:T(8,128)S(1)}, u32[]{:S(2)}, u32[]{:S(2)}) collective-permute-start(f32[64,4]{1,0:T(8,128)S(1)} %add.6), channel_id=1, source_target_pairs={{0,1},{1,0},{2,3},{3,2},{4,5},{5,4},{6,7},{7,6},{8,9},{9,8},{10,11... | collective-permute-start | bytes 3080 | tf_op jit(solution)/shard_map/ppermute | solution.py:22

commit v3 on v0

v3 whole, which is shorter than its diff:
```python
import functools

import jax
import jax.numpy as jnp
from jax import lax
from jax.experimental import pallas as pl
from jax.experimental.pallas import tpu as pltpu
from jax.sharding import PartitionSpec as P

EXPERTS = 4
MOST = 34
BF = jnp.bfloat16
F32 = jnp.float32
VMEM_LIMIT = 24 * 1024 * 1024
SMALL_LIMIT = 4 * 1024 * 1024
FF_TILE = 256
K_TILE = 512


def swap(value, axis, bit):
    size = lax.axis_size(axis)
    return lax.ppermute(value, axis, [(i, i ^ bit) for i in range(size)])


VMEM = pl.BlockSpec(memory_space=pltpu.VMEM)
SMEM = pl.BlockSpec(memory_space=pltpu.SMEM)
ANY = pl.BlockSpec(memory_space=pl.ANY)
SMALL = dict(
    compiler_params=pltpu.CompilerParams(vmem_limit_bytes=SMALL_LIMIT),
    cost_estimate=pl.CostEstimate(flops=1000, bytes_accessed=1000, transcendentals=0),
)


def routing(ids, me):
    rows = ids.shape[1]
    upper = (
        lax.broadcasted_iota(jnp.int32, (rows, rows), 0) < lax.broadcasted_iota(jnp.int32, (rows, rows), 1)
    ).astype(F32).astype(BF)
    slot = lax.broadcasted_iota(jnp.int32, (MOST, rows), 0)
    hits, picks = [], []
    for step in range(EXPERTS):
        hit = (ids == (me ^ step)).astype(F32)
        member = jnp.sum(hit, axis=0, keepdims=True)
        before = jnp.dot(
            jnp.broadcast_to(member, (16, rows)).astype(BF), upper, preferred_element_type=F32
        )[:1]
        place = jnp.where(member > 0.5, before.astype(jnp.int32), -1)
        hits.append(hit)
        picks.append((slot == place).astype(F32))
    return hits, picks


def select_kernel(me_ref, t_ref, ids_ref, tokens_ref, *out_refs):
    _, picks = routing(ids_ref[...], me_ref[0])
    for pick, out_ref in zip(picks, out_refs):
        out_ref[...] = jnp.dot(pick.astype(BF), tokens_ref[...], preferred_element_type=F32).astype(BF)


def select_rows(me, t, ids_t, tokens):
    width = tokens.shape[1]
    return pl.pallas_call(
        select_kernel,
        out_shape=[jax.ShapeDtypeStruct((MOST, width), BF)] * EXPERTS,
        in_specs=[SMEM, SMEM, VMEM, VMEM],
        out_specs=[VMEM] * EXPERTS,
        name="select_rows",
        **SMALL,
    )(me, t, ids_t, tokens)


def pack_kernel(*refs):
    blocks = refs[:EXPERTS]
    refs[-1][...] = jnp.concatenate([b[...].astype(F32) for b in blocks], axis=0).astype(BF)


def pack(blocks, after):
    return pl.pallas_call(
        pack_kernel,
        out_shape=jax.ShapeDtypeStruct((EXPERTS * MOST, blocks[0].shape[1]), BF),
        in_specs=[VMEM] * EXPERTS + [ANY] * len(after),
        out_specs=VMEM,
        name="pack",
        **SMALL,
    )(*blocks, *after)


def hold(value, after):
    return pl.pallas_call(
        lambda *refs: None,
        out_shape=jax.ShapeDtypeStruct(value.shape, value.dtype),
        in_specs=[ANY] * (1 + len(after)),
        out_specs=ANY,
        input_output_aliases={0: 0},
        name="hold",
        **SMALL,
    )(value, *after)


def load_kernel(runs, count, *refs):
    weight_refs = refs[:count]
    out_refs, sems = refs[-1 - len(runs) * count:-1], refs[-1]
    copies = []
    for n, (start, size) in enumerate(runs):
        for m, weight in enumerate(weight_refs):
            copies.append(
                pltpu.make_async_copy(
                    weight.at[0, :, pl.ds(start, size)], out_refs[n * count + m], sems.at[n * count + m]
                )
            )
    for copy in copies:
        copy.start()
    for copy in copies:
        copy.wait()


def load(weights, runs, after=()):
    depth = weights[0].shape[1]
    count = len(weights)
    moved = sum(2 * depth * size * count for _, size in runs)
    return pl.pallas_call(
        functools.partial(load_kernel, runs, count),
        out_shape=[pltpu.VMEM((depth, size), BF) for _, size in runs for _ in weights],
        in_specs=[ANY] * (count + len(after)),
        out_specs=[ANY] * (len(runs) * count),
        scratch_shapes=[pltpu.SemaphoreType.DMA((len(runs) * count,))],
        compiler_params=pltpu.CompilerParams(vmem_limit_bytes=SMALL_LIMIT),
        cost_estimate=pl.CostEstimate(flops=0, bytes_accessed=2 * moved, transcendentals=0),
        name="load",
    )(*weights, *after)


def hidden_kernel(parts, number, t_ref, *refs):
    x_refs = refs[:parts]
    gate_ref, up_ref, down_ref = refs[parts:parts + 3]
    out_ref, share_ref, sem = refs[-3:]
    slab = share_ref.shape[0]
    row = pl.multiple_of((t_ref[0] ^ number) * slab, slab)
    copy = pltpu.make_async_copy(down_ref.at[0, pl.ds(row, slab), :], share_ref, sem)
    copy.start()
    depth = x_refs[0].shape[1]
    for tile in range(0, out_ref.shape[1], FF_TILE):
        columns = slice(tile, tile + FF_TILE)
        gate = up = None
        for j in range(parts):
            at = pl.ds(pl.multiple_of((t_ref[0] ^ j) * depth, depth), depth)
            x = x_refs[j][...]
            g = jnp.dot(x, gate_ref[at, columns], preferred_element_type=F32)
            u = jnp.dot(x, up_ref[at, columns], preferred_element_type=F32)
            gate = g if gate is None else gate + g
            up = u if up is None else up + u
        out_ref[:, tile:tile + FF_TILE] = (gate * jax.nn.sigmoid(gate) * up).astype(BF)
    copy.wait()


def hidden_part(t, xs, gate_run, up_run, down_weight, number, slab, after=()):
    rows, size = xs[0].shape[0], gate_run.shape[1]
    width = down_weight.shape[2]
    return pl.pallas_call(
        functools.partial(hidden_kernel, len(xs), number),
        out_shape=[jax.ShapeDtypeStruct((rows, size), BF), pltpu.VMEM((slab, width), BF)],
        in_specs=[SMEM] + [VMEM] * (len(xs) + 2) + [ANY] * (1 + len(after)),
        out_specs=[VMEM, ANY],
        scratch_shapes=[pltpu.SemaphoreType.DMA],
        compiler_params=pltpu.CompilerParams(vmem_limit_bytes=SMALL_LIMIT),
        cost_estimate=pl.CostEstimate(flops=1000, bytes_accessed=1000, transcendentals=0),
        name="hidden_part",
    )(t, *xs, gate_run, up_run, down_weight, *after)


def down_kernel(count, where, has_sum, last, *refs):
    pieces = refs[:count]
    weight_refs = refs[count:count + EXPERTS]
    rest = refs[count + EXPERTS:]
    outs = rest[has_sum:]
    total = rest[0][...] if has_sum else None
    for piece, (j, first) in zip(pieces, where):
        size = piece.shape[1]
        term = jnp.dot(piece[...], weight_refs[j][first:first + size, :], preferred_element_type=F32)
        total = term if total is None else total + term
    if last:
        for k, out in enumerate(outs):
            out[...] = total[k * MOST:(k + 1) * MOST].astype(BF)
    else:
        outs[0][...] = total


def down_part(pieces, where, weights, running, last):
    rows = pieces[0].shape[0]
    width = weights[0].shape[1]
    has_sum = running is not None
    if last:
        out_shape = [jax.ShapeDtypeStruct((MOST, width), BF)] * EXPERTS
    else:
        out_shape = [jax.ShapeDtypeStruct((rows, width), F32)]
    return pl.pallas_call(
        functools.partial(down_kernel, len(pieces), where, has_sum, last),
        out_shape=out_shape,
        in_specs=[VMEM] * (len(pieces) + len(weights) + has_sum),
        out_specs=[VMEM] * len(out_shape),
        compiler_params=pltpu.CompilerParams(vmem_limit_bytes=SMALL_LIMIT),
        cost_estimate=pl.CostEstimate(
            flops=2 * rows * width * sum(p.shape[1] for p in pieces), bytes_accessed=1000, transcendentals=0
        ),
        name="down_part",
    )(*pieces, *weights, *([running] if has_sum else []))


def combine_kernel(me_ref, ids_ref, probs_ref, grad_ref, *refs):
    back_refs = refs[:EXPERTS]
    mixed_ref, gate_grad_ref = refs[EXPERTS:]
    rows = grad_ref.shape[0]
    hits, picks = routing(ids_ref[...], me_ref[0])
    grad = grad_ref[...].astype(F32)
    column = lax.broadcasted_iota(jnp.int32, (rows, 128), 1)
    dots = jnp.zeros((rows, 128), F32)
    routes = jnp.concatenate(
        [jnp.sum(h * probs_ref[...], axis=0, keepdims=True) for h in hits]
        + [jnp.zeros((128 - EXPERTS, rows), F32)],
        axis=0,
    )
    routes = jnp.concatenate([routes, jnp.zeros((128, 128 - rows), F32)], axis=1).T
    mixed = None
    for k in range(EXPERTS):
        out = lax.dot_general(
            picks[k].astype(BF), back_refs[k][...], (((0,), (0,)), ((), ())), preferred_element_type=F32
        )
        term = routes[:rows, k:k + 1] * out
        mixed = term if mixed is None else mixed + term
        dots = jnp.where(column == k, jnp.sum(grad * out, axis=1, keepdims=True), dots)
    mixed_ref[...] = mixed.astype(BF)
    turned = jnp.concatenate([dots, jnp.zeros((128 - rows, 128), F32)], axis=0).T
    gate_grad = None
    for k in range(EXPERTS):
        term = hits[k] * turned[k:k + 1, :rows]
        gate_grad = term if gate_grad is None else gate_grad + term
    gate_grad_ref[...] = gate_grad


def combine(me, ids_t, probs_t, out_grad, back):
    return pl.pallas_call(
        combine_kernel,
        out_shape=[
            jax.ShapeDtypeStruct(out_grad.shape, BF),
            jax.ShapeDtypeStruct(probs_t.shape, F32),
        ],
        in_specs=[SMEM] + [VMEM] * (3 + EXPERTS),
        out_specs=[VMEM] * 2,
        name="combine",
        **SMALL,
    )(me, ids_t, probs_t, out_grad, *back)


CHUNKS = (512, 512, 512, 512)


def per_device(tokens, expert_ids, gate_probs, out_grad, gate_weight, up_weight, down_weight):
    me = lax.axis_index("expert").astype(jnp.int32).reshape(1)
    t_index = lax.axis_index("tensor").astype(jnp.int32).reshape(1)
    slab = gate_weight.shape[2]
    ids_t, probs_t = expert_ids.T, gate_probs.T
    gate_weight, up_weight, down_weight = (
        pltpu.with_memory_space_constraint(w, pltpu.HBM) for w in (gate_weight, up_weight, down_weight)
    )

    rows = select_rows(me, t_index, ids_t, tokens)
    starts = [sum(CHUNKS[:i]) for i in range(len(CHUNKS))]
    runs = list(zip(starts, CHUNKS))
    half = len(runs) // 2
    loaded = list(load([gate_weight, up_weight], runs[:half], [rows[0]]))
    arrived = [rows[0]] + [swap(rows[k], "expert", k) for k in (1, 2, 3)]
    own = pack(arrived, loaded[:1])
    loaded += load([gate_weight, up_weight], runs[half:], [own])
    across = hold(swap(own, "tensor", 2), loaded[-1:])
    xs = [own, swap(own, "tensor", 1), across, swap(across, "tensor", 1)]

    pieces, shares = [], []
    for i in range(len(CHUNKS)):
        after = [pieces[i - 2][2]] if i >= 2 else loaded[2 * half:2 * half + 1]
        h, share = hidden_part(t_index, xs, loaded[2 * i], loaded[2 * i + 1], down_weight, i, slab, after)
        far = swap(h, "tensor", 2)
        pieces.append([h, swap(h, "tensor", 1), far, swap(far, "tensor", 1)])
        shares.append(share)
    running = None
    for i, start in enumerate(starts):
        use = [(i, 2), (i, 3)]
        if i == 0:
            use = [(0, 0), (0, 1)] + use
        if i + 1 < len(starts):
            use += [(i + 1, 0), (i + 1, 1)]
        result = down_part(
            [pieces[n][j] for n, j in use], [(j, starts[n]) for n, j in use], shares, running, i + 1 == len(starts)
        )
        running = result[0]
    back = [result[0]] + [swap(result[k], "expert", k) for k in (1, 2, 3)]
    mixed, gate_grad = combine(me, ids_t, probs_t, out_grad, back)
    gate_grad = gate_grad + swap(gate_grad, "tensor", 2)
    gate_grad = gate_grad + swap(gate_grad, "tensor", 1)
    return mixed, gate_grad.T


def per_device_any(tokens, expert_ids, gate_probs, out_grad, gate_weight, up_weight, down_weight):
    span_count = lax.axis_size("expert") // EXPERTS
    hits = expert_ids[:, :, None] == jnp.arange(EXPERTS, dtype=jnp.int32)[None, None, :]
    hit_float = hits.astype(F32)
    member = jnp.sum(hits.astype(jnp.int32), axis=1)
    place = jnp.cumsum(member, axis=0) - member
    placed = (place[None, :, :] == jnp.arange(MOST, dtype=jnp.int32)[:, None, None]) & (member[None, :, :] == 1)
    select = jnp.transpose(placed, (2, 0, 1)).astype(F32)
    route = jnp.sum(hit_float * gate_probs[:, :, None], axis=1)
    rows = jnp.einsum("est,td->esd", select.astype(BF), tokens, preferred_element_type=F32).astype(BF)
    arrived = lax.all_to_all(
        jnp.repeat(rows, span_count, axis=0), "expert", split_axis=0, concat_axis=0, tiled=True
    )
    full = lax.all_gather(arrived, "tensor", axis=2, tiled=True)
    gate = jnp.einsum("smd,df->smf", full, gate_weight[0], preferred_element_type=F32)
    up = jnp.einsum("smd,df->smf", full, up_weight[0], preferred_element_type=F32)
    hidden = (gate * jax.nn.sigmoid(gate) * up).astype(BF)
    partial_out = jnp.einsum(
        "smf,fd->smd",
        lax.all_gather(hidden, "tensor", axis=2, tiled=True),
        down_weight[0],
        preferred_element_type=F32,
    )
    back = lax.all_to_all(partial_out, "expert", split_axis=0, concat_axis=0, tiled=True)
    expert_out = jnp.sum(back.reshape(EXPERTS, span_count, MOST, tokens.shape[1]), axis=1)
    token_out = jnp.einsum("est,esd->ted", select, expert_out, precision=lax.Precision.HIGHEST)
    mixed = jnp.sum(route[:, :, None] * token_out, axis=1).astype(BF)
    dots = lax.psum(jnp.sum(out_grad.astype(F32)[:, None, :] * token_out, axis=2), "tensor")
    return mixed, jnp.sum(hit_float * dots[:, None, :], axis=2)


def solution(mesh):
    in_specs = (
        P(("groups", "expert"), "tensor"),
        P(("groups", "expert"), None),
        P(("groups", "expert"), None),
        P(("groups", "expert"), "tensor"),
        P("expert", None, "tensor"),
        P("expert", None, "tensor"),
        P("expert", None, "tensor"),
    )
    out_specs = (P(("groups", "expert"), "tensor"), P(("groups", "expert"), None))
    direct = mesh.shape["expert"] == EXPERTS and mesh.shape["tensor"] == 4
    return jax.shard_map(
        per_device if direct else per_device_any,
        mesh=mesh, in_specs=in_specs, out_specs=out_specs, check_vma=False,
    )
```

time: 111 us -> 62 us (0.56)
  blocking collectives: 30.2 us -> 0 us
  Pallas kernels: 0 us -> 24.2 us
  waiting for transfers between devices: 38.1 us -> 15.3 us
  matrix products: 20.4 us -> 0 us
  starting transfers between devices: 4.64 us -> 19.3 us
  between operations: 14.1 us -> 0.86 us
    pallas_call x0 -> x14, Pallas kernels: none -> 24.2 us  [the longest x4 10.6 us: hidden_part(): pl.pallas_call(functools.partial(hidden_kernel, len(xs), number), out_sha...]
    all_gather x1 -> x0, waiting for transfers between devices: 24 us -> none  [per_device(): lax.all_gather(hidden, 'tensor', axis=2, tiled=True)]
    dot_general x5 -> x0, matrix products: 20.4 us -> none  [the longest x1 8.51 us: per_device(): jnp.einsum('smf,fd->smd', lax.all_gather(hidden, 'tensor', axis=2, tiled=...]
    ppermute x0 -> x23, starting transfers between devices: none -> 19.3 us  [swap(): return lax.ppermute(value, axis, [(i, i ^ bit) for i in range(size)])]
    ppermute x0 -> x23, waiting for transfers between devices: none -> 15.3 us  [swap(): return lax.ppermute(value, axis, [(i, i ^ bit) for i in range(size)])]
    all_to_all x1 -> x0, blocking collectives: 14.6 us -> none  [per_device(): lax.all_to_all(token_send, 'expert', split_axis=0, concat_axis=0, tiled=T...]
    all_to_all x1 -> x0, waiting for transfers between devices: 14.1 us -> none  [per_device(): lax.all_to_all(partial_out, 'expert', split_axis=0, concat_axis=0, tiled=...]
    all_gather x1 -> x0, blocking collectives: 9.65 us -> none  [per_device(): piece = lax.all_gather(arrived, 'tensor', axis=2, tiled=True)]
  transfers between devices with their start and end apart: 2 -> 23, of which waited for: 2 -> 8; matrix products, arithmetic and copies ran while one was open for 0% -> 0% of each run, Pallas kernels for 0% -> 32%
where the time goes in v3:
time: 62 us; the launch traced here: 61.7 us
  Pallas kernels  24.2 us (39%)
  starting transfers between devices  19.3 us (31%)
  waiting for transfers between devices  15.3 us (25%)
  local copies, waits for them, and re-layouts  1.58 us (3%)
  between operations  0.86 us (1%)
    ppermute x23, starting transfers between devices, swap(): return lax.ppermute(value, axis, [(i, i ^ bit) for i in range(size)])  19.3 us
    ppermute x23, waiting for transfers between devices, swap(): return lax.ppermute(value, axis, [(i, i ^ bit) for i in range(size)])  15.3 us
    pallas_call x4, Pallas kernels, hidden_part(): pl.pallas_call(functools.partial(hidden_kernel, len(xs), number), out_sha...  10.6 us
    pallas_call x2, Pallas kernels, load(): pl.pallas_call(functools.partial(load_kernel, runs, count), out_shape=[pl...  9.46 us
    pallas_call x4, Pallas kernels, down_part(): pl.pallas_call(functools.partial(down_kernel, len(pieces), where, has_sum...  2.53 us
    unnamed x10, local copies, waits for them, and re-layouts  1.58 us
  transfers between devices with their start and end apart: 23, of which 8 were waited for; matrix products, arithmetic and copies ran while one was open for 0% of the time, Pallas kernels for 32%

profile of v3, /device:TPU:0, one launch (start us, length us, event | category | flops | bytes accessed | tf_op | source)
XLA Modules:
  0.0 61.7 jit_solution(263038918450354183)
XLA Ops:
  0.6 0.9 %copy-done = bf16[64,768]{1,0:T(8,128)(2,1)S(1)} copy-done((bf16[64,768]{1,0:T(8,128)(2,1)S(1)}, bf16[64,768]{1,0:T(8,128)(2,1)}, u32[]{:S(2)}) %copy-start) | copy-done | bytes 98328
  1.5 0.7 %copy-done.2 = s32[64,2]{0,1:T(2,128)S(1)} copy-done((s32[64,2]{0,1:T(2,128)S(1)}, s32[64,2]{0,1:T(2,128)}, u32[]{:S(2)}) %copy-start.2) | copy-done | bytes 536
  2.2 0.3 select_rows.1
  2.5 3.1 %collective-permute-start = (bf16[34,768]{1,0:T(8,128)(2,1)S(1)}, bf16[34,768]{1,0:T(8,128)(2,1)S(1)}, u32[]{:S(2)}, u32[]{:S(2)}) collective-permute-start(bf16[34,768]{1,0:T(8,128)(2,1)S(1)} %get-tuple-element.29), channel_id=1, source_target_pairs={{0,4},{4,0},{8,12},{12,8},{1,5},{5,1},{9,13},{13,9},{2,6},{6,2},{1... | collective-permute-start | bytes 156680 | tf_op jit(solution)/shard_map/ppermute | solution.py:22
  5.6 2.6 %collective-permute-start.1 = (bf16[34,768]{1,0:T(8,128)(2,1)S(1)}, bf16[34,768]{1,0:T(8,128)(2,1)S(1)}, u32[]{:S(2)}, u32[]{:S(2)}) collective-permute-start(bf16[34,768]{1,0:T(8,128)(2,1)S(1)} %get-tuple-element.30), channel_id=1, source_target_pairs={{0,8},{4,12},{8,0},{12,4},{1,9},{5,13},{9,1},{13,5},{2,10},{6,14},... | collective-permute-start | bytes 156680 | tf_op jit(solution)/shard_map/ppermute | solution.py:22
  8.2 0.0 collective-permute-start.2
  8.2 4.7 %load.2 = (bf16[3072,512]{1,0:T(8,128)(2,1)S(1)}, bf16[3072,512]{1,0:T(8,128)(2,1)S(1)}, bf16[3072,512]{1,0:T(8,128)(2,1)S(1)}, bf16[3072,512]{1,0:T(8,128)(2,1)S(1)}) custom-call(bf16[1,3072,2048]{2,1,0:T(8,128)(2,1)} %refs_0_.3, bf16[1,3072,2048]{2,1,0:T(8,128)(2,1)} %refs_1_.3, bf16[34,768]{1,0:T(8,128)(2,1)S(1)} %get-tuple-element.28.refs_2_.refs_0_), custom_call_target="tpu_custom_call" | custom-call | bytes 25165824 | tf_op jit(solution)/shard_map/load/pallas_call | solution.py:120
  13.0 0.0 collective-permute-done.refs_1_
  13.0 0.0 collective-permute-done.1.refs_2_
  13.0 1.3 %collective-permute-done.2.refs_3_ = bf16[34,768]{1,0:T(8,128)(2,1)S(1)} collective-permute-done((bf16[34,768]{1,0:T(8,128)(2,1)S(1)}, bf16[34,768]{1,0:T(8,128)(2,1)S(1)}, u32[]{:S(2)}, u32[]{:S(2)}) %collective-permute-start.2) | collective-permute-done | bytes 52256 | tf_op jit(solution)/shard_map/ppermute | solution.py:22
  14.3 1.6 %collective-permute-start.4 = (bf16[136,768]{1,0:T(8,128)(2,1)S(1)}, bf16[136,768]{1,0:T(8,128)(2,1)S(1)}, u32[]{:S(2)}, u32[]{:S(2)}) collective-permute-start(bf16[136,768]{1,0:T(8,128)(2,1)S(1)} %pack.1.refs_2_.refs_0_), channel_id=1, source_target_pairs={{0,2},{1,3},{2,0},{3,1},{4,6},{5,7},{6,4},{7,5},{8,10},{9,11},{10,... | collective-permute-start | bytes 626696 | tf_op jit(solution)/shard_map/ppermute | solution.py:22
  15.9 0.0 collective-permute-start.3
  15.9 4.7 %load.3 = (bf16[3072,512]{1,0:T(8,128)(2,1)S(1)}, bf16[3072,512]{1,0:T(8,128)(2,1)S(1)}, bf16[3072,512]{1,0:T(8,128)(2,1)S(1)}, bf16[3072,512]{1,0:T(8,128)(2,1)S(1)}) custom-call(bf16[1,3072,2048]{2,1,0:T(8,128)(2,1)} %refs_0_.3, bf16[1,3072,2048]{2,1,0:T(8,128)(2,1)} %refs_1_.3, bf16[136,768]{1,0:T(8,128)(2,1)S(1)} %pack.1.refs_2_.refs_0_), custom_call_target="tpu_custom_call" | custom-call | bytes 25165824 | tf_op jit(solution)/shard_map/load/pallas_call | solution.py:120
  20.6 0.0 collective-permute-done.4.refs_0_
  20.6 0.6 collective-permute-start.5
  21.2 0.0 collective-permute-done.3.refs_1_
  21.2 1.1 %collective-permute-done.5.refs_3_ = bf16[136,768]{1,0:T(8,128)(2,1)S(1)} collective-permute-done((bf16[136,768]{1,0:T(8,128)(2,1)S(1)}, bf16[136,768]{1,0:T(8,128)(2,1)S(1)}, u32[]{:S(2)}, u32[]{:S(2)}) %collective-permute-start.5) | collective-permute-done | bytes 208928 | tf_op jit(solution)/shard_map/ppermute | solution.py:22
  22.3 2.5 %hidden_part.6 = (bf16[136,512]{1,0:T(8,128)(2,1)S(1)}, bf16[2048,768]{1,0:T(8,128)(2,1)S(1)}) custom-call(s32[1]{0:T(128)} %bitcast.3.t_ref, bf16[136,768]{1,0:T(8,128)(2,1)S(1)} %pack.1.refs_2_.refs_0_, bf16[136,768]{1,0:T(8,128)(2,1)S(1)} %collective-permute-done.3.refs_1_, bf16[136,768]{1,0:T(8,128)(2,1)S(1)} %hold.1.refs_2_, ...), custom_call_target="tpu_custom_call" | custom-call | flops 1000 | bytes 1000 | tf_op jit(solution)/shard_map/hidden_part/pallas_call | solution.py:158
  24.8 0.9 %collective-permute-start.9 = (bf16[136,512]{1,0:T(8,128)(2,1)S(1)}, bf16[136,512]{1,0:T(8,128)(2,1)S(1)}, u32[]{:S(2)}, u32[]{:S(2)}) collective-permute-start(bf16[136,512]{1,0:T(8,128)(2,1)S(1)} %get-tuple-element.44.refs_0_), channel_id=1, source_target_pairs={{0,2},{1,3},{2,0},{3,1},{4,6},{5,7},{6,4},{7,5},{8,10},{9,11},{10,... | collective-permute-start | bytes 417800 | tf_op jit(solution)/shard_map/ppermute | solution.py:22
  25.7 2.7 %hidden_part.4 = (bf16[136,512]{1,0:T(8,128)(2,1)S(1)}, bf16[2048,768]{1,0:T(8,128)(2,1)S(1)}) custom-call(s32[1]{0:T(128)} %bitcast.3.t_ref, bf16[136,768]{1,0:T(8,128)(2,1)S(1)} %pack.1.refs_2_.refs_0_, bf16[136,768]{1,0:T(8,128)(2,1)S(1)} %collective-permute-done.3.refs_1_, bf16[136,768]{1,0:T(8,128)(2,1)S(1)} %hold.1.refs_2_, ...), custom_call_target="tpu_custom_call" | custom-call | flops 1000 | bytes 1000 | tf_op jit(solution)/shard_map/hidden_part/pallas_call | solution.py:158
  28.4 1.3 %collective-permute-start.6 = (bf16[136,512]{1,0:T(8,128)(2,1)S(1)}, bf16[136,512]{1,0:T(8,128)(2,1)S(1)}, u32[]{:S(2)}, u32[]{:S(2)}) collective-permute-start(bf16[136,512]{1,0:T(8,128)(2,1)S(1)} %get-tuple-element.38.refs_4_), channel_id=1, source_target_pairs={{0,2},{1,3},{2,0},{3,1},{4,6},{5,7},{6,4},{7,5},{8,10},{9,11},{10,... | collective-permute-start | bytes 417800 | tf_op jit(solution)/shard_map/ppermute | solution.py:22
  29.7 0.0 collective-permute-start.15
  29.7 0.5 collective-permute-start.17
  30.2 0.6 %collective-permute-done.9.refs_7_.refs_2_ = bf16[136,512]{1,0:T(8,128)(2,1)S(1)} collective-permute-done((bf16[136,512]{1,0:T(8,128)(2,1)S(1)}, bf16[136,512]{1,0:T(8,128)(2,1)S(1)}, u32[]{:S(2)}, u32[]{:S(2)}) %collective-permute-start.9) | collective-permute-done | bytes 139296 | tf_op jit(solution)/shard_map/ppermute | solution.py:22
  30.8 2.7 %hidden_part.7 = (bf16[136,512]{1,0:T(8,128)(2,1)S(1)}, bf16[2048,768]{1,0:T(8,128)(2,1)S(1)}) custom-call(s32[1]{0:T(128)} %bitcast.3.t_ref, bf16[136,768]{1,0:T(8,128)(2,1)S(1)} %pack.1.refs_2_.refs_0_, bf16[136,768]{1,0:T(8,128)(2,1)S(1)} %collective-permute-done.3.refs_1_, bf16[136,768]{1,0:T(8,128)(2,1)S(1)} %hold.1.refs_2_, ...), custom_call_target="tpu_custom_call" | custom-call | flops 1000 | bytes 1000 | tf_op jit(solution)/shard_map/hidden_part/pallas_call | solution.py:158
  33.5 0.7 %collective-permute-start.10 = (bf16[136,512]{1,0:T(8,128)(2,1)S(1)}, bf16[136,512]{1,0:T(8,128)(2,1)S(1)}, u32[]{:S(2)}, u32[]{:S(2)}) collective-permute-start(bf16[136,512]{1,0:T(8,128)(2,1)S(1)} %get-tuple-element.47.refs_2_), channel_id=1, source_target_pairs={{0,2},{1,3},{2,0},{3,1},{4,6},{5,7},{6,4},{7,5},{8,10},{9,11},{10,... | collective-permute-start | bytes 417800 | tf_op jit(solution)/shard_map/ppermute | solution.py:22
  34.2 0.0 collective-permute-start.16
  34.2 0.0 collective-permute-done.6.refs_7_.refs_0_
  34.2 2.7 %hidden_part.5 = (bf16[136,512]{1,0:T(8,128)(2,1)S(1)}, bf16[2048,768]{1,0:T(8,128)(2,1)S(1)}) custom-call(s32[1]{0:T(128)} %bitcast.3.t_ref, bf16[136,768]{1,0:T(8,128)(2,1)S(1)} %pack.1.refs_2_.refs_0_, bf16[136,768]{1,0:T(8,128)(2,1)S(1)} %collective-permute-done.3.refs_1_, bf16[136,768]{1,0:T(8,128)(2,1)S(1)} %hold.1.refs_2_, ...), custom_call_target="tpu_custom_call" | custom-call | flops 1000 | bytes 1000 | tf_op jit(solution)/shard_map/hidden_part/pallas_call | solution.py:158
  36.9 1.5 %collective-permute-start.7 = (bf16[136,512]{1,0:T(8,128)(2,1)S(1)}, bf16[136,512]{1,0:T(8,128)(2,1)S(1)}, u32[]{:S(2)}, u32[]{:S(2)}) collective-permute-start(bf16[136,512]{1,0:T(8,128)(2,1)S(1)} %get-tuple-element.39.refs_2_), channel_id=1, source_target_pairs={{0,2},{1,3},{2,0},{3,1},{4,6},{5,7},{6,4},{7,5},{8,10},{9,11},{10,... | collective-permute-start | bytes 417800 | tf_op jit(solution)/shard_map/ppermute | solution.py:22
  38.4 0.0 collective-permute-done.15.refs_1_
  38.4 0.2 collective-permute-start.14
  38.6 0.0 collective-permute-done.17.refs_5_
  38.6 0.3 collective-permute-start.13
  38.9 0.0 collective-permute-done.10.refs_0_
  38.9 0.2 collective-permute-start.12
  39.1 0.0 collective-permute-done.16.refs_3_
  39.1 0.3 collective-permute-start.11
  39.4 3.6 %collective-permute-done.7.refs_0_ = bf16[136,512]{1,0:T(8,128)(2,1)S(1)} collective-permute-done((bf16[136,512]{1,0:T(8,128)(2,1)S(1)}, bf16[136,512]{1,0:T(8,128)(2,1)S(1)}, u32[]{:S(2)}, u32[]{:S(2)}) %collective-permute-start.7) | collective-permute-done | bytes 139296 | tf_op jit(solution)/shard_map/ppermute | solution.py:22
  43.1 0.0 collective-permute-start.8
  43.1 0.9 %down_part.4.refs_8_ = f32[136,768]{1,0:T(8,128)S(1)} custom-call(bf16[136,512]{1,0:T(8,128)(2,1)S(1)} %get-tuple-element.44.refs_0_, bf16[136,512]{1,0:T(8,128)(2,1)S(1)} %collective-permute-done.15.refs_1_, bf16[136,512]{1,0:T(8,128)(2,1)S(1)} %collective-permute-done.9.refs_7_.refs_2_, bf16[136,512]{1,0:T(8,128)(2,1)S(1)} %collective-permute-done.16.refs_3_, ...), custom_call_target="tpu_custom_call" | custom-call | flops 641728512 | bytes 1000 | tf_op jit(solution)/shard_map/down_part/pallas_call | solution.py:195
  43.9 0.0 collective-permute-done.14.refs_3_
  43.9 0.0 collective-permute-done.13.refs_1_
  43.9 0.6 %down_part.5.refs_8_ = f32[136,768]{1,0:T(8,128)S(1)} custom-call(bf16[136,512]{1,0:T(8,128)(2,1)S(1)} %collective-permute-done.6.refs_7_.refs_0_, bf16[136,512]{1,0:T(8,128)(2,1)S(1)} %collective-permute-done.13.refs_1_, bf16[136,512]{1,0:T(8,128)(2,1)S(1)} %get-tuple-element.47.refs_2_, bf16[136,512]{1,0:T(8,128)(2,1)S(1)} %collective-permute-done.14.refs_3_, ...), custom_call_target="tpu_custom_call" | custom-call | flops 427819008 | bytes 1000 | tf_op jit(solution)/shard_map/down_part/pallas_call | solution.py:195
  44.6 0.0 collective-permute-done.12.refs_3_
  44.6 0.0 collective-permute-done.11.refs_1_
  44.6 0.6 %down_part.6.refs_6_ = f32[136,768]{1,0:T(8,128)S(1)} custom-call(bf16[136,512]{1,0:T(8,128)(2,1)S(1)} %collective-permute-done.10.refs_0_, bf16[136,512]{1,0:T(8,128)(2,1)S(1)} %collective-permute-done.11.refs_1_, bf16[136,512]{1,0:T(8,128)(2,1)S(1)} %get-tuple-element.39.refs_2_, bf16[136,512]{1,0:T(8,128)(2,1)S(1)} %collective-permute-done.12.refs_3_, ...), custom_call_target="tpu_custom_call" | custom-call | flops 427819008 | bytes 1000 | tf_op jit(solution)/shard_map/down_part/pallas_call | solution.py:195
  45.2 0.0 copy-start.1
  45.3 0.0 copy-start.3
  45.3 0.0 copy-start.4
  45.3 0.0 collective-permute-done.8.refs_1_
  45.3 0.4 down_part.7
  45.7 0.1 collective-permute-start.18
  45.8 3.4 %collective-permute-start.19 = (bf16[34,768]{1,0:T(8,128)(2,1)S(1)}, bf16[34,768]{1,0:T(8,128)(2,1)S(1)}, u32[]{:S(2)}, u32[]{:S(2)}) collective-permute-start(bf16[34,768]{1,0:T(8,128)(2,1)S(1)} %get-tuple-element.50), channel_id=1, source_target_pairs={{0,8},{4,12},{8,0},{12,4},{1,9},{5,13},{9,1},{13,5},{2,10},{6,14},... | collective-permute-start | bytes 156680 | tf_op jit(solution)/shard_map/ppermute | solution.py:22
  49.2 1.0 %collective-permute-start.20 = (bf16[34,768]{1,0:T(8,128)(2,1)S(1)}, bf16[34,768]{1,0:T(8,128)(2,1)S(1)}, u32[]{:S(2)}, u32[]{:S(2)}) collective-permute-start(bf16[34,768]{1,0:T(8,128)(2,1)S(1)} %get-tuple-element.51), channel_id=1, source_target_pairs={{0,12},{4,8},{8,4},{12,0},{1,13},{5,9},{9,5},{13,1},{2,14},{6,10},... | collective-permute-start | bytes 156680 | tf_op jit(solution)/shard_map/ppermute | solution.py:22
  50.2 0.0 collective-permute-done.18.refs_1_
  50.2 3.0 %collective-permute-done.19.refs_2_ = bf16[34,768]{1,0:T(8,128)(2,1)S(1)} collective-permute-done((bf16[34,768]{1,0:T(8,128)(2,1)S(1)}, bf16[34,768]{1,0:T(8,128)(2,1)S(1)}, u32[]{:S(2)}, u32[]{:S(2)}) %collective-permute-start.19) | collective-permute-done | bytes 52256 | tf_op jit(solution)/shard_map/ppermute | solution.py:22
  53.2 2.1 %collective-permute-done.20.refs_3_ = bf16[34,768]{1,0:T(8,128)(2,1)S(1)} collective-permute-done((bf16[34,768]{1,0:T(8,128)(2,1)S(1)}, bf16[34,768]{1,0:T(8,128)(2,1)S(1)}, u32[]{:S(2)}, u32[]{:S(2)}) %collective-permute-start.20) | collective-permute-done | bytes 52256 | tf_op jit(solution)/shard_map/ppermute | solution.py:22
  55.3 1.2 %combine.1 = (bf16[64,768]{1,0:T(8,128)(2,1)}, f32[2,64]{1,0:T(2,128)S(1)}) custom-call(s32[1]{0:T(128)} %bitcast.me_ref, s32[2,64]{1,0:T(2,128)S(1)} %bitcast.7, f32[2,64]{1,0:T(2,128)S(1)} %bitcast.8, bf16[64,768]{1,0:T(8,128)(2,1)S(1)} %copy-done.1, bf16[34,768]{1,0:T(8,128)(2,1)S(1)} %get-tuple-element.48.refs_0_, ...), custom_call_target="tpu_custom_call" | custom-call | flops 1000 | bytes 1000 | tf_op jit(solution)/shard_map/combine/pallas_call | solution.py:240
  56.5 1.2 %collective-permute-start.21 = (f32[2,64]{1,0:T(2,128)S(1)}, f32[2,64]{1,0:T(2,128)S(1)}, u32[]{:S(2)}, u32[]{:S(2)}) collective-permute-start(f32[2,64]{1,0:T(2,128)S(1)} %get-tuple-element.53), channel_id=1, source_target_pairs={{0,2},{1,3},{2,0},{3,1},{4,6},{5,7},{6,4},{7,5},{8,10},{9,11},{10,... | collective-permute-start | bytes 1544 | tf_op jit(solution)/shard_map/ppermute | solution.py:22
  57.6 2.4 %collective-permute-done.21 = f32[2,64]{1,0:T(2,128)S(1)} collective-permute-done((f32[2,64]{1,0:T(2,128)S(1)}, f32[2,64]{1,0:T(2,128)S(1)}, u32[]{:S(2)}, u32[]{:S(2)}) %collective-permute-start.21) | collective-permute-done | bytes 544 | tf_op jit(solution)/shard_map/ppermute | solution.py:22
  60.0 0.0 collective-permute-start.22
  60.0 1.1 %collective-permute-done.22 = f32[2,64]{1,0:T(2,128)S(1)} collective-permute-done((f32[2,64]{1,0:T(2,128)S(1)}, f32[2,64]{1,0:T(2,128)S(1)}, u32[]{:S(2)}, u32[]{:S(2)}) %collective-permute-start.22) | collective-permute-done | bytes 544 | tf_op jit(solution)/shard_map/ppermute | solution.py:22
  61.2 0.6 add_bitcast_fusion
  (8 shorter events, 0.1 us)
Async XLA Ops:
  0.6 0.9 %copy-start = (bf16[64,768]{1,0:T(8,128)(2,1)S(1)}, bf16[64,768]{1,0:T(8,128)(2,1)}, u32[]{:S(2)}) copy-start(bf16[64,768]{1,0:T(8,128)(2,1)} %tokens_ref.1) | copy-start | bytes 294916
  1.5 0.7 %copy-start.2 = (s32[64,2]{0,1:T(2,128)S(1)}, s32[64,2]{0,1:T(2,128)}, u32[]{:S(2)}) copy-start(s32[64,2]{0,1:T(2,128)} %param.8) | copy-start | bytes 1540
  2.5 10.4 %collective-permute-start = (bf16[34,768]{1,0:T(8,128)(2,1)S(1)}, bf16[34,768]{1,0:T(8,128)(2,1)S(1)}, u32[]{:S(2)}, u32[]{:S(2)}) collective-permute-start(bf16[34,768]{1,0:T(8,128)(2,1)S(1)} %get-tuple-element.29), channel_id=1, source_target_pairs={{0,4},{4,0},{8,12},{12,8},{1,5},{5,1},{9,13},{13,9},{2,6},{6,2},{1... | collective-permute-start | bytes 156680 | tf_op jit(solution)/shard_map/ppermute | solution.py:22
  5.6 7.3 %collective-permute-start.1 = (bf16[34,768]{1,0:T(8,128)(2,1)S(1)}, bf16[34,768]{1,0:T(8,128)(2,1)S(1)}, u32[]{:S(2)}, u32[]{:S(2)}) collective-permute-start(bf16[34,768]{1,0:T(8,128)(2,1)S(1)} %get-tuple-element.30), channel_id=1, source_target_pairs={{0,8},{4,12},{8,0},{12,4},{1,9},{5,13},{9,1},{13,5},{2,10},{6,14},... | collective-permute-start | bytes 156680 | tf_op jit(solution)/shard_map/ppermute | solution.py:22
  8.2 6.0 %collective-permute-start.2 = (bf16[34,768]{1,0:T(8,128)(2,1)S(1)}, bf16[34,768]{1,0:T(8,128)(2,1)S(1)}, u32[]{:S(2)}, u32[]{:S(2)}) collective-permute-start(bf16[34,768]{1,0:T(8,128)(2,1)S(1)} %get-tuple-element.31), channel_id=1, source_target_pairs={{0,12},{4,8},{8,4},{12,0},{1,13},{5,9},{9,5},{13,1},{2,14},{6,10},... | collective-permute-start | bytes 156680 | tf_op jit(solution)/shard_map/ppermute | solution.py:22
  14.3 6.3 %collective-permute-start.4 = (bf16[136,768]{1,0:T(8,128)(2,1)S(1)}, bf16[136,768]{1,0:T(8,128)(2,1)S(1)}, u32[]{:S(2)}, u32[]{:S(2)}) collective-permute-start(bf16[136,768]{1,0:T(8,128)(2,1)S(1)} %pack.1.refs_2_.refs_0_), channel_id=1, source_target_pairs={{0,2},{1,3},{2,0},{3,1},{4,6},{5,7},{6,4},{7,5},{8,10},{9,11},{10,... | collective-permute-start | bytes 626696 | tf_op jit(solution)/shard_map/ppermute | solution.py:22
  15.9 5.3 %collective-permute-start.3 = (bf16[136,768]{1,0:T(8,128)(2,1)S(1)}, bf16[136,768]{1,0:T(8,128)(2,1)S(1)}, u32[]{:S(2)}, u32[]{:S(2)}) collective-permute-start(bf16[136,768]{1,0:T(8,128)(2,1)S(1)} %pack.1.refs_2_.refs_0_), channel_id=1, source_target_pairs={{0,1},{1,0},{2,3},{3,2},{4,5},{5,4},{6,7},{7,6},{8,9},{9,8},{10,11... | collective-permute-start | bytes 626696 | tf_op jit(solution)/shard_map/ppermute | solution.py:22
  20.6 1.7 %collective-permute-start.5 = (bf16[136,768]{1,0:T(8,128)(2,1)S(1)}, bf16[136,768]{1,0:T(8,128)(2,1)S(1)}, u32[]{:S(2)}, u32[]{:S(2)}) collective-permute-start(bf16[136,768]{1,0:T(8,128)(2,1)S(1)} %hold.1.refs_2_), channel_id=1, source_target_pairs={{0,1},{1,0},{2,3},{3,2},{4,5},{5,4},{6,7},{7,6},{8,9},{9,8},{10,11... | collective-permute-start | bytes 626696 | tf_op jit(solution)/shard_map/ppermute | solution.py:22
  24.8 6.0 %collective-permute-start.9 = (bf16[136,512]{1,0:T(8,128)(2,1)S(1)}, bf16[136,512]{1,0:T(8,128)(2,1)S(1)}, u32[]{:S(2)}, u32[]{:S(2)}) collective-permute-start(bf16[136,512]{1,0:T(8,128)(2,1)S(1)} %get-tuple-element.44.refs_0_), channel_id=1, source_target_pairs={{0,2},{1,3},{2,0},{3,1},{4,6},{5,7},{6,4},{7,5},{8,10},{9,11},{10,... | collective-permute-start | bytes 417800 | tf_op jit(solution)/shard_map/ppermute | solution.py:22
  28.4 5.8 %collective-permute-start.6 = (bf16[136,512]{1,0:T(8,128)(2,1)S(1)}, bf16[136,512]{1,0:T(8,128)(2,1)S(1)}, u32[]{:S(2)}, u32[]{:S(2)}) collective-permute-start(bf16[136,512]{1,0:T(8,128)(2,1)S(1)} %get-tuple-element.38.refs_4_), channel_id=1, source_target_pairs={{0,2},{1,3},{2,0},{3,1},{4,6},{5,7},{6,4},{7,5},{8,10},{9,11},{10,... | collective-permute-start | bytes 417800 | tf_op jit(solution)/shard_map/ppermute | solution.py:22
  29.7 8.7 %collective-permute-start.15 = (bf16[136,512]{1,0:T(8,128)(2,1)S(1)}, bf16[136,512]{1,0:T(8,128)(2,1)S(1)}, u32[]{:S(2)}, u32[]{:S(2)}) collective-permute-start(bf16[136,512]{1,0:T(8,128)(2,1)S(1)} %get-tuple-element.44.refs_0_), channel_id=1, source_target_pairs={{0,1},{1,0},{2,3},{3,2},{4,5},{5,4},{6,7},{7,6},{8,9},{9,8},{10,11... | collective-permute-start | bytes 417800 | tf_op jit(solution)/shard_map/ppermute | solution.py:22
  29.7 8.9 %collective-permute-start.17 = (bf16[136,512]{1,0:T(8,128)(2,1)S(1)}, bf16[136,512]{1,0:T(8,128)(2,1)S(1)}, u32[]{:S(2)}, u32[]{:S(2)}) collective-permute-start(bf16[136,512]{1,0:T(8,128)(2,1)S(1)} %get-tuple-element.38.refs_4_), channel_id=1, source_target_pairs={{0,1},{1,0},{2,3},{3,2},{4,5},{5,4},{6,7},{7,6},{8,9},{9,8},{10,11... | collective-permute-start | bytes 417800 | tf_op jit(solution)/shard_map/ppermute | solution.py:22
  33.5 5.4 %collective-permute-start.10 = (bf16[136,512]{1,0:T(8,128)(2,1)S(1)}, bf16[136,512]{1,0:T(8,128)(2,1)S(1)}, u32[]{:S(2)}, u32[]{:S(2)}) collective-permute-start(bf16[136,512]{1,0:T(8,128)(2,1)S(1)} %get-tuple-element.47.refs_2_), channel_id=1, source_target_pairs={{0,2},{1,3},{2,0},{3,1},{4,6},{5,7},{6,4},{7,5},{8,10},{9,11},{10,... | collective-permute-start | bytes 417800 | tf_op jit(solution)/shard_map/ppermute | solution.py:22
  34.2 4.9 %collective-permute-start.16 = (bf16[136,512]{1,0:T(8,128)(2,1)S(1)}, bf16[136,512]{1,0:T(8,128)(2,1)S(1)}, u32[]{:S(2)}, u32[]{:S(2)}) collective-permute-start(bf16[136,512]{1,0:T(8,128)(2,1)S(1)} %collective-permute-done.9.refs_7_.refs_2_), channel_id=1, source_target_pairs={{0,1},{1,0},{2,3},{3,2},{4,5},{5,4},{6,7},{7,6},{8,9},{9,8},{10,11... | collective-permute-start | bytes 417800 | tf_op jit(solution)/shard_map/ppermute | solution.py:22
  36.9 6.2 %collective-permute-start.7 = (bf16[136,512]{1,0:T(8,128)(2,1)S(1)}, bf16[136,512]{1,0:T(8,128)(2,1)S(1)}, u32[]{:S(2)}, u32[]{:S(2)}) collective-permute-start(bf16[136,512]{1,0:T(8,128)(2,1)S(1)} %get-tuple-element.39.refs_2_), channel_id=1, source_target_pairs={{0,2},{1,3},{2,0},{3,1},{4,6},{5,7},{6,4},{7,5},{8,10},{9,11},{10,... | collective-permute-start | bytes 417800 | tf_op jit(solution)/shard_map/ppermute | solution.py:22
  38.4 5.5 %collective-permute-start.14 = (bf16[136,512]{1,0:T(8,128)(2,1)S(1)}, bf16[136,512]{1,0:T(8,128)(2,1)S(1)}, u32[]{:S(2)}, u32[]{:S(2)}) collective-permute-start(bf16[136,512]{1,0:T(8,128)(2,1)S(1)} %get-tuple-element.47.refs_2_), channel_id=1, source_target_pairs={{0,1},{1,0},{2,3},{3,2},{4,5},{5,4},{6,7},{7,6},{8,9},{9,8},{10,11... | collective-permute-start | bytes 417800 | tf_op jit(solution)/shard_map/ppermute | solution.py:22
  38.6 5.3 %collective-permute-start.13 = (bf16[136,512]{1,0:T(8,128)(2,1)S(1)}, bf16[136,512]{1,0:T(8,128)(2,1)S(1)}, u32[]{:S(2)}, u32[]{:S(2)}) collective-permute-start(bf16[136,512]{1,0:T(8,128)(2,1)S(1)} %collective-permute-done.6.refs_7_.refs_0_), channel_id=1, source_target_pairs={{0,1},{1,0},{2,3},{3,2},{4,5},{5,4},{6,7},{7,6},{8,9},{9,8},{10,11... | collective-permute-start | bytes 417800 | tf_op jit(solution)/shard_map/ppermute | solution.py:22
  38.9 5.7 %collective-permute-start.12 = (bf16[136,512]{1,0:T(8,128)(2,1)S(1)}, bf16[136,512]{1,0:T(8,128)(2,1)S(1)}, u32[]{:S(2)}, u32[]{:S(2)}) collective-permute-start(bf16[136,512]{1,0:T(8,128)(2,1)S(1)} %get-tuple-element.39.refs_2_), channel_id=1, source_target_pairs={{0,1},{1,0},{2,3},{3,2},{4,5},{5,4},{6,7},{7,6},{8,9},{9,8},{10,11... | collective-permute-start | bytes 417800 | tf_op jit(solution)/shard_map/ppermute | solution.py:22
  39.1 5.5 %collective-permute-start.11 = (bf16[136,512]{1,0:T(8,128)(2,1)S(1)}, bf16[136,512]{1,0:T(8,128)(2,1)S(1)}, u32[]{:S(2)}, u32[]{:S(2)}) collective-permute-start(bf16[136,512]{1,0:T(8,128)(2,1)S(1)} %collective-permute-done.10.refs_0_), channel_id=1, source_target_pairs={{0,1},{1,0},{2,3},{3,2},{4,5},{5,4},{6,7},{7,6},{8,9},{9,8},{10,11... | collective-permute-start | bytes 417800 | tf_op jit(solution)/shard_map/ppermute | solution.py:22
  43.1 2.2 %collective-permute-start.8 = (bf16[136,512]{1,0:T(8,128)(2,1)S(1)}, bf16[136,512]{1,0:T(8,128)(2,1)S(1)}, u32[]{:S(2)}, u32[]{:S(2)}) collective-permute-start(bf16[136,512]{1,0:T(8,128)(2,1)S(1)} %collective-permute-done.7.refs_0_), channel_id=1, source_target_pairs={{0,1},{1,0},{2,3},{3,2},{4,5},{5,4},{6,7},{7,6},{8,9},{9,8},{10,11... | collective-permute-start | bytes 417800 | tf_op jit(solution)/shard_map/ppermute | solution.py:22
  45.2 10.0 %copy-start.1 = (bf16[64,768]{1,0:T(8,128)(2,1)S(1)}, bf16[64,768]{1,0:T(8,128)(2,1)}, u32[]{:S(2)}) copy-start(bf16[64,768]{1,0:T(8,128)(2,1)} %grad_ref.1) | copy-start | bytes 294916
  45.3 10.0 %copy-start.3 = (s32[64,2]{0,1:T(2,128)S(1)}, s32[64,2]{0,1:T(2,128)}, u32[]{:S(2)}) copy-start(s32[64,2]{0,1:T(2,128)} %param.8) | copy-start | bytes 1540
  45.3 10.0 %copy-start.4 = (f32[64,2]{0,1:T(2,128)S(1)}, f32[64,2]{0,1:T(2,128)}, u32[]{:S(2)}) copy-start(f32[64,2]{0,1:T(2,128)} %param.9) | copy-start | bytes 1540
  45.7 4.5 %collective-permute-start.18 = (bf16[34,768]{1,0:T(8,128)(2,1)S(1)}, bf16[34,768]{1,0:T(8,128)(2,1)S(1)}, u32[]{:S(2)}, u32[]{:S(2)}) collective-permute-start(bf16[34,768]{1,0:T(8,128)(2,1)S(1)} %get-tuple-element.49), channel_id=1, source_target_pairs={{0,4},{4,0},{8,12},{12,8},{1,5},{5,1},{9,13},{13,9},{2,6},{6,2},{1... | collective-permute-start | bytes 156680 | tf_op jit(solution)/shard_map/ppermute | solution.py:22
  45.8 7.4 %collective-permute-start.19 = (bf16[34,768]{1,0:T(8,128)(2,1)S(1)}, bf16[34,768]{1,0:T(8,128)(2,1)S(1)}, u32[]{:S(2)}, u32[]{:S(2)}) collective-permute-start(bf16[34,768]{1,0:T(8,128)(2,1)S(1)} %get-tuple-element.50), channel_id=1, source_target_pairs={{0,8},{4,12},{8,0},{12,4},{1,9},{5,13},{9,1},{13,5},{2,10},{6,14},... | collective-permute-start | bytes 156680 | tf_op jit(solution)/shard_map/ppermute | solution.py:22
  49.2 6.1 %collective-permute-start.20 = (bf16[34,768]{1,0:T(8,128)(2,1)S(1)}, bf16[34,768]{1,0:T(8,128)(2,1)S(1)}, u32[]{:S(2)}, u32[]{:S(2)}) collective-permute-start(bf16[34,768]{1,0:T(8,128)(2,1)S(1)} %get-tuple-element.51), channel_id=1, source_target_pairs={{0,12},{4,8},{8,4},{12,0},{1,13},{5,9},{9,5},{13,1},{2,14},{6,10},... | collective-permute-start | bytes 156680 | tf_op jit(solution)/shard_map/ppermute | solution.py:22
  56.5 3.6 %collective-permute-start.21 = (f32[2,64]{1,0:T(2,128)S(1)}, f32[2,64]{1,0:T(2,128)S(1)}, u32[]{:S(2)}, u32[]{:S(2)}) collective-permute-start(f32[2,64]{1,0:T(2,128)S(1)} %get-tuple-element.53), channel_id=1, source_target_pairs={{0,2},{1,3},{2,0},{3,1},{4,6},{5,7},{6,4},{7,5},{8,10},{9,11},{10,... | collective-permute-start | bytes 1544 | tf_op jit(solution)/shard_map/ppermute | solution.py:22
  60.0 1.1 %collective-permute-start.22 = (f32[2,64]{1,0:T(2,128)S(1)}, f32[2,64]{1,0:T(2,128)S(1)}, u32[]{:S(2)}, u32[]{:S(2)}) collective-permute-start(f32[2,64]{1,0:T(2,128)S(1)} %add.6), channel_id=1, source_target_pairs={{0,1},{1,0},{2,3},{3,2},{4,5},{5,4},{6,7},{7,6},{8,9},{9,8},{10,11... | collective-permute-start | bytes 1544 | tf_op jit(solution)/shard_map/ppermute | solution.py:22

commit v4 on v3

--- a/solution.py
+++ b/solution.py
@@ -14,7 +14,7 @@
 VMEM_LIMIT = 24 * 1024 * 1024
 SMALL_LIMIT = 4 * 1024 * 1024
 FF_TILE = 256
-K_TILE = 512
+K_TILE = 256
 
 
 def swap(value, axis, bit):
@@ -50,8 +50,16 @@
     return hits, picks
 
 
-def select_kernel(me_ref, t_ref, ids_ref, tokens_ref, *out_refs):
+def select_kernel(me_ref, t_ref, ids_hbm, tokens_hbm, *refs):
+    out_refs = refs[:EXPERTS]
+    ids_ref, tokens_ref, sems = refs[EXPERTS:]
+    ids_copy = pltpu.make_async_copy(ids_hbm, ids_ref, sems.at[0])
+    tokens_copy = pltpu.make_async_copy(tokens_hbm, tokens_ref, sems.at[1])
+    ids_copy.start()
+    tokens_copy.start()
+    ids_copy.wait()
     _, picks = routing(ids_ref[...], me_ref[0])
+    tokens_copy.wait()
     for pick, out_ref in zip(picks, out_refs):
         out_ref[...] = jnp.dot(pick.astype(BF), tokens_ref[...], preferred_element_type=F32).astype(BF)
 
@@ -61,11 +69,16 @@
     return pl.pallas_call(
         select_kernel,
         out_shape=[jax.ShapeDtypeStruct((MOST, width), BF)] * EXPERTS,
-        in_specs=[SMEM, SMEM, VMEM, VMEM],
+        in_specs=[SMEM, SMEM, ANY, ANY],
         out_specs=[VMEM] * EXPERTS,
+        scratch_shapes=[
+            pltpu.VMEM(ids_t.shape, ids_t.dtype),
+            pltpu.VMEM(tokens.shape, tokens.dtype),
+            pltpu.SemaphoreType.DMA((2,)),
+        ],
         name="select_rows",
         **SMALL,
-    )(me, t, ids_t, tokens)
+    )(me, t, *(pltpu.with_memory_space_constraint(v, pltpu.HBM) for v in (ids_t, tokens)))
 
 
 def pack_kernel(*refs):
@@ -129,14 +142,10 @@
     )(*weights, *after)
 
 
-def hidden_kernel(parts, number, t_ref, *refs):
+def hidden_kernel(parts, t_ref, *refs):
     x_refs = refs[:parts]
-    gate_ref, up_ref, down_ref = refs[parts:parts + 3]
-    out_ref, share_ref, sem = refs[-3:]
-    slab = share_ref.shape[0]
-    row = pl.multiple_of((t_ref[0] ^ number) * slab, slab)
-    copy = pltpu.make_async_copy(down_ref.at[0, pl.ds(row, slab), :], share_ref, sem)
-    copy.start()
+    gate_ref, up_ref = refs[parts:parts + 2]
+    out_ref = refs[-1]
     depth = x_refs[0].shape[1]
     for tile in range(0, out_ref.shape[1], FF_TILE):
         columns = slice(tile, tile + FF_TILE)
@@ -149,33 +158,31 @@
             gate = g if gate is None else gate + g
             up = u if up is None else up + u
         out_ref[:, tile:tile + FF_TILE] = (gate * jax.nn.sigmoid(gate) * up).astype(BF)
-    copy.wait()
-
-
-def hidden_part(t, xs, gate_run, up_run, down_weight, number, slab, after=()):
+
+
+def hidden_part(t, xs, gate_run, up_run, after=()):
     rows, size = xs[0].shape[0], gate_run.shape[1]
-    width = down_weight.shape[2]
-    return pl.pallas_call(
-        functools.partial(hidden_kernel, len(xs), number),
-        out_shape=[jax.ShapeDtypeStruct((rows, size), BF), pltpu.VMEM((slab, width), BF)],
-        in_specs=[SMEM] + [VMEM] * (len(xs) + 2) + [ANY] * (1 + len(after)),
-        out_specs=[VMEM, ANY],
-        scratch_shapes=[pltpu.SemaphoreType.DMA],
+    return pl.pallas_call(
+        functools.partial(hidden_kernel, len(xs)),
+        out_shape=jax.ShapeDtypeStruct((rows, size), BF),
+        in_specs=[SMEM] + [VMEM] * (len(xs) + 2) + [ANY] * len(after),
+        out_specs=VMEM,
         compiler_params=pltpu.CompilerParams(vmem_limit_bytes=SMALL_LIMIT),
         cost_estimate=pl.CostEstimate(flops=1000, bytes_accessed=1000, transcendentals=0),
         name="hidden_part",
-    )(t, *xs, gate_run, up_run, down_weight, *after)
-
-
-def down_kernel(count, where, has_sum, last, *refs):
+    )(t, *xs, gate_run, up_run, *after)
+
+
+def down_kernel(count, where, slab, has_sum, last, t_ref, *refs):
     pieces = refs[:count]
-    weight_refs = refs[count:count + EXPERTS]
-    rest = refs[count + EXPERTS:]
+    weight_ref = refs[count]
+    rest = refs[count + 1:]
     outs = rest[has_sum:]
     total = rest[0][...] if has_sum else None
     for piece, (j, first) in zip(pieces, where):
         size = piece.shape[1]
-        term = jnp.dot(piece[...], weight_refs[j][first:first + size, :], preferred_element_type=F32)
+        row = pl.multiple_of((t_ref[0] ^ j) * slab + first, K_TILE)
+        term = jnp.dot(piece[...], weight_ref[0, pl.ds(row, size), :], preferred_element_type=F32)
         total = term if total is None else total + term
     if last:
         for k, out in enumerate(outs):
@@ -184,25 +191,25 @@
         outs[0][...] = total
 
 
-def down_part(pieces, where, weights, running, last):
+def down_part(t, slab, pieces, where, weight, running, last):
     rows = pieces[0].shape[0]
-    width = weights[0].shape[1]
+    width = weight.shape[2]
     has_sum = running is not None
     if last:
         out_shape = [jax.ShapeDtypeStruct((MOST, width), BF)] * EXPERTS
     else:
         out_shape = [jax.ShapeDtypeStruct((rows, width), F32)]
     return pl.pallas_call(
-        functools.partial(down_kernel, len(pieces), where, has_sum, last),
+        functools.partial(down_kernel, len(pieces), where, slab, has_sum, last),
         out_shape=out_shape,
-        in_specs=[VMEM] * (len(pieces) + len(weights) + has_sum),
+        in_specs=[SMEM] + [VMEM] * (len(pieces) + 1 + has_sum),
         out_specs=[VMEM] * len(out_shape),
         compiler_params=pltpu.CompilerParams(vmem_limit_bytes=SMALL_LIMIT),
         cost_estimate=pl.CostEstimate(
             flops=2 * rows * width * sum(p.shape[1] for p in pieces), bytes_accessed=1000, transcendentals=0
         ),
         name="down_part",
-    )(*pieces, *weights, *([running] if has_sum else []))
+    )(t, *pieces, weight, *([running] if has_sum else []))
 
 
 def combine_kernel(me_ref, ids_ref, probs_ref, grad_ref, *refs):
@@ -258,8 +265,8 @@
     t_index = lax.axis_index("tensor").astype(jnp.int32).reshape(1)
     slab = gate_weight.shape[2]
     ids_t, probs_t = expert_ids.T, gate_probs.T
-    gate_weight, up_weight, down_weight = (
-        pltpu.with_memory_space_constraint(w, pltpu.HBM) for w in (gate_weight, up_weight, down_weight)
+    gate_weight, up_weight = (
+        pltpu.with_memory_space_constraint(w, pltpu.HBM) for w in (gate_weight, up_weight)
     )
 
     rows = select_rows(me, t_index, ids_t, tokens)
@@ -273,24 +280,25 @@
     across = hold(swap(own, "tensor", 2), loaded[-1:])
     xs = [own, swap(own, "tensor", 1), across, swap(across, "tensor", 1)]
 
-    pieces, shares = [], []
+    pieces = []
     for i in range(len(CHUNKS)):
         after = [pieces[i - 2][2]] if i >= 2 else loaded[2 * half:2 * half + 1]
-        h, share = hidden_part(t_index, xs, loaded[2 * i], loaded[2 * i + 1], down_weight, i, slab, after)
-        far = swap(h, "tensor", 2)
-        pieces.append([h, swap(h, "tensor", 1), far, swap(far, "tensor", 1)])
-        shares.append(share)
-    running = None
+        h = hidden_part(t_index, xs, loaded[2 * i], loaded[2 * i + 1], after)
+        pieces.append([h, swap(h, "tensor", 1), swap(h, "tensor", 2)])
+    sums = []
     for i, start in enumerate(starts):
+        far = hold(pieces[i][2], sums[i - 2:i - 1]) if i >= 2 else pieces[i][2]
+        pieces[i] = pieces[i][:2] + [far, swap(far, "tensor", 1)]
         use = [(i, 2), (i, 3)]
         if i == 0:
             use = [(0, 0), (0, 1)] + use
         if i + 1 < len(starts):
             use += [(i + 1, 0), (i + 1, 1)]
         result = down_part(
-            [pieces[n][j] for n, j in use], [(j, starts[n]) for n, j in use], shares, running, i + 1 == len(starts)
+            t_index, slab, [pieces[n][j] for n, j in use], [(j, starts[n]) for n, j in use], down_weight,
+            sums[-1] if sums else None, i + 1 == len(starts),
         )
-        running = result[0]
+        sums.append(result[0])
     back = [result[0]] + [swap(result[k], "expert", k) for k in (1, 2, 3)]
     mixed, gate_grad = combine(me, ids_t, probs_t, out_grad, back)
     gate_grad = gate_grad + swap(gate_grad, "tensor", 2)

time: 62 us -> 57.2 us (0.923)
  Pallas kernels: 24.2 us -> 18.8 us
  waiting for transfers between devices: 15.3 us -> 18.8 us
  local copies, waits for them, and re-layouts: 1.58 us -> 0.03 us
  starting transfers between devices: 19.3 us -> 18 us
    pallas_call x8, Pallas kernels: 13.1 us -> 6.94 us  [the longest x4 4.39 us: hidden_part(): pl.pallas_call(functools.partial(hidden_kernel, len(xs)), out_shape=jax.S...]
    ppermute x23, waiting for transfers between devices: 15.3 us -> 18.8 us  [swap(): return lax.ppermute(value, axis, [(i, i ^ bit) for i in range(size)])]
    unnamed x10 -> x12, local copies, waits for them, and re-layouts: 1.58 us -> 0.03 us
    ppermute x23, starting transfers between devices: 19.3 us -> 18 us  [swap(): return lax.ppermute(value, axis, [(i, i ^ bit) for i in range(size)])]
    pallas_call x1, Pallas kernels: 0.33 us -> 1.14 us  [select_rows(): pl.pallas_call(select_kernel, out_shape=[jax.ShapeDtypeStruct((MOST, widt...]
  transfers between devices with their start and end apart: 23 -> 23, of which waited for: 8 -> 12; matrix products, arithmetic and copies ran while one was open for 0% -> 0% of each run, Pallas kernels for 32% -> 26%
where the time goes in v4:
time: 57.2 us; the launch traced here: 57 us
  Pallas kernels  18.8 us (33%)
  waiting for transfers between devices  18.8 us (33%)
  starting transfers between devices  18 us (31%)
  between operations  0.85 us (1%)
    ppermute x23, waiting for transfers between devices, swap(): return lax.ppermute(value, axis, [(i, i ^ bit) for i in range(size)])  18.8 us
    ppermute x23, starting transfers between devices, swap(): return lax.ppermute(value, axis, [(i, i ^ bit) for i in range(size)])  18 us
    pallas_call x2, Pallas kernels, load(): pl.pallas_call(functools.partial(load_kernel, runs, count), out_shape=[pl...  9.46 us
    pallas_call x4, Pallas kernels, hidden_part(): pl.pallas_call(functools.partial(hidden_kernel, len(xs)), out_shape=jax.S...  4.39 us
    pallas_call x4, Pallas kernels, down_part(): pl.pallas_call(functools.partial(down_kernel, len(pieces), where, slab, h...  2.55 us
    pallas_call x1, Pallas kernels, combine(): pl.pallas_call(combine_kernel, out_shape=[jax.ShapeDtypeStruct(out_grad.s...  1.2 us
    pallas_call x1, Pallas kernels, select_rows(): pl.pallas_call(select_kernel, out_shape=[jax.ShapeDtypeStruct((MOST, widt...  1.14 us
  transfers between devices with their start and end apart: 23, of which 12 were waited for; matrix products, arithmetic and copies ran while one was open for 0% of the time, Pallas kernels for 26%

profile of v4, /device:TPU:0, one launch (start us, length us, event | category | flops | bytes accessed | tf_op | source)
XLA Modules:
  0.0 57.0 jit_solution(6041629855651387249)
XLA Ops:
  0.6 1.1 %select_rows.1 = (bf16[34,768]{1,0:T(8,128)(2,1)S(1)}, bf16[34,768]{1,0:T(8,128)(2,1)S(1)}, bf16[34,768]{1,0:T(8,128)(2,1)S(1)}, bf16[34,768]{1,0:T(8,128)(2,1)S(1)}) custom-call(s32[1]{0:T(128)} %bitcast.me_ref, s32[1]{0:T(128)} %bitcast.3.t_ref, s32[2,64]{1,0:T(2,128)} %bitcast.8, bf16[64,768]{1,0:T(8,128)(2,1)} %tokens_hbm.1), custom_call_target="tpu_custom_call" | custom-call | flops 1000 | bytes 1000 | tf_op jit(solution)/shard_map/select_rows/pallas_call | solution.py:69
  1.8 3.1 %collective-permute-start = (bf16[34,768]{1,0:T(8,128)(2,1)S(1)}, bf16[34,768]{1,0:T(8,128)(2,1)S(1)}, u32[]{:S(2)}, u32[]{:S(2)}) collective-permute-start(bf16[34,768]{1,0:T(8,128)(2,1)S(1)} %get-tuple-element.21), channel_id=1, source_target_pairs={{0,4},{4,0},{8,12},{12,8},{1,5},{5,1},{9,13},{13,9},{2,6},{6,2},{1... | collective-permute-start | bytes 156680 | tf_op jit(solution)/shard_map/ppermute | solution.py:22
  4.9 2.6 %collective-permute-start.1 = (bf16[34,768]{1,0:T(8,128)(2,1)S(1)}, bf16[34,768]{1,0:T(8,128)(2,1)S(1)}, u32[]{:S(2)}, u32[]{:S(2)}) collective-permute-start(bf16[34,768]{1,0:T(8,128)(2,1)S(1)} %get-tuple-element.22), channel_id=1, source_target_pairs={{0,8},{4,12},{8,0},{12,4},{1,9},{5,13},{9,1},{13,5},{2,10},{6,14},... | collective-permute-start | bytes 156680 | tf_op jit(solution)/shard_map/ppermute | solution.py:22
  7.5 0.0 collective-permute-start.2
  7.5 4.7 %load.2 = (bf16[3072,512]{1,0:T(8,128)(2,1)S(1)}, bf16[3072,512]{1,0:T(8,128)(2,1)S(1)}, bf16[3072,512]{1,0:T(8,128)(2,1)S(1)}, bf16[3072,512]{1,0:T(8,128)(2,1)S(1)}) custom-call(bf16[1,3072,2048]{2,1,0:T(8,128)(2,1)} %refs_0_.3, bf16[1,3072,2048]{2,1,0:T(8,128)(2,1)} %refs_1_.3, bf16[34,768]{1,0:T(8,128)(2,1)S(1)} %get-tuple-element.20.refs_2_.refs_0_), custom_call_target="tpu_custom_call" | custom-call | bytes 25165824 | tf_op jit(solution)/shard_map/load/pallas_call | solution.py:133
  12.2 0.0 collective-permute-done.refs_1_
  12.2 0.0 collective-permute-done.1.refs_2_
  12.2 1.3 %collective-permute-done.2.refs_3_ = bf16[34,768]{1,0:T(8,128)(2,1)S(1)} collective-permute-done((bf16[34,768]{1,0:T(8,128)(2,1)S(1)}, bf16[34,768]{1,0:T(8,128)(2,1)S(1)}, u32[]{:S(2)}, u32[]{:S(2)}) %collective-permute-start.2) | collective-permute-done | bytes 52256 | tf_op jit(solution)/shard_map/ppermute | solution.py:22
  13.5 1.6 %collective-permute-start.4 = (bf16[136,768]{1,0:T(8,128)(2,1)S(1)}, bf16[136,768]{1,0:T(8,128)(2,1)S(1)}, u32[]{:S(2)}, u32[]{:S(2)}) collective-permute-start(bf16[136,768]{1,0:T(8,128)(2,1)S(1)} %pack.1.refs_2_.refs_0_), channel_id=1, source_target_pairs={{0,2},{1,3},{2,0},{3,1},{4,6},{5,7},{6,4},{7,5},{8,10},{9,11},{10,... | collective-permute-start | bytes 626696 | tf_op jit(solution)/shard_map/ppermute | solution.py:22
  15.1 0.0 collective-permute-start.3
  15.1 4.7 %load.3 = (bf16[3072,512]{1,0:T(8,128)(2,1)S(1)}, bf16[3072,512]{1,0:T(8,128)(2,1)S(1)}, bf16[3072,512]{1,0:T(8,128)(2,1)S(1)}, bf16[3072,512]{1,0:T(8,128)(2,1)S(1)}) custom-call(bf16[1,3072,2048]{2,1,0:T(8,128)(2,1)} %refs_0_.3, bf16[1,3072,2048]{2,1,0:T(8,128)(2,1)} %refs_1_.3, bf16[136,768]{1,0:T(8,128)(2,1)S(1)} %pack.1.refs_2_.refs_0_), custom_call_target="tpu_custom_call" | custom-call | bytes 25165824 | tf_op jit(solution)/shard_map/load/pallas_call | solution.py:133
  19.8 0.0 collective-permute-done.4.refs_0_
  19.9 0.6 %collective-permute-start.5 = (bf16[136,768]{1,0:T(8,128)(2,1)S(1)}, bf16[136,768]{1,0:T(8,128)(2,1)S(1)}, u32[]{:S(2)}, u32[]{:S(2)}) collective-permute-start(bf16[136,768]{1,0:T(8,128)(2,1)S(1)} %hold.3.refs_2_), channel_id=1, source_target_pairs={{0,1},{1,0},{2,3},{3,2},{4,5},{5,4},{6,7},{7,6},{8,9},{9,8},{10,11... | collective-permute-start | bytes 626696 | tf_op jit(solution)/shard_map/ppermute | solution.py:22
  20.4 0.0 collective-permute-done.3.refs_1_
  20.4 1.1 %collective-permute-done.5.refs_3_ = bf16[136,768]{1,0:T(8,128)(2,1)S(1)} collective-permute-done((bf16[136,768]{1,0:T(8,128)(2,1)S(1)}, bf16[136,768]{1,0:T(8,128)(2,1)S(1)}, u32[]{:S(2)}, u32[]{:S(2)}) %collective-permute-start.5) | collective-permute-done | bytes 208928 | tf_op jit(solution)/shard_map/ppermute | solution.py:22
  21.5 1.1 %hidden_part.6.refs_0_ = bf16[136,512]{1,0:T(8,128)(2,1)S(1)} custom-call(s32[1]{0:T(128)} %bitcast.3.t_ref, bf16[136,768]{1,0:T(8,128)(2,1)S(1)} %pack.1.refs_2_.refs_0_, bf16[136,768]{1,0:T(8,128)(2,1)S(1)} %collective-permute-done.3.refs_1_, bf16[136,768]{1,0:T(8,128)(2,1)S(1)} %hold.3.refs_2_, bf16[136,768]{1,0:T(8,128)(2,1)S(1)} %collective-permute-done.5.refs_3_, ...), custom_call_target="tpu_custom_call" | custom-call | flops 1000 | bytes 1000 | tf_op jit(solution)/shard_map/hidden_part/pallas_call | solution.py:165
  22.6 0.9 %collective-permute-start.9 = (bf16[136,512]{1,0:T(8,128)(2,1)S(1)}, bf16[136,512]{1,0:T(8,128)(2,1)S(1)}, u32[]{:S(2)}, u32[]{:S(2)}) collective-permute-start(bf16[136,512]{1,0:T(8,128)(2,1)S(1)} %hidden_part.6.refs_0_), channel_id=1, source_target_pairs={{0,2},{1,3},{2,0},{3,1},{4,6},{5,7},{6,4},{7,5},{8,10},{9,11},{10,... | collective-permute-start | bytes 417800 | tf_op jit(solution)/shard_map/ppermute | solution.py:22
  23.5 1.1 %hidden_part.4.refs_4_ = bf16[136,512]{1,0:T(8,128)(2,1)S(1)} custom-call(s32[1]{0:T(128)} %bitcast.3.t_ref, bf16[136,768]{1,0:T(8,128)(2,1)S(1)} %pack.1.refs_2_.refs_0_, bf16[136,768]{1,0:T(8,128)(2,1)S(1)} %collective-permute-done.3.refs_1_, bf16[136,768]{1,0:T(8,128)(2,1)S(1)} %hold.3.refs_2_, bf16[136,768]{1,0:T(8,128)(2,1)S(1)} %collective-permute-done.5.refs_3_, ...), custom_call_target="tpu_custom_call" | custom-call | flops 1000 | bytes 1000 | tf_op jit(solution)/shard_map/hidden_part/pallas_call | solution.py:165
  24.6 1.3 %collective-permute-start.6 = (bf16[136,512]{1,0:T(8,128)(2,1)S(1)}, bf16[136,512]{1,0:T(8,128)(2,1)S(1)}, u32[]{:S(2)}, u32[]{:S(2)}) collective-permute-start(bf16[136,512]{1,0:T(8,128)(2,1)S(1)} %hidden_part.4.refs_4_), channel_id=1, source_target_pairs={{0,2},{1,3},{2,0},{3,1},{4,6},{5,7},{6,4},{7,5},{8,10},{9,11},{10,... | collective-permute-start | bytes 417800 | tf_op jit(solution)/shard_map/ppermute | solution.py:22
  25.9 0.0 collective-permute-start.13
  25.9 0.5 collective-permute-start.11
  26.4 2.8 %collective-permute-done.9.refs_6_.refs_2_ = bf16[136,512]{1,0:T(8,128)(2,1)S(1)} collective-permute-done((bf16[136,512]{1,0:T(8,128)(2,1)S(1)}, bf16[136,512]{1,0:T(8,128)(2,1)S(1)}, u32[]{:S(2)}, u32[]{:S(2)}) %collective-permute-start.9) | collective-permute-done | bytes 139296 | tf_op jit(solution)/shard_map/ppermute | solution.py:22
  29.2 0.0 collective-permute-start.12
  29.2 1.1 %hidden_part.7.refs_2_ = bf16[136,512]{1,0:T(8,128)(2,1)S(1)} custom-call(s32[1]{0:T(128)} %bitcast.3.t_ref, bf16[136,768]{1,0:T(8,128)(2,1)S(1)} %pack.1.refs_2_.refs_0_, bf16[136,768]{1,0:T(8,128)(2,1)S(1)} %collective-permute-done.3.refs_1_, bf16[136,768]{1,0:T(8,128)(2,1)S(1)} %hold.3.refs_2_, bf16[136,768]{1,0:T(8,128)(2,1)S(1)} %collective-permute-done.5.refs_3_, ...), custom_call_target="tpu_custom_call" | custom-call | flops 1000 | bytes 1000 | tf_op jit(solution)/shard_map/hidden_part/pallas_call | solution.py:165
  30.3 0.7 %collective-permute-start.15 = (bf16[136,512]{1,0:T(8,128)(2,1)S(1)}, bf16[136,512]{1,0:T(8,128)(2,1)S(1)}, u32[]{:S(2)}, u32[]{:S(2)}) collective-permute-start(bf16[136,512]{1,0:T(8,128)(2,1)S(1)} %hidden_part.7.refs_2_), channel_id=1, source_target_pairs={{0,2},{1,3},{2,0},{3,1},{4,6},{5,7},{6,4},{7,5},{8,10},{9,11},{10,... | collective-permute-start | bytes 417800 | tf_op jit(solution)/shard_map/ppermute | solution.py:22
  31.0 0.6 %collective-permute-done.6.refs_6_.refs_0_ = bf16[136,512]{1,0:T(8,128)(2,1)S(1)} collective-permute-done((bf16[136,512]{1,0:T(8,128)(2,1)S(1)}, bf16[136,512]{1,0:T(8,128)(2,1)S(1)}, u32[]{:S(2)}, u32[]{:S(2)}) %collective-permute-start.6) | collective-permute-done | bytes 139296 | tf_op jit(solution)/shard_map/ppermute | solution.py:22
  31.6 0.0 collective-permute-start.8
  31.6 0.0 collective-permute-done.13.refs_5_
  31.6 0.5 collective-permute-start.10
  32.1 1.1 %hidden_part.5.refs_2_ = bf16[136,512]{1,0:T(8,128)(2,1)S(1)} custom-call(s32[1]{0:T(128)} %bitcast.3.t_ref, bf16[136,768]{1,0:T(8,128)(2,1)S(1)} %pack.1.refs_2_.refs_0_, bf16[136,768]{1,0:T(8,128)(2,1)S(1)} %collective-permute-done.3.refs_1_, bf16[136,768]{1,0:T(8,128)(2,1)S(1)} %hold.3.refs_2_, bf16[136,768]{1,0:T(8,128)(2,1)S(1)} %collective-permute-done.5.refs_3_, ...), custom_call_target="tpu_custom_call" | custom-call | flops 1000 | bytes 1000 | tf_op jit(solution)/shard_map/hidden_part/pallas_call | solution.py:165
  33.2 0.0 collective-permute-done.11.refs_1_
  33.2 0.8 %collective-permute-start.7 = (bf16[136,512]{1,0:T(8,128)(2,1)S(1)}, bf16[136,512]{1,0:T(8,128)(2,1)S(1)}, u32[]{:S(2)}, u32[]{:S(2)}) collective-permute-start(bf16[136,512]{1,0:T(8,128)(2,1)S(1)} %hidden_part.5.refs_2_), channel_id=1, source_target_pairs={{0,2},{1,3},{2,0},{3,1},{4,6},{5,7},{6,4},{7,5},{8,10},{9,11},{10,... | collective-permute-start | bytes 417800 | tf_op jit(solution)/shard_map/ppermute | solution.py:22
  34.1 0.0 collective-permute-done.12.refs_3_
  34.1 0.0 collective-permute-start.17
  34.1 0.0 slice-done
  34.1 0.9 %down_part.4.refs_5_.refs_1_ = f32[136,768]{1,0:T(8,128)S(1)} custom-call(s32[1]{0:T(128)} %bitcast.3.t_ref, bf16[136,512]{1,0:T(8,128)(2,1)S(1)} %hidden_part.6.refs_0_, bf16[136,512]{1,0:T(8,128)(2,1)S(1)} %collective-permute-done.11.refs_1_, bf16[136,512]{1,0:T(8,128)(2,1)S(1)} %collective-permute-done.9.refs_6_.refs_2_, ...), custom_call_target="tpu_custom_call" | custom-call | flops 641728512 | bytes 1000 | tf_op jit(solution)/shard_map/down_part/pallas_call | solution.py:202
  35.0 1.8 %collective-permute-done.15.refs_0_ = bf16[136,512]{1,0:T(8,128)(2,1)S(1)} collective-permute-done((bf16[136,512]{1,0:T(8,128)(2,1)S(1)}, bf16[136,512]{1,0:T(8,128)(2,1)S(1)}, u32[]{:S(2)}, u32[]{:S(2)}) %collective-permute-start.15) | collective-permute-done | bytes 139296 | tf_op jit(solution)/shard_map/ppermute | solution.py:22
  36.8 0.0 collective-permute-start.16
  36.8 0.0 collective-permute-done.8.refs_1_
  36.8 0.0 collective-permute-done.10.refs_3_
  36.8 0.6 %down_part.5.refs_1_.refs_5_ = f32[136,768]{1,0:T(8,128)S(1)} custom-call(s32[1]{0:T(128)} %bitcast.3.t_ref, bf16[136,512]{1,0:T(8,128)(2,1)S(1)} %collective-permute-done.6.refs_6_.refs_0_, bf16[136,512]{1,0:T(8,128)(2,1)S(1)} %collective-permute-done.8.refs_1_, bf16[136,512]{1,0:T(8,128)(2,1)S(1)} %hidden_part.7.refs_2_, ...), custom_call_target="tpu_custom_call" | custom-call | flops 427819008 | bytes 1000 | tf_op jit(solution)/shard_map/down_part/pallas_call | solution.py:202
  37.5 1.9 %collective-permute-done.7.refs_0_ = bf16[136,512]{1,0:T(8,128)(2,1)S(1)} collective-permute-done((bf16[136,512]{1,0:T(8,128)(2,1)S(1)}, bf16[136,512]{1,0:T(8,128)(2,1)S(1)}, u32[]{:S(2)}, u32[]{:S(2)}) %collective-permute-start.7) | collective-permute-done | bytes 139296 | tf_op jit(solution)/shard_map/ppermute | solution.py:22
  39.4 0.0 collective-permute-start.14
  39.4 0.0 collective-permute-done.17.refs_3_
  39.4 0.0 collective-permute-done.16.refs_1_
  39.5 0.6 %down_part.6.refs_3_ = f32[136,768]{1,0:T(8,128)S(1)} custom-call(s32[1]{0:T(128)} %bitcast.3.t_ref, bf16[136,512]{1,0:T(8,128)(2,1)S(1)} %hold.5.refs_0_, bf16[136,512]{1,0:T(8,128)(2,1)S(1)} %collective-permute-done.16.refs_1_, bf16[136,512]{1,0:T(8,128)(2,1)S(1)} %hidden_part.5.refs_2_, bf16[136,512]{1,0:T(8,128)(2,1)S(1)} %collective-permute-done.17.refs_3_, ...), custom_call_target="tpu_custom_call" | custom-call | flops 427819008 | bytes 1000 | tf_op jit(solution)/shard_map/down_part/pallas_call | solution.py:202
  40.1 0.0 copy-start
  40.1 0.0 copy-start.1
  40.1 0.0 copy-start.2
  40.1 0.7 %collective-permute-done.14.refs_1_ = bf16[136,512]{1,0:T(8,128)(2,1)S(1)} collective-permute-done((bf16[136,512]{1,0:T(8,128)(2,1)S(1)}, bf16[136,512]{1,0:T(8,128)(2,1)S(1)}, u32[]{:S(2)}, u32[]{:S(2)}) %collective-permute-start.14) | collective-permute-done | bytes 139296 | tf_op jit(solution)/shard_map/ppermute | solution.py:22
  40.8 0.4 down_part.7
  41.2 0.1 collective-permute-start.18
  41.3 3.1 %collective-permute-start.19 = (bf16[34,768]{1,0:T(8,128)(2,1)S(1)}, bf16[34,768]{1,0:T(8,128)(2,1)S(1)}, u32[]{:S(2)}, u32[]{:S(2)}) collective-permute-start(bf16[34,768]{1,0:T(8,128)(2,1)S(1)} %get-tuple-element.34), channel_id=1, source_target_pairs={{0,8},{4,12},{8,0},{12,4},{1,9},{5,13},{9,1},{13,5},{2,10},{6,14},... | collective-permute-start | bytes 156680 | tf_op jit(solution)/shard_map/ppermute | solution.py:22
  44.4 1.2 %collective-permute-start.20 = (bf16[34,768]{1,0:T(8,128)(2,1)S(1)}, bf16[34,768]{1,0:T(8,128)(2,1)S(1)}, u32[]{:S(2)}, u32[]{:S(2)}) collective-permute-start(bf16[34,768]{1,0:T(8,128)(2,1)S(1)} %get-tuple-element.35), channel_id=1, source_target_pairs={{0,12},{4,8},{8,4},{12,0},{1,13},{5,9},{9,5},{13,1},{2,14},{6,10},... | collective-permute-start | bytes 156680 | tf_op jit(solution)/shard_map/ppermute | solution.py:22
  45.7 0.7 %collective-permute-done.18.refs_1_ = bf16[34,768]{1,0:T(8,128)(2,1)S(1)} collective-permute-done((bf16[34,768]{1,0:T(8,128)(2,1)S(1)}, bf16[34,768]{1,0:T(8,128)(2,1)S(1)}, u32[]{:S(2)}, u32[]{:S(2)}) %collective-permute-start.18) | collective-permute-done | bytes 52256 | tf_op jit(solution)/shard_map/ppermute | solution.py:22
  46.4 1.9 %collective-permute-done.19.refs_2_ = bf16[34,768]{1,0:T(8,128)(2,1)S(1)} collective-permute-done((bf16[34,768]{1,0:T(8,128)(2,1)S(1)}, bf16[34,768]{1,0:T(8,128)(2,1)S(1)}, u32[]{:S(2)}, u32[]{:S(2)}) %collective-permute-start.19) | collective-permute-done | bytes 52256 | tf_op jit(solution)/shard_map/ppermute | solution.py:22
  48.3 2.2 %collective-permute-done.20.refs_3_ = bf16[34,768]{1,0:T(8,128)(2,1)S(1)} collective-permute-done((bf16[34,768]{1,0:T(8,128)(2,1)S(1)}, bf16[34,768]{1,0:T(8,128)(2,1)S(1)}, u32[]{:S(2)}, u32[]{:S(2)}) %collective-permute-start.20) | collective-permute-done | bytes 52256 | tf_op jit(solution)/shard_map/ppermute | solution.py:22
  50.6 0.0 copy-done.1
  50.6 1.2 %combine.1 = (bf16[64,768]{1,0:T(8,128)(2,1)}, f32[2,64]{1,0:T(2,128)S(1)}) custom-call(s32[1]{0:T(128)} %bitcast.me_ref, s32[2,64]{1,0:T(2,128)S(1)} %bitcast.9, f32[2,64]{1,0:T(2,128)S(1)} %bitcast.10, bf16[64,768]{1,0:T(8,128)(2,1)S(1)} %copy-done, bf16[34,768]{1,0:T(8,128)(2,1)S(1)} %get-tuple-element.32.refs_0_, ...), custom_call_target="tpu_custom_call" | custom-call | flops 1000 | bytes 1000 | tf_op jit(solution)/shard_map/combine/pallas_call | solution.py:247
  51.8 1.0 %collective-permute-start.21 = (f32[2,64]{1,0:T(2,128)S(1)}, f32[2,64]{1,0:T(2,128)S(1)}, u32[]{:S(2)}, u32[]{:S(2)}) collective-permute-start(f32[2,64]{1,0:T(2,128)S(1)} %get-tuple-element.37), channel_id=1, source_target_pairs={{0,2},{1,3},{2,0},{3,1},{4,6},{5,7},{6,4},{7,5},{8,10},{9,11},{10,... | collective-permute-start | bytes 1544 | tf_op jit(solution)/shard_map/ppermute | solution.py:22
  52.8 2.6 %collective-permute-done.21 = f32[2,64]{1,0:T(2,128)S(1)} collective-permute-done((f32[2,64]{1,0:T(2,128)S(1)}, f32[2,64]{1,0:T(2,128)S(1)}, u32[]{:S(2)}, u32[]{:S(2)}) %collective-permute-start.21) | collective-permute-done | bytes 544 | tf_op jit(solution)/shard_map/ppermute | solution.py:22
  55.3 0.0 collective-permute-start.22
  55.3 1.1 %collective-permute-done.22 = f32[2,64]{1,0:T(2,128)S(1)} collective-permute-done((f32[2,64]{1,0:T(2,128)S(1)}, f32[2,64]{1,0:T(2,128)S(1)}, u32[]{:S(2)}, u32[]{:S(2)}) %collective-permute-start.22) | collective-permute-done | bytes 544 | tf_op jit(solution)/shard_map/ppermute | solution.py:22
  56.5 0.6 add_bitcast_fusion
  (13 shorter events, 0.1 us)
Async XLA Ops:
  1.8 10.4 %collective-permute-start = (bf16[34,768]{1,0:T(8,128)(2,1)S(1)}, bf16[34,768]{1,0:T(8,128)(2,1)S(1)}, u32[]{:S(2)}, u32[]{:S(2)}) collective-permute-start(bf16[34,768]{1,0:T(8,128)(2,1)S(1)} %get-tuple-element.21), channel_id=1, source_target_pairs={{0,4},{4,0},{8,12},{12,8},{1,5},{5,1},{9,13},{13,9},{2,6},{6,2},{1... | collective-permute-start | bytes 156680 | tf_op jit(solution)/shard_map/ppermute | solution.py:22
  4.9 7.3 %collective-permute-start.1 = (bf16[34,768]{1,0:T(8,128)(2,1)S(1)}, bf16[34,768]{1,0:T(8,128)(2,1)S(1)}, u32[]{:S(2)}, u32[]{:S(2)}) collective-permute-start(bf16[34,768]{1,0:T(8,128)(2,1)S(1)} %get-tuple-element.22), channel_id=1, source_target_pairs={{0,8},{4,12},{8,0},{12,4},{1,9},{5,13},{9,1},{13,5},{2,10},{6,14},... | collective-permute-start | bytes 156680 | tf_op jit(solution)/shard_map/ppermute | solution.py:22
  7.5 6.0 %collective-permute-start.2 = (bf16[34,768]{1,0:T(8,128)(2,1)S(1)}, bf16[34,768]{1,0:T(8,128)(2,1)S(1)}, u32[]{:S(2)}, u32[]{:S(2)}) collective-permute-start(bf16[34,768]{1,0:T(8,128)(2,1)S(1)} %get-tuple-element.23), channel_id=1, source_target_pairs={{0,12},{4,8},{8,4},{12,0},{1,13},{5,9},{9,5},{13,1},{2,14},{6,10},... | collective-permute-start | bytes 156680 | tf_op jit(solution)/shard_map/ppermute | solution.py:22
  13.5 6.3 %collective-permute-start.4 = (bf16[136,768]{1,0:T(8,128)(2,1)S(1)}, bf16[136,768]{1,0:T(8,128)(2,1)S(1)}, u32[]{:S(2)}, u32[]{:S(2)}) collective-permute-start(bf16[136,768]{1,0:T(8,128)(2,1)S(1)} %pack.1.refs_2_.refs_0_), channel_id=1, source_target_pairs={{0,2},{1,3},{2,0},{3,1},{4,6},{5,7},{6,4},{7,5},{8,10},{9,11},{10,... | collective-permute-start | bytes 626696 | tf_op jit(solution)/shard_map/ppermute | solution.py:22
  15.1 5.3 %collective-permute-start.3 = (bf16[136,768]{1,0:T(8,128)(2,1)S(1)}, bf16[136,768]{1,0:T(8,128)(2,1)S(1)}, u32[]{:S(2)}, u32[]{:S(2)}) collective-permute-start(bf16[136,768]{1,0:T(8,128)(2,1)S(1)} %pack.1.refs_2_.refs_0_), channel_id=1, source_target_pairs={{0,1},{1,0},{2,3},{3,2},{4,5},{5,4},{6,7},{7,6},{8,9},{9,8},{10,11... | collective-permute-start | bytes 626696 | tf_op jit(solution)/shard_map/ppermute | solution.py:22
  19.9 1.7 %collective-permute-start.5 = (bf16[136,768]{1,0:T(8,128)(2,1)S(1)}, bf16[136,768]{1,0:T(8,128)(2,1)S(1)}, u32[]{:S(2)}, u32[]{:S(2)}) collective-permute-start(bf16[136,768]{1,0:T(8,128)(2,1)S(1)} %hold.3.refs_2_), channel_id=1, source_target_pairs={{0,1},{1,0},{2,3},{3,2},{4,5},{5,4},{6,7},{7,6},{8,9},{9,8},{10,11... | collective-permute-start | bytes 626696 | tf_op jit(solution)/shard_map/ppermute | solution.py:22
  22.6 6.6 %collective-permute-start.9 = (bf16[136,512]{1,0:T(8,128)(2,1)S(1)}, bf16[136,512]{1,0:T(8,128)(2,1)S(1)}, u32[]{:S(2)}, u32[]{:S(2)}) collective-permute-start(bf16[136,512]{1,0:T(8,128)(2,1)S(1)} %hidden_part.6.refs_0_), channel_id=1, source_target_pairs={{0,2},{1,3},{2,0},{3,1},{4,6},{5,7},{6,4},{7,5},{8,10},{9,11},{10,... | collective-permute-start | bytes 417800 | tf_op jit(solution)/shard_map/ppermute | solution.py:22
  23.5 10.6 %slice-start = ((s8[12582912]{0:T(1024)(128)(4,1)}), s8[4194304]{0:T(1024)(128)(4,1)S(1)}, s32[]{:S(2)}) async-start(s8[12582912]{0:T(1024)(128)(4,1)} %bitcast.6), calls=%async_computation | async-start | bytes 8388608
  23.5 10.6 %slice-start.1 = ((s8[12582912]{0:T(1024)(128)(4,1)}), s8[4194304]{0:T(1024)(128)(4,1)S(1)}, s32[]{:S(2)}) async-start(s8[12582912]{0:T(1024)(128)(4,1)} %bitcast.6), calls=%async_computation.1 | async-start | bytes 8388608
  24.6 7.0 %collective-permute-start.6 = (bf16[136,512]{1,0:T(8,128)(2,1)S(1)}, bf16[136,512]{1,0:T(8,128)(2,1)S(1)}, u32[]{:S(2)}, u32[]{:S(2)}) collective-permute-start(bf16[136,512]{1,0:T(8,128)(2,1)S(1)} %hidden_part.4.refs_4_), channel_id=1, source_target_pairs={{0,2},{1,3},{2,0},{3,1},{4,6},{5,7},{6,4},{7,5},{8,10},{9,11},{10,... | collective-permute-start | bytes 417800 | tf_op jit(solution)/shard_map/ppermute | solution.py:22
  25.9 5.7 %collective-permute-start.13 = (bf16[136,512]{1,0:T(8,128)(2,1)S(1)}, bf16[136,512]{1,0:T(8,128)(2,1)S(1)}, u32[]{:S(2)}, u32[]{:S(2)}) collective-permute-start(bf16[136,512]{1,0:T(8,128)(2,1)S(1)} %hidden_part.4.refs_4_), channel_id=1, source_target_pairs={{0,1},{1,0},{2,3},{3,2},{4,5},{5,4},{6,7},{7,6},{8,9},{9,8},{10,11... | collective-permute-start | bytes 417800 | tf_op jit(solution)/shard_map/ppermute | solution.py:22
  25.9 7.3 %collective-permute-start.11 = (bf16[136,512]{1,0:T(8,128)(2,1)S(1)}, bf16[136,512]{1,0:T(8,128)(2,1)S(1)}, u32[]{:S(2)}, u32[]{:S(2)}) collective-permute-start(bf16[136,512]{1,0:T(8,128)(2,1)S(1)} %hidden_part.6.refs_0_), channel_id=1, source_target_pairs={{0,1},{1,0},{2,3},{3,2},{4,5},{5,4},{6,7},{7,6},{8,9},{9,8},{10,11... | collective-permute-start | bytes 417800 | tf_op jit(solution)/shard_map/ppermute | solution.py:22
  29.2 4.9 %collective-permute-start.12 = (bf16[136,512]{1,0:T(8,128)(2,1)S(1)}, bf16[136,512]{1,0:T(8,128)(2,1)S(1)}, u32[]{:S(2)}, u32[]{:S(2)}) collective-permute-start(bf16[136,512]{1,0:T(8,128)(2,1)S(1)} %collective-permute-done.9.refs_6_.refs_2_), channel_id=1, source_target_pairs={{0,1},{1,0},{2,3},{3,2},{4,5},{5,4},{6,7},{7,6},{8,9},{9,8},{10,11... | collective-permute-start | bytes 417800 | tf_op jit(solution)/shard_map/ppermute | solution.py:22
  29.2 4.9 %slice-start.2 = ((s8[12582912]{0:T(1024)(128)(4,1)}), s8[4194304]{0:T(1024)(128)(4,1)S(1)}, s32[]{:S(2)}) async-start(s8[12582912]{0:T(1024)(128)(4,1)} %bitcast.6), calls=%async_computation.2 | async-start | bytes 8388608
  30.3 6.5 %collective-permute-start.15 = (bf16[136,512]{1,0:T(8,128)(2,1)S(1)}, bf16[136,512]{1,0:T(8,128)(2,1)S(1)}, u32[]{:S(2)}, u32[]{:S(2)}) collective-permute-start(bf16[136,512]{1,0:T(8,128)(2,1)S(1)} %hidden_part.7.refs_2_), channel_id=1, source_target_pairs={{0,2},{1,3},{2,0},{3,1},{4,6},{5,7},{6,4},{7,5},{8,10},{9,11},{10,... | collective-permute-start | bytes 417800 | tf_op jit(solution)/shard_map/ppermute | solution.py:22
  31.6 5.2 %collective-permute-start.8 = (bf16[136,512]{1,0:T(8,128)(2,1)S(1)}, bf16[136,512]{1,0:T(8,128)(2,1)S(1)}, u32[]{:S(2)}, u32[]{:S(2)}) collective-permute-start(bf16[136,512]{1,0:T(8,128)(2,1)S(1)} %collective-permute-done.6.refs_6_.refs_0_), channel_id=1, source_target_pairs={{0,1},{1,0},{2,3},{3,2},{4,5},{5,4},{6,7},{7,6},{8,9},{9,8},{10,11... | collective-permute-start | bytes 417800 | tf_op jit(solution)/shard_map/ppermute | solution.py:22
  31.6 5.2 %collective-permute-start.10 = (bf16[136,512]{1,0:T(8,128)(2,1)S(1)}, bf16[136,512]{1,0:T(8,128)(2,1)S(1)}, u32[]{:S(2)}, u32[]{:S(2)}) collective-permute-start(bf16[136,512]{1,0:T(8,128)(2,1)S(1)} %hidden_part.7.refs_2_), channel_id=1, source_target_pairs={{0,1},{1,0},{2,3},{3,2},{4,5},{5,4},{6,7},{7,6},{8,9},{9,8},{10,11... | collective-permute-start | bytes 417800 | tf_op jit(solution)/shard_map/ppermute | solution.py:22
  33.2 6.2 %collective-permute-start.7 = (bf16[136,512]{1,0:T(8,128)(2,1)S(1)}, bf16[136,512]{1,0:T(8,128)(2,1)S(1)}, u32[]{:S(2)}, u32[]{:S(2)}) collective-permute-start(bf16[136,512]{1,0:T(8,128)(2,1)S(1)} %hidden_part.5.refs_2_), channel_id=1, source_target_pairs={{0,2},{1,3},{2,0},{3,1},{4,6},{5,7},{6,4},{7,5},{8,10},{9,11},{10,... | collective-permute-start | bytes 417800 | tf_op jit(solution)/shard_map/ppermute | solution.py:22
  34.1 5.4 %collective-permute-start.17 = (bf16[136,512]{1,0:T(8,128)(2,1)S(1)}, bf16[136,512]{1,0:T(8,128)(2,1)S(1)}, u32[]{:S(2)}, u32[]{:S(2)}) collective-permute-start(bf16[136,512]{1,0:T(8,128)(2,1)S(1)} %hidden_part.5.refs_2_), channel_id=1, source_target_pairs={{0,1},{1,0},{2,3},{3,2},{4,5},{5,4},{6,7},{7,6},{8,9},{9,8},{10,11... | collective-permute-start | bytes 417800 | tf_op jit(solution)/shard_map/ppermute | solution.py:22
  36.8 2.6 %collective-permute-start.16 = (bf16[136,512]{1,0:T(8,128)(2,1)S(1)}, bf16[136,512]{1,0:T(8,128)(2,1)S(1)}, u32[]{:S(2)}, u32[]{:S(2)}) collective-permute-start(bf16[136,512]{1,0:T(8,128)(2,1)S(1)} %hold.5.refs_0_), channel_id=1, source_target_pairs={{0,1},{1,0},{2,3},{3,2},{4,5},{5,4},{6,7},{7,6},{8,9},{9,8},{10,11... | collective-permute-start | bytes 417800 | tf_op jit(solution)/shard_map/ppermute | solution.py:22
  39.4 1.4 %collective-permute-start.14 = (bf16[136,512]{1,0:T(8,128)(2,1)S(1)}, bf16[136,512]{1,0:T(8,128)(2,1)S(1)}, u32[]{:S(2)}, u32[]{:S(2)}) collective-permute-start(bf16[136,512]{1,0:T(8,128)(2,1)S(1)} %hold.4.refs_0_), channel_id=1, source_target_pairs={{0,1},{1,0},{2,3},{3,2},{4,5},{5,4},{6,7},{7,6},{8,9},{9,8},{10,11... | collective-permute-start | bytes 417800 | tf_op jit(solution)/shard_map/ppermute | solution.py:22
  40.1 10.5 %copy-start = (bf16[64,768]{1,0:T(8,128)(2,1)S(1)}, bf16[64,768]{1,0:T(8,128)(2,1)}, u32[]{:S(2)}) copy-start(bf16[64,768]{1,0:T(8,128)(2,1)} %grad_ref.1) | copy-start | bytes 294916
  40.1 10.4 %copy-start.1 = (s32[64,2]{0,1:T(2,128)S(1)}, s32[64,2]{0,1:T(2,128)}, u32[]{:S(2)}) copy-start(s32[64,2]{0,1:T(2,128)} %param.8) | copy-start | bytes 1540
  40.1 10.4 %copy-start.2 = (f32[64,2]{0,1:T(2,128)S(1)}, f32[64,2]{0,1:T(2,128)}, u32[]{:S(2)}) copy-start(f32[64,2]{0,1:T(2,128)} %param.9) | copy-start | bytes 1540
  41.2 5.2 %collective-permute-start.18 = (bf16[34,768]{1,0:T(8,128)(2,1)S(1)}, bf16[34,768]{1,0:T(8,128)(2,1)S(1)}, u32[]{:S(2)}, u32[]{:S(2)}) collective-permute-start(bf16[34,768]{1,0:T(8,128)(2,1)S(1)} %get-tuple-element.33), channel_id=1, source_target_pairs={{0,4},{4,0},{8,12},{12,8},{1,5},{5,1},{9,13},{13,9},{2,6},{6,2},{1... | collective-permute-start | bytes 156680 | tf_op jit(solution)/shard_map/ppermute | solution.py:22
  41.3 7.1 %collective-permute-start.19 = (bf16[34,768]{1,0:T(8,128)(2,1)S(1)}, bf16[34,768]{1,0:T(8,128)(2,1)S(1)}, u32[]{:S(2)}, u32[]{:S(2)}) collective-permute-start(bf16[34,768]{1,0:T(8,128)(2,1)S(1)} %get-tuple-element.34), channel_id=1, source_target_pairs={{0,8},{4,12},{8,0},{12,4},{1,9},{5,13},{9,1},{13,5},{2,10},{6,14},... | collective-permute-start | bytes 156680 | tf_op jit(solution)/shard_map/ppermute | solution.py:22
  44.4 6.1 %collective-permute-start.20 = (bf16[34,768]{1,0:T(8,128)(2,1)S(1)}, bf16[34,768]{1,0:T(8,128)(2,1)S(1)}, u32[]{:S(2)}, u32[]{:S(2)}) collective-permute-start(bf16[34,768]{1,0:T(8,128)(2,1)S(1)} %get-tuple-element.35), channel_id=1, source_target_pairs={{0,12},{4,8},{8,4},{12,0},{1,13},{5,9},{9,5},{13,1},{2,14},{6,10},... | collective-permute-start | bytes 156680 | tf_op jit(solution)/shard_map/ppermute | solution.py:22
  51.8 3.6 %collective-permute-start.21 = (f32[2,64]{1,0:T(2,128)S(1)}, f32[2,64]{1,0:T(2,128)S(1)}, u32[]{:S(2)}, u32[]{:S(2)}) collective-permute-start(f32[2,64]{1,0:T(2,128)S(1)} %get-tuple-element.37), channel_id=1, source_target_pairs={{0,2},{1,3},{2,0},{3,1},{4,6},{5,7},{6,4},{7,5},{8,10},{9,11},{10,... | collective-permute-start | bytes 1544 | tf_op jit(solution)/shard_map/ppermute | solution.py:22
  55.3 1.1 %collective-permute-start.22 = (f32[2,64]{1,0:T(2,128)S(1)}, f32[2,64]{1,0:T(2,128)S(1)}, u32[]{:S(2)}, u32[]{:S(2)}) collective-permute-start(f32[2,64]{1,0:T(2,128)S(1)} %add.6), channel_id=1, source_target_pairs={{0,1},{1,0},{2,3},{3,2},{4,5},{5,4},{6,7},{7,6},{8,9},{9,8},{10,11... | collective-permute-start | bytes 1544 | tf_op jit(solution)/shard_map/ppermute | solution.py:22

commit v5 on v4

--- a/solution.py
+++ b/solution.py
@@ -77,7 +77,8 @@
             pltpu.SemaphoreType.DMA((2,)),
         ],
         name="select_rows",
-        **SMALL,
+        compiler_params=pltpu.CompilerParams(vmem_limit_bytes=SMALL_LIMIT),
+        cost_estimate=pl.CostEstimate(flops=8_000_000_000, bytes_accessed=1000, transcendentals=0),
     )(me, t, *(pltpu.with_memory_space_constraint(v, pltpu.HBM) for v in (ids_t, tokens)))
 
 
@@ -109,68 +110,35 @@
     )(value, *after)
 
 
-def load_kernel(runs, count, *refs):
-    weight_refs = refs[:count]
-    out_refs, sems = refs[-1 - len(runs) * count:-1], refs[-1]
-    copies = []
-    for n, (start, size) in enumerate(runs):
-        for m, weight in enumerate(weight_refs):
-            copies.append(
-                pltpu.make_async_copy(
-                    weight.at[0, :, pl.ds(start, size)], out_refs[n * count + m], sems.at[n * count + m]
-                )
-            )
-    for copy in copies:
-        copy.start()
-    for copy in copies:
-        copy.wait()
-
-
-def load(weights, runs, after=()):
-    depth = weights[0].shape[1]
-    count = len(weights)
-    moved = sum(2 * depth * size * count for _, size in runs)
-    return pl.pallas_call(
-        functools.partial(load_kernel, runs, count),
-        out_shape=[pltpu.VMEM((depth, size), BF) for _, size in runs for _ in weights],
-        in_specs=[ANY] * (count + len(after)),
-        out_specs=[ANY] * (len(runs) * count),
-        scratch_shapes=[pltpu.SemaphoreType.DMA((len(runs) * count,))],
-        compiler_params=pltpu.CompilerParams(vmem_limit_bytes=SMALL_LIMIT),
-        cost_estimate=pl.CostEstimate(flops=0, bytes_accessed=2 * moved, transcendentals=0),
-        name="load",
-    )(*weights, *after)
-
-
-def hidden_kernel(parts, t_ref, *refs):
+def hidden_kernel(parts, start, t_ref, *refs):
     x_refs = refs[:parts]
     gate_ref, up_ref = refs[parts:parts + 2]
     out_ref = refs[-1]
     depth = x_refs[0].shape[1]
     for tile in range(0, out_ref.shape[1], FF_TILE):
-        columns = slice(tile, tile + FF_TILE)
+        columns = slice(start + tile, start + tile + FF_TILE)
         gate = up = None
         for j in range(parts):
             at = pl.ds(pl.multiple_of((t_ref[0] ^ j) * depth, depth), depth)
             x = x_refs[j][...]
-            g = jnp.dot(x, gate_ref[at, columns], preferred_element_type=F32)
-            u = jnp.dot(x, up_ref[at, columns], preferred_element_type=F32)
+            g = jnp.dot(x, gate_ref[0, at, columns], preferred_element_type=F32)
+            u = jnp.dot(x, up_ref[0, at, columns], preferred_element_type=F32)
             gate = g if gate is None else gate + g
             up = u if up is None else up + u
         out_ref[:, tile:tile + FF_TILE] = (gate * jax.nn.sigmoid(gate) * up).astype(BF)
 
 
-def hidden_part(t, xs, gate_run, up_run, after=()):
-    rows, size = xs[0].shape[0], gate_run.shape[1]
-    return pl.pallas_call(
-        functools.partial(hidden_kernel, len(xs)),
+def hidden_part(t, xs, gate_weight, up_weight, start, size, after=()):
+    rows = xs[0].shape[0]
+    return pl.pallas_call(
+        functools.partial(hidden_kernel, len(xs), start),
         out_shape=jax.ShapeDtypeStruct((rows, size), BF),
         in_specs=[SMEM] + [VMEM] * (len(xs) + 2) + [ANY] * len(after),
         out_specs=VMEM,
         compiler_params=pltpu.CompilerParams(vmem_limit_bytes=SMALL_LIMIT),
         cost_estimate=pl.CostEstimate(flops=1000, bytes_accessed=1000, transcendentals=0),
         name="hidden_part",
-    )(t, *xs, gate_run, up_run, *after)
+    )(t, *xs, gate_weight, up_weight, *after)
 
 
 def down_kernel(count, where, slab, has_sum, last, t_ref, *refs):
@@ -257,7 +225,7 @@
     )(me, ids_t, probs_t, out_grad, *back)
 
 
-CHUNKS = (512, 512, 512, 512)
+CHUNKS = (512, 1024, 512)
 
 
 def per_device(tokens, expert_ids, gate_probs, out_grad, gate_weight, up_weight, down_weight):
@@ -265,25 +233,18 @@
     t_index = lax.axis_index("tensor").astype(jnp.int32).reshape(1)
     slab = gate_weight.shape[2]
     ids_t, probs_t = expert_ids.T, gate_probs.T
-    gate_weight, up_weight = (
-        pltpu.with_memory_space_constraint(w, pltpu.HBM) for w in (gate_weight, up_weight)
-    )
 
     rows = select_rows(me, t_index, ids_t, tokens)
     starts = [sum(CHUNKS[:i]) for i in range(len(CHUNKS))]
-    runs = list(zip(starts, CHUNKS))
-    half = len(runs) // 2
-    loaded = list(load([gate_weight, up_weight], runs[:half], [rows[0]]))
     arrived = [rows[0]] + [swap(rows[k], "expert", k) for k in (1, 2, 3)]
-    own = pack(arrived, loaded[:1])
-    loaded += load([gate_weight, up_weight], runs[half:], [own])
-    across = hold(swap(own, "tensor", 2), loaded[-1:])
+    own = pack(arrived, [])
+    across = swap(own, "tensor", 2)
     xs = [own, swap(own, "tensor", 1), across, swap(across, "tensor", 1)]
 
     pieces = []
-    for i in range(len(CHUNKS)):
-        after = [pieces[i - 2][2]] if i >= 2 else loaded[2 * half:2 * half + 1]
-        h = hidden_part(t_index, xs, loaded[2 * i], loaded[2 * i + 1], after)
+    for i, (start, size) in enumerate(zip(starts, CHUNKS)):
+        after = [p[2] for p in pieces[i - 2:i - 1] if i >= 2] + [p[0] for p in pieces[-1:]]
+        h = hidden_part(t_index, xs, gate_weight, up_weight, start, size, after)
         pieces.append([h, swap(h, "tensor", 1), swap(h, "tensor", 2)])
     sums = []
     for i, start in enumerate(starts):

time: 57.2 us -> 60.1 us (1.051)
  waiting for transfers between devices: 18.8 us -> 31.3 us
  Pallas kernels: 18.8 us -> 9.33 us
    ppermute x23 -> x20, waiting for transfers between devices: 18.8 us -> 31.3 us  [swap(): return lax.ppermute(value, axis, [(i, i ^ bit) for i in range(size)])]
    pallas_call x6 -> x3, Pallas kernels: 13.8 us -> 4.37 us  [hidden_part(): pl.pallas_call(functools.partial(hidden_kernel, len(xs), start), out_shap...]
    pallas_call x4 -> x3, Pallas kernels: 2.55 us -> 2.42 us  [down_part(): pl.pallas_call(functools.partial(down_kernel, len(pieces), where, slab, h...]
    ppermute x23 -> x20, starting transfers between devices: 18 us -> 17.9 us  [swap(): return lax.ppermute(value, axis, [(i, i ^ bit) for i in range(size)])]
  transfers between devices with their start and end apart: 23 -> 20, of which waited for: 12 -> 11; matrix products, arithmetic and copies ran while one was open for 0% -> 0% of each run, Pallas kernels for 26% -> 5%
where the time goes in v5:
time: 60.1 us; the launch traced here: 60 us
  waiting for transfers between devices  31.3 us (52%)
  starting transfers between devices  17.9 us (30%)
  Pallas kernels  9.33 us (16%)
  between operations  0.84 us (1%)
    ppermute x20, waiting for transfers between devices, swap(): return lax.ppermute(value, axis, [(i, i ^ bit) for i in range(size)])  31.3 us
    ppermute x20, starting transfers between devices, swap(): return lax.ppermute(value, axis, [(i, i ^ bit) for i in range(size)])  17.9 us
    pallas_call x3, Pallas kernels, hidden_part(): pl.pallas_call(functools.partial(hidden_kernel, len(xs), start), out_shap...  4.37 us
    pallas_call x3, Pallas kernels, down_part(): pl.pallas_call(functools.partial(down_kernel, len(pieces), where, slab, h...  2.42 us
    pallas_call x1, Pallas kernels, select_rows(): pl.pallas_call(select_kernel, out_shape=[jax.ShapeDtypeStruct((MOST, widt...  1.3 us
  transfers between devices with their start and end apart: 20, of which 11 were waited for; matrix products, arithmetic and copies ran while one was open for 0% of the time, Pallas kernels for 5%

profile of v5, /device:TPU:0, one launch (start us, length us, event | category | flops | bytes accessed | tf_op | source)
XLA Modules:
  0.0 60.0 jit_solution(14155699451630175178)
XLA Ops:
  0.6 0.0 copy-start
  0.6 0.0 copy-start.1
  0.7 1.3 %select_rows.1 = (bf16[34,768]{1,0:T(8,128)(2,1)S(1)}, bf16[34,768]{1,0:T(8,128)(2,1)S(1)}, bf16[34,768]{1,0:T(8,128)(2,1)S(1)}, bf16[34,768]{1,0:T(8,128)(2,1)S(1)}) custom-call(s32[1]{0:T(128)} %bitcast.me_ref, s32[1]{0:T(128)} %bitcast.3.t_ref, s32[2,64]{1,0:T(2,128)} %bitcast.8, bf16[64,768]{1,0:T(8,128)(2,1)} %tokens_hbm.1), custom_call_target="tpu_custom_call" | custom-call | flops 8000000000 | bytes 1000 | tf_op jit(solution)/shard_map/select_rows/pallas_call | solution.py:69
  2.0 3.1 %collective-permute-start = (bf16[34,768]{1,0:T(8,128)(2,1)S(1)}, bf16[34,768]{1,0:T(8,128)(2,1)S(1)}, u32[]{:S(2)}, u32[]{:S(2)}) collective-permute-start(bf16[34,768]{1,0:T(8,128)(2,1)S(1)} %get-tuple-element.13), channel_id=1, source_target_pairs={{0,4},{4,0},{8,12},{12,8},{1,5},{5,1},{9,13},{13,9},{2,6},{6,2},{1... | collective-permute-start | bytes 156680 | tf_op jit(solution)/shard_map/ppermute | solution.py:22
  5.0 2.6 %collective-permute-start.1 = (bf16[34,768]{1,0:T(8,128)(2,1)S(1)}, bf16[34,768]{1,0:T(8,128)(2,1)S(1)}, u32[]{:S(2)}, u32[]{:S(2)}) collective-permute-start(bf16[34,768]{1,0:T(8,128)(2,1)S(1)} %get-tuple-element.14), channel_id=1, source_target_pairs={{0,8},{4,12},{8,0},{12,4},{1,9},{5,13},{9,1},{13,5},{2,10},{6,14},... | collective-permute-start | bytes 156680 | tf_op jit(solution)/shard_map/ppermute | solution.py:22
  7.6 0.0 collective-permute-start.2
  7.6 0.0 collective-permute-done.refs_1_
  7.6 3.8 %collective-permute-done.1.refs_2_ = bf16[34,768]{1,0:T(8,128)(2,1)S(1)} collective-permute-done((bf16[34,768]{1,0:T(8,128)(2,1)S(1)}, bf16[34,768]{1,0:T(8,128)(2,1)S(1)}, u32[]{:S(2)}, u32[]{:S(2)}) %collective-permute-start.1) | collective-permute-done | bytes 52256 | tf_op jit(solution)/shard_map/ppermute | solution.py:22
  11.4 2.3 %collective-permute-done.2.refs_3_ = bf16[34,768]{1,0:T(8,128)(2,1)S(1)} collective-permute-done((bf16[34,768]{1,0:T(8,128)(2,1)S(1)}, bf16[34,768]{1,0:T(8,128)(2,1)S(1)}, u32[]{:S(2)}, u32[]{:S(2)}) %collective-permute-start.2) | collective-permute-done | bytes 52256 | tf_op jit(solution)/shard_map/ppermute | solution.py:22
  13.7 1.6 %collective-permute-start.4 = (bf16[136,768]{1,0:T(8,128)(2,1)S(1)}, bf16[136,768]{1,0:T(8,128)(2,1)S(1)}, u32[]{:S(2)}, u32[]{:S(2)}) collective-permute-start(bf16[136,768]{1,0:T(8,128)(2,1)S(1)} %pack.1.refs_0_), channel_id=1, source_target_pairs={{0,2},{1,3},{2,0},{3,1},{4,6},{5,7},{6,4},{7,5},{8,10},{9,11},{10,... | collective-permute-start | bytes 626696 | tf_op jit(solution)/shard_map/ppermute | solution.py:22
  15.3 0.0 collective-permute-start.3
  15.3 4.3 %collective-permute-done.4.refs_2_ = bf16[136,768]{1,0:T(8,128)(2,1)S(1)} collective-permute-done((bf16[136,768]{1,0:T(8,128)(2,1)S(1)}, bf16[136,768]{1,0:T(8,128)(2,1)S(1)}, u32[]{:S(2)}, u32[]{:S(2)}) %collective-permute-start.4) | collective-permute-done | bytes 208928 | tf_op jit(solution)/shard_map/ppermute | solution.py:22
  19.6 0.0 collective-permute-start.5
  19.6 0.0 collective-permute-done.3.refs_1_
  19.6 1.5 %collective-permute-done.5.refs_3_ = bf16[136,768]{1,0:T(8,128)(2,1)S(1)} collective-permute-done((bf16[136,768]{1,0:T(8,128)(2,1)S(1)}, bf16[136,768]{1,0:T(8,128)(2,1)S(1)}, u32[]{:S(2)}, u32[]{:S(2)}) %collective-permute-start.5) | collective-permute-done | bytes 208928 | tf_op jit(solution)/shard_map/ppermute | solution.py:22
  21.0 0.0 copy-done
  21.0 0.0 copy-done.1
  21.0 1.1 %hidden_part.3.refs_6_.refs_0_ = bf16[136,512]{1,0:T(8,128)(2,1)S(1)} custom-call(s32[1]{0:T(128)} %bitcast.3.t_ref, bf16[136,768]{1,0:T(8,128)(2,1)S(1)} %pack.1.refs_0_, bf16[136,768]{1,0:T(8,128)(2,1)S(1)} %collective-permute-done.3.refs_1_, bf16[136,768]{1,0:T(8,128)(2,1)S(1)} %collective-permute-done.4.refs_2_, ...), custom_call_target="tpu_custom_call" | custom-call | flops 1000 | bytes 1000 | tf_op jit(solution)/shard_map/hidden_part/pallas_call | solution.py:133
  22.2 0.0 slice-start
  22.2 0.0 slice-start.1
  22.2 2.1 %hidden_part.4.refs_7_.refs_4_ = bf16[136,1024]{1,0:T(8,128)(2,1)S(1)} custom-call(s32[1]{0:T(128)} %bitcast.3.t_ref, bf16[136,768]{1,0:T(8,128)(2,1)S(1)} %pack.1.refs_0_, bf16[136,768]{1,0:T(8,128)(2,1)S(1)} %collective-permute-done.3.refs_1_, bf16[136,768]{1,0:T(8,128)(2,1)S(1)} %collective-permute-done.4.refs_2_, ...), custom_call_target="tpu_custom_call" | custom-call | flops 1000 | bytes 1000 | tf_op jit(solution)/shard_map/hidden_part/pallas_call | solution.py:133
  24.3 0.0 slice-start.2
  24.3 1.6 %collective-permute-start.12 = (bf16[136,1024]{1,0:T(8,128)(2,1)S(1)}, bf16[136,1024]{1,0:T(8,128)(2,1)S(1)}, u32[]{:S(2)}, u32[]{:S(2)}) collective-permute-start(bf16[136,1024]{1,0:T(8,128)(2,1)S(1)} %hidden_part.4.refs_7_.refs_4_), channel_id=1, source_target_pairs={{0,2},{1,3},{2,0},{3,1},{4,6},{5,7},{6,4},{7,5},{8,10},{9,11},{10,... | collective-permute-start | bytes 835592 | tf_op jit(solution)/shard_map/ppermute | solution.py:22
  25.9 0.5 collective-permute-start.6
  26.4 0.0 collective-permute-start.10
  26.4 0.5 collective-permute-start.8
  26.9 9.1 %collective-permute-done.6.refs_6_.refs_2_ = bf16[136,512]{1,0:T(8,128)(2,1)S(1)} collective-permute-done((bf16[136,512]{1,0:T(8,128)(2,1)S(1)}, bf16[136,512]{1,0:T(8,128)(2,1)S(1)}, u32[]{:S(2)}, u32[]{:S(2)}) %collective-permute-start.6) | collective-permute-done | bytes 139296 | tf_op jit(solution)/shard_map/ppermute | solution.py:22
  36.1 0.0 collective-permute-start.9
  36.1 0.0 collective-permute-done.12.refs_0_
  36.1 0.5 collective-permute-start.13
  36.6 1.1 %hidden_part.5.refs_2_ = bf16[136,512]{1,0:T(8,128)(2,1)S(1)} custom-call(s32[1]{0:T(128)} %bitcast.3.t_ref, bf16[136,768]{1,0:T(8,128)(2,1)S(1)} %pack.1.refs_0_, bf16[136,768]{1,0:T(8,128)(2,1)S(1)} %collective-permute-done.3.refs_1_, bf16[136,768]{1,0:T(8,128)(2,1)S(1)} %collective-permute-done.4.refs_2_, ...), custom_call_target="tpu_custom_call" | custom-call | flops 1000 | bytes 1000 | tf_op jit(solution)/shard_map/hidden_part/pallas_call | solution.py:133
  37.7 1.6 %collective-permute-start.7 = (bf16[136,512]{1,0:T(8,128)(2,1)S(1)}, bf16[136,512]{1,0:T(8,128)(2,1)S(1)}, u32[]{:S(2)}, u32[]{:S(2)}) collective-permute-start(bf16[136,512]{1,0:T(8,128)(2,1)S(1)} %hidden_part.5.refs_2_), channel_id=1, source_target_pairs={{0,2},{1,3},{2,0},{3,1},{4,6},{5,7},{6,4},{7,5},{8,10},{9,11},{10,... | collective-permute-start | bytes 417800 | tf_op jit(solution)/shard_map/ppermute | solution.py:22
  39.3 0.0 collective-permute-done.8.refs_1_
  39.3 0.0 collective-permute-start.14
  39.3 0.0 collective-permute-done.10.refs_5_
  39.3 0.0 collective-permute-done.9.refs_3_
  39.3 0.0 slice-done
  39.3 0.0 slice-done.1
  39.3 0.0 slice-done.2
  39.4 1.1 %down_part.3.refs_1_.refs_5_ = f32[136,768]{1,0:T(8,128)S(1)} custom-call(s32[1]{0:T(128)} %bitcast.3.t_ref, bf16[136,512]{1,0:T(8,128)(2,1)S(1)} %hidden_part.3.refs_6_.refs_0_, bf16[136,512]{1,0:T(8,128)(2,1)S(1)} %collective-permute-done.8.refs_1_, bf16[136,512]{1,0:T(8,128)(2,1)S(1)} %collective-permute-done.6.refs_6_.refs_2_, ...), custom_call_target="tpu_custom_call" | custom-call | flops 855638016 | bytes 1000 | tf_op jit(solution)/shard_map/down_part/pallas_call | solution.py:170
  40.5 2.9 %collective-permute-done.7.refs_0_ = bf16[136,512]{1,0:T(8,128)(2,1)S(1)} collective-permute-done((bf16[136,512]{1,0:T(8,128)(2,1)S(1)}, bf16[136,512]{1,0:T(8,128)(2,1)S(1)}, u32[]{:S(2)}, u32[]{:S(2)}) %collective-permute-start.7) | collective-permute-done | bytes 139296 | tf_op jit(solution)/shard_map/ppermute | solution.py:22
  43.4 0.0 copy-start.2
  43.4 0.0 copy-start.3
  43.4 0.1 collective-permute-start.11
  43.5 0.0 collective-permute-done.14.refs_3_
  43.5 0.0 collective-permute-done.13.refs_1_
  43.5 0.9 %down_part.4.refs_3_ = f32[136,768]{1,0:T(8,128)S(1)} custom-call(s32[1]{0:T(128)} %bitcast.3.t_ref, bf16[136,1024]{1,0:T(8,128)(2,1)S(1)} %collective-permute-done.12.refs_0_, bf16[136,1024]{1,0:T(8,128)(2,1)S(1)} %collective-permute-done.13.refs_1_, bf16[136,512]{1,0:T(8,128)(2,1)S(1)} %hidden_part.5.refs_2_, ...), custom_call_target="tpu_custom_call" | custom-call | flops 641728512 | bytes 1000 | tf_op jit(solution)/shard_map/down_part/pallas_call | solution.py:170
  44.4 0.4 collective-permute-done.11.refs_1_
  44.8 0.4 down_part.5
  45.2 0.1 collective-permute-start.15
  45.3 2.1 %collective-permute-start.16 = (bf16[34,768]{1,0:T(8,128)(2,1)S(1)}, bf16[34,768]{1,0:T(8,128)(2,1)S(1)}, u32[]{:S(2)}, u32[]{:S(2)}) collective-permute-start(bf16[34,768]{1,0:T(8,128)(2,1)S(1)} %get-tuple-element.18), channel_id=1, source_target_pairs={{0,8},{4,12},{8,0},{12,4},{1,9},{5,13},{9,1},{13,5},{2,10},{6,14},... | collective-permute-start | bytes 156680 | tf_op jit(solution)/shard_map/ppermute | solution.py:22
  47.4 2.3 %collective-permute-start.17 = (bf16[34,768]{1,0:T(8,128)(2,1)S(1)}, bf16[34,768]{1,0:T(8,128)(2,1)S(1)}, u32[]{:S(2)}, u32[]{:S(2)}) collective-permute-start(bf16[34,768]{1,0:T(8,128)(2,1)S(1)} %get-tuple-element.19), channel_id=1, source_target_pairs={{0,12},{4,8},{8,4},{12,0},{1,13},{5,9},{9,5},{13,1},{2,14},{6,10},... | collective-permute-start | bytes 156680 | tf_op jit(solution)/shard_map/ppermute | solution.py:22
  49.7 0.9 %collective-permute-done.15.refs_1_ = bf16[34,768]{1,0:T(8,128)(2,1)S(1)} collective-permute-done((bf16[34,768]{1,0:T(8,128)(2,1)S(1)}, bf16[34,768]{1,0:T(8,128)(2,1)S(1)}, u32[]{:S(2)}, u32[]{:S(2)}) %collective-permute-start.15) | collective-permute-done | bytes 52256 | tf_op jit(solution)/shard_map/ppermute | solution.py:22
  50.5 2.9 %collective-permute-done.16.refs_2_ = bf16[34,768]{1,0:T(8,128)(2,1)S(1)} collective-permute-done((bf16[34,768]{1,0:T(8,128)(2,1)S(1)}, bf16[34,768]{1,0:T(8,128)(2,1)S(1)}, u32[]{:S(2)}, u32[]{:S(2)}) %collective-permute-start.16) | collective-permute-done | bytes 52256 | tf_op jit(solution)/shard_map/ppermute | solution.py:22
  53.5 0.0 collective-permute-done.17.refs_3_
  53.5 0.0 copy-done.2
  53.5 0.0 copy-done.3
  53.5 0.0 copy-done.4
  53.5 1.2 %combine.1 = (bf16[64,768]{1,0:T(8,128)(2,1)}, f32[2,64]{1,0:T(2,128)S(1)}) custom-call(s32[1]{0:T(128)} %bitcast.me_ref, s32[2,64]{1,0:T(2,128)S(1)} %bitcast.9, f32[2,64]{1,0:T(2,128)S(1)} %bitcast.10, bf16[64,768]{1,0:T(8,128)(2,1)S(1)} %copy-done.2, bf16[34,768]{1,0:T(8,128)(2,1)S(1)} %get-tuple-element.16.refs_0_, ...), custom_call_target="tpu_custom_call" | custom-call | flops 1000 | bytes 1000 | tf_op jit(solution)/shard_map/combine/pallas_call | solution.py:215
  54.7 1.5 %collective-permute-start.18 = (f32[2,64]{1,0:T(2,128)S(1)}, f32[2,64]{1,0:T(2,128)S(1)}, u32[]{:S(2)}, u32[]{:S(2)}) collective-permute-start(f32[2,64]{1,0:T(2,128)S(1)} %get-tuple-element.21), channel_id=1, source_target_pairs={{0,2},{1,3},{2,0},{3,1},{4,6},{5,7},{6,4},{7,5},{8,10},{9,11},{10,... | collective-permute-start | bytes 1544 | tf_op jit(solution)/shard_map/ppermute | solution.py:22
  56.2 2.1 %collective-permute-done.18 = f32[2,64]{1,0:T(2,128)S(1)} collective-permute-done((f32[2,64]{1,0:T(2,128)S(1)}, f32[2,64]{1,0:T(2,128)S(1)}, u32[]{:S(2)}, u32[]{:S(2)}) %collective-permute-start.18) | collective-permute-done | bytes 544 | tf_op jit(solution)/shard_map/ppermute | solution.py:22
  58.3 0.0 collective-permute-start.19
  58.3 1.1 %collective-permute-done.19 = f32[2,64]{1,0:T(2,128)S(1)} collective-permute-done((f32[2,64]{1,0:T(2,128)S(1)}, f32[2,64]{1,0:T(2,128)S(1)}, u32[]{:S(2)}, u32[]{:S(2)}) %collective-permute-start.19) | collective-permute-done | bytes 544 | tf_op jit(solution)/shard_map/ppermute | solution.py:22
  59.4 0.6 add_bitcast_fusion
  (5 shorter events, 0.1 us)
Async XLA Ops:
  0.6 20.4 %copy-start = (bf16[1,3072,2048]{2,1,0:T(8,128)(2,1)S(1)}, bf16[1,3072,2048]{2,1,0:T(8,128)(2,1)}, u32[]{:S(2)}) copy-start(bf16[1,3072,2048]{2,1,0:T(8,128)(2,1)} %refs_4_.6) | copy-start | bytes 37748740
  0.6 20.4 %copy-start.1 = (bf16[1,3072,2048]{2,1,0:T(8,128)(2,1)S(1)}, bf16[1,3072,2048]{2,1,0:T(8,128)(2,1)}, u32[]{:S(2)}) copy-start(bf16[1,3072,2048]{2,1,0:T(8,128)(2,1)} %refs_5_.5) | copy-start | bytes 37748740
  2.0 5.7 %collective-permute-start = (bf16[34,768]{1,0:T(8,128)(2,1)S(1)}, bf16[34,768]{1,0:T(8,128)(2,1)S(1)}, u32[]{:S(2)}, u32[]{:S(2)}) collective-permute-start(bf16[34,768]{1,0:T(8,128)(2,1)S(1)} %get-tuple-element.13), channel_id=1, source_target_pairs={{0,4},{4,0},{8,12},{12,8},{1,5},{5,1},{9,13},{13,9},{2,6},{6,2},{1... | collective-permute-start | bytes 156680 | tf_op jit(solution)/shard_map/ppermute | solution.py:22
  5.0 6.4 %collective-permute-start.1 = (bf16[34,768]{1,0:T(8,128)(2,1)S(1)}, bf16[34,768]{1,0:T(8,128)(2,1)S(1)}, u32[]{:S(2)}, u32[]{:S(2)}) collective-permute-start(bf16[34,768]{1,0:T(8,128)(2,1)S(1)} %get-tuple-element.14), channel_id=1, source_target_pairs={{0,8},{4,12},{8,0},{12,4},{1,9},{5,13},{9,1},{13,5},{2,10},{6,14},... | collective-permute-start | bytes 156680 | tf_op jit(solution)/shard_map/ppermute | solution.py:22
  7.6 6.0 %collective-permute-start.2 = (bf16[34,768]{1,0:T(8,128)(2,1)S(1)}, bf16[34,768]{1,0:T(8,128)(2,1)S(1)}, u32[]{:S(2)}, u32[]{:S(2)}) collective-permute-start(bf16[34,768]{1,0:T(8,128)(2,1)S(1)} %get-tuple-element.15), channel_id=1, source_target_pairs={{0,12},{4,8},{8,4},{12,0},{1,13},{5,9},{9,5},{13,1},{2,14},{6,10},... | collective-permute-start | bytes 156680 | tf_op jit(solution)/shard_map/ppermute | solution.py:22
  13.7 5.9 %collective-permute-start.4 = (bf16[136,768]{1,0:T(8,128)(2,1)S(1)}, bf16[136,768]{1,0:T(8,128)(2,1)S(1)}, u32[]{:S(2)}, u32[]{:S(2)}) collective-permute-start(bf16[136,768]{1,0:T(8,128)(2,1)S(1)} %pack.1.refs_0_), channel_id=1, source_target_pairs={{0,2},{1,3},{2,0},{3,1},{4,6},{5,7},{6,4},{7,5},{8,10},{9,11},{10,... | collective-permute-start | bytes 626696 | tf_op jit(solution)/shard_map/ppermute | solution.py:22
  15.3 4.3 %collective-permute-start.3 = (bf16[136,768]{1,0:T(8,128)(2,1)S(1)}, bf16[136,768]{1,0:T(8,128)(2,1)S(1)}, u32[]{:S(2)}, u32[]{:S(2)}) collective-permute-start(bf16[136,768]{1,0:T(8,128)(2,1)S(1)} %pack.1.refs_0_), channel_id=1, source_target_pairs={{0,1},{1,0},{2,3},{3,2},{4,5},{5,4},{6,7},{7,6},{8,9},{9,8},{10,11... | collective-permute-start | bytes 626696 | tf_op jit(solution)/shard_map/ppermute | solution.py:22
  19.6 1.5 %collective-permute-start.5 = (bf16[136,768]{1,0:T(8,128)(2,1)S(1)}, bf16[136,768]{1,0:T(8,128)(2,1)S(1)}, u32[]{:S(2)}, u32[]{:S(2)}) collective-permute-start(bf16[136,768]{1,0:T(8,128)(2,1)S(1)} %collective-permute-done.4.refs_2_), channel_id=1, source_target_pairs={{0,1},{1,0},{2,3},{3,2},{4,5},{5,4},{6,7},{7,6},{8,9},{9,8},{10,11... | collective-permute-start | bytes 626696 | tf_op jit(solution)/shard_map/ppermute | solution.py:22
  22.2 17.1 %slice-start = ((s8[12582912]{0:T(1024)(128)(4,1)}), s8[4194304]{0:T(1024)(128)(4,1)S(1)}, s32[]{:S(2)}) async-start(s8[12582912]{0:T(1024)(128)(4,1)} %bitcast.6), calls=%async_computation | async-start | bytes 8388608
  22.2 17.1 %slice-start.1 = ((s8[12582912]{0:T(1024)(128)(4,1)}), s8[4194304]{0:T(1024)(128)(4,1)S(1)}, s32[]{:S(2)}) async-start(s8[12582912]{0:T(1024)(128)(4,1)} %bitcast.6), calls=%async_computation.1 | async-start | bytes 8388608
  24.3 15.0 %slice-start.2 = ((s8[12582912]{0:T(1024)(128)(4,1)}), s8[4194304]{0:T(1024)(128)(4,1)S(1)}, s32[]{:S(2)}) async-start(s8[12582912]{0:T(1024)(128)(4,1)} %bitcast.6), calls=%async_computation.2 | async-start | bytes 8388608
  24.3 11.8 %collective-permute-start.12 = (bf16[136,1024]{1,0:T(8,128)(2,1)S(1)}, bf16[136,1024]{1,0:T(8,128)(2,1)S(1)}, u32[]{:S(2)}, u32[]{:S(2)}) collective-permute-start(bf16[136,1024]{1,0:T(8,128)(2,1)S(1)} %hidden_part.4.refs_7_.refs_4_), channel_id=1, source_target_pairs={{0,2},{1,3},{2,0},{3,1},{4,6},{5,7},{6,4},{7,5},{8,10},{9,11},{10,... | collective-permute-start | bytes 835592 | tf_op jit(solution)/shard_map/ppermute | solution.py:22
  25.9 10.2 %collective-permute-start.6 = (bf16[136,512]{1,0:T(8,128)(2,1)S(1)}, bf16[136,512]{1,0:T(8,128)(2,1)S(1)}, u32[]{:S(2)}, u32[]{:S(2)}) collective-permute-start(bf16[136,512]{1,0:T(8,128)(2,1)S(1)} %hidden_part.3.refs_6_.refs_0_), channel_id=1, source_target_pairs={{0,2},{1,3},{2,0},{3,1},{4,6},{5,7},{6,4},{7,5},{8,10},{9,11},{10,... | collective-permute-start | bytes 417800 | tf_op jit(solution)/shard_map/ppermute | solution.py:22
  26.4 12.9 %collective-permute-start.10 = (bf16[136,1024]{1,0:T(8,128)(2,1)S(1)}, bf16[136,1024]{1,0:T(8,128)(2,1)S(1)}, u32[]{:S(2)}, u32[]{:S(2)}) collective-permute-start(bf16[136,1024]{1,0:T(8,128)(2,1)S(1)} %hidden_part.4.refs_7_.refs_4_), channel_id=1, source_target_pairs={{0,1},{1,0},{2,3},{3,2},{4,5},{5,4},{6,7},{7,6},{8,9},{9,8},{10,11... | collective-permute-start | bytes 835592 | tf_op jit(solution)/shard_map/ppermute | solution.py:22
  26.4 12.9 %collective-permute-start.8 = (bf16[136,512]{1,0:T(8,128)(2,1)S(1)}, bf16[136,512]{1,0:T(8,128)(2,1)S(1)}, u32[]{:S(2)}, u32[]{:S(2)}) collective-permute-start(bf16[136,512]{1,0:T(8,128)(2,1)S(1)} %hidden_part.3.refs_6_.refs_0_), channel_id=1, source_target_pairs={{0,1},{1,0},{2,3},{3,2},{4,5},{5,4},{6,7},{7,6},{8,9},{9,8},{10,11... | collective-permute-start | bytes 417800 | tf_op jit(solution)/shard_map/ppermute | solution.py:22
  36.1 3.2 %collective-permute-start.9 = (bf16[136,512]{1,0:T(8,128)(2,1)S(1)}, bf16[136,512]{1,0:T(8,128)(2,1)S(1)}, u32[]{:S(2)}, u32[]{:S(2)}) collective-permute-start(bf16[136,512]{1,0:T(8,128)(2,1)S(1)} %collective-permute-done.6.refs_6_.refs_2_), channel_id=1, source_target_pairs={{0,1},{1,0},{2,3},{3,2},{4,5},{5,4},{6,7},{7,6},{8,9},{9,8},{10,11... | collective-permute-start | bytes 417800 | tf_op jit(solution)/shard_map/ppermute | solution.py:22
  36.1 7.4 %collective-permute-start.13 = (bf16[136,1024]{1,0:T(8,128)(2,1)S(1)}, bf16[136,1024]{1,0:T(8,128)(2,1)S(1)}, u32[]{:S(2)}, u32[]{:S(2)}) collective-permute-start(bf16[136,1024]{1,0:T(8,128)(2,1)S(1)} %collective-permute-done.12.refs_0_), channel_id=1, source_target_pairs={{0,1},{1,0},{2,3},{3,2},{4,5},{5,4},{6,7},{7,6},{8,9},{9,8},{10,11... | collective-permute-start | bytes 835592 | tf_op jit(solution)/shard_map/ppermute | solution.py:22
  37.7 5.6 %collective-permute-start.7 = (bf16[136,512]{1,0:T(8,128)(2,1)S(1)}, bf16[136,512]{1,0:T(8,128)(2,1)S(1)}, u32[]{:S(2)}, u32[]{:S(2)}) collective-permute-start(bf16[136,512]{1,0:T(8,128)(2,1)S(1)} %hidden_part.5.refs_2_), channel_id=1, source_target_pairs={{0,2},{1,3},{2,0},{3,1},{4,6},{5,7},{6,4},{7,5},{8,10},{9,11},{10,... | collective-permute-start | bytes 417800 | tf_op jit(solution)/shard_map/ppermute | solution.py:22
  39.3 4.2 %collective-permute-start.14 = (bf16[136,512]{1,0:T(8,128)(2,1)S(1)}, bf16[136,512]{1,0:T(8,128)(2,1)S(1)}, u32[]{:S(2)}, u32[]{:S(2)}) collective-permute-start(bf16[136,512]{1,0:T(8,128)(2,1)S(1)} %hidden_part.5.refs_2_), channel_id=1, source_target_pairs={{0,1},{1,0},{2,3},{3,2},{4,5},{5,4},{6,7},{7,6},{8,9},{9,8},{10,11... | collective-permute-start | bytes 417800 | tf_op jit(solution)/shard_map/ppermute | solution.py:22
  43.4 10.1 %copy-start.2 = (bf16[64,768]{1,0:T(8,128)(2,1)S(1)}, bf16[64,768]{1,0:T(8,128)(2,1)}, u32[]{:S(2)}) copy-start(bf16[64,768]{1,0:T(8,128)(2,1)} %grad_ref.1) | copy-start | bytes 294916
  43.4 10.1 %copy-start.3 = (s32[64,2]{0,1:T(2,128)S(1)}, s32[64,2]{0,1:T(2,128)}, u32[]{:S(2)}) copy-start(s32[64,2]{0,1:T(2,128)} %param.8) | copy-start | bytes 1540
  43.4 10.1 %copy-start.4 = (f32[64,2]{0,1:T(2,128)S(1)}, f32[64,2]{0,1:T(2,128)}, u32[]{:S(2)}) copy-start(f32[64,2]{0,1:T(2,128)} %param.9) | copy-start | bytes 1540
  43.4 1.4 %collective-permute-start.11 = (bf16[136,512]{1,0:T(8,128)(2,1)S(1)}, bf16[136,512]{1,0:T(8,128)(2,1)S(1)}, u32[]{:S(2)}, u32[]{:S(2)}) collective-permute-start(bf16[136,512]{1,0:T(8,128)(2,1)S(1)} %hold.1.refs_0_), channel_id=1, source_target_pairs={{0,1},{1,0},{2,3},{3,2},{4,5},{5,4},{6,7},{7,6},{8,9},{9,8},{10,11... | collective-permute-start | bytes 417800 | tf_op jit(solution)/shard_map/ppermute | solution.py:22
  45.2 5.3 %collective-permute-start.15 = (bf16[34,768]{1,0:T(8,128)(2,1)S(1)}, bf16[34,768]{1,0:T(8,128)(2,1)S(1)}, u32[]{:S(2)}, u32[]{:S(2)}) collective-permute-start(bf16[34,768]{1,0:T(8,128)(2,1)S(1)} %get-tuple-element.17), channel_id=1, source_target_pairs={{0,4},{4,0},{8,12},{12,8},{1,5},{5,1},{9,13},{13,9},{2,6},{6,2},{1... | collective-permute-start | bytes 156680 | tf_op jit(solution)/shard_map/ppermute | solution.py:22
  45.3 8.2 %collective-permute-start.16 = (bf16[34,768]{1,0:T(8,128)(2,1)S(1)}, bf16[34,768]{1,0:T(8,128)(2,1)S(1)}, u32[]{:S(2)}, u32[]{:S(2)}) collective-permute-start(bf16[34,768]{1,0:T(8,128)(2,1)S(1)} %get-tuple-element.18), channel_id=1, source_target_pairs={{0,8},{4,12},{8,0},{12,4},{1,9},{5,13},{9,1},{13,5},{2,10},{6,14},... | collective-permute-start | bytes 156680 | tf_op jit(solution)/shard_map/ppermute | solution.py:22
  47.4 6.1 %collective-permute-start.17 = (bf16[34,768]{1,0:T(8,128)(2,1)S(1)}, bf16[34,768]{1,0:T(8,128)(2,1)S(1)}, u32[]{:S(2)}, u32[]{:S(2)}) collective-permute-start(bf16[34,768]{1,0:T(8,128)(2,1)S(1)} %get-tuple-element.19), channel_id=1, source_target_pairs={{0,12},{4,8},{8,4},{12,0},{1,13},{5,9},{9,5},{13,1},{2,14},{6,10},... | collective-permute-start | bytes 156680 | tf_op jit(solution)/shard_map/ppermute | solution.py:22
  54.7 3.6 %collective-permute-start.18 = (f32[2,64]{1,0:T(2,128)S(1)}, f32[2,64]{1,0:T(2,128)S(1)}, u32[]{:S(2)}, u32[]{:S(2)}) collective-permute-start(f32[2,64]{1,0:T(2,128)S(1)} %get-tuple-element.21), channel_id=1, source_target_pairs={{0,2},{1,3},{2,0},{3,1},{4,6},{5,7},{6,4},{7,5},{8,10},{9,11},{10,... | collective-permute-start | bytes 1544 | tf_op jit(solution)/shard_map/ppermute | solution.py:22
  58.3 1.1 %collective-permute-start.19 = (f32[2,64]{1,0:T(2,128)S(1)}, f32[2,64]{1,0:T(2,128)S(1)}, u32[]{:S(2)}, u32[]{:S(2)}) collective-permute-start(f32[2,64]{1,0:T(2,128)S(1)} %add.6), channel_id=1, source_target_pairs={{0,1},{1,0},{2,3},{3,2},{4,5},{5,4},{6,7},{7,6},{8,9},{9,8},{10,11... | collective-permute-start | bytes 1544 | tf_op jit(solution)/shard_map/ppermute | solution.py:22

commit v6 on v5

--- a/solution.py
+++ b/solution.py
@@ -225,7 +225,7 @@
     )(me, ids_t, probs_t, out_grad, *back)
 
 
-CHUNKS = (512, 1024, 512)
+CHUNKS = (256, 512, 768, 512)
 
 
 def per_device(tokens, expert_ids, gate_probs, out_grad, gate_weight, up_weight, down_weight):
@@ -243,7 +243,7 @@
 
     pieces = []
     for i, (start, size) in enumerate(zip(starts, CHUNKS)):
-        after = [p[2] for p in pieces[i - 2:i - 1] if i >= 2] + [p[0] for p in pieces[-1:]]
+        after = [pieces[i - 2][2]] if i >= 2 else []
         h = hidden_part(t_index, xs, gate_weight, up_weight, start, size, after)
         pieces.append([h, swap(h, "tensor", 1), swap(h, "tensor", 2)])
     sums = []

time: 60.1 us -> 54.9 us (0.913)
  waiting for transfers between devices: 31.3 us -> 25.8 us
    ppermute x20 -> x23, waiting for transfers between devices: 31.3 us -> 25.8 us  [swap(): return lax.ppermute(value, axis, [(i, i ^ bit) for i in range(size)])]
    pallas_call x3 -> x4, Pallas kernels: 4.37 us -> 4.53 us  [hidden_part(): pl.pallas_call(functools.partial(hidden_kernel, len(xs), start), out_shap...]
    pallas_call x3 -> x4, Pallas kernels: 2.42 us -> 2.56 us  [down_part(): pl.pallas_call(functools.partial(down_kernel, len(pieces), where, slab, h...]
    ppermute x20 -> x23, starting transfers between devices: 17.9 us -> 18 us  [swap(): return lax.ppermute(value, axis, [(i, i ^ bit) for i in range(size)])]
  transfers between devices with their start and end apart: 20 -> 23, of which waited for: 11 -> 13; matrix products, arithmetic and copies ran while one was open for 0% -> 0% of each run, Pallas kernels for 5% -> 11%
where the time goes in v6:
time: 54.9 us; the launch traced here: 54.8 us
  waiting for transfers between devices  25.8 us (47%)
  starting transfers between devices  18 us (33%)
  Pallas kernels  9.63 us (18%)
  between operations  0.83 us (2%)
  other arithmetic  0.57 us (1%)
    ppermute x23, waiting for transfers between devices, swap(): return lax.ppermute(value, axis, [(i, i ^ bit) for i in range(size)])  25.8 us
    ppermute x23, starting transfers between devices, swap(): return lax.ppermute(value, axis, [(i, i ^ bit) for i in range(size)])  18 us
    pallas_call x4, Pallas kernels, hidden_part(): pl.pallas_call(functools.partial(hidden_kernel, len(xs), start), out_shap...  4.53 us
    pallas_call x4, Pallas kernels, down_part(): pl.pallas_call(functools.partial(down_kernel, len(pieces), where, slab, h...  2.56 us
    pallas_call x1, Pallas kernels, select_rows(): pl.pallas_call(select_kernel, out_shape=[jax.ShapeDtypeStruct((MOST, widt...  1.3 us
    pallas_call x1, Pallas kernels, combine(): pl.pallas_call(combine_kernel, out_shape=[jax.ShapeDtypeStruct(out_grad.s...  1.19 us
  transfers between devices with their start and end apart: 23, of which 13 were waited for; matrix products, arithmetic and copies ran while one was open for 0% of the time, Pallas kernels for 11%

profile of v6, /device:TPU:0, one launch (start us, length us, event | category | flops | bytes accessed | tf_op | source)
XLA Modules:
  0.0 54.8 jit_solution(14114381783854023020)
XLA Ops:
  0.6 0.0 copy-start
  0.6 0.0 copy-start.1
  0.7 1.3 %select_rows.1 = (bf16[34,768]{1,0:T(8,128)(2,1)S(1)}, bf16[34,768]{1,0:T(8,128)(2,1)S(1)}, bf16[34,768]{1,0:T(8,128)(2,1)S(1)}, bf16[34,768]{1,0:T(8,128)(2,1)S(1)}) custom-call(s32[1]{0:T(128)} %bitcast.me_ref, s32[1]{0:T(128)} %bitcast.3.t_ref, s32[2,64]{1,0:T(2,128)} %bitcast.8, bf16[64,768]{1,0:T(8,128)(2,1)} %tokens_hbm.1), custom_call_target="tpu_custom_call" | custom-call | flops 8000000000 | bytes 1000 | tf_op jit(solution)/shard_map/select_rows/pallas_call | solution.py:69
  2.0 3.1 %collective-permute-start = (bf16[34,768]{1,0:T(8,128)(2,1)S(1)}, bf16[34,768]{1,0:T(8,128)(2,1)S(1)}, u32[]{:S(2)}, u32[]{:S(2)}) collective-permute-start(bf16[34,768]{1,0:T(8,128)(2,1)S(1)} %get-tuple-element.13), channel_id=1, source_target_pairs={{0,4},{4,0},{8,12},{12,8},{1,5},{5,1},{9,13},{13,9},{2,6},{6,2},{1... | collective-permute-start | bytes 156680 | tf_op jit(solution)/shard_map/ppermute | solution.py:22
  5.0 2.6 %collective-permute-start.1 = (bf16[34,768]{1,0:T(8,128)(2,1)S(1)}, bf16[34,768]{1,0:T(8,128)(2,1)S(1)}, u32[]{:S(2)}, u32[]{:S(2)}) collective-permute-start(bf16[34,768]{1,0:T(8,128)(2,1)S(1)} %get-tuple-element.14), channel_id=1, source_target_pairs={{0,8},{4,12},{8,0},{12,4},{1,9},{5,13},{9,1},{13,5},{2,10},{6,14},... | collective-permute-start | bytes 156680 | tf_op jit(solution)/shard_map/ppermute | solution.py:22
  7.6 0.0 collective-permute-start.2
  7.6 0.0 collective-permute-done.refs_1_
  7.6 3.8 %collective-permute-done.1.refs_2_ = bf16[34,768]{1,0:T(8,128)(2,1)S(1)} collective-permute-done((bf16[34,768]{1,0:T(8,128)(2,1)S(1)}, bf16[34,768]{1,0:T(8,128)(2,1)S(1)}, u32[]{:S(2)}, u32[]{:S(2)}) %collective-permute-start.1) | collective-permute-done | bytes 52256 | tf_op jit(solution)/shard_map/ppermute | solution.py:22
  11.4 2.3 %collective-permute-done.2.refs_3_ = bf16[34,768]{1,0:T(8,128)(2,1)S(1)} collective-permute-done((bf16[34,768]{1,0:T(8,128)(2,1)S(1)}, bf16[34,768]{1,0:T(8,128)(2,1)S(1)}, u32[]{:S(2)}, u32[]{:S(2)}) %collective-permute-start.2) | collective-permute-done | bytes 52256 | tf_op jit(solution)/shard_map/ppermute | solution.py:22
  13.7 1.6 %collective-permute-start.4 = (bf16[136,768]{1,0:T(8,128)(2,1)S(1)}, bf16[136,768]{1,0:T(8,128)(2,1)S(1)}, u32[]{:S(2)}, u32[]{:S(2)}) collective-permute-start(bf16[136,768]{1,0:T(8,128)(2,1)S(1)} %pack.1.refs_0_), channel_id=1, source_target_pairs={{0,2},{1,3},{2,0},{3,1},{4,6},{5,7},{6,4},{7,5},{8,10},{9,11},{10,... | collective-permute-start | bytes 626696 | tf_op jit(solution)/shard_map/ppermute | solution.py:22
  15.3 0.0 collective-permute-start.3
  15.3 4.3 %collective-permute-done.4.refs_2_ = bf16[136,768]{1,0:T(8,128)(2,1)S(1)} collective-permute-done((bf16[136,768]{1,0:T(8,128)(2,1)S(1)}, bf16[136,768]{1,0:T(8,128)(2,1)S(1)}, u32[]{:S(2)}, u32[]{:S(2)}) %collective-permute-start.4) | collective-permute-done | bytes 208928 | tf_op jit(solution)/shard_map/ppermute | solution.py:22
  19.6 0.0 collective-permute-start.5
  19.6 0.0 collective-permute-done.3.refs_1_
  19.6 1.5 %collective-permute-done.5.refs_3_ = bf16[136,768]{1,0:T(8,128)(2,1)S(1)} collective-permute-done((bf16[136,768]{1,0:T(8,128)(2,1)S(1)}, bf16[136,768]{1,0:T(8,128)(2,1)S(1)}, u32[]{:S(2)}, u32[]{:S(2)}) %collective-permute-start.5) | collective-permute-done | bytes 208928 | tf_op jit(solution)/shard_map/ppermute | solution.py:22
  21.0 0.0 copy-done
  21.0 0.0 copy-done.1
  21.0 0.7 %hidden_part.6.refs_0_ = bf16[136,256]{1,0:T(8,128)(2,1)S(1)} custom-call(s32[1]{0:T(128)} %bitcast.3.t_ref, bf16[136,768]{1,0:T(8,128)(2,1)S(1)} %pack.1.refs_0_, bf16[136,768]{1,0:T(8,128)(2,1)S(1)} %collective-permute-done.3.refs_1_, bf16[136,768]{1,0:T(8,128)(2,1)S(1)} %collective-permute-done.4.refs_2_, ...), custom_call_target="tpu_custom_call" | custom-call | flops 1000 | bytes 1000 | tf_op jit(solution)/shard_map/hidden_part/pallas_call | solution.py:133
  21.7 1.6 %collective-permute-start.9 = (bf16[136,256]{1,0:T(8,128)(2,1)S(1)}, bf16[136,256]{1,0:T(8,128)(2,1)S(1)}, u32[]{:S(2)}, u32[]{:S(2)}) collective-permute-start(bf16[136,256]{1,0:T(8,128)(2,1)S(1)} %hidden_part.6.refs_0_), channel_id=1, source_target_pairs={{0,2},{1,3},{2,0},{3,1},{4,6},{5,7},{6,4},{7,5},{8,10},{9,11},{10,... | collective-permute-start | bytes 208904 | tf_op jit(solution)/shard_map/ppermute | solution.py:22
  23.3 1.1 %hidden_part.4.refs_4_ = bf16[136,512]{1,0:T(8,128)(2,1)S(1)} custom-call(s32[1]{0:T(128)} %bitcast.3.t_ref, bf16[136,768]{1,0:T(8,128)(2,1)S(1)} %pack.1.refs_0_, bf16[136,768]{1,0:T(8,128)(2,1)S(1)} %collective-permute-done.3.refs_1_, bf16[136,768]{1,0:T(8,128)(2,1)S(1)} %collective-permute-done.4.refs_2_, ...), custom_call_target="tpu_custom_call" | custom-call | flops 1000 | bytes 1000 | tf_op jit(solution)/shard_map/hidden_part/pallas_call | solution.py:133
  24.4 0.6 %collective-permute-start.6 = (bf16[136,512]{1,0:T(8,128)(2,1)S(1)}, bf16[136,512]{1,0:T(8,128)(2,1)S(1)}, u32[]{:S(2)}, u32[]{:S(2)}) collective-permute-start(bf16[136,512]{1,0:T(8,128)(2,1)S(1)} %hidden_part.4.refs_4_), channel_id=1, source_target_pairs={{0,2},{1,3},{2,0},{3,1},{4,6},{5,7},{6,4},{7,5},{8,10},{9,11},{10,... | collective-permute-start | bytes 417800 | tf_op jit(solution)/shard_map/ppermute | solution.py:22
  25.0 1.1 %collective-permute-done.9.refs_6_.refs_2_ = bf16[136,256]{1,0:T(8,128)(2,1)S(1)} collective-permute-done((bf16[136,256]{1,0:T(8,128)(2,1)S(1)}, bf16[136,256]{1,0:T(8,128)(2,1)S(1)}, u32[]{:S(2)}, u32[]{:S(2)}) %collective-permute-start.9) | collective-permute-done | bytes 69664 | tf_op jit(solution)/shard_map/ppermute | solution.py:22
  26.1 1.6 %hidden_part.7.refs_2_ = bf16[136,768]{1,0:T(8,128)(2,1)S(1)} custom-call(s32[1]{0:T(128)} %bitcast.3.t_ref, bf16[136,768]{1,0:T(8,128)(2,1)S(1)} %pack.1.refs_0_, bf16[136,768]{1,0:T(8,128)(2,1)S(1)} %collective-permute-done.3.refs_1_, bf16[136,768]{1,0:T(8,128)(2,1)S(1)} %collective-permute-done.4.refs_2_, ...), custom_call_target="tpu_custom_call" | custom-call | flops 1000 | bytes 1000 | tf_op jit(solution)/shard_map/hidden_part/pallas_call | solution.py:133
  27.7 0.0 slice-start.2
  27.7 1.7 %collective-permute-start.15 = (bf16[136,768]{1,0:T(8,128)(2,1)S(1)}, bf16[136,768]{1,0:T(8,128)(2,1)S(1)}, u32[]{:S(2)}, u32[]{:S(2)}) collective-permute-start(bf16[136,768]{1,0:T(8,128)(2,1)S(1)} %hidden_part.7.refs_2_), channel_id=1, source_target_pairs={{0,2},{1,3},{2,0},{3,1},{4,6},{5,7},{6,4},{7,5},{8,10},{9,11},{10,... | collective-permute-start | bytes 626696 | tf_op jit(solution)/shard_map/ppermute | solution.py:22
  29.5 0.0 collective-permute-start.11
  29.5 0.5 collective-permute-start.13
  30.0 0.0 collective-permute-start.10
  30.0 0.7 %collective-permute-done.11.refs_1_ = bf16[136,256]{1,0:T(8,128)(2,1)S(1)} collective-permute-done((bf16[136,256]{1,0:T(8,128)(2,1)S(1)}, bf16[136,256]{1,0:T(8,128)(2,1)S(1)}, u32[]{:S(2)}, u32[]{:S(2)}) %collective-permute-start.11) | collective-permute-done | bytes 69664 | tf_op jit(solution)/shard_map/ppermute | solution.py:22
  30.7 0.2 collective-permute-start.12
  30.9 0.0 collective-permute-done.6.refs_6_.refs_0_
  30.9 0.4 collective-permute-start.8
  31.2 1.1 %hidden_part.5.refs_2_ = bf16[136,512]{1,0:T(8,128)(2,1)S(1)} custom-call(s32[1]{0:T(128)} %bitcast.3.t_ref, bf16[136,768]{1,0:T(8,128)(2,1)S(1)} %pack.1.refs_0_, bf16[136,768]{1,0:T(8,128)(2,1)S(1)} %collective-permute-done.3.refs_1_, bf16[136,768]{1,0:T(8,128)(2,1)S(1)} %collective-permute-done.4.refs_2_, ...), custom_call_target="tpu_custom_call" | custom-call | flops 1000 | bytes 1000 | tf_op jit(solution)/shard_map/hidden_part/pallas_call | solution.py:133
  32.4 0.0 collective-permute-done.12.refs_3_
  32.4 0.4 collective-permute-start.7
  32.8 0.0 collective-permute-done.13.refs_5_
  32.8 0.0 slice-done
  32.8 0.6 %down_part.4.refs_5_.refs_1_ = f32[136,768]{1,0:T(8,128)S(1)} custom-call(s32[1]{0:T(128)} %bitcast.3.t_ref, bf16[136,256]{1,0:T(8,128)(2,1)S(1)} %hidden_part.6.refs_0_, bf16[136,256]{1,0:T(8,128)(2,1)S(1)} %collective-permute-done.11.refs_1_, bf16[136,256]{1,0:T(8,128)(2,1)S(1)} %collective-permute-done.9.refs_6_.refs_2_, ...), custom_call_target="tpu_custom_call" | custom-call | flops 427819008 | bytes 1000 | tf_op jit(solution)/shard_map/down_part/pallas_call | solution.py:170
  33.5 0.9 %collective-permute-done.15.refs_0_ = bf16[136,768]{1,0:T(8,128)(2,1)S(1)} collective-permute-done((bf16[136,768]{1,0:T(8,128)(2,1)S(1)}, bf16[136,768]{1,0:T(8,128)(2,1)S(1)}, u32[]{:S(2)}, u32[]{:S(2)}) %collective-permute-start.15) | collective-permute-done | bytes 208928 | tf_op jit(solution)/shard_map/ppermute | solution.py:22
  34.4 0.0 collective-permute-start.16
  34.4 0.5 collective-permute-start.17
  34.9 0.0 collective-permute-done.10.refs_3_
  34.9 0.0 collective-permute-done.8.refs_1_
  34.9 0.8 %down_part.5.refs_1_.refs_5_ = f32[136,768]{1,0:T(8,128)S(1)} custom-call(s32[1]{0:T(128)} %bitcast.3.t_ref, bf16[136,512]{1,0:T(8,128)(2,1)S(1)} %collective-permute-done.6.refs_6_.refs_0_, bf16[136,512]{1,0:T(8,128)(2,1)S(1)} %collective-permute-done.8.refs_1_, bf16[136,768]{1,0:T(8,128)(2,1)S(1)} %hidden_part.7.refs_2_, ...), custom_call_target="tpu_custom_call" | custom-call | flops 534773760 | bytes 1000 | tf_op jit(solution)/shard_map/down_part/pallas_call | solution.py:170
  35.7 2.5 %collective-permute-done.7.refs_0_ = bf16[136,512]{1,0:T(8,128)(2,1)S(1)} collective-permute-done((bf16[136,512]{1,0:T(8,128)(2,1)S(1)}, bf16[136,512]{1,0:T(8,128)(2,1)S(1)}, u32[]{:S(2)}, u32[]{:S(2)}) %collective-permute-start.7) | collective-permute-done | bytes 139296 | tf_op jit(solution)/shard_map/ppermute | solution.py:22
  38.2 0.1 collective-permute-start.14
  38.3 0.0 collective-permute-done.17.refs_3_
  38.3 0.0 collective-permute-done.16.refs_1_
  38.3 0.8 %down_part.6.refs_3_ = f32[136,768]{1,0:T(8,128)S(1)} custom-call(s32[1]{0:T(128)} %bitcast.3.t_ref, bf16[136,768]{1,0:T(8,128)(2,1)S(1)} %hold.3.refs_0_, bf16[136,768]{1,0:T(8,128)(2,1)S(1)} %collective-permute-done.16.refs_1_, bf16[136,512]{1,0:T(8,128)(2,1)S(1)} %hidden_part.5.refs_2_, bf16[136,512]{1,0:T(8,128)(2,1)S(1)} %collective-permute-done.17.refs_3_, ...), custom_call_target="tpu_custom_call" | custom-call | flops 534773760 | bytes 1000 | tf_op jit(solution)/shard_map/down_part/pallas_call | solution.py:170
  39.0 0.6 %collective-permute-done.14.refs_1_ = bf16[136,512]{1,0:T(8,128)(2,1)S(1)} collective-permute-done((bf16[136,512]{1,0:T(8,128)(2,1)S(1)}, bf16[136,512]{1,0:T(8,128)(2,1)S(1)}, u32[]{:S(2)}, u32[]{:S(2)}) %collective-permute-start.14) | collective-permute-done | bytes 139296 | tf_op jit(solution)/shard_map/ppermute | solution.py:22
  39.6 0.4 down_part.7
  40.0 0.1 collective-permute-start.18
  40.1 2.1 %collective-permute-start.19 = (bf16[34,768]{1,0:T(8,128)(2,1)S(1)}, bf16[34,768]{1,0:T(8,128)(2,1)S(1)}, u32[]{:S(2)}, u32[]{:S(2)}) collective-permute-start(bf16[34,768]{1,0:T(8,128)(2,1)S(1)} %get-tuple-element.18), channel_id=1, source_target_pairs={{0,8},{4,12},{8,0},{12,4},{1,9},{5,13},{9,1},{13,5},{2,10},{6,14},... | collective-permute-start | bytes 156680 | tf_op jit(solution)/shard_map/ppermute | solution.py:22
  42.2 2.3 %collective-permute-start.20 = (bf16[34,768]{1,0:T(8,128)(2,1)S(1)}, bf16[34,768]{1,0:T(8,128)(2,1)S(1)}, u32[]{:S(2)}, u32[]{:S(2)}) collective-permute-start(bf16[34,768]{1,0:T(8,128)(2,1)S(1)} %get-tuple-element.19), channel_id=1, source_target_pairs={{0,12},{4,8},{8,4},{12,0},{1,13},{5,9},{9,5},{13,1},{2,14},{6,10},... | collective-permute-start | bytes 156680 | tf_op jit(solution)/shard_map/ppermute | solution.py:22
  44.5 0.9 %collective-permute-done.18.refs_1_ = bf16[34,768]{1,0:T(8,128)(2,1)S(1)} collective-permute-done((bf16[34,768]{1,0:T(8,128)(2,1)S(1)}, bf16[34,768]{1,0:T(8,128)(2,1)S(1)}, u32[]{:S(2)}, u32[]{:S(2)}) %collective-permute-start.18) | collective-permute-done | bytes 52256 | tf_op jit(solution)/shard_map/ppermute | solution.py:22
  45.3 2.9 %collective-permute-done.19.refs_2_ = bf16[34,768]{1,0:T(8,128)(2,1)S(1)} collective-permute-done((bf16[34,768]{1,0:T(8,128)(2,1)S(1)}, bf16[34,768]{1,0:T(8,128)(2,1)S(1)}, u32[]{:S(2)}, u32[]{:S(2)}) %collective-permute-start.19) | collective-permute-done | bytes 52256 | tf_op jit(solution)/shard_map/ppermute | solution.py:22
  48.3 0.0 collective-permute-done.20.refs_3_
  48.3 0.0 copy-done.4
  48.3 1.2 %combine.1 = (bf16[64,768]{1,0:T(8,128)(2,1)}, f32[2,64]{1,0:T(2,128)S(1)}) custom-call(s32[1]{0:T(128)} %bitcast.me_ref, s32[2,64]{1,0:T(2,128)S(1)} %bitcast.9, f32[2,64]{1,0:T(2,128)S(1)} %bitcast.10, bf16[64,768]{1,0:T(8,128)(2,1)S(1)} %copy-done.2, bf16[34,768]{1,0:T(8,128)(2,1)S(1)} %get-tuple-element.16.refs_0_, ...), custom_call_target="tpu_custom_call" | custom-call | flops 1000 | bytes 1000 | tf_op jit(solution)/shard_map/combine/pallas_call | solution.py:215
  49.5 0.4 collective-permute-start.21
  49.9 3.2 %collective-permute-done.21 = f32[2,64]{1,0:T(2,128)S(1)} collective-permute-done((f32[2,64]{1,0:T(2,128)S(1)}, f32[2,64]{1,0:T(2,128)S(1)}, u32[]{:S(2)}, u32[]{:S(2)}) %collective-permute-start.21) | collective-permute-done | bytes 544 | tf_op jit(solution)/shard_map/ppermute | solution.py:22
  53.1 0.0 collective-permute-start.22
  53.1 1.1 %collective-permute-done.22 = f32[2,64]{1,0:T(2,128)S(1)} collective-permute-done((f32[2,64]{1,0:T(2,128)S(1)}, f32[2,64]{1,0:T(2,128)S(1)}, u32[]{:S(2)}, u32[]{:S(2)}) %collective-permute-start.22) | collective-permute-done | bytes 544 | tf_op jit(solution)/shard_map/ppermute | solution.py:22
  54.2 0.6 %add_bitcast_fusion = f32[64,2]{0,1:T(2,128)} fusion(f32[2,64]{1,0:T(2,128)S(1)} %add.6, f32[2,64]{1,0:T(2,128)S(1)} %collective-permute-done.22), kind=kLoop, calls=%fused_computation | loop fusion | flops 128 | bytes 1536 | tf_op jit(solution)/shard_map/transpose | solution.py:267
  (14 shorter events, 0.1 us)
Async XLA Ops:
  0.6 20.4 %copy-start = (bf16[1,3072,2048]{2,1,0:T(8,128)(2,1)S(1)}, bf16[1,3072,2048]{2,1,0:T(8,128)(2,1)}, u32[]{:S(2)}) copy-start(bf16[1,3072,2048]{2,1,0:T(8,128)(2,1)} %refs_4_.9) | copy-start | bytes 37748740
  0.6 20.4 %copy-start.1 = (bf16[1,3072,2048]{2,1,0:T(8,128)(2,1)S(1)}, bf16[1,3072,2048]{2,1,0:T(8,128)(2,1)}, u32[]{:S(2)}) copy-start(bf16[1,3072,2048]{2,1,0:T(8,128)(2,1)} %refs_5_.7) | copy-start | bytes 37748740
  2.0 5.7 %collective-permute-start = (bf16[34,768]{1,0:T(8,128)(2,1)S(1)}, bf16[34,768]{1,0:T(8,128)(2,1)S(1)}, u32[]{:S(2)}, u32[]{:S(2)}) collective-permute-start(bf16[34,768]{1,0:T(8,128)(2,1)S(1)} %get-tuple-element.13), channel_id=1, source_target_pairs={{0,4},{4,0},{8,12},{12,8},{1,5},{5,1},{9,13},{13,9},{2,6},{6,2},{1... | collective-permute-start | bytes 156680 | tf_op jit(solution)/shard_map/ppermute | solution.py:22
  5.0 6.4 %collective-permute-start.1 = (bf16[34,768]{1,0:T(8,128)(2,1)S(1)}, bf16[34,768]{1,0:T(8,128)(2,1)S(1)}, u32[]{:S(2)}, u32[]{:S(2)}) collective-permute-start(bf16[34,768]{1,0:T(8,128)(2,1)S(1)} %get-tuple-element.14), channel_id=1, source_target_pairs={{0,8},{4,12},{8,0},{12,4},{1,9},{5,13},{9,1},{13,5},{2,10},{6,14},... | collective-permute-start | bytes 156680 | tf_op jit(solution)/shard_map/ppermute | solution.py:22
  7.6 6.0 %collective-permute-start.2 = (bf16[34,768]{1,0:T(8,128)(2,1)S(1)}, bf16[34,768]{1,0:T(8,128)(2,1)S(1)}, u32[]{:S(2)}, u32[]{:S(2)}) collective-permute-start(bf16[34,768]{1,0:T(8,128)(2,1)S(1)} %get-tuple-element.15), channel_id=1, source_target_pairs={{0,12},{4,8},{8,4},{12,0},{1,13},{5,9},{9,5},{13,1},{2,14},{6,10},... | collective-permute-start | bytes 156680 | tf_op jit(solution)/shard_map/ppermute | solution.py:22
  13.7 5.9 %collective-permute-start.4 = (bf16[136,768]{1,0:T(8,128)(2,1)S(1)}, bf16[136,768]{1,0:T(8,128)(2,1)S(1)}, u32[]{:S(2)}, u32[]{:S(2)}) collective-permute-start(bf16[136,768]{1,0:T(8,128)(2,1)S(1)} %pack.1.refs_0_), channel_id=1, source_target_pairs={{0,2},{1,3},{2,0},{3,1},{4,6},{5,7},{6,4},{7,5},{8,10},{9,11},{10,... | collective-permute-start | bytes 626696 | tf_op jit(solution)/shard_map/ppermute | solution.py:22
  15.3 4.3 %collective-permute-start.3 = (bf16[136,768]{1,0:T(8,128)(2,1)S(1)}, bf16[136,768]{1,0:T(8,128)(2,1)S(1)}, u32[]{:S(2)}, u32[]{:S(2)}) collective-permute-start(bf16[136,768]{1,0:T(8,128)(2,1)S(1)} %pack.1.refs_0_), channel_id=1, source_target_pairs={{0,1},{1,0},{2,3},{3,2},{4,5},{5,4},{6,7},{7,6},{8,9},{9,8},{10,11... | collective-permute-start | bytes 626696 | tf_op jit(solution)/shard_map/ppermute | solution.py:22
  19.6 1.5 %collective-permute-start.5 = (bf16[136,768]{1,0:T(8,128)(2,1)S(1)}, bf16[136,768]{1,0:T(8,128)(2,1)S(1)}, u32[]{:S(2)}, u32[]{:S(2)}) collective-permute-start(bf16[136,768]{1,0:T(8,128)(2,1)S(1)} %collective-permute-done.4.refs_2_), channel_id=1, source_target_pairs={{0,1},{1,0},{2,3},{3,2},{4,5},{5,4},{6,7},{7,6},{8,9},{9,8},{10,11... | collective-permute-start | bytes 626696 | tf_op jit(solution)/shard_map/ppermute | solution.py:22
  21.7 4.4 %collective-permute-start.9 = (bf16[136,256]{1,0:T(8,128)(2,1)S(1)}, bf16[136,256]{1,0:T(8,128)(2,1)S(1)}, u32[]{:S(2)}, u32[]{:S(2)}) collective-permute-start(bf16[136,256]{1,0:T(8,128)(2,1)S(1)} %hidden_part.6.refs_0_), channel_id=1, source_target_pairs={{0,2},{1,3},{2,0},{3,1},{4,6},{5,7},{6,4},{7,5},{8,10},{9,11},{10,... | collective-permute-start | bytes 208904 | tf_op jit(solution)/shard_map/ppermute | solution.py:22
  24.4 6.5 %collective-permute-start.6 = (bf16[136,512]{1,0:T(8,128)(2,1)S(1)}, bf16[136,512]{1,0:T(8,128)(2,1)S(1)}, u32[]{:S(2)}, u32[]{:S(2)}) collective-permute-start(bf16[136,512]{1,0:T(8,128)(2,1)S(1)} %hidden_part.4.refs_4_), channel_id=1, source_target_pairs={{0,2},{1,3},{2,0},{3,1},{4,6},{5,7},{6,4},{7,5},{8,10},{9,11},{10,... | collective-permute-start | bytes 417800 | tf_op jit(solution)/shard_map/ppermute | solution.py:22
  26.1 6.7 %slice-start = ((s8[12582912]{0:T(1024)(128)(4,1)}), s8[4194304]{0:T(1024)(128)(4,1)S(1)}, s32[]{:S(2)}) async-start(s8[12582912]{0:T(1024)(128)(4,1)} %bitcast.6), calls=%async_computation | async-start | bytes 8388608
  26.1 6.7 %slice-start.1 = ((s8[12582912]{0:T(1024)(128)(4,1)}), s8[4194304]{0:T(1024)(128)(4,1)S(1)}, s32[]{:S(2)}) async-start(s8[12582912]{0:T(1024)(128)(4,1)} %bitcast.6), calls=%async_computation.1 | async-start | bytes 8388608
  27.7 5.1 %slice-start.2 = ((s8[12582912]{0:T(1024)(128)(4,1)}), s8[4194304]{0:T(1024)(128)(4,1)S(1)}, s32[]{:S(2)}) async-start(s8[12582912]{0:T(1024)(128)(4,1)} %bitcast.6), calls=%async_computation.2 | async-start | bytes 8388608
  27.7 6.6 %collective-permute-start.15 = (bf16[136,768]{1,0:T(8,128)(2,1)S(1)}, bf16[136,768]{1,0:T(8,128)(2,1)S(1)}, u32[]{:S(2)}, u32[]{:S(2)}) collective-permute-start(bf16[136,768]{1,0:T(8,128)(2,1)S(1)} %hidden_part.7.refs_2_), channel_id=1, source_target_pairs={{0,2},{1,3},{2,0},{3,1},{4,6},{5,7},{6,4},{7,5},{8,10},{9,11},{10,... | collective-permute-start | bytes 626696 | tf_op jit(solution)/shard_map/ppermute | solution.py:22
  29.5 1.3 %collective-permute-start.11 = (bf16[136,256]{1,0:T(8,128)(2,1)S(1)}, bf16[136,256]{1,0:T(8,128)(2,1)S(1)}, u32[]{:S(2)}, u32[]{:S(2)}) collective-permute-start(bf16[136,256]{1,0:T(8,128)(2,1)S(1)} %hidden_part.6.refs_0_), channel_id=1, source_target_pairs={{0,1},{1,0},{2,3},{3,2},{4,5},{5,4},{6,7},{7,6},{8,9},{9,8},{10,11... | collective-permute-start | bytes 208904 | tf_op jit(solution)/shard_map/ppermute | solution.py:22
  29.5 3.4 %collective-permute-start.13 = (bf16[136,512]{1,0:T(8,128)(2,1)S(1)}, bf16[136,512]{1,0:T(8,128)(2,1)S(1)}, u32[]{:S(2)}, u32[]{:S(2)}) collective-permute-start(bf16[136,512]{1,0:T(8,128)(2,1)S(1)} %hidden_part.4.refs_4_), channel_id=1, source_target_pairs={{0,1},{1,0},{2,3},{3,2},{4,5},{5,4},{6,7},{7,6},{8,9},{9,8},{10,11... | collective-permute-start | bytes 417800 | tf_op jit(solution)/shard_map/ppermute | solution.py:22
  30.0 4.9 %collective-permute-start.10 = (bf16[136,768]{1,0:T(8,128)(2,1)S(1)}, bf16[136,768]{1,0:T(8,128)(2,1)S(1)}, u32[]{:S(2)}, u32[]{:S(2)}) collective-permute-start(bf16[136,768]{1,0:T(8,128)(2,1)S(1)} %hidden_part.7.refs_2_), channel_id=1, source_target_pairs={{0,1},{1,0},{2,3},{3,2},{4,5},{5,4},{6,7},{7,6},{8,9},{9,8},{10,11... | collective-permute-start | bytes 626696 | tf_op jit(solution)/shard_map/ppermute | solution.py:22
  30.7 1.6 %collective-permute-start.12 = (bf16[136,256]{1,0:T(8,128)(2,1)S(1)}, bf16[136,256]{1,0:T(8,128)(2,1)S(1)}, u32[]{:S(2)}, u32[]{:S(2)}) collective-permute-start(bf16[136,256]{1,0:T(8,128)(2,1)S(1)} %collective-permute-done.9.refs_6_.refs_2_), channel_id=1, source_target_pairs={{0,1},{1,0},{2,3},{3,2},{4,5},{5,4},{6,7},{7,6},{8,9},{9,8},{10,11... | collective-permute-start | bytes 208904 | tf_op jit(solution)/shard_map/ppermute | solution.py:22
  30.9 4.0 %collective-permute-start.8 = (bf16[136,512]{1,0:T(8,128)(2,1)S(1)}, bf16[136,512]{1,0:T(8,128)(2,1)S(1)}, u32[]{:S(2)}, u32[]{:S(2)}) collective-permute-start(bf16[136,512]{1,0:T(8,128)(2,1)S(1)} %collective-permute-done.6.refs_6_.refs_0_), channel_id=1, source_target_pairs={{0,1},{1,0},{2,3},{3,2},{4,5},{5,4},{6,7},{7,6},{8,9},{9,8},{10,11... | collective-permute-start | bytes 417800 | tf_op jit(solution)/shard_map/ppermute | solution.py:22
  32.4 5.8 %collective-permute-start.7 = (bf16[136,512]{1,0:T(8,128)(2,1)S(1)}, bf16[136,512]{1,0:T(8,128)(2,1)S(1)}, u32[]{:S(2)}, u32[]{:S(2)}) collective-permute-start(bf16[136,512]{1,0:T(8,128)(2,1)S(1)} %hidden_part.5.refs_2_), channel_id=1, source_target_pairs={{0,2},{1,3},{2,0},{3,1},{4,6},{5,7},{6,4},{7,5},{8,10},{9,11},{10,... | collective-permute-start | bytes 417800 | tf_op jit(solution)/shard_map/ppermute | solution.py:22
  34.4 3.9 %collective-permute-start.16 = (bf16[136,768]{1,0:T(8,128)(2,1)S(1)}, bf16[136,768]{1,0:T(8,128)(2,1)S(1)}, u32[]{:S(2)}, u32[]{:S(2)}) collective-permute-start(bf16[136,768]{1,0:T(8,128)(2,1)S(1)} %hold.3.refs_0_), channel_id=1, source_target_pairs={{0,1},{1,0},{2,3},{3,2},{4,5},{5,4},{6,7},{7,6},{8,9},{9,8},{10,11... | collective-permute-start | bytes 626696 | tf_op jit(solution)/shard_map/ppermute | solution.py:22
  34.4 3.9 %collective-permute-start.17 = (bf16[136,512]{1,0:T(8,128)(2,1)S(1)}, bf16[136,512]{1,0:T(8,128)(2,1)S(1)}, u32[]{:S(2)}, u32[]{:S(2)}) collective-permute-start(bf16[136,512]{1,0:T(8,128)(2,1)S(1)} %hidden_part.5.refs_2_), channel_id=1, source_target_pairs={{0,1},{1,0},{2,3},{3,2},{4,5},{5,4},{6,7},{7,6},{8,9},{9,8},{10,11... | collective-permute-start | bytes 417800 | tf_op jit(solution)/shard_map/ppermute | solution.py:22
  38.2 10.1 %copy-start.2 = (bf16[64,768]{1,0:T(8,128)(2,1)S(1)}, bf16[64,768]{1,0:T(8,128)(2,1)}, u32[]{:S(2)}) copy-start(bf16[64,768]{1,0:T(8,128)(2,1)} %grad_ref.1) | copy-start | bytes 294916
  38.2 10.1 %copy-start.3 = (s32[64,2]{0,1:T(2,128)S(1)}, s32[64,2]{0,1:T(2,128)}, u32[]{:S(2)}) copy-start(s32[64,2]{0,1:T(2,128)} %param.8) | copy-start | bytes 1540
  38.2 10.1 %copy-start.4 = (f32[64,2]{0,1:T(2,128)S(1)}, f32[64,2]{0,1:T(2,128)}, u32[]{:S(2)}) copy-start(f32[64,2]{0,1:T(2,128)} %param.9) | copy-start | bytes 1540
  38.2 1.4 %collective-permute-start.14 = (bf16[136,512]{1,0:T(8,128)(2,1)S(1)}, bf16[136,512]{1,0:T(8,128)(2,1)S(1)}, u32[]{:S(2)}, u32[]{:S(2)}) collective-permute-start(bf16[136,512]{1,0:T(8,128)(2,1)S(1)} %hold.2.refs_0_), channel_id=1, source_target_pairs={{0,1},{1,0},{2,3},{3,2},{4,5},{5,4},{6,7},{7,6},{8,9},{9,8},{10,11... | collective-permute-start | bytes 417800 | tf_op jit(solution)/shard_map/ppermute | solution.py:22
  40.0 5.3 %collective-permute-start.18 = (bf16[34,768]{1,0:T(8,128)(2,1)S(1)}, bf16[34,768]{1,0:T(8,128)(2,1)S(1)}, u32[]{:S(2)}, u32[]{:S(2)}) collective-permute-start(bf16[34,768]{1,0:T(8,128)(2,1)S(1)} %get-tuple-element.17), channel_id=1, source_target_pairs={{0,4},{4,0},{8,12},{12,8},{1,5},{5,1},{9,13},{13,9},{2,6},{6,2},{1... | collective-permute-start | bytes 156680 | tf_op jit(solution)/shard_map/ppermute | solution.py:22
  40.1 8.2 %collective-permute-start.19 = (bf16[34,768]{1,0:T(8,128)(2,1)S(1)}, bf16[34,768]{1,0:T(8,128)(2,1)S(1)}, u32[]{:S(2)}, u32[]{:S(2)}) collective-permute-start(bf16[34,768]{1,0:T(8,128)(2,1)S(1)} %get-tuple-element.18), channel_id=1, source_target_pairs={{0,8},{4,12},{8,0},{12,4},{1,9},{5,13},{9,1},{13,5},{2,10},{6,14},... | collective-permute-start | bytes 156680 | tf_op jit(solution)/shard_map/ppermute | solution.py:22
  42.2 6.1 %collective-permute-start.20 = (bf16[34,768]{1,0:T(8,128)(2,1)S(1)}, bf16[34,768]{1,0:T(8,128)(2,1)S(1)}, u32[]{:S(2)}, u32[]{:S(2)}) collective-permute-start(bf16[34,768]{1,0:T(8,128)(2,1)S(1)} %get-tuple-element.19), channel_id=1, source_target_pairs={{0,12},{4,8},{8,4},{12,0},{1,13},{5,9},{9,5},{13,1},{2,14},{6,10},... | collective-permute-start | bytes 156680 | tf_op jit(solution)/shard_map/ppermute | solution.py:22
  49.5 3.6 %collective-permute-start.21 = (f32[2,64]{1,0:T(2,128)S(1)}, f32[2,64]{1,0:T(2,128)S(1)}, u32[]{:S(2)}, u32[]{:S(2)}) collective-permute-start(f32[2,64]{1,0:T(2,128)S(1)} %get-tuple-element.21), channel_id=1, source_target_pairs={{0,2},{1,3},{2,0},{3,1},{4,6},{5,7},{6,4},{7,5},{8,10},{9,11},{10,... | collective-permute-start | bytes 1544 | tf_op jit(solution)/shard_map/ppermute | solution.py:22
  53.1 1.1 %collective-permute-start.22 = (f32[2,64]{1,0:T(2,128)S(1)}, f32[2,64]{1,0:T(2,128)S(1)}, u32[]{:S(2)}, u32[]{:S(2)}) collective-permute-start(f32[2,64]{1,0:T(2,128)S(1)} %add.6), channel_id=1, source_target_pairs={{0,1},{1,0},{2,3},{3,2},{4,5},{5,4},{6,7},{7,6},{8,9},{9,8},{10,11... | collective-permute-start | bytes 1544 | tf_op jit(solution)/shard_map/ppermute | solution.py:22

commit v7 on v6

--- a/solution.py
+++ b/solution.py
@@ -50,6 +50,18 @@
     return hits, picks
 
 
+def fold(block):
+    return jnp.concatenate([block[:, c:c + 128] for c in range(0, block.shape[1], 128)], axis=0)
+
+
+def unfold(block):
+    return jnp.concatenate([block[r:r + MOST] for r in range(0, block.shape[0], MOST)], axis=1)
+
+
+def folded(width):
+    return jax.ShapeDtypeStruct((width // 128 * MOST, 128), BF)
+
+
 def select_kernel(me_ref, t_ref, ids_hbm, tokens_hbm, *refs):
     out_refs = refs[:EXPERTS]
     ids_ref, tokens_ref, sems = refs[EXPERTS:]
@@ -60,15 +72,16 @@
     ids_copy.wait()
     _, picks = routing(ids_ref[...], me_ref[0])
     tokens_copy.wait()
-    for pick, out_ref in zip(picks, out_refs):
-        out_ref[...] = jnp.dot(pick.astype(BF), tokens_ref[...], preferred_element_type=F32).astype(BF)
+    for k, (pick, out_ref) in enumerate(zip(picks, out_refs)):
+        block = jnp.dot(pick.astype(BF), tokens_ref[...], preferred_element_type=F32)
+        out_ref[...] = (block if k == 0 else fold(block)).astype(BF)
 
 
 def select_rows(me, t, ids_t, tokens):
     width = tokens.shape[1]
     return pl.pallas_call(
         select_kernel,
-        out_shape=[jax.ShapeDtypeStruct((MOST, width), BF)] * EXPERTS,
+        out_shape=[jax.ShapeDtypeStruct((MOST, width), BF)] + [folded(width)] * (EXPERTS - 1),
         in_specs=[SMEM, SMEM, ANY, ANY],
         out_specs=[VMEM] * EXPERTS,
         scratch_shapes=[
@@ -82,20 +95,41 @@
     )(me, t, *(pltpu.with_memory_space_constraint(v, pltpu.HBM) for v in (ids_t, tokens)))
 
 
-def pack_kernel(*refs):
-    blocks = refs[:EXPERTS]
-    refs[-1][...] = jnp.concatenate([b[...].astype(F32) for b in blocks], axis=0).astype(BF)
-
-
-def pack(blocks, after):
-    return pl.pallas_call(
-        pack_kernel,
-        out_shape=jax.ShapeDtypeStruct((EXPERTS * MOST, blocks[0].shape[1]), BF),
-        in_specs=[VMEM] * EXPERTS + [ANY] * len(after),
+CUT = 2 * MOST // 16 * 16
+
+
+def near_kernel(own_ref, next_ref, out_ref):
+    both = jnp.concatenate([own_ref[...].astype(F32), unfold(next_ref[...].astype(F32))], axis=0)
+    out_ref[...] = both[:CUT].astype(BF)
+
+
+def far_kernel(next_ref, third_ref, fourth_ref, out_ref):
+    rest = unfold(next_ref[...].astype(F32))[CUT - MOST:]
+    blocks = [rest] + [unfold(r[...].astype(F32)) for r in (third_ref, fourth_ref)]
+    out_ref[...] = jnp.concatenate(blocks, axis=0).astype(BF)
+
+
+def pack_near(own, following):
+    return pl.pallas_call(
+        near_kernel,
+        out_shape=jax.ShapeDtypeStruct((CUT, own.shape[1]), BF),
+        in_specs=[VMEM] * 2,
         out_specs=VMEM,
-        name="pack",
+        name="pack_near",
         **SMALL,
-    )(*blocks, *after)
+    )(own, following)
+
+
+def pack_far(blocks, width):
+    return pl.pallas_call(
+        far_kernel,
+        out_shape=jax.ShapeDtypeStruct((EXPERTS * MOST - CUT, width), BF),
+        in_specs=[VMEM] * 3,
+        out_specs=VMEM,
+        name="pack_far",
+        compiler_params=pltpu.CompilerParams(vmem_limit_bytes=SMALL_LIMIT),
+        cost_estimate=pl.CostEstimate(flops=1_000_000_000, bytes_accessed=1000, transcendentals=0),
+    )(*blocks)
 
 
 def hold(value, after):
@@ -110,17 +144,23 @@
     )(value, *after)
 
 
-def hidden_kernel(parts, start, t_ref, *refs):
-    x_refs = refs[:parts]
-    gate_ref, up_ref = refs[parts:parts + 2]
-    out_ref = refs[-1]
-    depth = x_refs[0].shape[1]
+def hidden_kernel(joined, parts, start, t_ref, *refs):
+    if joined:
+        out_ref, x_ref = refs[-1], refs[0]
+        gate_ref, up_ref = refs[1:3]
+    else:
+        out_ref, x_ref = refs[-2:]
+        gate_ref, up_ref = refs[2 * parts:2 * parts + 2]
+        for j in range(parts):
+            x_ref[j, :CUT, :] = refs[2 * j][...]
+            x_ref[j, CUT:, :] = refs[2 * j + 1][...]
+    depth = x_ref.shape[2]
     for tile in range(0, out_ref.shape[1], FF_TILE):
         columns = slice(start + tile, start + tile + FF_TILE)
         gate = up = None
         for j in range(parts):
             at = pl.ds(pl.multiple_of((t_ref[0] ^ j) * depth, depth), depth)
-            x = x_refs[j][...]
+            x = x_ref[j]
             g = jnp.dot(x, gate_ref[0, at, columns], preferred_element_type=F32)
             u = jnp.dot(x, up_ref[0, at, columns], preferred_element_type=F32)
             gate = g if gate is None else gate + g
@@ -129,12 +169,17 @@
 
 
 def hidden_part(t, xs, gate_weight, up_weight, start, size, after=()):
-    rows = xs[0].shape[0]
-    return pl.pallas_call(
-        functools.partial(hidden_kernel, len(xs), start),
-        out_shape=jax.ShapeDtypeStruct((rows, size), BF),
+    joined = len(xs) == 1
+    parts = xs[0].shape[0] if joined else len(xs) // 2
+    rows = EXPERTS * MOST
+    out_shape = [jax.ShapeDtypeStruct((rows, size), BF)]
+    if not joined:
+        out_shape.append(jax.ShapeDtypeStruct((parts, rows, xs[0].shape[1]), BF))
+    return pl.pallas_call(
+        functools.partial(hidden_kernel, joined, parts, start),
+        out_shape=out_shape,
         in_specs=[SMEM] + [VMEM] * (len(xs) + 2) + [ANY] * len(after),
-        out_specs=VMEM,
+        out_specs=[VMEM] * len(out_shape),
         compiler_params=pltpu.CompilerParams(vmem_limit_bytes=SMALL_LIMIT),
         cost_estimate=pl.CostEstimate(flops=1000, bytes_accessed=1000, transcendentals=0),
         name="hidden_part",
@@ -154,7 +199,8 @@
         total = term if total is None else total + term
     if last:
         for k, out in enumerate(outs):
-            out[...] = total[k * MOST:(k + 1) * MOST].astype(BF)
+            block = total[k * MOST:(k + 1) * MOST]
+            out[...] = (block if k == 0 else fold(block)).astype(BF)
     else:
         outs[0][...] = total
 
@@ -164,7 +210,7 @@
     width = weight.shape[2]
     has_sum = running is not None
     if last:
-        out_shape = [jax.ShapeDtypeStruct((MOST, width), BF)] * EXPERTS
+        out_shape = [jax.ShapeDtypeStruct((MOST, width), BF)] + [folded(width)] * (EXPERTS - 1)
     else:
         out_shape = [jax.ShapeDtypeStruct((rows, width), F32)]
     return pl.pallas_call(
@@ -196,8 +242,9 @@
     routes = jnp.concatenate([routes, jnp.zeros((128, 128 - rows), F32)], axis=1).T
     mixed = None
     for k in range(EXPERTS):
+        block = back_refs[k][...] if k == 0 else unfold(back_refs[k][...].astype(F32)).astype(BF)
         out = lax.dot_general(
-            picks[k].astype(BF), back_refs[k][...], (((0,), (0,)), ((), ())), preferred_element_type=F32
+            picks[k].astype(BF), block, (((0,), (0,)), ((), ())), preferred_element_type=F32
         )
         term = routes[:rows, k:k + 1] * out
         mixed = term if mixed is None else mixed + term
@@ -225,6 +272,7 @@
     )(me, ids_t, probs_t, out_grad, *back)
 
 
+Z_ORDER = (1, 2, 3)
 CHUNKS = (256, 512, 768, 512)
 
 
@@ -236,15 +284,20 @@
 
     rows = select_rows(me, t_index, ids_t, tokens)
     starts = [sum(CHUNKS[:i]) for i in range(len(CHUNKS))]
-    arrived = [rows[0]] + [swap(rows[k], "expert", k) for k in (1, 2, 3)]
-    own = pack(arrived, [])
-    across = swap(own, "tensor", 2)
-    xs = [own, swap(own, "tensor", 1), across, swap(across, "tensor", 1)]
+    arrived = {k: swap(rows[k], "expert", k) for k in Z_ORDER}
+    near = pack_near(rows[0], arrived[1])
+    near_across = swap(near, "tensor", 2)
+    far = hold(pack_far([arrived[k] for k in (1, 2, 3)], tokens.shape[1]), [near_across])
+    far_across = swap(far, "tensor", 2)
+    sides = [swap(v, "tensor", 1) for v in (near, far, near_across)]
+    far_across = hold(far_across, sides)
+    xs = [near, far, sides[0], sides[1], near_across, far_across, sides[2], swap(far_across, "tensor", 1)]
 
     pieces = []
     for i, (start, size) in enumerate(zip(starts, CHUNKS)):
         after = [pieces[i - 2][2]] if i >= 2 else []
-        h = hidden_part(t_index, xs, gate_weight, up_weight, start, size, after)
+        h, *whole = hidden_part(t_index, xs, gate_weight, up_weight, start, size, after)
+        xs = whole or xs
         pieces.append([h, swap(h, "tensor", 1), swap(h, "tensor", 2)])
     sums = []
     for i, start in enumerate(starts):

time: 54.9 us -> 55.5 us (1.011)
  waiting for transfers between devices: 25.8 us -> 22.6 us
  starting transfers between devices: 18 us -> 20.3 us
  local copies, waits for them, and re-layouts: 0.03 us -> 1.24 us
    ppermute x23 -> x26, waiting for transfers between devices: 25.8 us -> 22.6 us  [swap(): return lax.ppermute(value, axis, [(i, i ^ bit) for i in range(size)])]
    ppermute x23 -> x26, starting transfers between devices: 18 us -> 20.3 us  [swap(): return lax.ppermute(value, axis, [(i, i ^ bit) for i in range(size)])]
    unnamed x16 -> x26, local copies, waits for them, and re-layouts: 0.03 us -> 1.24 us
    pallas_call x5 -> x6, Pallas kernels: 4.58 us -> 4.68 us  [the longest x4 4.6 us: hidden_part(): pl.pallas_call(functools.partial(hidden_kernel, joined, parts, start), ou...]
  transfers between devices with their start and end apart: 23 -> 26, of which waited for: 13 -> 16; matrix products, arithmetic and copies ran while one was open for 0% -> 0% of each run, Pallas kernels for 11% -> 11%
where the time goes in v7:
time: 55.5 us; the launch traced here: 55.4 us
  waiting for transfers between devices  22.6 us (41%)
  starting transfers between devices  20.3 us (37%)
  Pallas kernels  9.72 us (18%)
  local copies, waits for them, and re-layouts  1.24 us (2%)
  between operations  0.9 us (2%)
  other arithmetic  0.57 us (1%)
    ppermute x26, waiting for transfers between devices, swap(): return lax.ppermute(value, axis, [(i, i ^ bit) for i in range(size)])  22.6 us
    ppermute x26, starting transfers between devices, swap(): return lax.ppermute(value, axis, [(i, i ^ bit) for i in range(size)])  20.3 us
    pallas_call x4, Pallas kernels, hidden_part(): pl.pallas_call(functools.partial(hidden_kernel, joined, parts, start), ou...  4.6 us
    pallas_call x4, Pallas kernels, down_part(): pl.pallas_call(functools.partial(down_kernel, len(pieces), where, slab, h...  2.55 us
    pallas_call x1, Pallas kernels, select_rows(): pl.pallas_call(select_kernel, out_shape=[jax.ShapeDtypeStruct((MOST, widt...  1.3 us
    unnamed x26, local copies, waits for them, and re-layouts  1.24 us
    pallas_call x1, Pallas kernels, combine(): pl.pallas_call(combine_kernel, out_shape=[jax.ShapeDtypeStruct(out_grad.s...  1.19 us
  transfers between devices with their start and end apart: 26, of which 16 were waited for; matrix products, arithmetic and copies ran while one was open for 0% of the time, Pallas kernels for 11%

profile of v7, /device:TPU:0, one launch (start us, length us, event | category | flops | bytes accessed | tf_op | source)
XLA Modules:
  0.0 55.4 jit_solution(4723776141293075803)
XLA Ops:
  0.6 0.0 slice-start
  0.6 0.0 slice-start.1
  0.7 0.0 slice-start.2
  0.7 1.3 %select_rows.1 = (bf16[34,768]{1,0:T(8,128)(2,1)S(1)}, bf16[204,128]{1,0:T(8,128)(2,1)S(1)}, bf16[204,128]{1,0:T(8,128)(2,1)S(1)}, bf16[204,128]{1,0:T(8,128)(2,1)S(1)}) custom-call(s32[1]{0:T(128)} %bitcast.me_ref, s32[1]{0:T(128)} %bitcast.3.t_ref, s32[2,64]{1,0:T(2,128)} %bitcast.12, bf16[64,768]{1,0:T(8,128)(2,1)} %tokens_hbm.1), custom_call_target="tpu_custom_call" | custom-call | flops 8000000000 | bytes 1000 | tf_op jit(solution)/shard_map/select_rows/pallas_call | solution.py:82
  2.0 3.1 %collective-permute-start = (bf16[204,128]{1,0:T(8,128)(2,1)S(1)}, bf16[204,128]{1,0:T(8,128)(2,1)S(1)}, u32[]{:S(2)}, u32[]{:S(2)}) collective-permute-start(bf16[204,128]{1,0:T(8,128)(2,1)S(1)} %get-tuple-element.15), channel_id=1, source_target_pairs={{0,4},{4,0},{8,12},{12,8},{1,5},{5,1},{9,13},{13,9},{2,6},{6,2},{1... | collective-permute-start | bytes 156680 | tf_op jit(solution)/shard_map/ppermute | solution.py:22
  5.1 2.6 %collective-permute-start.1 = (bf16[204,128]{1,0:T(8,128)(2,1)S(1)}, bf16[204,128]{1,0:T(8,128)(2,1)S(1)}, u32[]{:S(2)}, u32[]{:S(2)}) collective-permute-start(bf16[204,128]{1,0:T(8,128)(2,1)S(1)} %get-tuple-element.16), channel_id=1, source_target_pairs={{0,8},{4,12},{8,0},{12,4},{1,9},{5,13},{9,1},{13,5},{2,10},{6,14},... | collective-permute-start | bytes 156680 | tf_op jit(solution)/shard_map/ppermute | solution.py:22
  7.7 1.8 %collective-permute-start.3 = (bf16[64,768]{1,0:T(8,128)(2,1)S(1)}, bf16[64,768]{1,0:T(8,128)(2,1)S(1)}, u32[]{:S(2)}, u32[]{:S(2)}) collective-permute-start(bf16[64,768]{1,0:T(8,128)(2,1)S(1)} %pack_near.1.refs_0_), channel_id=1, source_target_pairs={{0,2},{1,3},{2,0},{3,1},{4,6},{5,7},{6,4},{7,5},{8,10},{9,11},{10,... | collective-permute-start | bytes 294920 | tf_op jit(solution)/shard_map/ppermute | solution.py:22
  9.5 1.7 %collective-permute-done.1.third_ref = bf16[204,128]{1,0:T(8,128)(2,1)S(1)} collective-permute-done((bf16[204,128]{1,0:T(8,128)(2,1)S(1)}, bf16[204,128]{1,0:T(8,128)(2,1)S(1)}, u32[]{:S(2)}, u32[]{:S(2)}) %collective-permute-start.1) | collective-permute-done | bytes 52256 | tf_op jit(solution)/shard_map/ppermute | solution.py:22
  11.1 2.5 %collective-permute-done.2.fourth_ref = bf16[204,128]{1,0:T(8,128)(2,1)S(1)} collective-permute-done((bf16[204,128]{1,0:T(8,128)(2,1)S(1)}, bf16[204,128]{1,0:T(8,128)(2,1)S(1)}, u32[]{:S(2)}, u32[]{:S(2)}) %collective-permute-start.2) | collective-permute-done | bytes 52256 | tf_op jit(solution)/shard_map/ppermute | solution.py:22
  13.6 0.0 collective-permute-done.3.refs_1_.refs_4_
  13.7 0.1 collective-permute-start.5
  13.7 1.6 %collective-permute-start.6 = (bf16[72,768]{1,0:T(8,128)(2,1)S(1)}, bf16[72,768]{1,0:T(8,128)(2,1)S(1)}, u32[]{:S(2)}, u32[]{:S(2)}) collective-permute-start(bf16[72,768]{1,0:T(8,128)(2,1)S(1)} %hold.4.refs_1_), channel_id=1, source_target_pairs={{0,2},{1,3},{2,0},{3,1},{4,6},{5,7},{6,4},{7,5},{8,10},{9,11},{10,... | collective-permute-start | bytes 331784 | tf_op jit(solution)/shard_map/ppermute | solution.py:22
  15.3 0.2 collective-permute-start.4
  15.5 0.3 collective-permute-start.7
  15.8 0.8 %collective-permute-done.4.refs_1_.refs_2_ = bf16[64,768]{1,0:T(8,128)(2,1)S(1)} collective-permute-done((bf16[64,768]{1,0:T(8,128)(2,1)S(1)}, bf16[64,768]{1,0:T(8,128)(2,1)S(1)}, u32[]{:S(2)}, u32[]{:S(2)}) %collective-permute-start.4) | collective-permute-done | bytes 98336 | tf_op jit(solution)/shard_map/ppermute | solution.py:22
  16.6 0.2 collective-permute-done.7.refs_3_.refs_6_
  16.8 0.0 collective-permute-done.5.refs_2_.refs_3_
  16.8 2.5 %collective-permute-done.6.refs_0_ = bf16[72,768]{1,0:T(8,128)(2,1)S(1)} collective-permute-done((bf16[72,768]{1,0:T(8,128)(2,1)S(1)}, bf16[72,768]{1,0:T(8,128)(2,1)S(1)}, u32[]{:S(2)}, u32[]{:S(2)}) %collective-permute-start.6) | collective-permute-done | bytes 110624 | tf_op jit(solution)/shard_map/ppermute | solution.py:22
  19.2 0.0 collective-permute-start.8
  19.2 1.3 %collective-permute-done.8.refs_7_ = bf16[72,768]{1,0:T(8,128)(2,1)S(1)} collective-permute-done((bf16[72,768]{1,0:T(8,128)(2,1)S(1)}, bf16[72,768]{1,0:T(8,128)(2,1)S(1)}, u32[]{:S(2)}, u32[]{:S(2)}) %collective-permute-start.8) | collective-permute-done | bytes 110624 | tf_op jit(solution)/shard_map/ppermute | solution.py:22
  20.6 0.7 %hidden_part.4 = (bf16[136,256]{1,0:T(8,128)(2,1)S(1)}, bf16[4,136,768]{2,1,0:T(8,128)(2,1)S(1)}) custom-call(s32[1]{0:T(128)} %bitcast.3.t_ref, bf16[64,768]{1,0:T(8,128)(2,1)S(1)} %pack_near.1.refs_0_, bf16[72,768]{1,0:T(8,128)(2,1)S(1)} %hold.4.refs_1_, bf16[64,768]{1,0:T(8,128)(2,1)S(1)} %collective-permute-done.4.refs_1_.refs_2_, ...), custom_call_target="tpu_custom_call" | custom-call | flops 1000 | bytes 1000 | tf_op jit(solution)/shard_map/hidden_part/pallas_call | solution.py:178
  21.3 1.5 %collective-permute-start.12 = (bf16[136,256]{1,0:T(8,128)(2,1)S(1)}, bf16[136,256]{1,0:T(8,128)(2,1)S(1)}, u32[]{:S(2)}, u32[]{:S(2)}) collective-permute-start(bf16[136,256]{1,0:T(8,128)(2,1)S(1)} %get-tuple-element.19.refs_0_), channel_id=1, source_target_pairs={{0,2},{1,3},{2,0},{3,1},{4,6},{5,7},{6,4},{7,5},{8,10},{9,11},{10,... | collective-permute-start | bytes 208904 | tf_op jit(solution)/shard_map/ppermute | solution.py:22
  22.8 1.1 %hidden_part.5.refs_4_ = bf16[136,512]{1,0:T(8,128)(2,1)S(1)} custom-call(s32[1]{0:T(128)} %bitcast.3.t_ref, bf16[4,136,768]{2,1,0:T(8,128)(2,1)S(1)} %get-tuple-element.18.refs_0_, bf16[1,3072,2048]{2,1,0:T(8,128)(2,1)S(1)} %bitcast.7, bf16[1,3072,2048]{2,1,0:T(8,128)(2,1)S(1)} %copy-done), custom_call_target="tpu_custom_call" | custom-call | flops 1000 | bytes 1000 | tf_op jit(solution)/shard_map/hidden_part/pallas_call | solution.py:178
  23.9 0.6 %collective-permute-start.9 = (bf16[136,512]{1,0:T(8,128)(2,1)S(1)}, bf16[136,512]{1,0:T(8,128)(2,1)S(1)}, u32[]{:S(2)}, u32[]{:S(2)}) collective-permute-start(bf16[136,512]{1,0:T(8,128)(2,1)S(1)} %hidden_part.5.refs_4_), channel_id=1, source_target_pairs={{0,2},{1,3},{2,0},{3,1},{4,6},{5,7},{6,4},{7,5},{8,10},{9,11},{10,... | collective-permute-start | bytes 417800 | tf_op jit(solution)/shard_map/ppermute | solution.py:22
  24.6 1.1 %collective-permute-done.12.refs_3_.refs_2_ = bf16[136,256]{1,0:T(8,128)(2,1)S(1)} collective-permute-done((bf16[136,256]{1,0:T(8,128)(2,1)S(1)}, bf16[136,256]{1,0:T(8,128)(2,1)S(1)}, u32[]{:S(2)}, u32[]{:S(2)}) %collective-permute-start.12) | collective-permute-done | bytes 69664 | tf_op jit(solution)/shard_map/ppermute | solution.py:22
  25.6 1.6 %hidden_part.7.refs_2_ = bf16[136,768]{1,0:T(8,128)(2,1)S(1)} custom-call(s32[1]{0:T(128)} %bitcast.3.t_ref, bf16[4,136,768]{2,1,0:T(8,128)(2,1)S(1)} %get-tuple-element.18.refs_0_, bf16[1,3072,2048]{2,1,0:T(8,128)(2,1)S(1)} %bitcast.7, bf16[1,3072,2048]{2,1,0:T(8,128)(2,1)S(1)} %copy-done, bf16[136,256]{1,0:T(8,128)(2,1)S(1)} %collective-permute-done.12.refs_3_.refs_2_), custom_call_target="tpu_custom_call" | custom-call | flops 1000 | bytes 1000 | tf_op jit(solution)/shard_map/hidden_part/pallas_call | solution.py:178
  27.3 0.0 slice-start.5
  27.3 1.7 %collective-permute-start.18 = (bf16[136,768]{1,0:T(8,128)(2,1)S(1)}, bf16[136,768]{1,0:T(8,128)(2,1)S(1)}, u32[]{:S(2)}, u32[]{:S(2)}) collective-permute-start(bf16[136,768]{1,0:T(8,128)(2,1)S(1)} %hidden_part.7.refs_2_), channel_id=1, source_target_pairs={{0,2},{1,3},{2,0},{3,1},{4,6},{5,7},{6,4},{7,5},{8,10},{9,11},{10,... | collective-permute-start | bytes 626696 | tf_op jit(solution)/shard_map/ppermute | solution.py:22
  29.0 0.0 collective-permute-start.14
  29.0 0.5 collective-permute-start.16
  29.5 0.0 collective-permute-start.13
  29.5 0.7 %collective-permute-done.14.refs_1_ = bf16[136,256]{1,0:T(8,128)(2,1)S(1)} collective-permute-done((bf16[136,256]{1,0:T(8,128)(2,1)S(1)}, bf16[136,256]{1,0:T(8,128)(2,1)S(1)}, u32[]{:S(2)}, u32[]{:S(2)}) %collective-permute-start.14) | collective-permute-done | bytes 69664 | tf_op jit(solution)/shard_map/ppermute | solution.py:22
  30.2 0.2 collective-permute-start.15
  30.4 0.0 collective-permute-done.9.refs_3_.refs_0_
  30.4 0.4 collective-permute-start.11
  30.8 1.2 %hidden_part.6.refs_2_ = bf16[136,512]{1,0:T(8,128)(2,1)S(1)} custom-call(s32[1]{0:T(128)} %bitcast.3.t_ref, bf16[4,136,768]{2,1,0:T(8,128)(2,1)S(1)} %get-tuple-element.18.refs_0_, bf16[1,3072,2048]{2,1,0:T(8,128)(2,1)S(1)} %bitcast.7, bf16[1,3072,2048]{2,1,0:T(8,128)(2,1)S(1)} %copy-done, bf16[136,512]{1,0:T(8,128)(2,1)S(1)} %collective-permute-done.9.refs_3_.refs_0_), custom_call_target="tpu_custom_call" | custom-call | flops 1000 | bytes 1000 | tf_op jit(solution)/shard_map/hidden_part/pallas_call | solution.py:178
  31.9 0.0 slice-start.8
  31.9 0.5 collective-permute-start.10
  32.4 0.0 collective-permute-done.16.refs_5_
  32.4 0.6 %down_part.4.refs_5_.refs_1_ = f32[136,768]{1,0:T(8,128)S(1)} custom-call(s32[1]{0:T(128)} %bitcast.3.t_ref, bf16[136,256]{1,0:T(8,128)(2,1)S(1)} %get-tuple-element.19.refs_0_, bf16[136,256]{1,0:T(8,128)(2,1)S(1)} %collective-permute-done.14.refs_1_, bf16[136,256]{1,0:T(8,128)(2,1)S(1)} %collective-permute-done.12.refs_3_.refs_2_, ...), custom_call_target="tpu_custom_call" | custom-call | flops 427819008 | bytes 1000 | tf_op jit(solution)/shard_map/down_part/pallas_call | solution.py:216
  33.1 0.8 %collective-permute-done.18.refs_0_ = bf16[136,768]{1,0:T(8,128)(2,1)S(1)} collective-permute-done((bf16[136,768]{1,0:T(8,128)(2,1)S(1)}, bf16[136,768]{1,0:T(8,128)(2,1)S(1)}, u32[]{:S(2)}, u32[]{:S(2)}) %collective-permute-start.18) | collective-permute-done | bytes 208928 | tf_op jit(solution)/shard_map/ppermute | solution.py:22
  33.9 0.0 collective-permute-start.19
  33.9 0.5 collective-permute-start.20
  34.4 0.0 collective-permute-done.11.refs_1_
  34.5 1.2 %slice-done.8 = s8[4194304]{0:T(1024)(128)(4,1)S(1)} async-done(((s8[12582912]{0:T(1024)(128)(4,1)}), s8[4194304]{0:T(1024)(128)(4,1)S(1)}, s32[]{:S(2)}) %slice-start.8) | async-done | bytes 4194328
  35.6 0.7 %down_part.5.refs_1_.refs_5_ = f32[136,768]{1,0:T(8,128)S(1)} custom-call(s32[1]{0:T(128)} %bitcast.3.t_ref, bf16[136,512]{1,0:T(8,128)(2,1)S(1)} %collective-permute-done.9.refs_3_.refs_0_, bf16[136,512]{1,0:T(8,128)(2,1)S(1)} %collective-permute-done.11.refs_1_, bf16[136,768]{1,0:T(8,128)(2,1)S(1)} %hidden_part.7.refs_2_, ...), custom_call_target="tpu_custom_call" | custom-call | flops 534773760 | bytes 1000 | tf_op jit(solution)/shard_map/down_part/pallas_call | solution.py:216
  36.4 1.4 %collective-permute-done.10.refs_0_ = bf16[136,512]{1,0:T(8,128)(2,1)S(1)} collective-permute-done((bf16[136,512]{1,0:T(8,128)(2,1)S(1)}, bf16[136,512]{1,0:T(8,128)(2,1)S(1)}, u32[]{:S(2)}, u32[]{:S(2)}) %collective-permute-start.10) | collective-permute-done | bytes 139296 | tf_op jit(solution)/shard_map/ppermute | solution.py:22
  37.8 0.1 collective-permute-start.17
  37.8 0.0 collective-permute-done.20.refs_3_
  37.9 0.8 %down_part.6.refs_3_ = f32[136,768]{1,0:T(8,128)S(1)} custom-call(s32[1]{0:T(128)} %bitcast.3.t_ref, bf16[136,768]{1,0:T(8,128)(2,1)S(1)} %hold.7.refs_0_, bf16[136,768]{1,0:T(8,128)(2,1)S(1)} %collective-permute-done.19.refs_1_, bf16[136,512]{1,0:T(8,128)(2,1)S(1)} %hidden_part.6.refs_2_, bf16[136,512]{1,0:T(8,128)(2,1)S(1)} %collective-permute-done.20.refs_3_, ...), custom_call_target="tpu_custom_call" | custom-call | flops 534773760 | bytes 1000 | tf_op jit(solution)/shard_map/down_part/pallas_call | solution.py:216
  38.6 0.6 %collective-permute-done.17.refs_1_ = bf16[136,512]{1,0:T(8,128)(2,1)S(1)} collective-permute-done((bf16[136,512]{1,0:T(8,128)(2,1)S(1)}, bf16[136,512]{1,0:T(8,128)(2,1)S(1)}, u32[]{:S(2)}, u32[]{:S(2)}) %collective-permute-start.17) | collective-permute-done | bytes 139296 | tf_op jit(solution)/shard_map/ppermute | solution.py:22
  39.2 0.4 down_part.7
  39.6 0.3 collective-permute-start.21
  39.9 3.1 %collective-permute-start.22 = (bf16[204,128]{1,0:T(8,128)(2,1)S(1)}, bf16[204,128]{1,0:T(8,128)(2,1)S(1)}, u32[]{:S(2)}, u32[]{:S(2)}) collective-permute-start(bf16[204,128]{1,0:T(8,128)(2,1)S(1)} %get-tuple-element.22), channel_id=1, source_target_pairs={{0,8},{4,12},{8,0},{12,4},{1,9},{5,13},{9,1},{13,5},{2,10},{6,14},... | collective-permute-start | bytes 156680 | tf_op jit(solution)/shard_map/ppermute | solution.py:22
  43.0 1.1 %collective-permute-start.23 = (bf16[204,128]{1,0:T(8,128)(2,1)S(1)}, bf16[204,128]{1,0:T(8,128)(2,1)S(1)}, u32[]{:S(2)}, u32[]{:S(2)}) collective-permute-start(bf16[204,128]{1,0:T(8,128)(2,1)S(1)} %get-tuple-element.23), channel_id=1, source_target_pairs={{0,12},{4,8},{8,4},{12,0},{1,13},{5,9},{9,5},{13,1},{2,14},{6,10},... | collective-permute-start | bytes 156680 | tf_op jit(solution)/shard_map/ppermute | solution.py:22
  44.0 0.3 collective-permute-done.21.refs_1_
  44.4 2.3 %collective-permute-done.22.refs_2_ = bf16[204,128]{1,0:T(8,128)(2,1)S(1)} collective-permute-done((bf16[204,128]{1,0:T(8,128)(2,1)S(1)}, bf16[204,128]{1,0:T(8,128)(2,1)S(1)}, u32[]{:S(2)}, u32[]{:S(2)}) %collective-permute-start.22) | collective-permute-done | bytes 52256 | tf_op jit(solution)/shard_map/ppermute | solution.py:22
  46.7 2.2 %collective-permute-done.23.refs_3_ = bf16[204,128]{1,0:T(8,128)(2,1)S(1)} collective-permute-done((bf16[204,128]{1,0:T(8,128)(2,1)S(1)}, bf16[204,128]{1,0:T(8,128)(2,1)S(1)}, u32[]{:S(2)}, u32[]{:S(2)}) %collective-permute-start.23) | collective-permute-done | bytes 52256 | tf_op jit(solution)/shard_map/ppermute | solution.py:22
  48.9 1.2 %combine.1 = (bf16[64,768]{1,0:T(8,128)(2,1)}, f32[2,64]{1,0:T(2,128)S(1)}) custom-call(s32[1]{0:T(128)} %bitcast.me_ref, s32[2,64]{1,0:T(2,128)S(1)} %bitcast.13, f32[2,64]{1,0:T(2,128)S(1)} %bitcast.14, bf16[64,768]{1,0:T(8,128)(2,1)S(1)} %copy-done.1, bf16[34,768]{1,0:T(8,128)(2,1)S(1)} %get-tuple-element.20.refs_0_, ...), custom_call_target="tpu_custom_call" | custom-call | flops 1000 | bytes 1000 | tf_op jit(solution)/shard_map/combine/pallas_call | solution.py:262
  50.1 0.4 collective-permute-start.24
  50.5 3.2 %collective-permute-done.24 = f32[2,64]{1,0:T(2,128)S(1)} collective-permute-done((f32[2,64]{1,0:T(2,128)S(1)}, f32[2,64]{1,0:T(2,128)S(1)}, u32[]{:S(2)}, u32[]{:S(2)}) %collective-permute-start.24) | collective-permute-done | bytes 544 | tf_op jit(solution)/shard_map/ppermute | solution.py:22
  53.7 0.0 collective-permute-start.25
  53.7 1.1 %collective-permute-done.25 = f32[2,64]{1,0:T(2,128)S(1)} collective-permute-done((f32[2,64]{1,0:T(2,128)S(1)}, f32[2,64]{1,0:T(2,128)S(1)}, u32[]{:S(2)}, u32[]{:S(2)}) %collective-permute-start.25) | collective-permute-done | bytes 544 | tf_op jit(solution)/shard_map/ppermute | solution.py:22
  54.8 0.6 %add_bitcast_fusion = f32[64,2]{0,1:T(2,128)} fusion(f32[2,64]{1,0:T(2,128)S(1)} %add.6, f32[2,64]{1,0:T(2,128)S(1)} %collective-permute-done.25), kind=kLoop, calls=%fused_computation | loop fusion | flops 128 | bytes 1536 | tf_op jit(solution)/shard_map/transpose | solution.py:320
  (35 shorter events, 0.1 us)
Async XLA Ops:
  0.6 19.9 %slice-start = ((s8[12582912]{0:T(1024)(128)(4,1)}), s8[4194304]{0:T(1024)(128)(4,1)S(1)}, s32[]{:S(2)}) async-start(s8[12582912]{0:T(1024)(128)(4,1)} %bitcast.6), calls=%async_computation | async-start | bytes 8388608
  0.6 19.9 %slice-start.1 = ((s8[12582912]{0:T(1024)(128)(4,1)}), s8[4194304]{0:T(1024)(128)(4,1)S(1)}, s32[]{:S(2)}) async-start(s8[12582912]{0:T(1024)(128)(4,1)} %bitcast.6), calls=%async_computation.1 | async-start | bytes 8388608
  0.7 19.9 %slice-start.2 = ((s8[12582912]{0:T(1024)(128)(4,1)}), s8[4194304]{0:T(1024)(128)(4,1)S(1)}, s32[]{:S(2)}) async-start(s8[12582912]{0:T(1024)(128)(4,1)} %bitcast.6), calls=%async_computation.2 | async-start | bytes 8388608
  0.7 19.9 %copy-start = (bf16[1,3072,2048]{2,1,0:T(8,128)(2,1)S(1)}, bf16[1,3072,2048]{2,1,0:T(8,128)(2,1)}, u32[]{:S(2)}) copy-start(bf16[1,3072,2048]{2,1,0:T(8,128)(2,1)} %refs_2_.6) | copy-start | bytes 37748740
  2.0 5.7 %collective-permute-start = (bf16[204,128]{1,0:T(8,128)(2,1)S(1)}, bf16[204,128]{1,0:T(8,128)(2,1)S(1)}, u32[]{:S(2)}, u32[]{:S(2)}) collective-permute-start(bf16[204,128]{1,0:T(8,128)(2,1)S(1)} %get-tuple-element.15), channel_id=1, source_target_pairs={{0,4},{4,0},{8,12},{12,8},{1,5},{5,1},{9,13},{13,9},{2,6},{6,2},{1... | collective-permute-start | bytes 156680 | tf_op jit(solution)/shard_map/ppermute | solution.py:22
  5.1 6.1 %collective-permute-start.1 = (bf16[204,128]{1,0:T(8,128)(2,1)S(1)}, bf16[204,128]{1,0:T(8,128)(2,1)S(1)}, u32[]{:S(2)}, u32[]{:S(2)}) collective-permute-start(bf16[204,128]{1,0:T(8,128)(2,1)S(1)} %get-tuple-element.16), channel_id=1, source_target_pairs={{0,8},{4,12},{8,0},{12,4},{1,9},{5,13},{9,1},{13,5},{2,10},{6,14},... | collective-permute-start | bytes 156680 | tf_op jit(solution)/shard_map/ppermute | solution.py:22
  7.7 5.9 %collective-permute-start.2 = (bf16[204,128]{1,0:T(8,128)(2,1)S(1)}, bf16[204,128]{1,0:T(8,128)(2,1)S(1)}, u32[]{:S(2)}, u32[]{:S(2)}) collective-permute-start(bf16[204,128]{1,0:T(8,128)(2,1)S(1)} %get-tuple-element.17), channel_id=1, source_target_pairs={{0,12},{4,8},{8,4},{12,0},{1,13},{5,9},{9,5},{13,1},{2,14},{6,10},... | collective-permute-start | bytes 156680 | tf_op jit(solution)/shard_map/ppermute | solution.py:22
  7.7 5.9 %collective-permute-start.3 = (bf16[64,768]{1,0:T(8,128)(2,1)S(1)}, bf16[64,768]{1,0:T(8,128)(2,1)S(1)}, u32[]{:S(2)}, u32[]{:S(2)}) collective-permute-start(bf16[64,768]{1,0:T(8,128)(2,1)S(1)} %pack_near.1.refs_0_), channel_id=1, source_target_pairs={{0,2},{1,3},{2,0},{3,1},{4,6},{5,7},{6,4},{7,5},{8,10},{9,11},{10,... | collective-permute-start | bytes 294920 | tf_op jit(solution)/shard_map/ppermute | solution.py:22
  13.7 3.1 %collective-permute-start.5 = (bf16[72,768]{1,0:T(8,128)(2,1)S(1)}, bf16[72,768]{1,0:T(8,128)(2,1)S(1)}, u32[]{:S(2)}, u32[]{:S(2)}) collective-permute-start(bf16[72,768]{1,0:T(8,128)(2,1)S(1)} %hold.4.refs_1_), channel_id=1, source_target_pairs={{0,1},{1,0},{2,3},{3,2},{4,5},{5,4},{6,7},{7,6},{8,9},{9,8},{10,11... | collective-permute-start | bytes 331784 | tf_op jit(solution)/shard_map/ppermute | solution.py:22
  13.7 5.5 %collective-permute-start.6 = (bf16[72,768]{1,0:T(8,128)(2,1)S(1)}, bf16[72,768]{1,0:T(8,128)(2,1)S(1)}, u32[]{:S(2)}, u32[]{:S(2)}) collective-permute-start(bf16[72,768]{1,0:T(8,128)(2,1)S(1)} %hold.4.refs_1_), channel_id=1, source_target_pairs={{0,2},{1,3},{2,0},{3,1},{4,6},{5,7},{6,4},{7,5},{8,10},{9,11},{10,... | collective-permute-start | bytes 331784 | tf_op jit(solution)/shard_map/ppermute | solution.py:22
  15.3 1.3 %collective-permute-start.4 = (bf16[64,768]{1,0:T(8,128)(2,1)S(1)}, bf16[64,768]{1,0:T(8,128)(2,1)S(1)}, u32[]{:S(2)}, u32[]{:S(2)}) collective-permute-start(bf16[64,768]{1,0:T(8,128)(2,1)S(1)} %pack_near.1.refs_0_), channel_id=1, source_target_pairs={{0,1},{1,0},{2,3},{3,2},{4,5},{5,4},{6,7},{7,6},{8,9},{9,8},{10,11... | collective-permute-start | bytes 294920 | tf_op jit(solution)/shard_map/ppermute | solution.py:22
  15.5 1.3 %collective-permute-start.7 = (bf16[64,768]{1,0:T(8,128)(2,1)S(1)}, bf16[64,768]{1,0:T(8,128)(2,1)S(1)}, u32[]{:S(2)}, u32[]{:S(2)}) collective-permute-start(bf16[64,768]{1,0:T(8,128)(2,1)S(1)} %collective-permute-done.3.refs_1_.refs_4_), channel_id=1, source_target_pairs={{0,1},{1,0},{2,3},{3,2},{4,5},{5,4},{6,7},{7,6},{8,9},{9,8},{10,11... | collective-permute-start | bytes 294920 | tf_op jit(solution)/shard_map/ppermute | solution.py:22
  19.2 1.3 %collective-permute-start.8 = (bf16[72,768]{1,0:T(8,128)(2,1)S(1)}, bf16[72,768]{1,0:T(8,128)(2,1)S(1)}, u32[]{:S(2)}, u32[]{:S(2)}) collective-permute-start(bf16[72,768]{1,0:T(8,128)(2,1)S(1)} %hold.5.refs_5_), channel_id=1, source_target_pairs={{0,1},{1,0},{2,3},{3,2},{4,5},{5,4},{6,7},{7,6},{8,9},{9,8},{10,11... | collective-permute-start | bytes 331784 | tf_op jit(solution)/shard_map/ppermute | solution.py:22
  21.3 4.4 %collective-permute-start.12 = (bf16[136,256]{1,0:T(8,128)(2,1)S(1)}, bf16[136,256]{1,0:T(8,128)(2,1)S(1)}, u32[]{:S(2)}, u32[]{:S(2)}) collective-permute-start(bf16[136,256]{1,0:T(8,128)(2,1)S(1)} %get-tuple-element.19.refs_0_), channel_id=1, source_target_pairs={{0,2},{1,3},{2,0},{3,1},{4,6},{5,7},{6,4},{7,5},{8,10},{9,11},{10,... | collective-permute-start | bytes 208904 | tf_op jit(solution)/shard_map/ppermute | solution.py:22
  23.9 6.5 %collective-permute-start.9 = (bf16[136,512]{1,0:T(8,128)(2,1)S(1)}, bf16[136,512]{1,0:T(8,128)(2,1)S(1)}, u32[]{:S(2)}, u32[]{:S(2)}) collective-permute-start(bf16[136,512]{1,0:T(8,128)(2,1)S(1)} %hidden_part.5.refs_4_), channel_id=1, source_target_pairs={{0,2},{1,3},{2,0},{3,1},{4,6},{5,7},{6,4},{7,5},{8,10},{9,11},{10,... | collective-permute-start | bytes 417800 | tf_op jit(solution)/shard_map/ppermute | solution.py:22
  25.6 6.8 %slice-start.3 = ((s8[12582912]{0:T(1024)(128)(4,1)}), s8[4194304]{0:T(1024)(128)(4,1)S(1)}, s32[]{:S(2)}) async-start(s8[12582912]{0:T(1024)(128)(4,1)} %bitcast.8), calls=%async_computation.3 | async-start | bytes 8388608
  25.6 6.8 %slice-start.4 = ((s8[12582912]{0:T(1024)(128)(4,1)}), s8[4194304]{0:T(1024)(128)(4,1)S(1)}, s32[]{:S(2)}) async-start(s8[12582912]{0:T(1024)(128)(4,1)} %bitcast.8), calls=%async_computation.4 | async-start | bytes 8388608
  27.3 5.1 %slice-start.5 = ((s8[12582912]{0:T(1024)(128)(4,1)}), s8[4194304]{0:T(1024)(128)(4,1)S(1)}, s32[]{:S(2)}) async-start(s8[12582912]{0:T(1024)(128)(4,1)} %bitcast.8), calls=%async_computation.5 | async-start | bytes 8388608
  27.3 6.6 %collective-permute-start.18 = (bf16[136,768]{1,0:T(8,128)(2,1)S(1)}, bf16[136,768]{1,0:T(8,128)(2,1)S(1)}, u32[]{:S(2)}, u32[]{:S(2)}) collective-permute-start(bf16[136,768]{1,0:T(8,128)(2,1)S(1)} %hidden_part.7.refs_2_), channel_id=1, source_target_pairs={{0,2},{1,3},{2,0},{3,1},{4,6},{5,7},{6,4},{7,5},{8,10},{9,11},{10,... | collective-permute-start | bytes 626696 | tf_op jit(solution)/shard_map/ppermute | solution.py:22
  29.0 1.3 %collective-permute-start.14 = (bf16[136,256]{1,0:T(8,128)(2,1)S(1)}, bf16[136,256]{1,0:T(8,128)(2,1)S(1)}, u32[]{:S(2)}, u32[]{:S(2)}) collective-permute-start(bf16[136,256]{1,0:T(8,128)(2,1)S(1)} %get-tuple-element.19.refs_0_), channel_id=1, source_target_pairs={{0,1},{1,0},{2,3},{3,2},{4,5},{5,4},{6,7},{7,6},{8,9},{9,8},{10,11... | collective-permute-start | bytes 208904 | tf_op jit(solution)/shard_map/ppermute | solution.py:22
  29.0 3.4 %collective-permute-start.16 = (bf16[136,512]{1,0:T(8,128)(2,1)S(1)}, bf16[136,512]{1,0:T(8,128)(2,1)S(1)}, u32[]{:S(2)}, u32[]{:S(2)}) collective-permute-start(bf16[136,512]{1,0:T(8,128)(2,1)S(1)} %hidden_part.5.refs_4_), channel_id=1, source_target_pairs={{0,1},{1,0},{2,3},{3,2},{4,5},{5,4},{6,7},{7,6},{8,9},{9,8},{10,11... | collective-permute-start | bytes 417800 | tf_op jit(solution)/shard_map/ppermute | solution.py:22
  29.5 5.0 %collective-permute-start.13 = (bf16[136,768]{1,0:T(8,128)(2,1)S(1)}, bf16[136,768]{1,0:T(8,128)(2,1)S(1)}, u32[]{:S(2)}, u32[]{:S(2)}) collective-permute-start(bf16[136,768]{1,0:T(8,128)(2,1)S(1)} %hidden_part.7.refs_2_), channel_id=1, source_target_pairs={{0,1},{1,0},{2,3},{3,2},{4,5},{5,4},{6,7},{7,6},{8,9},{9,8},{10,11... | collective-permute-start | bytes 626696 | tf_op jit(solution)/shard_map/ppermute | solution.py:22
  30.2 1.7 %collective-permute-start.15 = (bf16[136,256]{1,0:T(8,128)(2,1)S(1)}, bf16[136,256]{1,0:T(8,128)(2,1)S(1)}, u32[]{:S(2)}, u32[]{:S(2)}) collective-permute-start(bf16[136,256]{1,0:T(8,128)(2,1)S(1)} %collective-permute-done.12.refs_3_.refs_2_), channel_id=1, source_target_pairs={{0,1},{1,0},{2,3},{3,2},{4,5},{5,4},{6,7},{7,6},{8,9},{9,8},{10,11... | collective-permute-start | bytes 208904 | tf_op jit(solution)/shard_map/ppermute | solution.py:22
  30.4 4.0 %collective-permute-start.11 = (bf16[136,512]{1,0:T(8,128)(2,1)S(1)}, bf16[136,512]{1,0:T(8,128)(2,1)S(1)}, u32[]{:S(2)}, u32[]{:S(2)}) collective-permute-start(bf16[136,512]{1,0:T(8,128)(2,1)S(1)} %collective-permute-done.9.refs_3_.refs_0_), channel_id=1, source_target_pairs={{0,1},{1,0},{2,3},{3,2},{4,5},{5,4},{6,7},{7,6},{8,9},{9,8},{10,11... | collective-permute-start | bytes 417800 | tf_op jit(solution)/shard_map/ppermute | solution.py:22
  30.8 3.7 %slice-start.6 = ((s8[12582912]{0:T(1024)(128)(4,1)}), s8[4194304]{0:T(1024)(128)(4,1)S(1)}, s32[]{:S(2)}) async-start(s8[12582912]{0:T(1024)(128)(4,1)} %bitcast.10), calls=%async_computation.6 | async-start | bytes 8388608
  30.8 3.7 %slice-start.7 = ((s8[12582912]{0:T(1024)(128)(4,1)}), s8[4194304]{0:T(1024)(128)(4,1)S(1)}, s32[]{:S(2)}) async-start(s8[12582912]{0:T(1024)(128)(4,1)} %bitcast.10), calls=%async_computation.7 | async-start | bytes 8388608
  31.9 3.7 %slice-start.8 = ((s8[12582912]{0:T(1024)(128)(4,1)}), s8[4194304]{0:T(1024)(128)(4,1)S(1)}, s32[]{:S(2)}) async-start(s8[12582912]{0:T(1024)(128)(4,1)} %bitcast.10), calls=%async_computation.8 | async-start | bytes 8388608
  31.9 5.8 %collective-permute-start.10 = (bf16[136,512]{1,0:T(8,128)(2,1)S(1)}, bf16[136,512]{1,0:T(8,128)(2,1)S(1)}, u32[]{:S(2)}, u32[]{:S(2)}) collective-permute-start(bf16[136,512]{1,0:T(8,128)(2,1)S(1)} %hidden_part.6.refs_2_), channel_id=1, source_target_pairs={{0,2},{1,3},{2,0},{3,1},{4,6},{5,7},{6,4},{7,5},{8,10},{9,11},{10,... | collective-permute-start | bytes 417800 | tf_op jit(solution)/shard_map/ppermute | solution.py:22
  33.9 3.9 %collective-permute-start.19 = (bf16[136,768]{1,0:T(8,128)(2,1)S(1)}, bf16[136,768]{1,0:T(8,128)(2,1)S(1)}, u32[]{:S(2)}, u32[]{:S(2)}) collective-permute-start(bf16[136,768]{1,0:T(8,128)(2,1)S(1)} %hold.7.refs_0_), channel_id=1, source_target_pairs={{0,1},{1,0},{2,3},{3,2},{4,5},{5,4},{6,7},{7,6},{8,9},{9,8},{10,11... | collective-permute-start | bytes 626696 | tf_op jit(solution)/shard_map/ppermute | solution.py:22
  33.9 3.9 %collective-permute-start.20 = (bf16[136,512]{1,0:T(8,128)(2,1)S(1)}, bf16[136,512]{1,0:T(8,128)(2,1)S(1)}, u32[]{:S(2)}, u32[]{:S(2)}) collective-permute-start(bf16[136,512]{1,0:T(8,128)(2,1)S(1)} %hidden_part.6.refs_2_), channel_id=1, source_target_pairs={{0,1},{1,0},{2,3},{3,2},{4,5},{5,4},{6,7},{7,6},{8,9},{9,8},{10,11... | collective-permute-start | bytes 417800 | tf_op jit(solution)/shard_map/ppermute | solution.py:22
  37.8 11.1 %copy-start.1 = (bf16[64,768]{1,0:T(8,128)(2,1)S(1)}, bf16[64,768]{1,0:T(8,128)(2,1)}, u32[]{:S(2)}) copy-start(bf16[64,768]{1,0:T(8,128)(2,1)} %grad_ref.1) | copy-start | bytes 294916
  37.8 11.1 %copy-start.2 = (s32[64,2]{0,1:T(2,128)S(1)}, s32[64,2]{0,1:T(2,128)}, u32[]{:S(2)}) copy-start(s32[64,2]{0,1:T(2,128)} %param.8) | copy-start | bytes 1540
  37.8 11.1 %copy-start.3 = (f32[64,2]{0,1:T(2,128)S(1)}, f32[64,2]{0,1:T(2,128)}, u32[]{:S(2)}) copy-start(f32[64,2]{0,1:T(2,128)} %param.9) | copy-start | bytes 1540
  37.8 1.4 %collective-permute-start.17 = (bf16[136,512]{1,0:T(8,128)(2,1)S(1)}, bf16[136,512]{1,0:T(8,128)(2,1)S(1)}, u32[]{:S(2)}, u32[]{:S(2)}) collective-permute-start(bf16[136,512]{1,0:T(8,128)(2,1)S(1)} %hold.6.refs_0_), channel_id=1, source_target_pairs={{0,1},{1,0},{2,3},{3,2},{4,5},{5,4},{6,7},{7,6},{8,9},{9,8},{10,11... | collective-permute-start | bytes 417800 | tf_op jit(solution)/shard_map/ppermute | solution.py:22
  39.6 4.8 %collective-permute-start.21 = (bf16[204,128]{1,0:T(8,128)(2,1)S(1)}, bf16[204,128]{1,0:T(8,128)(2,1)S(1)}, u32[]{:S(2)}, u32[]{:S(2)}) collective-permute-start(bf16[204,128]{1,0:T(8,128)(2,1)S(1)} %get-tuple-element.21), channel_id=1, source_target_pairs={{0,4},{4,0},{8,12},{12,8},{1,5},{5,1},{9,13},{13,9},{2,6},{6,2},{1... | collective-permute-start | bytes 156680 | tf_op jit(solution)/shard_map/ppermute | solution.py:22
  39.9 6.8 %collective-permute-start.22 = (bf16[204,128]{1,0:T(8,128)(2,1)S(1)}, bf16[204,128]{1,0:T(8,128)(2,1)S(1)}, u32[]{:S(2)}, u32[]{:S(2)}) collective-permute-start(bf16[204,128]{1,0:T(8,128)(2,1)S(1)} %get-tuple-element.22), channel_id=1, source_target_pairs={{0,8},{4,12},{8,0},{12,4},{1,9},{5,13},{9,1},{13,5},{2,10},{6,14},... | collective-permute-start | bytes 156680 | tf_op jit(solution)/shard_map/ppermute | solution.py:22
  43.0 5.9 %collective-permute-start.23 = (bf16[204,128]{1,0:T(8,128)(2,1)S(1)}, bf16[204,128]{1,0:T(8,128)(2,1)S(1)}, u32[]{:S(2)}, u32[]{:S(2)}) collective-permute-start(bf16[204,128]{1,0:T(8,128)(2,1)S(1)} %get-tuple-element.23), channel_id=1, source_target_pairs={{0,12},{4,8},{8,4},{12,0},{1,13},{5,9},{9,5},{13,1},{2,14},{6,10},... | collective-permute-start | bytes 156680 | tf_op jit(solution)/shard_map/ppermute | solution.py:22
  50.1 3.6 %collective-permute-start.24 = (f32[2,64]{1,0:T(2,128)S(1)}, f32[2,64]{1,0:T(2,128)S(1)}, u32[]{:S(2)}, u32[]{:S(2)}) collective-permute-start(f32[2,64]{1,0:T(2,128)S(1)} %get-tuple-element.25), channel_id=1, source_target_pairs={{0,2},{1,3},{2,0},{3,1},{4,6},{5,7},{6,4},{7,5},{8,10},{9,11},{10,... | collective-permute-start | bytes 1544 | tf_op jit(solution)/shard_map/ppermute | solution.py:22
  53.7 1.1 %collective-permute-start.25 = (f32[2,64]{1,0:T(2,128)S(1)}, f32[2,64]{1,0:T(2,128)S(1)}, u32[]{:S(2)}, u32[]{:S(2)}) collective-permute-start(f32[2,64]{1,0:T(2,128)S(1)} %add.6), channel_id=1, source_target_pairs={{0,1},{1,0},{2,3},{3,2},{4,5},{5,4},{6,7},{7,6},{8,9},{9,8},{10,11... | collective-permute-start | bytes 1544 | tf_op jit(solution)/shard_map/ppermute | solution.py:22

commit v8 on v7

--- a/solution.py
+++ b/solution.py
@@ -200,7 +200,7 @@
     if last:
         for k, out in enumerate(outs):
             block = total[k * MOST:(k + 1) * MOST]
-            out[...] = (block if k == 0 else fold(block)).astype(BF)
+            out[...] = fold(block).astype(BF)
     else:
         outs[0][...] = total
 
@@ -210,7 +210,7 @@
     width = weight.shape[2]
     has_sum = running is not None
     if last:
-        out_shape = [jax.ShapeDtypeStruct((MOST, width), BF)] + [folded(width)] * (EXPERTS - 1)
+        out_shape = [folded(width)] * EXPERTS
     else:
         out_shape = [jax.ShapeDtypeStruct((rows, width), F32)]
     return pl.pallas_call(
@@ -226,50 +226,82 @@
     )(t, *pieces, weight, *([running] if has_sum else []))
 
 
-def combine_kernel(me_ref, ids_ref, probs_ref, grad_ref, *refs):
-    back_refs = refs[:EXPERTS]
-    mixed_ref, gate_grad_ref = refs[EXPERTS:]
-    rows = grad_ref.shape[0]
+def prepare_kernel(me_ref, ids_ref, probs_ref, grad_ref, *refs):
+    hits_ref, routes_ref = refs[:2]
+    picks_refs, grads_refs = refs[2:2 + EXPERTS], refs[2 + EXPERTS:]
+    rows, width = grad_ref.shape
     hits, picks = routing(ids_ref[...], me_ref[0])
-    grad = grad_ref[...].astype(F32)
-    column = lax.broadcasted_iota(jnp.int32, (rows, 128), 1)
-    dots = jnp.zeros((rows, 128), F32)
+    for k in range(EXPERTS):
+        hits_ref[k] = hits[k]
+        picks_refs[k][...] = jnp.concatenate([picks[k]] * (width // 128), axis=0)
+        grads_refs[k][...] = fold(jnp.dot(picks[k].astype(BF), grad_ref[...], preferred_element_type=F32))
     routes = jnp.concatenate(
         [jnp.sum(h * probs_ref[...], axis=0, keepdims=True) for h in hits]
         + [jnp.zeros((128 - EXPERTS, rows), F32)],
         axis=0,
     )
-    routes = jnp.concatenate([routes, jnp.zeros((128, 128 - rows), F32)], axis=1).T
+    routes_ref[...] = jnp.concatenate([routes, jnp.zeros((128, 128 - rows), F32)], axis=1).T[:rows]
+
+
+def prepare(me, ids_t, probs_t, out_grad):
+    rows, width = out_grad.shape
+    tall = width // 128 * MOST
+    shapes = [(EXPERTS,) + ids_t.shape, (rows, 128)] + [(tall, rows)] * EXPERTS + [(tall, 128)] * EXPERTS
+    out = pl.pallas_call(
+        prepare_kernel,
+        out_shape=[jax.ShapeDtypeStruct(shape, F32) for shape in shapes],
+        in_specs=[SMEM] + [VMEM] * 3,
+        out_specs=[VMEM] * len(shapes),
+        name="prepare",
+        **SMALL,
+    )(me, ids_t, probs_t, out_grad)
+    return out[0], out[1], out[2:2 + EXPERTS], out[2 + EXPERTS:]
+
+
+def dots_kernel(hits_ref, *refs):
+    picks_refs, grads_refs, back_refs = (refs[n * EXPERTS:(n + 1) * EXPERTS] for n in range(3))
+    total = None
+    for k in range(EXPERTS):
+        slots = jnp.sum(grads_refs[k][...] * back_refs[k][...].astype(F32), axis=1, keepdims=True)
+        term = hits_ref[k] * jnp.sum(picks_refs[k][...] * slots, axis=0, keepdims=True)
+        total = term if total is None else total + term
+    refs[-1][...] = total
+
+
+def take_dots(hits, picks, grads, back):
+    return pl.pallas_call(
+        dots_kernel,
+        out_shape=jax.ShapeDtypeStruct(hits.shape[1:], F32),
+        in_specs=[VMEM] * (1 + 3 * EXPERTS),
+        out_specs=VMEM,
+        name="dots",
+        **SMALL,
+    )(hits, *picks, *grads, *back)
+
+
+def mix_kernel(routes_ref, *refs):
+    picks_refs, back_refs = refs[:EXPERTS], refs[EXPERTS:2 * EXPERTS]
     mixed = None
     for k in range(EXPERTS):
-        block = back_refs[k][...] if k == 0 else unfold(back_refs[k][...].astype(F32)).astype(BF)
         out = lax.dot_general(
-            picks[k].astype(BF), block, (((0,), (0,)), ((), ())), preferred_element_type=F32
+            picks_refs[k][:MOST].astype(BF), unfold(back_refs[k][...].astype(F32)).astype(BF),
+            (((0,), (0,)), ((), ())), preferred_element_type=F32,
         )
-        term = routes[:rows, k:k + 1] * out
+        term = routes_ref[:, k:k + 1] * out
         mixed = term if mixed is None else mixed + term
-        dots = jnp.where(column == k, jnp.sum(grad * out, axis=1, keepdims=True), dots)
-    mixed_ref[...] = mixed.astype(BF)
-    turned = jnp.concatenate([dots, jnp.zeros((128 - rows, 128), F32)], axis=0).T
-    gate_grad = None
-    for k in range(EXPERTS):
-        term = hits[k] * turned[k:k + 1, :rows]
-        gate_grad = term if gate_grad is None else gate_grad + term
-    gate_grad_ref[...] = gate_grad
-
-
-def combine(me, ids_t, probs_t, out_grad, back):
-    return pl.pallas_call(
-        combine_kernel,
-        out_shape=[
-            jax.ShapeDtypeStruct(out_grad.shape, BF),
-            jax.ShapeDtypeStruct(probs_t.shape, F32),
-        ],
-        in_specs=[SMEM] + [VMEM] * (3 + EXPERTS),
-        out_specs=[VMEM] * 2,
-        name="combine",
-        **SMALL,
-    )(me, ids_t, probs_t, out_grad, *back)
+    refs[-1][...] = mixed.astype(BF)
+
+
+def mix(routes, picks, back, width):
+    return pl.pallas_call(
+        mix_kernel,
+        out_shape=jax.ShapeDtypeStruct((routes.shape[0], width), BF),
+        in_specs=[VMEM] * (1 + 2 * EXPERTS),
+        out_specs=VMEM,
+        compiler_params=pltpu.CompilerParams(vmem_limit_bytes=SMALL_LIMIT),
+        cost_estimate=pl.CostEstimate(flops=1_000_000_000, bytes_accessed=1000, transcendentals=0),
+        name="mix",
+    )(routes, *picks, *back)
 
 
 Z_ORDER = (1, 2, 3)
@@ -292,6 +324,8 @@
     sides = [swap(v, "tensor", 1) for v in (near, far, near_across)]
     far_across = hold(far_across, sides)
     xs = [near, far, sides[0], sides[1], near_across, far_across, sides[2], swap(far_across, "tensor", 1)]
+
+    hits, routes, picks, grads = prepare(me, ids_t, probs_t, out_grad)
 
     pieces = []
     for i, (start, size) in enumerate(zip(starts, CHUNKS)):
@@ -314,8 +348,9 @@
         )
         sums.append(result[0])
     back = [result[0]] + [swap(result[k], "expert", k) for k in (1, 2, 3)]
-    mixed, gate_grad = combine(me, ids_t, probs_t, out_grad, back)
-    gate_grad = gate_grad + swap(gate_grad, "tensor", 2)
+    gate_grad = take_dots(hits, picks, grads, back)
+    mixed = mix(routes, picks, back, tokens.shape[1])
+    gate_grad = gate_grad + hold(swap(gate_grad, "tensor", 2), [mixed])
     gate_grad = gate_grad + swap(gate_grad, "tensor", 1)
     return mixed, gate_grad.T
 

time: 55.5 us -> 54.7 us (0.986)
  waiting for transfers between devices: 22.6 us -> 20.6 us
  local copies, waits for them, and re-layouts: 1.24 us -> 2.14 us
    ppermute x26, waiting for transfers between devices: 22.6 us -> 20.6 us  [swap(): return lax.ppermute(value, axis, [(i, i ^ bit) for i in range(size)])]
    unnamed x26 -> x28, local copies, waits for them, and re-layouts: 1.24 us -> 2.14 us
    pallas_call x1 -> x3, Pallas kernels: 1.19 us -> 1.48 us  [the longest x1 0.93 us: mix(): pl.pallas_call(mix_kernel, out_shape=jax.ShapeDtypeStruct((routes.shape[0...]
  transfers between devices with their start and end apart: 26 -> 26, of which waited for: 16 -> 15; matrix products, arithmetic and copies ran while one was open for 0% -> 0% of each run, Pallas kernels for 11% -> 14%
where the time goes in v8:
time: 54.7 us; the launch traced here: 54.6 us
  waiting for transfers between devices  20.6 us (38%)
  starting transfers between devices  20.3 us (37%)
  Pallas kernels  10 us (18%)
  local copies, waits for them, and re-layouts  2.14 us (4%)
  between operations  0.91 us (2%)
  other arithmetic  0.57 us (1%)
    ppermute x26, waiting for transfers between devices, swap(): return lax.ppermute(value, axis, [(i, i ^ bit) for i in range(size)])  20.6 us
    ppermute x26, starting transfers between devices, swap(): return lax.ppermute(value, axis, [(i, i ^ bit) for i in range(size)])  20.3 us
    pallas_call x4, Pallas kernels, hidden_part(): pl.pallas_call(functools.partial(hidden_kernel, joined, parts, start), ou...  4.59 us
    pallas_call x4, Pallas kernels, down_part(): pl.pallas_call(functools.partial(down_kernel, len(pieces), where, slab, h...  2.56 us
    unnamed x28, local copies, waits for them, and re-layouts  2.14 us
    pallas_call x1, Pallas kernels, select_rows(): pl.pallas_call(select_kernel, out_shape=[jax.ShapeDtypeStruct((MOST, widt...  1.3 us
  transfers between devices with their start and end apart: 26, of which 15 were waited for; matrix products, arithmetic and copies ran while one was open for 0% of the time, Pallas kernels for 14%

profile of v8, /device:TPU:0, one launch (start us, length us, event | category | flops | bytes accessed | tf_op | source)
XLA Modules:
  0.0 54.6 jit_solution(15505865382476113089)
XLA Ops:
  0.6 0.0 slice-start
  0.6 0.0 slice-start.1
  0.7 1.3 %select_rows.1 = (bf16[34,768]{1,0:T(8,128)(2,1)S(1)}, bf16[204,128]{1,0:T(8,128)(2,1)S(1)}, bf16[204,128]{1,0:T(8,128)(2,1)S(1)}, bf16[204,128]{1,0:T(8,128)(2,1)S(1)}) custom-call(s32[1]{0:T(128)} %bitcast.me_ref, s32[1]{0:T(128)} %bitcast.3.t_ref, s32[2,64]{1,0:T(2,128)} %bitcast.12, bf16[64,768]{1,0:T(8,128)(2,1)} %tokens_hbm.1), custom_call_target="tpu_custom_call" | custom-call | flops 8000000000 | bytes 1000 | tf_op jit(solution)/shard_map/select_rows/pallas_call | solution.py:82
  2.0 3.1 %collective-permute-start = (bf16[204,128]{1,0:T(8,128)(2,1)S(1)}, bf16[204,128]{1,0:T(8,128)(2,1)S(1)}, u32[]{:S(2)}, u32[]{:S(2)}) collective-permute-start(bf16[204,128]{1,0:T(8,128)(2,1)S(1)} %get-tuple-element.28), channel_id=1, source_target_pairs={{0,4},{4,0},{8,12},{12,8},{1,5},{5,1},{9,13},{13,9},{2,6},{6,2},{1... | collective-permute-start | bytes 156680 | tf_op jit(solution)/shard_map/ppermute | solution.py:22
  5.1 2.6 %collective-permute-start.1 = (bf16[204,128]{1,0:T(8,128)(2,1)S(1)}, bf16[204,128]{1,0:T(8,128)(2,1)S(1)}, u32[]{:S(2)}, u32[]{:S(2)}) collective-permute-start(bf16[204,128]{1,0:T(8,128)(2,1)S(1)} %get-tuple-element.29), channel_id=1, source_target_pairs={{0,8},{4,12},{8,0},{12,4},{1,9},{5,13},{9,1},{13,5},{2,10},{6,14},... | collective-permute-start | bytes 156680 | tf_op jit(solution)/shard_map/ppermute | solution.py:22
  7.7 0.0 collective-permute-start.2
  7.7 0.0 collective-permute-done.next_ref
  7.7 1.8 %collective-permute-start.3 = (bf16[64,768]{1,0:T(8,128)(2,1)S(1)}, bf16[64,768]{1,0:T(8,128)(2,1)S(1)}, u32[]{:S(2)}, u32[]{:S(2)}) collective-permute-start(bf16[64,768]{1,0:T(8,128)(2,1)S(1)} %pack_near.1.refs_0_), channel_id=1, source_target_pairs={{0,2},{1,3},{2,0},{3,1},{4,6},{5,7},{6,4},{7,5},{8,10},{9,11},{10,... | collective-permute-start | bytes 294920 | tf_op jit(solution)/shard_map/ppermute | solution.py:22
  9.5 1.7 %collective-permute-done.1.third_ref = bf16[204,128]{1,0:T(8,128)(2,1)S(1)} collective-permute-done((bf16[204,128]{1,0:T(8,128)(2,1)S(1)}, bf16[204,128]{1,0:T(8,128)(2,1)S(1)}, u32[]{:S(2)}, u32[]{:S(2)}) %collective-permute-start.1) | collective-permute-done | bytes 52256 | tf_op jit(solution)/shard_map/ppermute | solution.py:22
  11.1 2.5 %collective-permute-done.2.fourth_ref = bf16[204,128]{1,0:T(8,128)(2,1)S(1)} collective-permute-done((bf16[204,128]{1,0:T(8,128)(2,1)S(1)}, bf16[204,128]{1,0:T(8,128)(2,1)S(1)}, u32[]{:S(2)}, u32[]{:S(2)}) %collective-permute-start.2) | collective-permute-done | bytes 52256 | tf_op jit(solution)/shard_map/ppermute | solution.py:22
  13.7 1.6 %collective-permute-start.6 = (bf16[72,768]{1,0:T(8,128)(2,1)S(1)}, bf16[72,768]{1,0:T(8,128)(2,1)S(1)}, u32[]{:S(2)}, u32[]{:S(2)}) collective-permute-start(bf16[72,768]{1,0:T(8,128)(2,1)S(1)} %hold.5.refs_1_), channel_id=1, source_target_pairs={{0,2},{1,3},{2,0},{3,1},{4,6},{5,7},{6,4},{7,5},{8,10},{9,11},{10,... | collective-permute-start | bytes 331784 | tf_op jit(solution)/shard_map/ppermute | solution.py:22
  15.2 0.0 collective-permute-start.5
  15.2 0.5 collective-permute-start.4
  15.7 0.9 %collective-permute-done.4.refs_1_.refs_2_ = bf16[64,768]{1,0:T(8,128)(2,1)S(1)} collective-permute-done((bf16[64,768]{1,0:T(8,128)(2,1)S(1)}, bf16[64,768]{1,0:T(8,128)(2,1)S(1)}, u32[]{:S(2)}, u32[]{:S(2)}) %collective-permute-start.4) | collective-permute-done | bytes 98336 | tf_op jit(solution)/shard_map/ppermute | solution.py:22
  16.7 0.4 collective-permute-done.7.refs_3_.refs_6_
  17.0 1.4 %collective-permute-done.6.refs_0_ = bf16[72,768]{1,0:T(8,128)(2,1)S(1)} collective-permute-done((bf16[72,768]{1,0:T(8,128)(2,1)S(1)}, bf16[72,768]{1,0:T(8,128)(2,1)S(1)}, u32[]{:S(2)}, u32[]{:S(2)}) %collective-permute-start.6) | collective-permute-done | bytes 110624 | tf_op jit(solution)/shard_map/ppermute | solution.py:22
  18.5 0.0 collective-permute-done.5.refs_2_.refs_3_
  18.5 0.0 collective-permute-start.8
  18.5 1.3 %collective-permute-done.8.refs_7_ = bf16[72,768]{1,0:T(8,128)(2,1)S(1)} collective-permute-done((bf16[72,768]{1,0:T(8,128)(2,1)S(1)}, bf16[72,768]{1,0:T(8,128)(2,1)S(1)}, u32[]{:S(2)}, u32[]{:S(2)}) %collective-permute-start.8) | collective-permute-done | bytes 110624 | tf_op jit(solution)/shard_map/ppermute | solution.py:22
  19.8 0.7 %hidden_part.4 = (bf16[136,256]{1,0:T(8,128)(2,1)S(1)}, bf16[4,136,768]{2,1,0:T(8,128)(2,1)S(1)}) custom-call(s32[1]{0:T(128)} %bitcast.3.t_ref, bf16[64,768]{1,0:T(8,128)(2,1)S(1)} %pack_near.1.refs_0_, bf16[72,768]{1,0:T(8,128)(2,1)S(1)} %hold.5.refs_1_, bf16[64,768]{1,0:T(8,128)(2,1)S(1)} %collective-permute-done.4.refs_1_.refs_2_, ...), custom_call_target="tpu_custom_call" | custom-call | flops 1000 | bytes 1000 | tf_op jit(solution)/shard_map/hidden_part/pallas_call | solution.py:178
  20.5 1.6 %collective-permute-start.12 = (bf16[136,256]{1,0:T(8,128)(2,1)S(1)}, bf16[136,256]{1,0:T(8,128)(2,1)S(1)}, u32[]{:S(2)}, u32[]{:S(2)}) collective-permute-start(bf16[136,256]{1,0:T(8,128)(2,1)S(1)} %get-tuple-element.32.refs_0_), channel_id=1, source_target_pairs={{0,2},{1,3},{2,0},{3,1},{4,6},{5,7},{6,4},{7,5},{8,10},{9,11},{10,... | collective-permute-start | bytes 208904 | tf_op jit(solution)/shard_map/ppermute | solution.py:22
  22.1 1.1 %hidden_part.5.refs_4_ = bf16[136,512]{1,0:T(8,128)(2,1)S(1)} custom-call(s32[1]{0:T(128)} %bitcast.3.t_ref, bf16[4,136,768]{2,1,0:T(8,128)(2,1)S(1)} %get-tuple-element.31.refs_0_, bf16[1,3072,2048]{2,1,0:T(8,128)(2,1)S(1)} %bitcast.7, bf16[1,3072,2048]{2,1,0:T(8,128)(2,1)S(1)} %copy-done), custom_call_target="tpu_custom_call" | custom-call | flops 1000 | bytes 1000 | tf_op jit(solution)/shard_map/hidden_part/pallas_call | solution.py:178
  23.2 0.6 %collective-permute-start.9 = (bf16[136,512]{1,0:T(8,128)(2,1)S(1)}, bf16[136,512]{1,0:T(8,128)(2,1)S(1)}, u32[]{:S(2)}, u32[]{:S(2)}) collective-permute-start(bf16[136,512]{1,0:T(8,128)(2,1)S(1)} %hidden_part.5.refs_4_), channel_id=1, source_target_pairs={{0,2},{1,3},{2,0},{3,1},{4,6},{5,7},{6,4},{7,5},{8,10},{9,11},{10,... | collective-permute-start | bytes 417800 | tf_op jit(solution)/shard_map/ppermute | solution.py:22
  23.8 1.1 %collective-permute-done.12.refs_3_.refs_2_ = bf16[136,256]{1,0:T(8,128)(2,1)S(1)} collective-permute-done((bf16[136,256]{1,0:T(8,128)(2,1)S(1)}, bf16[136,256]{1,0:T(8,128)(2,1)S(1)}, u32[]{:S(2)}, u32[]{:S(2)}) %collective-permute-start.12) | collective-permute-done | bytes 69664 | tf_op jit(solution)/shard_map/ppermute | solution.py:22
  24.9 1.6 %hidden_part.7.refs_2_ = bf16[136,768]{1,0:T(8,128)(2,1)S(1)} custom-call(s32[1]{0:T(128)} %bitcast.3.t_ref, bf16[4,136,768]{2,1,0:T(8,128)(2,1)S(1)} %get-tuple-element.31.refs_0_, bf16[1,3072,2048]{2,1,0:T(8,128)(2,1)S(1)} %bitcast.7, bf16[1,3072,2048]{2,1,0:T(8,128)(2,1)S(1)} %copy-done, bf16[136,256]{1,0:T(8,128)(2,1)S(1)} %collective-permute-done.12.refs_3_.refs_2_), custom_call_target="tpu_custom_call" | custom-call | flops 1000 | bytes 1000 | tf_op jit(solution)/shard_map/hidden_part/pallas_call | solution.py:178
  26.5 0.0 slice-start.5
  26.5 1.7 %collective-permute-start.18 = (bf16[136,768]{1,0:T(8,128)(2,1)S(1)}, bf16[136,768]{1,0:T(8,128)(2,1)S(1)}, u32[]{:S(2)}, u32[]{:S(2)}) collective-permute-start(bf16[136,768]{1,0:T(8,128)(2,1)S(1)} %hidden_part.7.refs_2_), channel_id=1, source_target_pairs={{0,2},{1,3},{2,0},{3,1},{4,6},{5,7},{6,4},{7,5},{8,10},{9,11},{10,... | collective-permute-start | bytes 626696 | tf_op jit(solution)/shard_map/ppermute | solution.py:22
  28.3 0.0 collective-permute-start.14
  28.3 0.5 collective-permute-start.16
  28.8 0.0 collective-permute-start.13
  28.8 0.7 %collective-permute-done.14.refs_1_ = bf16[136,256]{1,0:T(8,128)(2,1)S(1)} collective-permute-done((bf16[136,256]{1,0:T(8,128)(2,1)S(1)}, bf16[136,256]{1,0:T(8,128)(2,1)S(1)}, u32[]{:S(2)}, u32[]{:S(2)}) %collective-permute-start.14) | collective-permute-done | bytes 69664 | tf_op jit(solution)/shard_map/ppermute | solution.py:22
  29.5 0.2 collective-permute-start.15
  29.7 0.0 collective-permute-done.9.refs_3_.refs_0_
  29.7 0.4 collective-permute-start.11
  30.0 1.2 %hidden_part.6.refs_2_ = bf16[136,512]{1,0:T(8,128)(2,1)S(1)} custom-call(s32[1]{0:T(128)} %bitcast.3.t_ref, bf16[4,136,768]{2,1,0:T(8,128)(2,1)S(1)} %get-tuple-element.31.refs_0_, bf16[1,3072,2048]{2,1,0:T(8,128)(2,1)S(1)} %bitcast.7, bf16[1,3072,2048]{2,1,0:T(8,128)(2,1)S(1)} %copy-done, bf16[136,512]{1,0:T(8,128)(2,1)S(1)} %collective-permute-done.9.refs_3_.refs_0_), custom_call_target="tpu_custom_call" | custom-call | flops 1000 | bytes 1000 | tf_op jit(solution)/shard_map/hidden_part/pallas_call | solution.py:178
  31.2 0.0 slice-start.8
  31.2 0.0 collective-permute-done.15.refs_3_
  31.2 0.4 collective-permute-start.10
  31.7 0.0 collective-permute-done.16.refs_5_
  31.7 0.6 %down_part.4.refs_5_.refs_1_ = f32[136,768]{1,0:T(8,128)S(1)} custom-call(s32[1]{0:T(128)} %bitcast.3.t_ref, bf16[136,256]{1,0:T(8,128)(2,1)S(1)} %get-tuple-element.32.refs_0_, bf16[136,256]{1,0:T(8,128)(2,1)S(1)} %collective-permute-done.14.refs_1_, bf16[136,256]{1,0:T(8,128)(2,1)S(1)} %collective-permute-done.12.refs_3_.refs_2_, ...), custom_call_target="tpu_custom_call" | custom-call | flops 427819008 | bytes 1000 | tf_op jit(solution)/shard_map/down_part/pallas_call | solution.py:216
  32.3 0.8 %collective-permute-done.18.refs_0_ = bf16[136,768]{1,0:T(8,128)(2,1)S(1)} collective-permute-done((bf16[136,768]{1,0:T(8,128)(2,1)S(1)}, bf16[136,768]{1,0:T(8,128)(2,1)S(1)}, u32[]{:S(2)}, u32[]{:S(2)}) %collective-permute-start.18) | collective-permute-done | bytes 208928 | tf_op jit(solution)/shard_map/ppermute | solution.py:22
  33.2 0.0 collective-permute-start.19
  33.2 0.5 collective-permute-start.20
  33.7 0.0 collective-permute-done.13.refs_3_
  33.7 1.2 %slice-done.8 = s8[4194304]{0:T(1024)(128)(4,1)S(1)} async-done(((s8[12582912]{0:T(1024)(128)(4,1)}), s8[4194304]{0:T(1024)(128)(4,1)S(1)}, s32[]{:S(2)}) %slice-start.8) | async-done | bytes 4194328
  34.9 0.7 %down_part.5.refs_1_.refs_5_ = f32[136,768]{1,0:T(8,128)S(1)} custom-call(s32[1]{0:T(128)} %bitcast.3.t_ref, bf16[136,512]{1,0:T(8,128)(2,1)S(1)} %collective-permute-done.9.refs_3_.refs_0_, bf16[136,512]{1,0:T(8,128)(2,1)S(1)} %collective-permute-done.11.refs_1_, bf16[136,768]{1,0:T(8,128)(2,1)S(1)} %hidden_part.7.refs_2_, ...), custom_call_target="tpu_custom_call" | custom-call | flops 534773760 | bytes 1000 | tf_op jit(solution)/shard_map/down_part/pallas_call | solution.py:216
  35.7 1.4 %collective-permute-done.10.refs_0_ = bf16[136,512]{1,0:T(8,128)(2,1)S(1)} collective-permute-done((bf16[136,512]{1,0:T(8,128)(2,1)S(1)}, bf16[136,512]{1,0:T(8,128)(2,1)S(1)}, u32[]{:S(2)}, u32[]{:S(2)}) %collective-permute-start.10) | collective-permute-done | bytes 139296 | tf_op jit(solution)/shard_map/ppermute | solution.py:22
  37.0 0.1 collective-permute-start.17
  37.1 0.8 %down_part.6.refs_3_ = f32[136,768]{1,0:T(8,128)S(1)} custom-call(s32[1]{0:T(128)} %bitcast.3.t_ref, bf16[136,768]{1,0:T(8,128)(2,1)S(1)} %hold.8.refs_0_, bf16[136,768]{1,0:T(8,128)(2,1)S(1)} %collective-permute-done.19.refs_1_, bf16[136,512]{1,0:T(8,128)(2,1)S(1)} %hidden_part.6.refs_2_, bf16[136,512]{1,0:T(8,128)(2,1)S(1)} %collective-permute-done.20.refs_3_, ...), custom_call_target="tpu_custom_call" | custom-call | flops 534773760 | bytes 1000 | tf_op jit(solution)/shard_map/down_part/pallas_call | solution.py:216
  37.9 0.6 %collective-permute-done.17.refs_1_ = bf16[136,512]{1,0:T(8,128)(2,1)S(1)} collective-permute-done((bf16[136,512]{1,0:T(8,128)(2,1)S(1)}, bf16[136,512]{1,0:T(8,128)(2,1)S(1)}, u32[]{:S(2)}, u32[]{:S(2)}) %collective-permute-start.17) | collective-permute-done | bytes 139296 | tf_op jit(solution)/shard_map/ppermute | solution.py:22
  38.5 0.4 down_part.7
  38.9 0.2 collective-permute-start.21
  39.1 3.1 %collective-permute-start.22 = (bf16[204,128]{1,0:T(8,128)(2,1)S(1)}, bf16[204,128]{1,0:T(8,128)(2,1)S(1)}, u32[]{:S(2)}, u32[]{:S(2)}) collective-permute-start(bf16[204,128]{1,0:T(8,128)(2,1)S(1)} %get-tuple-element.35), channel_id=1, source_target_pairs={{0,8},{4,12},{8,0},{12,4},{1,9},{5,13},{9,1},{13,5},{2,10},{6,14},... | collective-permute-start | bytes 156680 | tf_op jit(solution)/shard_map/ppermute | solution.py:22
  42.2 1.1 %collective-permute-start.23 = (bf16[204,128]{1,0:T(8,128)(2,1)S(1)}, bf16[204,128]{1,0:T(8,128)(2,1)S(1)}, u32[]{:S(2)}, u32[]{:S(2)}) collective-permute-start(bf16[204,128]{1,0:T(8,128)(2,1)S(1)} %get-tuple-element.36), channel_id=1, source_target_pairs={{0,12},{4,8},{8,4},{12,0},{1,13},{5,9},{9,5},{13,1},{2,14},{6,10},... | collective-permute-start | bytes 156680 | tf_op jit(solution)/shard_map/ppermute | solution.py:22
  43.3 0.3 prepare.1
  43.7 2.2 %collective-permute-done.22.refs_6_.refs_10_ = bf16[204,128]{1,0:T(8,128)(2,1)S(1)} collective-permute-done((bf16[204,128]{1,0:T(8,128)(2,1)S(1)}, bf16[204,128]{1,0:T(8,128)(2,1)S(1)}, u32[]{:S(2)}, u32[]{:S(2)}) %collective-permute-start.22) | collective-permute-done | bytes 52256 | tf_op jit(solution)/shard_map/ppermute | solution.py:22
  45.9 2.2 %collective-permute-done.23.refs_7_.refs_11_ = bf16[204,128]{1,0:T(8,128)(2,1)S(1)} collective-permute-done((bf16[204,128]{1,0:T(8,128)(2,1)S(1)}, bf16[204,128]{1,0:T(8,128)(2,1)S(1)}, u32[]{:S(2)}, u32[]{:S(2)}) %collective-permute-start.23) | collective-permute-done | bytes 52256 | tf_op jit(solution)/shard_map/ppermute | solution.py:22
  48.1 0.2 dots.1
  48.4 0.5 collective-permute-start.24
  48.8 0.9 %mix.1.refs_1_ = bf16[64,768]{1,0:T(8,128)(2,1)} custom-call(f32[64,128]{1,0:T(8,128)S(1)} %get-tuple-element.22.routes_ref, f32[204,64]{1,0:T(8,128)S(1)} %get-tuple-element.23.refs_0_, f32[204,64]{1,0:T(8,128)S(1)} %get-tuple-element.24.refs_1_, f32[204,64]{1,0:T(8,128)S(1)} %get-tuple-element.25.refs_2_, f32[204,64]{1,0:T(8,128)S(1)} %get-tuple-element.26.refs_3_, ...), custom_call_target="tpu_custom_call" | custom-call | flops 1000000000 | bytes 1000 | tf_op jit(solution)/shard_map/mix/pallas_call | solution.py:296
  49.8 2.2 %collective-permute-done.24.refs_0_ = f32[2,64]{1,0:T(2,128)S(1)} collective-permute-done((f32[2,64]{1,0:T(2,128)S(1)}, f32[2,64]{1,0:T(2,128)S(1)}, u32[]{:S(2)}, u32[]{:S(2)}) %collective-permute-start.24) | collective-permute-done | bytes 544 | tf_op jit(solution)/shard_map/ppermute | solution.py:22
  52.0 0.9 %copy-done.2 = bf16[64,768]{1,0:T(8,128)(2,1)S(1)} copy-done((bf16[64,768]{1,0:T(8,128)(2,1)S(1)}, bf16[64,768]{1,0:T(8,128)(2,1)}, u32[]{:S(2)}) %copy-start.2) | copy-done | bytes 98328
  52.9 1.1 %collective-permute-done.25 = f32[2,64]{1,0:T(2,128)S(1)} collective-permute-done((f32[2,64]{1,0:T(2,128)S(1)}, f32[2,64]{1,0:T(2,128)S(1)}, u32[]{:S(2)}, u32[]{:S(2)}) %collective-permute-start.25) | collective-permute-done | bytes 544 | tf_op jit(solution)/shard_map/ppermute | solution.py:22
  54.0 0.6 %add_bitcast_fusion = f32[64,2]{0,1:T(2,128)} fusion(f32[2,64]{1,0:T(2,128)S(1)} %add.6, f32[2,64]{1,0:T(2,128)S(1)} %collective-permute-done.25), kind=kLoop, calls=%fused_computation | loop fusion | flops 128 | bytes 1536 | tf_op jit(solution)/shard_map/transpose | solution.py:355
  (40 shorter events, 0.1 us)
Async XLA Ops:
  0.6 19.2 %slice-start = ((s8[12582912]{0:T(1024)(128)(4,1)}), s8[4194304]{0:T(1024)(128)(4,1)S(1)}, s32[]{:S(2)}) async-start(s8[12582912]{0:T(1024)(128)(4,1)} %bitcast.6), calls=%async_computation | async-start | bytes 8388608
  0.6 19.2 %slice-start.1 = ((s8[12582912]{0:T(1024)(128)(4,1)}), s8[4194304]{0:T(1024)(128)(4,1)S(1)}, s32[]{:S(2)}) async-start(s8[12582912]{0:T(1024)(128)(4,1)} %bitcast.6), calls=%async_computation.1 | async-start | bytes 8388608
  0.7 19.2 %slice-start.2 = ((s8[12582912]{0:T(1024)(128)(4,1)}), s8[4194304]{0:T(1024)(128)(4,1)S(1)}, s32[]{:S(2)}) async-start(s8[12582912]{0:T(1024)(128)(4,1)} %bitcast.6), calls=%async_computation.2 | async-start | bytes 8388608
  0.7 19.2 %copy-start = (bf16[1,3072,2048]{2,1,0:T(8,128)(2,1)S(1)}, bf16[1,3072,2048]{2,1,0:T(8,128)(2,1)}, u32[]{:S(2)}) copy-start(bf16[1,3072,2048]{2,1,0:T(8,128)(2,1)} %refs_2_.6) | copy-start | bytes 37748740
  2.0 5.7 %collective-permute-start = (bf16[204,128]{1,0:T(8,128)(2,1)S(1)}, bf16[204,128]{1,0:T(8,128)(2,1)S(1)}, u32[]{:S(2)}, u32[]{:S(2)}) collective-permute-start(bf16[204,128]{1,0:T(8,128)(2,1)S(1)} %get-tuple-element.28), channel_id=1, source_target_pairs={{0,4},{4,0},{8,12},{12,8},{1,5},{5,1},{9,13},{13,9},{2,6},{6,2},{1... | collective-permute-start | bytes 156680 | tf_op jit(solution)/shard_map/ppermute | solution.py:22
  5.1 6.1 %collective-permute-start.1 = (bf16[204,128]{1,0:T(8,128)(2,1)S(1)}, bf16[204,128]{1,0:T(8,128)(2,1)S(1)}, u32[]{:S(2)}, u32[]{:S(2)}) collective-permute-start(bf16[204,128]{1,0:T(8,128)(2,1)S(1)} %get-tuple-element.29), channel_id=1, source_target_pairs={{0,8},{4,12},{8,0},{12,4},{1,9},{5,13},{9,1},{13,5},{2,10},{6,14},... | collective-permute-start | bytes 156680 | tf_op jit(solution)/shard_map/ppermute | solution.py:22
  7.7 5.9 %collective-permute-start.2 = (bf16[204,128]{1,0:T(8,128)(2,1)S(1)}, bf16[204,128]{1,0:T(8,128)(2,1)S(1)}, u32[]{:S(2)}, u32[]{:S(2)}) collective-permute-start(bf16[204,128]{1,0:T(8,128)(2,1)S(1)} %get-tuple-element.30), channel_id=1, source_target_pairs={{0,12},{4,8},{8,4},{12,0},{1,13},{5,9},{9,5},{13,1},{2,14},{6,10},... | collective-permute-start | bytes 156680 | tf_op jit(solution)/shard_map/ppermute | solution.py:22
  7.7 5.9 %collective-permute-start.3 = (bf16[64,768]{1,0:T(8,128)(2,1)S(1)}, bf16[64,768]{1,0:T(8,128)(2,1)S(1)}, u32[]{:S(2)}, u32[]{:S(2)}) collective-permute-start(bf16[64,768]{1,0:T(8,128)(2,1)S(1)} %pack_near.1.refs_0_), channel_id=1, source_target_pairs={{0,2},{1,3},{2,0},{3,1},{4,6},{5,7},{6,4},{7,5},{8,10},{9,11},{10,... | collective-permute-start | bytes 294920 | tf_op jit(solution)/shard_map/ppermute | solution.py:22
  13.7 4.8 %collective-permute-start.6 = (bf16[72,768]{1,0:T(8,128)(2,1)S(1)}, bf16[72,768]{1,0:T(8,128)(2,1)S(1)}, u32[]{:S(2)}, u32[]{:S(2)}) collective-permute-start(bf16[72,768]{1,0:T(8,128)(2,1)S(1)} %hold.5.refs_1_), channel_id=1, source_target_pairs={{0,2},{1,3},{2,0},{3,1},{4,6},{5,7},{6,4},{7,5},{8,10},{9,11},{10,... | collective-permute-start | bytes 331784 | tf_op jit(solution)/shard_map/ppermute | solution.py:22
  15.2 3.3 %collective-permute-start.5 = (bf16[72,768]{1,0:T(8,128)(2,1)S(1)}, bf16[72,768]{1,0:T(8,128)(2,1)S(1)}, u32[]{:S(2)}, u32[]{:S(2)}) collective-permute-start(bf16[72,768]{1,0:T(8,128)(2,1)S(1)} %hold.5.refs_1_), channel_id=1, source_target_pairs={{0,1},{1,0},{2,3},{3,2},{4,5},{5,4},{6,7},{7,6},{8,9},{9,8},{10,11... | collective-permute-start | bytes 331784 | tf_op jit(solution)/shard_map/ppermute | solution.py:22
  15.2 1.5 %collective-permute-start.4 = (bf16[64,768]{1,0:T(8,128)(2,1)S(1)}, bf16[64,768]{1,0:T(8,128)(2,1)S(1)}, u32[]{:S(2)}, u32[]{:S(2)}) collective-permute-start(bf16[64,768]{1,0:T(8,128)(2,1)S(1)} %pack_near.1.refs_0_), channel_id=1, source_target_pairs={{0,1},{1,0},{2,3},{3,2},{4,5},{5,4},{6,7},{7,6},{8,9},{9,8},{10,11... | collective-permute-start | bytes 294920 | tf_op jit(solution)/shard_map/ppermute | solution.py:22
  15.7 1.3 %collective-permute-start.7 = (bf16[64,768]{1,0:T(8,128)(2,1)S(1)}, bf16[64,768]{1,0:T(8,128)(2,1)S(1)}, u32[]{:S(2)}, u32[]{:S(2)}) collective-permute-start(bf16[64,768]{1,0:T(8,128)(2,1)S(1)} %collective-permute-done.3.refs_1_.refs_4_), channel_id=1, source_target_pairs={{0,1},{1,0},{2,3},{3,2},{4,5},{5,4},{6,7},{7,6},{8,9},{9,8},{10,11... | collective-permute-start | bytes 294920 | tf_op jit(solution)/shard_map/ppermute | solution.py:22
  18.5 1.3 %collective-permute-start.8 = (bf16[72,768]{1,0:T(8,128)(2,1)S(1)}, bf16[72,768]{1,0:T(8,128)(2,1)S(1)}, u32[]{:S(2)}, u32[]{:S(2)}) collective-permute-start(bf16[72,768]{1,0:T(8,128)(2,1)S(1)} %hold.6.refs_5_), channel_id=1, source_target_pairs={{0,1},{1,0},{2,3},{3,2},{4,5},{5,4},{6,7},{7,6},{8,9},{9,8},{10,11... | collective-permute-start | bytes 331784 | tf_op jit(solution)/shard_map/ppermute | solution.py:22
  20.5 4.4 %collective-permute-start.12 = (bf16[136,256]{1,0:T(8,128)(2,1)S(1)}, bf16[136,256]{1,0:T(8,128)(2,1)S(1)}, u32[]{:S(2)}, u32[]{:S(2)}) collective-permute-start(bf16[136,256]{1,0:T(8,128)(2,1)S(1)} %get-tuple-element.32.refs_0_), channel_id=1, source_target_pairs={{0,2},{1,3},{2,0},{3,1},{4,6},{5,7},{6,4},{7,5},{8,10},{9,11},{10,... | collective-permute-start | bytes 208904 | tf_op jit(solution)/shard_map/ppermute | solution.py:22
  23.2 6.5 %collective-permute-start.9 = (bf16[136,512]{1,0:T(8,128)(2,1)S(1)}, bf16[136,512]{1,0:T(8,128)(2,1)S(1)}, u32[]{:S(2)}, u32[]{:S(2)}) collective-permute-start(bf16[136,512]{1,0:T(8,128)(2,1)S(1)} %hidden_part.5.refs_4_), channel_id=1, source_target_pairs={{0,2},{1,3},{2,0},{3,1},{4,6},{5,7},{6,4},{7,5},{8,10},{9,11},{10,... | collective-permute-start | bytes 417800 | tf_op jit(solution)/shard_map/ppermute | solution.py:22
  24.9 6.8 %slice-start.3 = ((s8[12582912]{0:T(1024)(128)(4,1)}), s8[4194304]{0:T(1024)(128)(4,1)S(1)}, s32[]{:S(2)}) async-start(s8[12582912]{0:T(1024)(128)(4,1)} %bitcast.8), calls=%async_computation.3 | async-start | bytes 8388608
  24.9 6.8 %slice-start.4 = ((s8[12582912]{0:T(1024)(128)(4,1)}), s8[4194304]{0:T(1024)(128)(4,1)S(1)}, s32[]{:S(2)}) async-start(s8[12582912]{0:T(1024)(128)(4,1)} %bitcast.8), calls=%async_computation.4 | async-start | bytes 8388608
  26.5 5.2 %slice-start.5 = ((s8[12582912]{0:T(1024)(128)(4,1)}), s8[4194304]{0:T(1024)(128)(4,1)S(1)}, s32[]{:S(2)}) async-start(s8[12582912]{0:T(1024)(128)(4,1)} %bitcast.8), calls=%async_computation.5 | async-start | bytes 8388608
  26.5 6.7 %collective-permute-start.18 = (bf16[136,768]{1,0:T(8,128)(2,1)S(1)}, bf16[136,768]{1,0:T(8,128)(2,1)S(1)}, u32[]{:S(2)}, u32[]{:S(2)}) collective-permute-start(bf16[136,768]{1,0:T(8,128)(2,1)S(1)} %hidden_part.7.refs_2_), channel_id=1, source_target_pairs={{0,2},{1,3},{2,0},{3,1},{4,6},{5,7},{6,4},{7,5},{8,10},{9,11},{10,... | collective-permute-start | bytes 626696 | tf_op jit(solution)/shard_map/ppermute | solution.py:22
  28.3 1.3 %collective-permute-start.14 = (bf16[136,256]{1,0:T(8,128)(2,1)S(1)}, bf16[136,256]{1,0:T(8,128)(2,1)S(1)}, u32[]{:S(2)}, u32[]{:S(2)}) collective-permute-start(bf16[136,256]{1,0:T(8,128)(2,1)S(1)} %get-tuple-element.32.refs_0_), channel_id=1, source_target_pairs={{0,1},{1,0},{2,3},{3,2},{4,5},{5,4},{6,7},{7,6},{8,9},{9,8},{10,11... | collective-permute-start | bytes 208904 | tf_op jit(solution)/shard_map/ppermute | solution.py:22
  28.3 3.4 %collective-permute-start.16 = (bf16[136,512]{1,0:T(8,128)(2,1)S(1)}, bf16[136,512]{1,0:T(8,128)(2,1)S(1)}, u32[]{:S(2)}, u32[]{:S(2)}) collective-permute-start(bf16[136,512]{1,0:T(8,128)(2,1)S(1)} %hidden_part.5.refs_4_), channel_id=1, source_target_pairs={{0,1},{1,0},{2,3},{3,2},{4,5},{5,4},{6,7},{7,6},{8,9},{9,8},{10,11... | collective-permute-start | bytes 417800 | tf_op jit(solution)/shard_map/ppermute | solution.py:22
  28.8 4.9 %collective-permute-start.13 = (bf16[136,768]{1,0:T(8,128)(2,1)S(1)}, bf16[136,768]{1,0:T(8,128)(2,1)S(1)}, u32[]{:S(2)}, u32[]{:S(2)}) collective-permute-start(bf16[136,768]{1,0:T(8,128)(2,1)S(1)} %hidden_part.7.refs_2_), channel_id=1, source_target_pairs={{0,1},{1,0},{2,3},{3,2},{4,5},{5,4},{6,7},{7,6},{8,9},{9,8},{10,11... | collective-permute-start | bytes 626696 | tf_op jit(solution)/shard_map/ppermute | solution.py:22
  29.5 1.7 %collective-permute-start.15 = (bf16[136,256]{1,0:T(8,128)(2,1)S(1)}, bf16[136,256]{1,0:T(8,128)(2,1)S(1)}, u32[]{:S(2)}, u32[]{:S(2)}) collective-permute-start(bf16[136,256]{1,0:T(8,128)(2,1)S(1)} %collective-permute-done.12.refs_3_.refs_2_), channel_id=1, source_target_pairs={{0,1},{1,0},{2,3},{3,2},{4,5},{5,4},{6,7},{7,6},{8,9},{9,8},{10,11... | collective-permute-start | bytes 208904 | tf_op jit(solution)/shard_map/ppermute | solution.py:22
  29.7 4.0 %collective-permute-start.11 = (bf16[136,512]{1,0:T(8,128)(2,1)S(1)}, bf16[136,512]{1,0:T(8,128)(2,1)S(1)}, u32[]{:S(2)}, u32[]{:S(2)}) collective-permute-start(bf16[136,512]{1,0:T(8,128)(2,1)S(1)} %collective-permute-done.9.refs_3_.refs_0_), channel_id=1, source_target_pairs={{0,1},{1,0},{2,3},{3,2},{4,5},{5,4},{6,7},{7,6},{8,9},{9,8},{10,11... | collective-permute-start | bytes 417800 | tf_op jit(solution)/shard_map/ppermute | solution.py:22
  30.0 3.7 %slice-start.6 = ((s8[12582912]{0:T(1024)(128)(4,1)}), s8[4194304]{0:T(1024)(128)(4,1)S(1)}, s32[]{:S(2)}) async-start(s8[12582912]{0:T(1024)(128)(4,1)} %bitcast.10), calls=%async_computation.6 | async-start | bytes 8388608
  30.0 3.7 %slice-start.7 = ((s8[12582912]{0:T(1024)(128)(4,1)}), s8[4194304]{0:T(1024)(128)(4,1)S(1)}, s32[]{:S(2)}) async-start(s8[12582912]{0:T(1024)(128)(4,1)} %bitcast.10), calls=%async_computation.7 | async-start | bytes 8388608
  31.2 3.7 %slice-start.8 = ((s8[12582912]{0:T(1024)(128)(4,1)}), s8[4194304]{0:T(1024)(128)(4,1)S(1)}, s32[]{:S(2)}) async-start(s8[12582912]{0:T(1024)(128)(4,1)} %bitcast.10), calls=%async_computation.8 | async-start | bytes 8388608
  31.2 5.8 %collective-permute-start.10 = (bf16[136,512]{1,0:T(8,128)(2,1)S(1)}, bf16[136,512]{1,0:T(8,128)(2,1)S(1)}, u32[]{:S(2)}, u32[]{:S(2)}) collective-permute-start(bf16[136,512]{1,0:T(8,128)(2,1)S(1)} %hidden_part.6.refs_2_), channel_id=1, source_target_pairs={{0,2},{1,3},{2,0},{3,1},{4,6},{5,7},{6,4},{7,5},{8,10},{9,11},{10,... | collective-permute-start | bytes 417800 | tf_op jit(solution)/shard_map/ppermute | solution.py:22
  33.2 3.9 %collective-permute-start.19 = (bf16[136,768]{1,0:T(8,128)(2,1)S(1)}, bf16[136,768]{1,0:T(8,128)(2,1)S(1)}, u32[]{:S(2)}, u32[]{:S(2)}) collective-permute-start(bf16[136,768]{1,0:T(8,128)(2,1)S(1)} %hold.8.refs_0_), channel_id=1, source_target_pairs={{0,1},{1,0},{2,3},{3,2},{4,5},{5,4},{6,7},{7,6},{8,9},{9,8},{10,11... | collective-permute-start | bytes 626696 | tf_op jit(solution)/shard_map/ppermute | solution.py:22
  33.2 3.9 %collective-permute-start.20 = (bf16[136,512]{1,0:T(8,128)(2,1)S(1)}, bf16[136,512]{1,0:T(8,128)(2,1)S(1)}, u32[]{:S(2)}, u32[]{:S(2)}) collective-permute-start(bf16[136,512]{1,0:T(8,128)(2,1)S(1)} %hidden_part.6.refs_2_), channel_id=1, source_target_pairs={{0,1},{1,0},{2,3},{3,2},{4,5},{5,4},{6,7},{7,6},{8,9},{9,8},{10,11... | collective-permute-start | bytes 417800 | tf_op jit(solution)/shard_map/ppermute | solution.py:22
  37.0 6.3 %copy-start.1 = (bf16[64,768]{1,0:T(8,128)(2,1)S(1)}, bf16[64,768]{1,0:T(8,128)(2,1)}, u32[]{:S(2)}) copy-start(bf16[64,768]{1,0:T(8,128)(2,1)} %grad_ref.1) | copy-start | bytes 294916
  37.0 6.3 %copy-start.3 = (s32[64,2]{0,1:T(2,128)S(1)}, s32[64,2]{0,1:T(2,128)}, u32[]{:S(2)}) copy-start(s32[64,2]{0,1:T(2,128)} %param.8) | copy-start | bytes 1540
  37.0 6.3 %copy-start.4 = (f32[64,2]{0,1:T(2,128)S(1)}, f32[64,2]{0,1:T(2,128)}, u32[]{:S(2)}) copy-start(f32[64,2]{0,1:T(2,128)} %param.9) | copy-start | bytes 1540
  37.0 1.4 %collective-permute-start.17 = (bf16[136,512]{1,0:T(8,128)(2,1)S(1)}, bf16[136,512]{1,0:T(8,128)(2,1)S(1)}, u32[]{:S(2)}, u32[]{:S(2)}) collective-permute-start(bf16[136,512]{1,0:T(8,128)(2,1)S(1)} %hold.7.refs_0_), channel_id=1, source_target_pairs={{0,1},{1,0},{2,3},{3,2},{4,5},{5,4},{6,7},{7,6},{8,9},{9,8},{10,11... | collective-permute-start | bytes 417800 | tf_op jit(solution)/shard_map/ppermute | solution.py:22
  38.9 4.8 %collective-permute-start.21 = (bf16[204,128]{1,0:T(8,128)(2,1)S(1)}, bf16[204,128]{1,0:T(8,128)(2,1)S(1)}, u32[]{:S(2)}, u32[]{:S(2)}) collective-permute-start(bf16[204,128]{1,0:T(8,128)(2,1)S(1)} %get-tuple-element.34), channel_id=1, source_target_pairs={{0,4},{4,0},{8,12},{12,8},{1,5},{5,1},{9,13},{13,9},{2,6},{6,2},{1... | collective-permute-start | bytes 156680 | tf_op jit(solution)/shard_map/ppermute | solution.py:22
  39.1 6.8 %collective-permute-start.22 = (bf16[204,128]{1,0:T(8,128)(2,1)S(1)}, bf16[204,128]{1,0:T(8,128)(2,1)S(1)}, u32[]{:S(2)}, u32[]{:S(2)}) collective-permute-start(bf16[204,128]{1,0:T(8,128)(2,1)S(1)} %get-tuple-element.35), channel_id=1, source_target_pairs={{0,8},{4,12},{8,0},{12,4},{1,9},{5,13},{9,1},{13,5},{2,10},{6,14},... | collective-permute-start | bytes 156680 | tf_op jit(solution)/shard_map/ppermute | solution.py:22
  42.2 5.9 %collective-permute-start.23 = (bf16[204,128]{1,0:T(8,128)(2,1)S(1)}, bf16[204,128]{1,0:T(8,128)(2,1)S(1)}, u32[]{:S(2)}, u32[]{:S(2)}) collective-permute-start(bf16[204,128]{1,0:T(8,128)(2,1)S(1)} %get-tuple-element.36), channel_id=1, source_target_pairs={{0,12},{4,8},{8,4},{12,0},{1,13},{5,9},{9,5},{13,1},{2,14},{6,10},... | collective-permute-start | bytes 156680 | tf_op jit(solution)/shard_map/ppermute | solution.py:22
  48.4 3.6 %collective-permute-start.24 = (f32[2,64]{1,0:T(2,128)S(1)}, f32[2,64]{1,0:T(2,128)S(1)}, u32[]{:S(2)}, u32[]{:S(2)}) collective-permute-start(f32[2,64]{1,0:T(2,128)S(1)} %dots.1), channel_id=1, source_target_pairs={{0,2},{1,3},{2,0},{3,1},{4,6},{5,7},{6,4},{7,5},{8,10},{9,11},{10,... | collective-permute-start | bytes 1544 | tf_op jit(solution)/shard_map/ppermute | solution.py:22
  52.0 0.9 %copy-start.2 = (bf16[64,768]{1,0:T(8,128)(2,1)S(1)}, bf16[64,768]{1,0:T(8,128)(2,1)}, u32[]{:S(2)}) copy-start(bf16[64,768]{1,0:T(8,128)(2,1)} %mix.1.refs_1_) | copy-start | bytes 294916
  52.9 1.1 %collective-permute-start.25 = (f32[2,64]{1,0:T(2,128)S(1)}, f32[2,64]{1,0:T(2,128)S(1)}, u32[]{:S(2)}, u32[]{:S(2)}) collective-permute-start(f32[2,64]{1,0:T(2,128)S(1)} %add.6), channel_id=1, source_target_pairs={{0,1},{1,0},{2,3},{3,2},{4,5},{5,4},{6,7},{7,6},{8,9},{9,8},{10,11... | collective-permute-start | bytes 1544 | tf_op jit(solution)/shard_map/ppermute | solution.py:22

commit v9 on v8

--- a/solution.py
+++ b/solution.py
@@ -289,15 +289,16 @@
         )
         term = routes_ref[:, k:k + 1] * out
         mixed = term if mixed is None else mixed + term
-    refs[-1][...] = mixed.astype(BF)
+    refs[-2][...] = mixed.astype(BF)
+    refs[-1][...] = jnp.zeros(refs[-1].shape, F32)
 
 
 def mix(routes, picks, back, width):
     return pl.pallas_call(
         mix_kernel,
-        out_shape=jax.ShapeDtypeStruct((routes.shape[0], width), BF),
+        out_shape=[jax.ShapeDtypeStruct((routes.shape[0], width), BF), jax.ShapeDtypeStruct((8, 128), F32)],
         in_specs=[VMEM] * (1 + 2 * EXPERTS),
-        out_specs=VMEM,
+        out_specs=[VMEM] * 2,
         compiler_params=pltpu.CompilerParams(vmem_limit_bytes=SMALL_LIMIT),
         cost_estimate=pl.CostEstimate(flops=1_000_000_000, bytes_accessed=1000, transcendentals=0),
         name="mix",
@@ -349,8 +350,8 @@
         sums.append(result[0])
     back = [result[0]] + [swap(result[k], "expert", k) for k in (1, 2, 3)]
     gate_grad = take_dots(hits, picks, grads, back)
-    mixed = mix(routes, picks, back, tokens.shape[1])
-    gate_grad = gate_grad + hold(swap(gate_grad, "tensor", 2), [mixed])
+    mixed, done = mix(routes, picks, back, tokens.shape[1])
+    gate_grad = gate_grad + hold(swap(gate_grad, "tensor", 2), [done])
     gate_grad = gate_grad + swap(gate_grad, "tensor", 1)
     return mixed, gate_grad.T
 

time: 54.7 us -> 53.9 us (0.985)
  local copies, waits for them, and re-layouts: 2.14 us -> 1.25 us
    unnamed x28 -> x26, local copies, waits for them, and re-layouts: 2.14 us -> 1.25 us
where the time goes in v9:
time: 53.9 us; the launch traced here: 53.7 us
  waiting for transfers between devices  20.6 us (38%)
  starting transfers between devices  20.3 us (38%)
  Pallas kernels  10 us (19%)
  local copies, waits for them, and re-layouts  1.25 us (2%)
  between operations  0.91 us (2%)
  other arithmetic  0.57 us (1%)
    ppermute x26, waiting for transfers between devices, swap(): return lax.ppermute(value, axis, [(i, i ^ bit) for i in range(size)])  20.6 us
    ppermute x26, starting transfers between devices, swap(): return lax.ppermute(value, axis, [(i, i ^ bit) for i in range(size)])  20.3 us
    pallas_call x4, Pallas kernels, hidden_part(): pl.pallas_call(functools.partial(hidden_kernel, joined, parts, start), ou...  4.59 us
    pallas_call x4, Pallas kernels, down_part(): pl.pallas_call(functools.partial(down_kernel, len(pieces), where, slab, h...  2.56 us
    pallas_call x1, Pallas kernels, select_rows(): pl.pallas_call(select_kernel, out_shape=[jax.ShapeDtypeStruct((MOST, widt...  1.3 us
    unnamed x26, local copies, waits for them, and re-layouts  1.25 us
  transfers between devices with their start and end apart: 26, of which 15 were waited for; matrix products, arithmetic and copies ran while one was open for 0% of the time, Pallas kernels for 14%

profile of v9, /device:TPU:0, one launch (start us, length us, event | category | flops | bytes accessed | tf_op | source)
XLA Modules:
  0.0 53.7 jit_solution(8508914156742433768)
XLA Ops:
  0.6 0.0 slice-start
  0.6 0.0 slice-start.1
  0.7 1.3 %select_rows.1 = (bf16[34,768]{1,0:T(8,128)(2,1)S(1)}, bf16[204,128]{1,0:T(8,128)(2,1)S(1)}, bf16[204,128]{1,0:T(8,128)(2,1)S(1)}, bf16[204,128]{1,0:T(8,128)(2,1)S(1)}) custom-call(s32[1]{0:T(128)} %bitcast.me_ref, s32[1]{0:T(128)} %bitcast.3.t_ref, s32[2,64]{1,0:T(2,128)} %bitcast.12, bf16[64,768]{1,0:T(8,128)(2,1)} %tokens_hbm.1), custom_call_target="tpu_custom_call" | custom-call | flops 8000000000 | bytes 1000 | tf_op jit(solution)/shard_map/select_rows/pallas_call | solution.py:82
  2.0 3.1 %collective-permute-start = (bf16[204,128]{1,0:T(8,128)(2,1)S(1)}, bf16[204,128]{1,0:T(8,128)(2,1)S(1)}, u32[]{:S(2)}, u32[]{:S(2)}) collective-permute-start(bf16[204,128]{1,0:T(8,128)(2,1)S(1)} %get-tuple-element.30), channel_id=1, source_target_pairs={{0,4},{4,0},{8,12},{12,8},{1,5},{5,1},{9,13},{13,9},{2,6},{6,2},{1... | collective-permute-start | bytes 156680 | tf_op jit(solution)/shard_map/ppermute | solution.py:22
  5.1 2.6 %collective-permute-start.1 = (bf16[204,128]{1,0:T(8,128)(2,1)S(1)}, bf16[204,128]{1,0:T(8,128)(2,1)S(1)}, u32[]{:S(2)}, u32[]{:S(2)}) collective-permute-start(bf16[204,128]{1,0:T(8,128)(2,1)S(1)} %get-tuple-element.31), channel_id=1, source_target_pairs={{0,8},{4,12},{8,0},{12,4},{1,9},{5,13},{9,1},{13,5},{2,10},{6,14},... | collective-permute-start | bytes 156680 | tf_op jit(solution)/shard_map/ppermute | solution.py:22
  7.7 0.0 collective-permute-start.2
  7.7 0.0 collective-permute-done.next_ref
  7.7 1.8 %collective-permute-start.3 = (bf16[64,768]{1,0:T(8,128)(2,1)S(1)}, bf16[64,768]{1,0:T(8,128)(2,1)S(1)}, u32[]{:S(2)}, u32[]{:S(2)}) collective-permute-start(bf16[64,768]{1,0:T(8,128)(2,1)S(1)} %pack_near.1.refs_0_), channel_id=1, source_target_pairs={{0,2},{1,3},{2,0},{3,1},{4,6},{5,7},{6,4},{7,5},{8,10},{9,11},{10,... | collective-permute-start | bytes 294920 | tf_op jit(solution)/shard_map/ppermute | solution.py:22
  9.5 1.7 %collective-permute-done.1.third_ref = bf16[204,128]{1,0:T(8,128)(2,1)S(1)} collective-permute-done((bf16[204,128]{1,0:T(8,128)(2,1)S(1)}, bf16[204,128]{1,0:T(8,128)(2,1)S(1)}, u32[]{:S(2)}, u32[]{:S(2)}) %collective-permute-start.1) | collective-permute-done | bytes 52256 | tf_op jit(solution)/shard_map/ppermute | solution.py:22
  11.1 2.5 %collective-permute-done.2.fourth_ref = bf16[204,128]{1,0:T(8,128)(2,1)S(1)} collective-permute-done((bf16[204,128]{1,0:T(8,128)(2,1)S(1)}, bf16[204,128]{1,0:T(8,128)(2,1)S(1)}, u32[]{:S(2)}, u32[]{:S(2)}) %collective-permute-start.2) | collective-permute-done | bytes 52256 | tf_op jit(solution)/shard_map/ppermute | solution.py:22
  13.7 1.6 %collective-permute-start.6 = (bf16[72,768]{1,0:T(8,128)(2,1)S(1)}, bf16[72,768]{1,0:T(8,128)(2,1)S(1)}, u32[]{:S(2)}, u32[]{:S(2)}) collective-permute-start(bf16[72,768]{1,0:T(8,128)(2,1)S(1)} %hold.5.refs_1_), channel_id=1, source_target_pairs={{0,2},{1,3},{2,0},{3,1},{4,6},{5,7},{6,4},{7,5},{8,10},{9,11},{10,... | collective-permute-start | bytes 331784 | tf_op jit(solution)/shard_map/ppermute | solution.py:22
  15.2 0.0 collective-permute-start.5
  15.2 0.5 collective-permute-start.4
  15.7 0.9 %collective-permute-done.4.refs_1_.refs_2_ = bf16[64,768]{1,0:T(8,128)(2,1)S(1)} collective-permute-done((bf16[64,768]{1,0:T(8,128)(2,1)S(1)}, bf16[64,768]{1,0:T(8,128)(2,1)S(1)}, u32[]{:S(2)}, u32[]{:S(2)}) %collective-permute-start.4) | collective-permute-done | bytes 98336 | tf_op jit(solution)/shard_map/ppermute | solution.py:22
  16.7 0.4 collective-permute-done.7.refs_3_.refs_6_
  17.0 1.4 %collective-permute-done.6.refs_0_ = bf16[72,768]{1,0:T(8,128)(2,1)S(1)} collective-permute-done((bf16[72,768]{1,0:T(8,128)(2,1)S(1)}, bf16[72,768]{1,0:T(8,128)(2,1)S(1)}, u32[]{:S(2)}, u32[]{:S(2)}) %collective-permute-start.6) | collective-permute-done | bytes 110624 | tf_op jit(solution)/shard_map/ppermute | solution.py:22
  18.5 0.0 collective-permute-done.5.refs_2_.refs_3_
  18.5 0.0 collective-permute-start.8
  18.5 1.3 %collective-permute-done.8.refs_7_ = bf16[72,768]{1,0:T(8,128)(2,1)S(1)} collective-permute-done((bf16[72,768]{1,0:T(8,128)(2,1)S(1)}, bf16[72,768]{1,0:T(8,128)(2,1)S(1)}, u32[]{:S(2)}, u32[]{:S(2)}) %collective-permute-start.8) | collective-permute-done | bytes 110624 | tf_op jit(solution)/shard_map/ppermute | solution.py:22
  19.8 0.7 %hidden_part.4 = (bf16[136,256]{1,0:T(8,128)(2,1)S(1)}, bf16[4,136,768]{2,1,0:T(8,128)(2,1)S(1)}) custom-call(s32[1]{0:T(128)} %bitcast.3.t_ref, bf16[64,768]{1,0:T(8,128)(2,1)S(1)} %pack_near.1.refs_0_, bf16[72,768]{1,0:T(8,128)(2,1)S(1)} %hold.5.refs_1_, bf16[64,768]{1,0:T(8,128)(2,1)S(1)} %collective-permute-done.4.refs_1_.refs_2_, ...), custom_call_target="tpu_custom_call" | custom-call | flops 1000 | bytes 1000 | tf_op jit(solution)/shard_map/hidden_part/pallas_call | solution.py:178
  20.5 1.6 %collective-permute-start.12 = (bf16[136,256]{1,0:T(8,128)(2,1)S(1)}, bf16[136,256]{1,0:T(8,128)(2,1)S(1)}, u32[]{:S(2)}, u32[]{:S(2)}) collective-permute-start(bf16[136,256]{1,0:T(8,128)(2,1)S(1)} %get-tuple-element.34.refs_0_), channel_id=1, source_target_pairs={{0,2},{1,3},{2,0},{3,1},{4,6},{5,7},{6,4},{7,5},{8,10},{9,11},{10,... | collective-permute-start | bytes 208904 | tf_op jit(solution)/shard_map/ppermute | solution.py:22
  22.1 1.1 %hidden_part.5.refs_4_ = bf16[136,512]{1,0:T(8,128)(2,1)S(1)} custom-call(s32[1]{0:T(128)} %bitcast.3.t_ref, bf16[4,136,768]{2,1,0:T(8,128)(2,1)S(1)} %get-tuple-element.33.refs_0_, bf16[1,3072,2048]{2,1,0:T(8,128)(2,1)S(1)} %bitcast.7, bf16[1,3072,2048]{2,1,0:T(8,128)(2,1)S(1)} %copy-done), custom_call_target="tpu_custom_call" | custom-call | flops 1000 | bytes 1000 | tf_op jit(solution)/shard_map/hidden_part/pallas_call | solution.py:178
  23.2 0.6 %collective-permute-start.9 = (bf16[136,512]{1,0:T(8,128)(2,1)S(1)}, bf16[136,512]{1,0:T(8,128)(2,1)S(1)}, u32[]{:S(2)}, u32[]{:S(2)}) collective-permute-start(bf16[136,512]{1,0:T(8,128)(2,1)S(1)} %hidden_part.5.refs_4_), channel_id=1, source_target_pairs={{0,2},{1,3},{2,0},{3,1},{4,6},{5,7},{6,4},{7,5},{8,10},{9,11},{10,... | collective-permute-start | bytes 417800 | tf_op jit(solution)/shard_map/ppermute | solution.py:22
  23.8 1.1 %collective-permute-done.12.refs_3_.refs_2_ = bf16[136,256]{1,0:T(8,128)(2,1)S(1)} collective-permute-done((bf16[136,256]{1,0:T(8,128)(2,1)S(1)}, bf16[136,256]{1,0:T(8,128)(2,1)S(1)}, u32[]{:S(2)}, u32[]{:S(2)}) %collective-permute-start.12) | collective-permute-done | bytes 69664 | tf_op jit(solution)/shard_map/ppermute | solution.py:22
  24.9 1.6 %hidden_part.7.refs_2_ = bf16[136,768]{1,0:T(8,128)(2,1)S(1)} custom-call(s32[1]{0:T(128)} %bitcast.3.t_ref, bf16[4,136,768]{2,1,0:T(8,128)(2,1)S(1)} %get-tuple-element.33.refs_0_, bf16[1,3072,2048]{2,1,0:T(8,128)(2,1)S(1)} %bitcast.7, bf16[1,3072,2048]{2,1,0:T(8,128)(2,1)S(1)} %copy-done, bf16[136,256]{1,0:T(8,128)(2,1)S(1)} %collective-permute-done.12.refs_3_.refs_2_), custom_call_target="tpu_custom_call" | custom-call | flops 1000 | bytes 1000 | tf_op jit(solution)/shard_map/hidden_part/pallas_call | solution.py:178
  26.5 0.0 slice-start.5
  26.5 1.7 %collective-permute-start.18 = (bf16[136,768]{1,0:T(8,128)(2,1)S(1)}, bf16[136,768]{1,0:T(8,128)(2,1)S(1)}, u32[]{:S(2)}, u32[]{:S(2)}) collective-permute-start(bf16[136,768]{1,0:T(8,128)(2,1)S(1)} %hidden_part.7.refs_2_), channel_id=1, source_target_pairs={{0,2},{1,3},{2,0},{3,1},{4,6},{5,7},{6,4},{7,5},{8,10},{9,11},{10,... | collective-permute-start | bytes 626696 | tf_op jit(solution)/shard_map/ppermute | solution.py:22
  28.3 0.0 collective-permute-start.14
  28.3 0.5 collective-permute-start.16
  28.8 0.0 collective-permute-start.13
  28.8 0.7 %collective-permute-done.14.refs_1_ = bf16[136,256]{1,0:T(8,128)(2,1)S(1)} collective-permute-done((bf16[136,256]{1,0:T(8,128)(2,1)S(1)}, bf16[136,256]{1,0:T(8,128)(2,1)S(1)}, u32[]{:S(2)}, u32[]{:S(2)}) %collective-permute-start.14) | collective-permute-done | bytes 69664 | tf_op jit(solution)/shard_map/ppermute | solution.py:22
  29.5 0.2 collective-permute-start.15
  29.7 0.0 collective-permute-done.9.refs_3_.refs_0_
  29.7 0.4 collective-permute-start.11
  30.0 1.2 %hidden_part.6.refs_2_ = bf16[136,512]{1,0:T(8,128)(2,1)S(1)} custom-call(s32[1]{0:T(128)} %bitcast.3.t_ref, bf16[4,136,768]{2,1,0:T(8,128)(2,1)S(1)} %get-tuple-element.33.refs_0_, bf16[1,3072,2048]{2,1,0:T(8,128)(2,1)S(1)} %bitcast.7, bf16[1,3072,2048]{2,1,0:T(8,128)(2,1)S(1)} %copy-done, bf16[136,512]{1,0:T(8,128)(2,1)S(1)} %collective-permute-done.9.refs_3_.refs_0_), custom_call_target="tpu_custom_call" | custom-call | flops 1000 | bytes 1000 | tf_op jit(solution)/shard_map/hidden_part/pallas_call | solution.py:178
  31.2 0.0 slice-start.8
  31.2 0.0 collective-permute-done.15.refs_3_
  31.2 0.4 collective-permute-start.10
  31.7 0.0 collective-permute-done.16.refs_5_
  31.7 0.6 %down_part.4.refs_5_.refs_1_ = f32[136,768]{1,0:T(8,128)S(1)} custom-call(s32[1]{0:T(128)} %bitcast.3.t_ref, bf16[136,256]{1,0:T(8,128)(2,1)S(1)} %get-tuple-element.34.refs_0_, bf16[136,256]{1,0:T(8,128)(2,1)S(1)} %collective-permute-done.14.refs_1_, bf16[136,256]{1,0:T(8,128)(2,1)S(1)} %collective-permute-done.12.refs_3_.refs_2_, ...), custom_call_target="tpu_custom_call" | custom-call | flops 427819008 | bytes 1000 | tf_op jit(solution)/shard_map/down_part/pallas_call | solution.py:216
  32.3 0.8 %collective-permute-done.18.refs_0_ = bf16[136,768]{1,0:T(8,128)(2,1)S(1)} collective-permute-done((bf16[136,768]{1,0:T(8,128)(2,1)S(1)}, bf16[136,768]{1,0:T(8,128)(2,1)S(1)}, u32[]{:S(2)}, u32[]{:S(2)}) %collective-permute-start.18) | collective-permute-done | bytes 208928 | tf_op jit(solution)/shard_map/ppermute | solution.py:22
  33.2 0.0 collective-permute-start.19
  33.2 0.5 collective-permute-start.20
  33.7 0.0 collective-permute-done.13.refs_3_
  33.7 1.2 %slice-done.8 = s8[4194304]{0:T(1024)(128)(4,1)S(1)} async-done(((s8[12582912]{0:T(1024)(128)(4,1)}), s8[4194304]{0:T(1024)(128)(4,1)S(1)}, s32[]{:S(2)}) %slice-start.8) | async-done | bytes 4194328
  34.9 0.7 %down_part.5.refs_1_.refs_5_ = f32[136,768]{1,0:T(8,128)S(1)} custom-call(s32[1]{0:T(128)} %bitcast.3.t_ref, bf16[136,512]{1,0:T(8,128)(2,1)S(1)} %collective-permute-done.9.refs_3_.refs_0_, bf16[136,512]{1,0:T(8,128)(2,1)S(1)} %collective-permute-done.11.refs_1_, bf16[136,768]{1,0:T(8,128)(2,1)S(1)} %hidden_part.7.refs_2_, ...), custom_call_target="tpu_custom_call" | custom-call | flops 534773760 | bytes 1000 | tf_op jit(solution)/shard_map/down_part/pallas_call | solution.py:216
  35.7 1.4 %collective-permute-done.10.refs_0_ = bf16[136,512]{1,0:T(8,128)(2,1)S(1)} collective-permute-done((bf16[136,512]{1,0:T(8,128)(2,1)S(1)}, bf16[136,512]{1,0:T(8,128)(2,1)S(1)}, u32[]{:S(2)}, u32[]{:S(2)}) %collective-permute-start.10) | collective-permute-done | bytes 139296 | tf_op jit(solution)/shard_map/ppermute | solution.py:22
  37.0 0.1 collective-permute-start.17
  37.1 0.0 collective-permute-done.20.refs_3_
  37.1 0.8 %down_part.6.refs_3_ = f32[136,768]{1,0:T(8,128)S(1)} custom-call(s32[1]{0:T(128)} %bitcast.3.t_ref, bf16[136,768]{1,0:T(8,128)(2,1)S(1)} %hold.8.refs_0_, bf16[136,768]{1,0:T(8,128)(2,1)S(1)} %collective-permute-done.19.refs_1_, bf16[136,512]{1,0:T(8,128)(2,1)S(1)} %hidden_part.6.refs_2_, bf16[136,512]{1,0:T(8,128)(2,1)S(1)} %collective-permute-done.20.refs_3_, ...), custom_call_target="tpu_custom_call" | custom-call | flops 534773760 | bytes 1000 | tf_op jit(solution)/shard_map/down_part/pallas_call | solution.py:216
  37.9 0.6 %collective-permute-done.17.refs_1_ = bf16[136,512]{1,0:T(8,128)(2,1)S(1)} collective-permute-done((bf16[136,512]{1,0:T(8,128)(2,1)S(1)}, bf16[136,512]{1,0:T(8,128)(2,1)S(1)}, u32[]{:S(2)}, u32[]{:S(2)}) %collective-permute-start.17) | collective-permute-done | bytes 139296 | tf_op jit(solution)/shard_map/ppermute | solution.py:22
  38.5 0.4 down_part.7
  38.9 0.2 collective-permute-start.21
  39.1 3.1 %collective-permute-start.22 = (bf16[204,128]{1,0:T(8,128)(2,1)S(1)}, bf16[204,128]{1,0:T(8,128)(2,1)S(1)}, u32[]{:S(2)}, u32[]{:S(2)}) collective-permute-start(bf16[204,128]{1,0:T(8,128)(2,1)S(1)} %get-tuple-element.37), channel_id=1, source_target_pairs={{0,8},{4,12},{8,0},{12,4},{1,9},{5,13},{9,1},{13,5},{2,10},{6,14},... | collective-permute-start | bytes 156680 | tf_op jit(solution)/shard_map/ppermute | solution.py:22
  42.2 1.1 %collective-permute-start.23 = (bf16[204,128]{1,0:T(8,128)(2,1)S(1)}, bf16[204,128]{1,0:T(8,128)(2,1)S(1)}, u32[]{:S(2)}, u32[]{:S(2)}) collective-permute-start(bf16[204,128]{1,0:T(8,128)(2,1)S(1)} %get-tuple-element.38), channel_id=1, source_target_pairs={{0,12},{4,8},{8,4},{12,0},{1,13},{5,9},{9,5},{13,1},{2,14},{6,10},... | collective-permute-start | bytes 156680 | tf_op jit(solution)/shard_map/ppermute | solution.py:22
  43.3 0.3 prepare.1
  43.7 2.2 %collective-permute-done.22.refs_6_.refs_10_ = bf16[204,128]{1,0:T(8,128)(2,1)S(1)} collective-permute-done((bf16[204,128]{1,0:T(8,128)(2,1)S(1)}, bf16[204,128]{1,0:T(8,128)(2,1)S(1)}, u32[]{:S(2)}, u32[]{:S(2)}) %collective-permute-start.22) | collective-permute-done | bytes 52256 | tf_op jit(solution)/shard_map/ppermute | solution.py:22
  45.9 2.2 %collective-permute-done.23.refs_7_.refs_11_ = bf16[204,128]{1,0:T(8,128)(2,1)S(1)} collective-permute-done((bf16[204,128]{1,0:T(8,128)(2,1)S(1)}, bf16[204,128]{1,0:T(8,128)(2,1)S(1)}, u32[]{:S(2)}, u32[]{:S(2)}) %collective-permute-start.23) | collective-permute-done | bytes 52256 | tf_op jit(solution)/shard_map/ppermute | solution.py:22
  48.1 0.2 dots.1
  48.4 0.5 collective-permute-start.24
  48.8 0.9 %mix.1 = (bf16[64,768]{1,0:T(8,128)(2,1)}, f32[8,128]{1,0:T(8,128)S(1)}) custom-call(f32[64,128]{1,0:T(8,128)S(1)} %get-tuple-element.24.routes_ref, f32[204,64]{1,0:T(8,128)S(1)} %get-tuple-element.25.refs_0_, f32[204,64]{1,0:T(8,128)S(1)} %get-tuple-element.26.refs_1_, f32[204,64]{1,0:T(8,128)S(1)} %get-tuple-element.27.refs_2_, ...), custom_call_target="tpu_custom_call" | custom-call | flops 1000000000 | bytes 1000 | tf_op jit(solution)/shard_map/mix/pallas_call | solution.py:297
  49.8 2.2 %collective-permute-done.24.refs_0_ = f32[2,64]{1,0:T(2,128)S(1)} collective-permute-done((f32[2,64]{1,0:T(2,128)S(1)}, f32[2,64]{1,0:T(2,128)S(1)}, u32[]{:S(2)}, u32[]{:S(2)}) %collective-permute-start.24) | collective-permute-done | bytes 544 | tf_op jit(solution)/shard_map/ppermute | solution.py:22
  52.0 1.1 %collective-permute-done.25 = f32[2,64]{1,0:T(2,128)S(1)} collective-permute-done((f32[2,64]{1,0:T(2,128)S(1)}, f32[2,64]{1,0:T(2,128)S(1)}, u32[]{:S(2)}, u32[]{:S(2)}) %collective-permute-start.25) | collective-permute-done | bytes 544 | tf_op jit(solution)/shard_map/ppermute | solution.py:22
  53.1 0.6 %add_bitcast_fusion = f32[64,2]{0,1:T(2,128)} fusion(f32[2,64]{1,0:T(2,128)S(1)} %add.6, f32[2,64]{1,0:T(2,128)S(1)} %collective-permute-done.25), kind=kLoop, calls=%fused_computation | loop fusion | flops 128 | bytes 1536 | tf_op jit(solution)/shard_map/transpose | solution.py:356
  (38 shorter events, 0.1 us)
Async XLA Ops:
  0.6 19.2 %slice-start = ((s8[12582912]{0:T(1024)(128)(4,1)}), s8[4194304]{0:T(1024)(128)(4,1)S(1)}, s32[]{:S(2)}) async-start(s8[12582912]{0:T(1024)(128)(4,1)} %bitcast.6), calls=%async_computation | async-start | bytes 8388608
  0.6 19.2 %slice-start.1 = ((s8[12582912]{0:T(1024)(128)(4,1)}), s8[4194304]{0:T(1024)(128)(4,1)S(1)}, s32[]{:S(2)}) async-start(s8[12582912]{0:T(1024)(128)(4,1)} %bitcast.6), calls=%async_computation.1 | async-start | bytes 8388608
  0.7 19.2 %slice-start.2 = ((s8[12582912]{0:T(1024)(128)(4,1)}), s8[4194304]{0:T(1024)(128)(4,1)S(1)}, s32[]{:S(2)}) async-start(s8[12582912]{0:T(1024)(128)(4,1)} %bitcast.6), calls=%async_computation.2 | async-start | bytes 8388608
  0.7 19.2 %copy-start = (bf16[1,3072,2048]{2,1,0:T(8,128)(2,1)S(1)}, bf16[1,3072,2048]{2,1,0:T(8,128)(2,1)}, u32[]{:S(2)}) copy-start(bf16[1,3072,2048]{2,1,0:T(8,128)(2,1)} %refs_2_.6) | copy-start | bytes 37748740
  2.0 5.7 %collective-permute-start = (bf16[204,128]{1,0:T(8,128)(2,1)S(1)}, bf16[204,128]{1,0:T(8,128)(2,1)S(1)}, u32[]{:S(2)}, u32[]{:S(2)}) collective-permute-start(bf16[204,128]{1,0:T(8,128)(2,1)S(1)} %get-tuple-element.30), channel_id=1, source_target_pairs={{0,4},{4,0},{8,12},{12,8},{1,5},{5,1},{9,13},{13,9},{2,6},{6,2},{1... | collective-permute-start | bytes 156680 | tf_op jit(solution)/shard_map/ppermute | solution.py:22
  5.1 6.1 %collective-permute-start.1 = (bf16[204,128]{1,0:T(8,128)(2,1)S(1)}, bf16[204,128]{1,0:T(8,128)(2,1)S(1)}, u32[]{:S(2)}, u32[]{:S(2)}) collective-permute-start(bf16[204,128]{1,0:T(8,128)(2,1)S(1)} %get-tuple-element.31), channel_id=1, source_target_pairs={{0,8},{4,12},{8,0},{12,4},{1,9},{5,13},{9,1},{13,5},{2,10},{6,14},... | collective-permute-start | bytes 156680 | tf_op jit(solution)/shard_map/ppermute | solution.py:22
  7.7 5.9 %collective-permute-start.2 = (bf16[204,128]{1,0:T(8,128)(2,1)S(1)}, bf16[204,128]{1,0:T(8,128)(2,1)S(1)}, u32[]{:S(2)}, u32[]{:S(2)}) collective-permute-start(bf16[204,128]{1,0:T(8,128)(2,1)S(1)} %get-tuple-element.32), channel_id=1, source_target_pairs={{0,12},{4,8},{8,4},{12,0},{1,13},{5,9},{9,5},{13,1},{2,14},{6,10},... | collective-permute-start | bytes 156680 | tf_op jit(solution)/shard_map/ppermute | solution.py:22
  7.7 5.9 %collective-permute-start.3 = (bf16[64,768]{1,0:T(8,128)(2,1)S(1)}, bf16[64,768]{1,0:T(8,128)(2,1)S(1)}, u32[]{:S(2)}, u32[]{:S(2)}) collective-permute-start(bf16[64,768]{1,0:T(8,128)(2,1)S(1)} %pack_near.1.refs_0_), channel_id=1, source_target_pairs={{0,2},{1,3},{2,0},{3,1},{4,6},{5,7},{6,4},{7,5},{8,10},{9,11},{10,... | collective-permute-start | bytes 294920 | tf_op jit(solution)/shard_map/ppermute | solution.py:22
  13.7 4.8 %collective-permute-start.6 = (bf16[72,768]{1,0:T(8,128)(2,1)S(1)}, bf16[72,768]{1,0:T(8,128)(2,1)S(1)}, u32[]{:S(2)}, u32[]{:S(2)}) collective-permute-start(bf16[72,768]{1,0:T(8,128)(2,1)S(1)} %hold.5.refs_1_), channel_id=1, source_target_pairs={{0,2},{1,3},{2,0},{3,1},{4,6},{5,7},{6,4},{7,5},{8,10},{9,11},{10,... | collective-permute-start | bytes 331784 | tf_op jit(solution)/shard_map/ppermute | solution.py:22
  15.2 3.3 %collective-permute-start.5 = (bf16[72,768]{1,0:T(8,128)(2,1)S(1)}, bf16[72,768]{1,0:T(8,128)(2,1)S(1)}, u32[]{:S(2)}, u32[]{:S(2)}) collective-permute-start(bf16[72,768]{1,0:T(8,128)(2,1)S(1)} %hold.5.refs_1_), channel_id=1, source_target_pairs={{0,1},{1,0},{2,3},{3,2},{4,5},{5,4},{6,7},{7,6},{8,9},{9,8},{10,11... | collective-permute-start | bytes 331784 | tf_op jit(solution)/shard_map/ppermute | solution.py:22
  15.2 1.5 %collective-permute-start.4 = (bf16[64,768]{1,0:T(8,128)(2,1)S(1)}, bf16[64,768]{1,0:T(8,128)(2,1)S(1)}, u32[]{:S(2)}, u32[]{:S(2)}) collective-permute-start(bf16[64,768]{1,0:T(8,128)(2,1)S(1)} %pack_near.1.refs_0_), channel_id=1, source_target_pairs={{0,1},{1,0},{2,3},{3,2},{4,5},{5,4},{6,7},{7,6},{8,9},{9,8},{10,11... | collective-permute-start | bytes 294920 | tf_op jit(solution)/shard_map/ppermute | solution.py:22
  15.7 1.3 %collective-permute-start.7 = (bf16[64,768]{1,0:T(8,128)(2,1)S(1)}, bf16[64,768]{1,0:T(8,128)(2,1)S(1)}, u32[]{:S(2)}, u32[]{:S(2)}) collective-permute-start(bf16[64,768]{1,0:T(8,128)(2,1)S(1)} %collective-permute-done.3.refs_1_.refs_4_), channel_id=1, source_target_pairs={{0,1},{1,0},{2,3},{3,2},{4,5},{5,4},{6,7},{7,6},{8,9},{9,8},{10,11... | collective-permute-start | bytes 294920 | tf_op jit(solution)/shard_map/ppermute | solution.py:22
  18.5 1.3 %collective-permute-start.8 = (bf16[72,768]{1,0:T(8,128)(2,1)S(1)}, bf16[72,768]{1,0:T(8,128)(2,1)S(1)}, u32[]{:S(2)}, u32[]{:S(2)}) collective-permute-start(bf16[72,768]{1,0:T(8,128)(2,1)S(1)} %hold.6.refs_5_), channel_id=1, source_target_pairs={{0,1},{1,0},{2,3},{3,2},{4,5},{5,4},{6,7},{7,6},{8,9},{9,8},{10,11... | collective-permute-start | bytes 331784 | tf_op jit(solution)/shard_map/ppermute | solution.py:22
  20.5 4.4 %collective-permute-start.12 = (bf16[136,256]{1,0:T(8,128)(2,1)S(1)}, bf16[136,256]{1,0:T(8,128)(2,1)S(1)}, u32[]{:S(2)}, u32[]{:S(2)}) collective-permute-start(bf16[136,256]{1,0:T(8,128)(2,1)S(1)} %get-tuple-element.34.refs_0_), channel_id=1, source_target_pairs={{0,2},{1,3},{2,0},{3,1},{4,6},{5,7},{6,4},{7,5},{8,10},{9,11},{10,... | collective-permute-start | bytes 208904 | tf_op jit(solution)/shard_map/ppermute | solution.py:22
  23.2 6.5 %collective-permute-start.9 = (bf16[136,512]{1,0:T(8,128)(2,1)S(1)}, bf16[136,512]{1,0:T(8,128)(2,1)S(1)}, u32[]{:S(2)}, u32[]{:S(2)}) collective-permute-start(bf16[136,512]{1,0:T(8,128)(2,1)S(1)} %hidden_part.5.refs_4_), channel_id=1, source_target_pairs={{0,2},{1,3},{2,0},{3,1},{4,6},{5,7},{6,4},{7,5},{8,10},{9,11},{10,... | collective-permute-start | bytes 417800 | tf_op jit(solution)/shard_map/ppermute | solution.py:22
  24.9 6.8 %slice-start.3 = ((s8[12582912]{0:T(1024)(128)(4,1)}), s8[4194304]{0:T(1024)(128)(4,1)S(1)}, s32[]{:S(2)}) async-start(s8[12582912]{0:T(1024)(128)(4,1)} %bitcast.8), calls=%async_computation.3 | async-start | bytes 8388608
  24.9 6.8 %slice-start.4 = ((s8[12582912]{0:T(1024)(128)(4,1)}), s8[4194304]{0:T(1024)(128)(4,1)S(1)}, s32[]{:S(2)}) async-start(s8[12582912]{0:T(1024)(128)(4,1)} %bitcast.8), calls=%async_computation.4 | async-start | bytes 8388608
  26.5 5.2 %slice-start.5 = ((s8[12582912]{0:T(1024)(128)(4,1)}), s8[4194304]{0:T(1024)(128)(4,1)S(1)}, s32[]{:S(2)}) async-start(s8[12582912]{0:T(1024)(128)(4,1)} %bitcast.8), calls=%async_computation.5 | async-start | bytes 8388608
  26.5 6.7 %collective-permute-start.18 = (bf16[136,768]{1,0:T(8,128)(2,1)S(1)}, bf16[136,768]{1,0:T(8,128)(2,1)S(1)}, u32[]{:S(2)}, u32[]{:S(2)}) collective-permute-start(bf16[136,768]{1,0:T(8,128)(2,1)S(1)} %hidden_part.7.refs_2_), channel_id=1, source_target_pairs={{0,2},{1,3},{2,0},{3,1},{4,6},{5,7},{6,4},{7,5},{8,10},{9,11},{10,... | collective-permute-start | bytes 626696 | tf_op jit(solution)/shard_map/ppermute | solution.py:22
  28.3 1.3 %collective-permute-start.14 = (bf16[136,256]{1,0:T(8,128)(2,1)S(1)}, bf16[136,256]{1,0:T(8,128)(2,1)S(1)}, u32[]{:S(2)}, u32[]{:S(2)}) collective-permute-start(bf16[136,256]{1,0:T(8,128)(2,1)S(1)} %get-tuple-element.34.refs_0_), channel_id=1, source_target_pairs={{0,1},{1,0},{2,3},{3,2},{4,5},{5,4},{6,7},{7,6},{8,9},{9,8},{10,11... | collective-permute-start | bytes 208904 | tf_op jit(solution)/shard_map/ppermute | solution.py:22
  28.3 3.4 %collective-permute-start.16 = (bf16[136,512]{1,0:T(8,128)(2,1)S(1)}, bf16[136,512]{1,0:T(8,128)(2,1)S(1)}, u32[]{:S(2)}, u32[]{:S(2)}) collective-permute-start(bf16[136,512]{1,0:T(8,128)(2,1)S(1)} %hidden_part.5.refs_4_), channel_id=1, source_target_pairs={{0,1},{1,0},{2,3},{3,2},{4,5},{5,4},{6,7},{7,6},{8,9},{9,8},{10,11... | collective-permute-start | bytes 417800 | tf_op jit(solution)/shard_map/ppermute | solution.py:22
  28.8 4.9 %collective-permute-start.13 = (bf16[136,768]{1,0:T(8,128)(2,1)S(1)}, bf16[136,768]{1,0:T(8,128)(2,1)S(1)}, u32[]{:S(2)}, u32[]{:S(2)}) collective-permute-start(bf16[136,768]{1,0:T(8,128)(2,1)S(1)} %hidden_part.7.refs_2_), channel_id=1, source_target_pairs={{0,1},{1,0},{2,3},{3,2},{4,5},{5,4},{6,7},{7,6},{8,9},{9,8},{10,11... | collective-permute-start | bytes 626696 | tf_op jit(solution)/shard_map/ppermute | solution.py:22
  29.5 1.7 %collective-permute-start.15 = (bf16[136,256]{1,0:T(8,128)(2,1)S(1)}, bf16[136,256]{1,0:T(8,128)(2,1)S(1)}, u32[]{:S(2)}, u32[]{:S(2)}) collective-permute-start(bf16[136,256]{1,0:T(8,128)(2,1)S(1)} %collective-permute-done.12.refs_3_.refs_2_), channel_id=1, source_target_pairs={{0,1},{1,0},{2,3},{3,2},{4,5},{5,4},{6,7},{7,6},{8,9},{9,8},{10,11... | collective-permute-start | bytes 208904 | tf_op jit(solution)/shard_map/ppermute | solution.py:22
  29.7 4.0 %collective-permute-start.11 = (bf16[136,512]{1,0:T(8,128)(2,1)S(1)}, bf16[136,512]{1,0:T(8,128)(2,1)S(1)}, u32[]{:S(2)}, u32[]{:S(2)}) collective-permute-start(bf16[136,512]{1,0:T(8,128)(2,1)S(1)} %collective-permute-done.9.refs_3_.refs_0_), channel_id=1, source_target_pairs={{0,1},{1,0},{2,3},{3,2},{4,5},{5,4},{6,7},{7,6},{8,9},{9,8},{10,11... | collective-permute-start | bytes 417800 | tf_op jit(solution)/shard_map/ppermute | solution.py:22
  30.0 3.7 %slice-start.6 = ((s8[12582912]{0:T(1024)(128)(4,1)}), s8[4194304]{0:T(1024)(128)(4,1)S(1)}, s32[]{:S(2)}) async-start(s8[12582912]{0:T(1024)(128)(4,1)} %bitcast.10), calls=%async_computation.6 | async-start | bytes 8388608
  30.0 3.7 %slice-start.7 = ((s8[12582912]{0:T(1024)(128)(4,1)}), s8[4194304]{0:T(1024)(128)(4,1)S(1)}, s32[]{:S(2)}) async-start(s8[12582912]{0:T(1024)(128)(4,1)} %bitcast.10), calls=%async_computation.7 | async-start | bytes 8388608
  31.2 3.7 %slice-start.8 = ((s8[12582912]{0:T(1024)(128)(4,1)}), s8[4194304]{0:T(1024)(128)(4,1)S(1)}, s32[]{:S(2)}) async-start(s8[12582912]{0:T(1024)(128)(4,1)} %bitcast.10), calls=%async_computation.8 | async-start | bytes 8388608
  31.2 5.8 %collective-permute-start.10 = (bf16[136,512]{1,0:T(8,128)(2,1)S(1)}, bf16[136,512]{1,0:T(8,128)(2,1)S(1)}, u32[]{:S(2)}, u32[]{:S(2)}) collective-permute-start(bf16[136,512]{1,0:T(8,128)(2,1)S(1)} %hidden_part.6.refs_2_), channel_id=1, source_target_pairs={{0,2},{1,3},{2,0},{3,1},{4,6},{5,7},{6,4},{7,5},{8,10},{9,11},{10,... | collective-permute-start | bytes 417800 | tf_op jit(solution)/shard_map/ppermute | solution.py:22
  33.2 3.9 %collective-permute-start.19 = (bf16[136,768]{1,0:T(8,128)(2,1)S(1)}, bf16[136,768]{1,0:T(8,128)(2,1)S(1)}, u32[]{:S(2)}, u32[]{:S(2)}) collective-permute-start(bf16[136,768]{1,0:T(8,128)(2,1)S(1)} %hold.8.refs_0_), channel_id=1, source_target_pairs={{0,1},{1,0},{2,3},{3,2},{4,5},{5,4},{6,7},{7,6},{8,9},{9,8},{10,11... | collective-permute-start | bytes 626696 | tf_op jit(solution)/shard_map/ppermute | solution.py:22
  33.2 3.9 %collective-permute-start.20 = (bf16[136,512]{1,0:T(8,128)(2,1)S(1)}, bf16[136,512]{1,0:T(8,128)(2,1)S(1)}, u32[]{:S(2)}, u32[]{:S(2)}) collective-permute-start(bf16[136,512]{1,0:T(8,128)(2,1)S(1)} %hidden_part.6.refs_2_), channel_id=1, source_target_pairs={{0,1},{1,0},{2,3},{3,2},{4,5},{5,4},{6,7},{7,6},{8,9},{9,8},{10,11... | collective-permute-start | bytes 417800 | tf_op jit(solution)/shard_map/ppermute | solution.py:22
  37.0 6.3 %copy-start.1 = (bf16[64,768]{1,0:T(8,128)(2,1)S(1)}, bf16[64,768]{1,0:T(8,128)(2,1)}, u32[]{:S(2)}) copy-start(bf16[64,768]{1,0:T(8,128)(2,1)} %grad_ref.1) | copy-start | bytes 294916
  37.0 6.3 %copy-start.2 = (s32[64,2]{0,1:T(2,128)S(1)}, s32[64,2]{0,1:T(2,128)}, u32[]{:S(2)}) copy-start(s32[64,2]{0,1:T(2,128)} %param.8) | copy-start | bytes 1540
  37.0 6.3 %copy-start.3 = (f32[64,2]{0,1:T(2,128)S(1)}, f32[64,2]{0,1:T(2,128)}, u32[]{:S(2)}) copy-start(f32[64,2]{0,1:T(2,128)} %param.9) | copy-start | bytes 1540
  37.0 1.4 %collective-permute-start.17 = (bf16[136,512]{1,0:T(8,128)(2,1)S(1)}, bf16[136,512]{1,0:T(8,128)(2,1)S(1)}, u32[]{:S(2)}, u32[]{:S(2)}) collective-permute-start(bf16[136,512]{1,0:T(8,128)(2,1)S(1)} %hold.7.refs_0_), channel_id=1, source_target_pairs={{0,1},{1,0},{2,3},{3,2},{4,5},{5,4},{6,7},{7,6},{8,9},{9,8},{10,11... | collective-permute-start | bytes 417800 | tf_op jit(solution)/shard_map/ppermute | solution.py:22
  38.9 4.8 %collective-permute-start.21 = (bf16[204,128]{1,0:T(8,128)(2,1)S(1)}, bf16[204,128]{1,0:T(8,128)(2,1)S(1)}, u32[]{:S(2)}, u32[]{:S(2)}) collective-permute-start(bf16[204,128]{1,0:T(8,128)(2,1)S(1)} %get-tuple-element.36), channel_id=1, source_target_pairs={{0,4},{4,0},{8,12},{12,8},{1,5},{5,1},{9,13},{13,9},{2,6},{6,2},{1... | collective-permute-start | bytes 156680 | tf_op jit(solution)/shard_map/ppermute | solution.py:22
  39.1 6.8 %collective-permute-start.22 = (bf16[204,128]{1,0:T(8,128)(2,1)S(1)}, bf16[204,128]{1,0:T(8,128)(2,1)S(1)}, u32[]{:S(2)}, u32[]{:S(2)}) collective-permute-start(bf16[204,128]{1,0:T(8,128)(2,1)S(1)} %get-tuple-element.37), channel_id=1, source_target_pairs={{0,8},{4,12},{8,0},{12,4},{1,9},{5,13},{9,1},{13,5},{2,10},{6,14},... | collective-permute-start | bytes 156680 | tf_op jit(solution)/shard_map/ppermute | solution.py:22
  42.2 5.9 %collective-permute-start.23 = (bf16[204,128]{1,0:T(8,128)(2,1)S(1)}, bf16[204,128]{1,0:T(8,128)(2,1)S(1)}, u32[]{:S(2)}, u32[]{:S(2)}) collective-permute-start(bf16[204,128]{1,0:T(8,128)(2,1)S(1)} %get-tuple-element.38), channel_id=1, source_target_pairs={{0,12},{4,8},{8,4},{12,0},{1,13},{5,9},{9,5},{13,1},{2,14},{6,10},... | collective-permute-start | bytes 156680 | tf_op jit(solution)/shard_map/ppermute | solution.py:22
  48.4 3.6 %collective-permute-start.24 = (f32[2,64]{1,0:T(2,128)S(1)}, f32[2,64]{1,0:T(2,128)S(1)}, u32[]{:S(2)}, u32[]{:S(2)}) collective-permute-start(f32[2,64]{1,0:T(2,128)S(1)} %dots.1), channel_id=1, source_target_pairs={{0,2},{1,3},{2,0},{3,1},{4,6},{5,7},{6,4},{7,5},{8,10},{9,11},{10,... | collective-permute-start | bytes 1544 | tf_op jit(solution)/shard_map/ppermute | solution.py:22
  52.0 1.1 %collective-permute-start.25 = (f32[2,64]{1,0:T(2,128)S(1)}, f32[2,64]{1,0:T(2,128)S(1)}, u32[]{:S(2)}, u32[]{:S(2)}) collective-permute-start(f32[2,64]{1,0:T(2,128)S(1)} %add.6), channel_id=1, source_target_pairs={{0,1},{1,0},{2,3},{3,2},{4,5},{5,4},{6,7},{7,6},{8,9},{9,8},{10,11... | collective-permute-start | bytes 1544 | tf_op jit(solution)/shard_map/ppermute | solution.py:22

commit v10 on v9

--- a/solution.py
+++ b/solution.py
@@ -55,11 +55,11 @@
 
 
 def unfold(block):
-    return jnp.concatenate([block[r:r + MOST] for r in range(0, block.shape[0], MOST)], axis=1)
-
-
-def folded(width):
-    return jax.ShapeDtypeStruct((width // 128 * MOST, 128), BF)
+    return jnp.concatenate([block[r:r + MOST] for r in range(0, block.shape[0] - MOST + 1, MOST)], axis=1)
+
+
+def folded(width, more=0):
+    return jax.ShapeDtypeStruct((width // 128 * MOST + more, 128), BF)
 
 
 def select_kernel(me_ref, t_ref, ids_hbm, tokens_hbm, *refs):
@@ -74,14 +74,17 @@
     tokens_copy.wait()
     for k, (pick, out_ref) in enumerate(zip(picks, out_refs)):
         block = jnp.dot(pick.astype(BF), tokens_ref[...], preferred_element_type=F32)
-        out_ref[...] = (block if k == 0 else fold(block)).astype(BF)
+        block = block if k == 0 else fold(block)
+        if out_ref.shape[0] > block.shape[0]:
+            block = jnp.concatenate([block, jnp.zeros((out_ref.shape[0] - block.shape[0], 128), F32)], axis=0)
+        out_ref[...] = block.astype(BF)
 
 
 def select_rows(me, t, ids_t, tokens):
     width = tokens.shape[1]
     return pl.pallas_call(
         select_kernel,
-        out_shape=[jax.ShapeDtypeStruct((MOST, width), BF)] + [folded(width)] * (EXPERTS - 1),
+        out_shape=[jax.ShapeDtypeStruct((MOST, width), BF), folded(width)] + [folded(width, 4)] * (EXPERTS - 2),
         in_specs=[SMEM, SMEM, ANY, ANY],
         out_specs=[VMEM] * EXPERTS,
         scratch_shapes=[
@@ -128,7 +131,7 @@
         out_specs=VMEM,
         name="pack_far",
         compiler_params=pltpu.CompilerParams(vmem_limit_bytes=SMALL_LIMIT),
-        cost_estimate=pl.CostEstimate(flops=1_000_000_000, bytes_accessed=1000, transcendentals=0),
+        cost_estimate=pl.CostEstimate(flops=2_000_000_000, bytes_accessed=1000, transcendentals=0),
     )(*blocks)
 
 
@@ -300,7 +303,7 @@
         in_specs=[VMEM] * (1 + 2 * EXPERTS),
         out_specs=[VMEM] * 2,
         compiler_params=pltpu.CompilerParams(vmem_limit_bytes=SMALL_LIMIT),
-        cost_estimate=pl.CostEstimate(flops=1_000_000_000, bytes_accessed=1000, transcendentals=0),
+        cost_estimate=pl.CostEstimate(flops=2_000_000_000, bytes_accessed=1000, transcendentals=0),
         name="mix",
     )(routes, *picks, *back)
 

time: 53.9 us -> 57.1 us (1.059)
  waiting for transfers between devices: 20.6 us -> 24.1 us
    ppermute x26, waiting for transfers between devices: 20.6 us -> 24.1 us  [swap(): return lax.ppermute(value, axis, [(i, i ^ bit) for i in range(size)])]
    unnamed x26 -> x30, local copies, waits for them, and re-layouts: 1.25 us -> 1.27 us
  transfers between devices with their start and end apart: 26 -> 26, of which waited for: 15 -> 16; matrix products, arithmetic and copies ran while one was open for 0% -> 0% of each run, Pallas kernels for 14% -> 13%
where the time goes in v10:
time: 57.1 us; the launch traced here: 56.9 us
  waiting for transfers between devices  24.1 us (42%)
  starting transfers between devices  20 us (35%)
  Pallas kernels  10 us (18%)
  local copies, waits for them, and re-layouts  1.27 us (2%)
  between operations  0.93 us (2%)
    ppermute x26, waiting for transfers between devices, swap(): return lax.ppermute(value, axis, [(i, i ^ bit) for i in range(size)])  24.1 us
    ppermute x26, starting transfers between devices, swap(): return lax.ppermute(value, axis, [(i, i ^ bit) for i in range(size)])  20 us
    pallas_call x4, Pallas kernels, hidden_part(): pl.pallas_call(functools.partial(hidden_kernel, joined, parts, start), ou...  4.62 us
    pallas_call x4, Pallas kernels, down_part(): pl.pallas_call(functools.partial(down_kernel, len(pieces), where, slab, h...  2.54 us
    pallas_call x1, Pallas kernels, select_rows(): pl.pallas_call(select_kernel, out_shape=[jax.ShapeDtypeStruct((MOST, widt...  1.3 us
    unnamed x30, local copies, waits for them, and re-layouts  1.27 us
  transfers between devices with their start and end apart: 26, of which 16 were waited for; matrix products, arithmetic and copies ran while one was open for 0% of the time, Pallas kernels for 13%

profile of v10, /device:TPU:0, one launch (start us, length us, event | category | flops | bytes accessed | tf_op | source)
XLA Modules:
  0.0 56.9 jit_solution(16234846730136544592)
XLA Ops:
  0.6 0.0 slice-start
  0.6 0.0 slice-start.3
  0.7 0.0 slice-start.2
  0.7 0.0 slice-start.4
  0.7 1.3 %select_rows.1 = (bf16[34,768]{1,0:T(8,128)(2,1)S(1)}, bf16[204,128]{1,0:T(8,128)(2,1)S(1)}, bf16[208,128]{1,0:T(8,128)(2,1)S(1)}, bf16[208,128]{1,0:T(8,128)(2,1)S(1)}) custom-call(s32[1]{0:T(128)} %bitcast.me_ref, s32[1]{0:T(128)} %bitcast.3.t_ref, s32[2,64]{1,0:T(2,128)} %bitcast.14, bf16[64,768]{1,0:T(8,128)(2,1)} %tokens_hbm.1), custom_call_target="tpu_custom_call" | custom-call | flops 8000000000 | bytes 1000 | tf_op jit(solution)/shard_map/select_rows/pallas_call | solution.py:85
  2.0 4.1 %collective-permute-start.1 = (bf16[208,128]{1,0:T(8,128)(2,1)S(1)}, bf16[208,128]{1,0:T(8,128)(2,1)S(1)}, u32[]{:S(2)}, u32[]{:S(2)}) collective-permute-start(bf16[208,128]{1,0:T(8,128)(2,1)S(1)} %get-tuple-element.31), channel_id=1, source_target_pairs={{0,8},{4,12},{8,0},{12,4},{1,9},{5,13},{9,1},{13,5},{2,10},{6,14},... | collective-permute-start | bytes 159752 | tf_op jit(solution)/shard_map/ppermute | solution.py:22
  6.1 1.4 %collective-permute-start.2 = (bf16[208,128]{1,0:T(8,128)(2,1)S(1)}, bf16[208,128]{1,0:T(8,128)(2,1)S(1)}, u32[]{:S(2)}, u32[]{:S(2)}) collective-permute-start(bf16[208,128]{1,0:T(8,128)(2,1)S(1)} %get-tuple-element.32), channel_id=1, source_target_pairs={{0,12},{4,8},{8,4},{12,0},{1,13},{5,9},{9,5},{13,1},{2,14},{6,10},... | collective-permute-start | bytes 159752 | tf_op jit(solution)/shard_map/ppermute | solution.py:22
  7.5 0.2 collective-permute-start
  7.7 4.5 %collective-permute-done.next_ref = bf16[204,128]{1,0:T(8,128)(2,1)S(1)} collective-permute-done((bf16[204,128]{1,0:T(8,128)(2,1)S(1)}, bf16[204,128]{1,0:T(8,128)(2,1)S(1)}, u32[]{:S(2)}, u32[]{:S(2)}) %collective-permute-start) | collective-permute-done | bytes 52256 | tf_op jit(solution)/shard_map/ppermute | solution.py:22
  12.2 1.6 %collective-permute-start.3 = (bf16[64,768]{1,0:T(8,128)(2,1)S(1)}, bf16[64,768]{1,0:T(8,128)(2,1)S(1)}, u32[]{:S(2)}, u32[]{:S(2)}) collective-permute-start(bf16[64,768]{1,0:T(8,128)(2,1)S(1)} %pack_near.1.refs_0_), channel_id=1, source_target_pairs={{0,2},{1,3},{2,0},{3,1},{4,6},{5,7},{6,4},{7,5},{8,10},{9,11},{10,... | collective-permute-start | bytes 294920 | tf_op jit(solution)/shard_map/ppermute | solution.py:22
  13.8 0.0 collective-permute-done.1.third_ref
  13.8 0.0 collective-permute-done.2.fourth_ref
  13.8 4.0 %collective-permute-done.3.refs_1_.refs_4_ = bf16[64,768]{1,0:T(8,128)(2,1)S(1)} collective-permute-done((bf16[64,768]{1,0:T(8,128)(2,1)S(1)}, bf16[64,768]{1,0:T(8,128)(2,1)S(1)}, u32[]{:S(2)}, u32[]{:S(2)}) %collective-permute-start.3) | collective-permute-done | bytes 98336 | tf_op jit(solution)/shard_map/ppermute | solution.py:22
  17.9 1.5 %collective-permute-start.6 = (bf16[72,768]{1,0:T(8,128)(2,1)S(1)}, bf16[72,768]{1,0:T(8,128)(2,1)S(1)}, u32[]{:S(2)}, u32[]{:S(2)}) collective-permute-start(bf16[72,768]{1,0:T(8,128)(2,1)S(1)} %hold.5.refs_1_), channel_id=1, source_target_pairs={{0,2},{1,3},{2,0},{3,1},{4,6},{5,7},{6,4},{7,5},{8,10},{9,11},{10,... | collective-permute-start | bytes 331784 | tf_op jit(solution)/shard_map/ppermute | solution.py:22
  19.4 0.5 collective-permute-start.4
  19.9 0.0 collective-permute-start.7
  19.9 0.9 %collective-permute-done.4.refs_1_.refs_2_ = bf16[64,768]{1,0:T(8,128)(2,1)S(1)} collective-permute-done((bf16[64,768]{1,0:T(8,128)(2,1)S(1)}, bf16[64,768]{1,0:T(8,128)(2,1)S(1)}, u32[]{:S(2)}, u32[]{:S(2)}) %collective-permute-start.4) | collective-permute-done | bytes 98336 | tf_op jit(solution)/shard_map/ppermute | solution.py:22
  20.8 0.4 collective-permute-done.7.refs_3_.refs_6_
  21.2 1.4 %collective-permute-done.6.refs_0_ = bf16[72,768]{1,0:T(8,128)(2,1)S(1)} collective-permute-done((bf16[72,768]{1,0:T(8,128)(2,1)S(1)}, bf16[72,768]{1,0:T(8,128)(2,1)S(1)}, u32[]{:S(2)}, u32[]{:S(2)}) %collective-permute-start.6) | collective-permute-done | bytes 110624 | tf_op jit(solution)/shard_map/ppermute | solution.py:22
  22.6 0.0 collective-permute-start.8
  22.6 1.3 %collective-permute-done.8.refs_7_ = bf16[72,768]{1,0:T(8,128)(2,1)S(1)} collective-permute-done((bf16[72,768]{1,0:T(8,128)(2,1)S(1)}, bf16[72,768]{1,0:T(8,128)(2,1)S(1)}, u32[]{:S(2)}, u32[]{:S(2)}) %collective-permute-start.8) | collective-permute-done | bytes 110624 | tf_op jit(solution)/shard_map/ppermute | solution.py:22
  24.0 0.7 %hidden_part.4 = (bf16[136,256]{1,0:T(8,128)(2,1)S(1)}, bf16[4,136,768]{2,1,0:T(8,128)(2,1)S(1)}) custom-call(s32[1]{0:T(128)} %bitcast.3.t_ref, bf16[64,768]{1,0:T(8,128)(2,1)S(1)} %pack_near.1.refs_0_, bf16[72,768]{1,0:T(8,128)(2,1)S(1)} %hold.5.refs_1_, bf16[64,768]{1,0:T(8,128)(2,1)S(1)} %collective-permute-done.4.refs_1_.refs_2_, ...), custom_call_target="tpu_custom_call" | custom-call | flops 1000 | bytes 1000 | tf_op jit(solution)/shard_map/hidden_part/pallas_call | solution.py:181
  24.7 1.6 %collective-permute-start.12 = (bf16[136,256]{1,0:T(8,128)(2,1)S(1)}, bf16[136,256]{1,0:T(8,128)(2,1)S(1)}, u32[]{:S(2)}, u32[]{:S(2)}) collective-permute-start(bf16[136,256]{1,0:T(8,128)(2,1)S(1)} %get-tuple-element.34.refs_0_), channel_id=1, source_target_pairs={{0,2},{1,3},{2,0},{3,1},{4,6},{5,7},{6,4},{7,5},{8,10},{9,11},{10,... | collective-permute-start | bytes 208904 | tf_op jit(solution)/shard_map/ppermute | solution.py:22
  26.2 1.1 %hidden_part.5.refs_4_ = bf16[136,512]{1,0:T(8,128)(2,1)S(1)} custom-call(s32[1]{0:T(128)} %bitcast.3.t_ref, bf16[4,136,768]{2,1,0:T(8,128)(2,1)S(1)} %get-tuple-element.33.refs_0_, bf16[1,3072,2048]{2,1,0:T(8,128)(2,1)S(1)} %bitcast.7, bf16[1,3072,2048]{2,1,0:T(8,128)(2,1)S(1)} %bitcast.9), custom_call_target="tpu_custom_call" | custom-call | flops 1000 | bytes 1000 | tf_op jit(solution)/shard_map/hidden_part/pallas_call | solution.py:181
  27.4 0.6 %collective-permute-start.9 = (bf16[136,512]{1,0:T(8,128)(2,1)S(1)}, bf16[136,512]{1,0:T(8,128)(2,1)S(1)}, u32[]{:S(2)}, u32[]{:S(2)}) collective-permute-start(bf16[136,512]{1,0:T(8,128)(2,1)S(1)} %hidden_part.5.refs_4_), channel_id=1, source_target_pairs={{0,2},{1,3},{2,0},{3,1},{4,6},{5,7},{6,4},{7,5},{8,10},{9,11},{10,... | collective-permute-start | bytes 417800 | tf_op jit(solution)/shard_map/ppermute | solution.py:22
  28.0 1.1 %collective-permute-done.12.refs_3_.refs_2_ = bf16[136,256]{1,0:T(8,128)(2,1)S(1)} collective-permute-done((bf16[136,256]{1,0:T(8,128)(2,1)S(1)}, bf16[136,256]{1,0:T(8,128)(2,1)S(1)}, u32[]{:S(2)}, u32[]{:S(2)}) %collective-permute-start.12) | collective-permute-done | bytes 69664 | tf_op jit(solution)/shard_map/ppermute | solution.py:22
  29.0 1.6 %hidden_part.7.refs_2_ = bf16[136,768]{1,0:T(8,128)(2,1)S(1)} custom-call(s32[1]{0:T(128)} %bitcast.3.t_ref, bf16[4,136,768]{2,1,0:T(8,128)(2,1)S(1)} %get-tuple-element.33.refs_0_, bf16[1,3072,2048]{2,1,0:T(8,128)(2,1)S(1)} %bitcast.7, bf16[1,3072,2048]{2,1,0:T(8,128)(2,1)S(1)} %bitcast.9, bf16[136,256]{1,0:T(8,128)(2,1)S(1)} %collective-permute-done.12.refs_3_.refs_2_), custom_call_target="tpu_custom_call" | custom-call | flops 1000 | bytes 1000 | tf_op jit(solution)/shard_map/hidden_part/pallas_call | solution.py:181
  30.7 0.0 slice-start.8
  30.7 1.7 %collective-permute-start.18 = (bf16[136,768]{1,0:T(8,128)(2,1)S(1)}, bf16[136,768]{1,0:T(8,128)(2,1)S(1)}, u32[]{:S(2)}, u32[]{:S(2)}) collective-permute-start(bf16[136,768]{1,0:T(8,128)(2,1)S(1)} %hidden_part.7.refs_2_), channel_id=1, source_target_pairs={{0,2},{1,3},{2,0},{3,1},{4,6},{5,7},{6,4},{7,5},{8,10},{9,11},{10,... | collective-permute-start | bytes 626696 | tf_op jit(solution)/shard_map/ppermute | solution.py:22
  32.4 0.5 collective-permute-start.16
  32.9 0.0 collective-permute-start.13
  32.9 0.7 %collective-permute-done.14.refs_1_ = bf16[136,256]{1,0:T(8,128)(2,1)S(1)} collective-permute-done((bf16[136,256]{1,0:T(8,128)(2,1)S(1)}, bf16[136,256]{1,0:T(8,128)(2,1)S(1)}, u32[]{:S(2)}, u32[]{:S(2)}) %collective-permute-start.14) | collective-permute-done | bytes 69664 | tf_op jit(solution)/shard_map/ppermute | solution.py:22
  33.7 0.2 collective-permute-start.15
  33.8 0.0 collective-permute-done.9.refs_3_.refs_0_
  33.9 0.4 collective-permute-start.11
  34.2 1.2 %hidden_part.6.refs_2_ = bf16[136,512]{1,0:T(8,128)(2,1)S(1)} custom-call(s32[1]{0:T(128)} %bitcast.3.t_ref, bf16[4,136,768]{2,1,0:T(8,128)(2,1)S(1)} %get-tuple-element.33.refs_0_, bf16[1,3072,2048]{2,1,0:T(8,128)(2,1)S(1)} %bitcast.7, bf16[1,3072,2048]{2,1,0:T(8,128)(2,1)S(1)} %bitcast.9, bf16[136,512]{1,0:T(8,128)(2,1)S(1)} %collective-permute-done.9.refs_3_.refs_0_), custom_call_target="tpu_custom_call" | custom-call | flops 1000 | bytes 1000 | tf_op jit(solution)/shard_map/hidden_part/pallas_call | solution.py:181
  35.4 0.0 slice-start.11
  35.4 0.4 collective-permute-start.10
  35.8 0.0 collective-permute-done.16.refs_5_
  35.9 0.6 %down_part.4.refs_5_.refs_1_ = f32[136,768]{1,0:T(8,128)S(1)} custom-call(s32[1]{0:T(128)} %bitcast.3.t_ref, bf16[136,256]{1,0:T(8,128)(2,1)S(1)} %get-tuple-element.34.refs_0_, bf16[136,256]{1,0:T(8,128)(2,1)S(1)} %collective-permute-done.14.refs_1_, bf16[136,256]{1,0:T(8,128)(2,1)S(1)} %collective-permute-done.12.refs_3_.refs_2_, ...), custom_call_target="tpu_custom_call" | custom-call | flops 427819008 | bytes 1000 | tf_op jit(solution)/shard_map/down_part/pallas_call | solution.py:219
  36.5 0.9 %collective-permute-done.18.refs_0_ = bf16[136,768]{1,0:T(8,128)(2,1)S(1)} collective-permute-done((bf16[136,768]{1,0:T(8,128)(2,1)S(1)}, bf16[136,768]{1,0:T(8,128)(2,1)S(1)}, u32[]{:S(2)}, u32[]{:S(2)}) %collective-permute-start.18) | collective-permute-done | bytes 208928 | tf_op jit(solution)/shard_map/ppermute | solution.py:22
  37.4 0.0 collective-permute-start.19
  37.4 0.5 collective-permute-start.20
  37.9 0.0 collective-permute-done.11.refs_1_
  37.9 1.2 %slice-done.11 = s8[4194304]{0:T(1024)(128)(4,1)S(1)} async-done(((s8[12582912]{0:T(1024)(128)(4,1)}), s8[4194304]{0:T(1024)(128)(4,1)S(1)}, s32[]{:S(2)}) %slice-start.11) | async-done | bytes 4194328
  39.1 0.7 %down_part.5.refs_1_.refs_5_ = f32[136,768]{1,0:T(8,128)S(1)} custom-call(s32[1]{0:T(128)} %bitcast.3.t_ref, bf16[136,512]{1,0:T(8,128)(2,1)S(1)} %collective-permute-done.9.refs_3_.refs_0_, bf16[136,512]{1,0:T(8,128)(2,1)S(1)} %collective-permute-done.11.refs_1_, bf16[136,768]{1,0:T(8,128)(2,1)S(1)} %hidden_part.7.refs_2_, ...), custom_call_target="tpu_custom_call" | custom-call | flops 534773760 | bytes 1000 | tf_op jit(solution)/shard_map/down_part/pallas_call | solution.py:219
  39.8 1.3 %collective-permute-done.10.refs_0_ = bf16[136,512]{1,0:T(8,128)(2,1)S(1)} collective-permute-done((bf16[136,512]{1,0:T(8,128)(2,1)S(1)}, bf16[136,512]{1,0:T(8,128)(2,1)S(1)}, u32[]{:S(2)}, u32[]{:S(2)}) %collective-permute-start.10) | collective-permute-done | bytes 139296 | tf_op jit(solution)/shard_map/ppermute | solution.py:22
  41.2 0.1 collective-permute-start.17
  41.3 0.8 %down_part.6.refs_3_ = f32[136,768]{1,0:T(8,128)S(1)} custom-call(s32[1]{0:T(128)} %bitcast.3.t_ref, bf16[136,768]{1,0:T(8,128)(2,1)S(1)} %hold.8.refs_0_, bf16[136,768]{1,0:T(8,128)(2,1)S(1)} %collective-permute-done.19.refs_1_, bf16[136,512]{1,0:T(8,128)(2,1)S(1)} %hidden_part.6.refs_2_, bf16[136,512]{1,0:T(8,128)(2,1)S(1)} %collective-permute-done.20.refs_3_, ...), custom_call_target="tpu_custom_call" | custom-call | flops 534773760 | bytes 1000 | tf_op jit(solution)/shard_map/down_part/pallas_call | solution.py:219
  42.1 0.6 collective-permute-done.17.refs_1_
  42.6 0.4 down_part.7
  43.0 0.1 collective-permute-start.21
  43.1 2.3 %collective-permute-start.22 = (bf16[204,128]{1,0:T(8,128)(2,1)S(1)}, bf16[204,128]{1,0:T(8,128)(2,1)S(1)}, u32[]{:S(2)}, u32[]{:S(2)}) collective-permute-start(bf16[204,128]{1,0:T(8,128)(2,1)S(1)} %get-tuple-element.37), channel_id=1, source_target_pairs={{0,8},{4,12},{8,0},{12,4},{1,9},{5,13},{9,1},{13,5},{2,10},{6,14},... | collective-permute-start | bytes 156680 | tf_op jit(solution)/shard_map/ppermute | solution.py:22
  45.4 2.1 %collective-permute-start.23 = (bf16[204,128]{1,0:T(8,128)(2,1)S(1)}, bf16[204,128]{1,0:T(8,128)(2,1)S(1)}, u32[]{:S(2)}, u32[]{:S(2)}) collective-permute-start(bf16[204,128]{1,0:T(8,128)(2,1)S(1)} %get-tuple-element.38), channel_id=1, source_target_pairs={{0,12},{4,8},{8,4},{12,0},{1,13},{5,9},{9,5},{13,1},{2,14},{6,10},... | collective-permute-start | bytes 156680 | tf_op jit(solution)/shard_map/ppermute | solution.py:22
  47.5 0.3 prepare.1
  47.8 0.1 collective-permute-done.21.refs_5_.refs_9_
  48.0 2.3 %collective-permute-done.22.refs_6_.refs_10_ = bf16[204,128]{1,0:T(8,128)(2,1)S(1)} collective-permute-done((bf16[204,128]{1,0:T(8,128)(2,1)S(1)}, bf16[204,128]{1,0:T(8,128)(2,1)S(1)}, u32[]{:S(2)}, u32[]{:S(2)}) %collective-permute-start.22) | collective-permute-done | bytes 52256 | tf_op jit(solution)/shard_map/ppermute | solution.py:22
  50.2 1.1 %collective-permute-done.23.refs_7_.refs_11_ = bf16[204,128]{1,0:T(8,128)(2,1)S(1)} collective-permute-done((bf16[204,128]{1,0:T(8,128)(2,1)S(1)}, bf16[204,128]{1,0:T(8,128)(2,1)S(1)}, u32[]{:S(2)}, u32[]{:S(2)}) %collective-permute-start.23) | collective-permute-done | bytes 52256 | tf_op jit(solution)/shard_map/ppermute | solution.py:22
  51.4 0.2 dots.1
  51.6 0.4 collective-permute-start.24
  52.0 0.9 %mix.1 = (bf16[64,768]{1,0:T(8,128)(2,1)}, f32[8,128]{1,0:T(8,128)S(1)}) custom-call(f32[64,128]{1,0:T(8,128)S(1)} %get-tuple-element.24.routes_ref, f32[204,64]{1,0:T(8,128)S(1)} %get-tuple-element.25.refs_0_, f32[204,64]{1,0:T(8,128)S(1)} %get-tuple-element.26.refs_1_, f32[204,64]{1,0:T(8,128)S(1)} %get-tuple-element.27.refs_2_, ...), custom_call_target="tpu_custom_call" | custom-call | flops 2000000000 | bytes 1000 | tf_op jit(solution)/shard_map/mix/pallas_call | solution.py:300
  53.0 2.3 %collective-permute-done.24.refs_0_ = f32[2,64]{1,0:T(2,128)S(1)} collective-permute-done((f32[2,64]{1,0:T(2,128)S(1)}, f32[2,64]{1,0:T(2,128)S(1)}, u32[]{:S(2)}, u32[]{:S(2)}) %collective-permute-start.24) | collective-permute-done | bytes 544 | tf_op jit(solution)/shard_map/ppermute | solution.py:22
  55.2 1.1 %collective-permute-done.25 = f32[2,64]{1,0:T(2,128)S(1)} collective-permute-done((f32[2,64]{1,0:T(2,128)S(1)}, f32[2,64]{1,0:T(2,128)S(1)}, u32[]{:S(2)}, u32[]{:S(2)}) %collective-permute-start.25) | collective-permute-done | bytes 544 | tf_op jit(solution)/shard_map/ppermute | solution.py:22
  56.4 0.6 add_bitcast_fusion
  (43 shorter events, 0.1 us)
Async XLA Ops:
  0.6 23.3 %slice-start = ((s8[12582912]{0:T(1024)(128)(4,1)}), s8[4194304]{0:T(1024)(128)(4,1)S(1)}, s32[]{:S(2)}) async-start(s8[12582912]{0:T(1024)(128)(4,1)} %bitcast.6), calls=%async_computation | async-start | bytes 8388608
  0.6 23.3 %slice-start.3 = ((s8[12582912]{0:T(1024)(128)(4,1)}), s8[4194304]{0:T(1024)(128)(4,1)S(1)}, s32[]{:S(2)}) async-start(s8[12582912]{0:T(1024)(128)(4,1)} %bitcast.8), calls=%async_computation.3 | async-start | bytes 8388608
  0.7 23.3 %slice-start.1 = ((s8[12582912]{0:T(1024)(128)(4,1)}), s8[4194304]{0:T(1024)(128)(4,1)S(1)}, s32[]{:S(2)}) async-start(s8[12582912]{0:T(1024)(128)(4,1)} %bitcast.6), calls=%async_computation.1 | async-start | bytes 8388608
  0.7 23.3 %slice-start.2 = ((s8[12582912]{0:T(1024)(128)(4,1)}), s8[4194304]{0:T(1024)(128)(4,1)S(1)}, s32[]{:S(2)}) async-start(s8[12582912]{0:T(1024)(128)(4,1)} %bitcast.6), calls=%async_computation.2 | async-start | bytes 8388608
  0.7 23.3 %slice-start.4 = ((s8[12582912]{0:T(1024)(128)(4,1)}), s8[4194304]{0:T(1024)(128)(4,1)S(1)}, s32[]{:S(2)}) async-start(s8[12582912]{0:T(1024)(128)(4,1)} %bitcast.8), calls=%async_computation.4 | async-start | bytes 8388608
  0.7 23.3 %slice-start.5 = ((s8[12582912]{0:T(1024)(128)(4,1)}), s8[4194304]{0:T(1024)(128)(4,1)S(1)}, s32[]{:S(2)}) async-start(s8[12582912]{0:T(1024)(128)(4,1)} %bitcast.8), calls=%async_computation.5 | async-start | bytes 8388608
  2.0 11.7 %collective-permute-start.1 = (bf16[208,128]{1,0:T(8,128)(2,1)S(1)}, bf16[208,128]{1,0:T(8,128)(2,1)S(1)}, u32[]{:S(2)}, u32[]{:S(2)}) collective-permute-start(bf16[208,128]{1,0:T(8,128)(2,1)S(1)} %get-tuple-element.31), channel_id=1, source_target_pairs={{0,8},{4,12},{8,0},{12,4},{1,9},{5,13},{9,1},{13,5},{2,10},{6,14},... | collective-permute-start | bytes 159752 | tf_op jit(solution)/shard_map/ppermute | solution.py:22
  6.1 7.7 %collective-permute-start.2 = (bf16[208,128]{1,0:T(8,128)(2,1)S(1)}, bf16[208,128]{1,0:T(8,128)(2,1)S(1)}, u32[]{:S(2)}, u32[]{:S(2)}) collective-permute-start(bf16[208,128]{1,0:T(8,128)(2,1)S(1)} %get-tuple-element.32), channel_id=1, source_target_pairs={{0,12},{4,8},{8,4},{12,0},{1,13},{5,9},{9,5},{13,1},{2,14},{6,10},... | collective-permute-start | bytes 159752 | tf_op jit(solution)/shard_map/ppermute | solution.py:22
  7.5 4.7 %collective-permute-start = (bf16[204,128]{1,0:T(8,128)(2,1)S(1)}, bf16[204,128]{1,0:T(8,128)(2,1)S(1)}, u32[]{:S(2)}, u32[]{:S(2)}) collective-permute-start(bf16[204,128]{1,0:T(8,128)(2,1)S(1)} %get-tuple-element.30), channel_id=1, source_target_pairs={{0,4},{4,0},{8,12},{12,8},{1,5},{5,1},{9,13},{13,9},{2,6},{6,2},{1... | collective-permute-start | bytes 156680 | tf_op jit(solution)/shard_map/ppermute | solution.py:22
  12.2 5.7 %collective-permute-start.3 = (bf16[64,768]{1,0:T(8,128)(2,1)S(1)}, bf16[64,768]{1,0:T(8,128)(2,1)S(1)}, u32[]{:S(2)}, u32[]{:S(2)}) collective-permute-start(bf16[64,768]{1,0:T(8,128)(2,1)S(1)} %pack_near.1.refs_0_), channel_id=1, source_target_pairs={{0,2},{1,3},{2,0},{3,1},{4,6},{5,7},{6,4},{7,5},{8,10},{9,11},{10,... | collective-permute-start | bytes 294920 | tf_op jit(solution)/shard_map/ppermute | solution.py:22
  17.9 4.7 %collective-permute-start.6 = (bf16[72,768]{1,0:T(8,128)(2,1)S(1)}, bf16[72,768]{1,0:T(8,128)(2,1)S(1)}, u32[]{:S(2)}, u32[]{:S(2)}) collective-permute-start(bf16[72,768]{1,0:T(8,128)(2,1)S(1)} %hold.5.refs_1_), channel_id=1, source_target_pairs={{0,2},{1,3},{2,0},{3,1},{4,6},{5,7},{6,4},{7,5},{8,10},{9,11},{10,... | collective-permute-start | bytes 331784 | tf_op jit(solution)/shard_map/ppermute | solution.py:22
  19.4 3.3 %collective-permute-start.5 = (bf16[72,768]{1,0:T(8,128)(2,1)S(1)}, bf16[72,768]{1,0:T(8,128)(2,1)S(1)}, u32[]{:S(2)}, u32[]{:S(2)}) collective-permute-start(bf16[72,768]{1,0:T(8,128)(2,1)S(1)} %hold.5.refs_1_), channel_id=1, source_target_pairs={{0,1},{1,0},{2,3},{3,2},{4,5},{5,4},{6,7},{7,6},{8,9},{9,8},{10,11... | collective-permute-start | bytes 331784 | tf_op jit(solution)/shard_map/ppermute | solution.py:22
  19.4 1.5 %collective-permute-start.4 = (bf16[64,768]{1,0:T(8,128)(2,1)S(1)}, bf16[64,768]{1,0:T(8,128)(2,1)S(1)}, u32[]{:S(2)}, u32[]{:S(2)}) collective-permute-start(bf16[64,768]{1,0:T(8,128)(2,1)S(1)} %pack_near.1.refs_0_), channel_id=1, source_target_pairs={{0,1},{1,0},{2,3},{3,2},{4,5},{5,4},{6,7},{7,6},{8,9},{9,8},{10,11... | collective-permute-start | bytes 294920 | tf_op jit(solution)/shard_map/ppermute | solution.py:22
  19.9 1.3 %collective-permute-start.7 = (bf16[64,768]{1,0:T(8,128)(2,1)S(1)}, bf16[64,768]{1,0:T(8,128)(2,1)S(1)}, u32[]{:S(2)}, u32[]{:S(2)}) collective-permute-start(bf16[64,768]{1,0:T(8,128)(2,1)S(1)} %collective-permute-done.3.refs_1_.refs_4_), channel_id=1, source_target_pairs={{0,1},{1,0},{2,3},{3,2},{4,5},{5,4},{6,7},{7,6},{8,9},{9,8},{10,11... | collective-permute-start | bytes 294920 | tf_op jit(solution)/shard_map/ppermute | solution.py:22
  22.6 1.3 %collective-permute-start.8 = (bf16[72,768]{1,0:T(8,128)(2,1)S(1)}, bf16[72,768]{1,0:T(8,128)(2,1)S(1)}, u32[]{:S(2)}, u32[]{:S(2)}) collective-permute-start(bf16[72,768]{1,0:T(8,128)(2,1)S(1)} %hold.6.refs_5_), channel_id=1, source_target_pairs={{0,1},{1,0},{2,3},{3,2},{4,5},{5,4},{6,7},{7,6},{8,9},{9,8},{10,11... | collective-permute-start | bytes 331784 | tf_op jit(solution)/shard_map/ppermute | solution.py:22
  24.7 4.4 %collective-permute-start.12 = (bf16[136,256]{1,0:T(8,128)(2,1)S(1)}, bf16[136,256]{1,0:T(8,128)(2,1)S(1)}, u32[]{:S(2)}, u32[]{:S(2)}) collective-permute-start(bf16[136,256]{1,0:T(8,128)(2,1)S(1)} %get-tuple-element.34.refs_0_), channel_id=1, source_target_pairs={{0,2},{1,3},{2,0},{3,1},{4,6},{5,7},{6,4},{7,5},{8,10},{9,11},{10,... | collective-permute-start | bytes 208904 | tf_op jit(solution)/shard_map/ppermute | solution.py:22
  27.4 6.5 %collective-permute-start.9 = (bf16[136,512]{1,0:T(8,128)(2,1)S(1)}, bf16[136,512]{1,0:T(8,128)(2,1)S(1)}, u32[]{:S(2)}, u32[]{:S(2)}) collective-permute-start(bf16[136,512]{1,0:T(8,128)(2,1)S(1)} %hidden_part.5.refs_4_), channel_id=1, source_target_pairs={{0,2},{1,3},{2,0},{3,1},{4,6},{5,7},{6,4},{7,5},{8,10},{9,11},{10,... | collective-permute-start | bytes 417800 | tf_op jit(solution)/shard_map/ppermute | solution.py:22
  29.0 6.8 %slice-start.6 = ((s8[12582912]{0:T(1024)(128)(4,1)}), s8[4194304]{0:T(1024)(128)(4,1)S(1)}, s32[]{:S(2)}) async-start(s8[12582912]{0:T(1024)(128)(4,1)} %bitcast.10), calls=%async_computation.6 | async-start | bytes 8388608
  29.0 6.8 %slice-start.7 = ((s8[12582912]{0:T(1024)(128)(4,1)}), s8[4194304]{0:T(1024)(128)(4,1)S(1)}, s32[]{:S(2)}) async-start(s8[12582912]{0:T(1024)(128)(4,1)} %bitcast.10), calls=%async_computation.7 | async-start | bytes 8388608
  30.7 5.1 %slice-start.8 = ((s8[12582912]{0:T(1024)(128)(4,1)}), s8[4194304]{0:T(1024)(128)(4,1)S(1)}, s32[]{:S(2)}) async-start(s8[12582912]{0:T(1024)(128)(4,1)} %bitcast.10), calls=%async_computation.8 | async-start | bytes 8388608
  30.7 6.7 %collective-permute-start.18 = (bf16[136,768]{1,0:T(8,128)(2,1)S(1)}, bf16[136,768]{1,0:T(8,128)(2,1)S(1)}, u32[]{:S(2)}, u32[]{:S(2)}) collective-permute-start(bf16[136,768]{1,0:T(8,128)(2,1)S(1)} %hidden_part.7.refs_2_), channel_id=1, source_target_pairs={{0,2},{1,3},{2,0},{3,1},{4,6},{5,7},{6,4},{7,5},{8,10},{9,11},{10,... | collective-permute-start | bytes 626696 | tf_op jit(solution)/shard_map/ppermute | solution.py:22
  32.4 1.3 %collective-permute-start.14 = (bf16[136,256]{1,0:T(8,128)(2,1)S(1)}, bf16[136,256]{1,0:T(8,128)(2,1)S(1)}, u32[]{:S(2)}, u32[]{:S(2)}) collective-permute-start(bf16[136,256]{1,0:T(8,128)(2,1)S(1)} %get-tuple-element.34.refs_0_), channel_id=1, source_target_pairs={{0,1},{1,0},{2,3},{3,2},{4,5},{5,4},{6,7},{7,6},{8,9},{9,8},{10,11... | collective-permute-start | bytes 208904 | tf_op jit(solution)/shard_map/ppermute | solution.py:22
  32.4 3.4 %collective-permute-start.16 = (bf16[136,512]{1,0:T(8,128)(2,1)S(1)}, bf16[136,512]{1,0:T(8,128)(2,1)S(1)}, u32[]{:S(2)}, u32[]{:S(2)}) collective-permute-start(bf16[136,512]{1,0:T(8,128)(2,1)S(1)} %hidden_part.5.refs_4_), channel_id=1, source_target_pairs={{0,1},{1,0},{2,3},{3,2},{4,5},{5,4},{6,7},{7,6},{8,9},{9,8},{10,11... | collective-permute-start | bytes 417800 | tf_op jit(solution)/shard_map/ppermute | solution.py:22
  32.9 4.9 %collective-permute-start.13 = (bf16[136,768]{1,0:T(8,128)(2,1)S(1)}, bf16[136,768]{1,0:T(8,128)(2,1)S(1)}, u32[]{:S(2)}, u32[]{:S(2)}) collective-permute-start(bf16[136,768]{1,0:T(8,128)(2,1)S(1)} %hidden_part.7.refs_2_), channel_id=1, source_target_pairs={{0,1},{1,0},{2,3},{3,2},{4,5},{5,4},{6,7},{7,6},{8,9},{9,8},{10,11... | collective-permute-start | bytes 626696 | tf_op jit(solution)/shard_map/ppermute | solution.py:22
  33.7 1.7 %collective-permute-start.15 = (bf16[136,256]{1,0:T(8,128)(2,1)S(1)}, bf16[136,256]{1,0:T(8,128)(2,1)S(1)}, u32[]{:S(2)}, u32[]{:S(2)}) collective-permute-start(bf16[136,256]{1,0:T(8,128)(2,1)S(1)} %collective-permute-done.12.refs_3_.refs_2_), channel_id=1, source_target_pairs={{0,1},{1,0},{2,3},{3,2},{4,5},{5,4},{6,7},{7,6},{8,9},{9,8},{10,11... | collective-permute-start | bytes 208904 | tf_op jit(solution)/shard_map/ppermute | solution.py:22
  33.9 4.0 %collective-permute-start.11 = (bf16[136,512]{1,0:T(8,128)(2,1)S(1)}, bf16[136,512]{1,0:T(8,128)(2,1)S(1)}, u32[]{:S(2)}, u32[]{:S(2)}) collective-permute-start(bf16[136,512]{1,0:T(8,128)(2,1)S(1)} %collective-permute-done.9.refs_3_.refs_0_), channel_id=1, source_target_pairs={{0,1},{1,0},{2,3},{3,2},{4,5},{5,4},{6,7},{7,6},{8,9},{9,8},{10,11... | collective-permute-start | bytes 417800 | tf_op jit(solution)/shard_map/ppermute | solution.py:22
  34.2 3.7 %slice-start.9 = ((s8[12582912]{0:T(1024)(128)(4,1)}), s8[4194304]{0:T(1024)(128)(4,1)S(1)}, s32[]{:S(2)}) async-start(s8[12582912]{0:T(1024)(128)(4,1)} %bitcast.12), calls=%async_computation.9 | async-start | bytes 8388608
  34.2 3.7 %slice-start.10 = ((s8[12582912]{0:T(1024)(128)(4,1)}), s8[4194304]{0:T(1024)(128)(4,1)S(1)}, s32[]{:S(2)}) async-start(s8[12582912]{0:T(1024)(128)(4,1)} %bitcast.12), calls=%async_computation.10 | async-start | bytes 8388608
  35.4 3.7 %slice-start.11 = ((s8[12582912]{0:T(1024)(128)(4,1)}), s8[4194304]{0:T(1024)(128)(4,1)S(1)}, s32[]{:S(2)}) async-start(s8[12582912]{0:T(1024)(128)(4,1)} %bitcast.12), calls=%async_computation.11 | async-start | bytes 8388608
  35.4 5.8 %collective-permute-start.10 = (bf16[136,512]{1,0:T(8,128)(2,1)S(1)}, bf16[136,512]{1,0:T(8,128)(2,1)S(1)}, u32[]{:S(2)}, u32[]{:S(2)}) collective-permute-start(bf16[136,512]{1,0:T(8,128)(2,1)S(1)} %hidden_part.6.refs_2_), channel_id=1, source_target_pairs={{0,2},{1,3},{2,0},{3,1},{4,6},{5,7},{6,4},{7,5},{8,10},{9,11},{10,... | collective-permute-start | bytes 417800 | tf_op jit(solution)/shard_map/ppermute | solution.py:22
  37.4 3.9 %collective-permute-start.19 = (bf16[136,768]{1,0:T(8,128)(2,1)S(1)}, bf16[136,768]{1,0:T(8,128)(2,1)S(1)}, u32[]{:S(2)}, u32[]{:S(2)}) collective-permute-start(bf16[136,768]{1,0:T(8,128)(2,1)S(1)} %hold.8.refs_0_), channel_id=1, source_target_pairs={{0,1},{1,0},{2,3},{3,2},{4,5},{5,4},{6,7},{7,6},{8,9},{9,8},{10,11... | collective-permute-start | bytes 626696 | tf_op jit(solution)/shard_map/ppermute | solution.py:22
  37.4 3.9 %collective-permute-start.20 = (bf16[136,512]{1,0:T(8,128)(2,1)S(1)}, bf16[136,512]{1,0:T(8,128)(2,1)S(1)}, u32[]{:S(2)}, u32[]{:S(2)}) collective-permute-start(bf16[136,512]{1,0:T(8,128)(2,1)S(1)} %hidden_part.6.refs_2_), channel_id=1, source_target_pairs={{0,1},{1,0},{2,3},{3,2},{4,5},{5,4},{6,7},{7,6},{8,9},{9,8},{10,11... | collective-permute-start | bytes 417800 | tf_op jit(solution)/shard_map/ppermute | solution.py:22
  41.2 6.3 %copy-start = (bf16[64,768]{1,0:T(8,128)(2,1)S(1)}, bf16[64,768]{1,0:T(8,128)(2,1)}, u32[]{:S(2)}) copy-start(bf16[64,768]{1,0:T(8,128)(2,1)} %grad_ref.1) | copy-start | bytes 294916
  41.2 6.3 %copy-start.1 = (s32[64,2]{0,1:T(2,128)S(1)}, s32[64,2]{0,1:T(2,128)}, u32[]{:S(2)}) copy-start(s32[64,2]{0,1:T(2,128)} %param.8) | copy-start | bytes 1540
  41.2 6.3 %copy-start.2 = (f32[64,2]{0,1:T(2,128)S(1)}, f32[64,2]{0,1:T(2,128)}, u32[]{:S(2)}) copy-start(f32[64,2]{0,1:T(2,128)} %param.9) | copy-start | bytes 1540
  41.2 1.4 %collective-permute-start.17 = (bf16[136,512]{1,0:T(8,128)(2,1)S(1)}, bf16[136,512]{1,0:T(8,128)(2,1)S(1)}, u32[]{:S(2)}, u32[]{:S(2)}) collective-permute-start(bf16[136,512]{1,0:T(8,128)(2,1)S(1)} %hold.7.refs_0_), channel_id=1, source_target_pairs={{0,1},{1,0},{2,3},{3,2},{4,5},{5,4},{6,7},{7,6},{8,9},{9,8},{10,11... | collective-permute-start | bytes 417800 | tf_op jit(solution)/shard_map/ppermute | solution.py:22
  43.0 4.9 %collective-permute-start.21 = (bf16[204,128]{1,0:T(8,128)(2,1)S(1)}, bf16[204,128]{1,0:T(8,128)(2,1)S(1)}, u32[]{:S(2)}, u32[]{:S(2)}) collective-permute-start(bf16[204,128]{1,0:T(8,128)(2,1)S(1)} %get-tuple-element.36), channel_id=1, source_target_pairs={{0,4},{4,0},{8,12},{12,8},{1,5},{5,1},{9,13},{13,9},{2,6},{6,2},{1... | collective-permute-start | bytes 156680 | tf_op jit(solution)/shard_map/ppermute | solution.py:22
  43.1 7.1 %collective-permute-start.22 = (bf16[204,128]{1,0:T(8,128)(2,1)S(1)}, bf16[204,128]{1,0:T(8,128)(2,1)S(1)}, u32[]{:S(2)}, u32[]{:S(2)}) collective-permute-start(bf16[204,128]{1,0:T(8,128)(2,1)S(1)} %get-tuple-element.37), channel_id=1, source_target_pairs={{0,8},{4,12},{8,0},{12,4},{1,9},{5,13},{9,1},{13,5},{2,10},{6,14},... | collective-permute-start | bytes 156680 | tf_op jit(solution)/shard_map/ppermute | solution.py:22
  45.4 6.0 %collective-permute-start.23 = (bf16[204,128]{1,0:T(8,128)(2,1)S(1)}, bf16[204,128]{1,0:T(8,128)(2,1)S(1)}, u32[]{:S(2)}, u32[]{:S(2)}) collective-permute-start(bf16[204,128]{1,0:T(8,128)(2,1)S(1)} %get-tuple-element.38), channel_id=1, source_target_pairs={{0,12},{4,8},{8,4},{12,0},{1,13},{5,9},{9,5},{13,1},{2,14},{6,10},... | collective-permute-start | bytes 156680 | tf_op jit(solution)/shard_map/ppermute | solution.py:22
  51.6 3.6 %collective-permute-start.24 = (f32[2,64]{1,0:T(2,128)S(1)}, f32[2,64]{1,0:T(2,128)S(1)}, u32[]{:S(2)}, u32[]{:S(2)}) collective-permute-start(f32[2,64]{1,0:T(2,128)S(1)} %dots.1), channel_id=1, source_target_pairs={{0,2},{1,3},{2,0},{3,1},{4,6},{5,7},{6,4},{7,5},{8,10},{9,11},{10,... | collective-permute-start | bytes 1544 | tf_op jit(solution)/shard_map/ppermute | solution.py:22
  55.2 1.1 %collective-permute-start.25 = (f32[2,64]{1,0:T(2,128)S(1)}, f32[2,64]{1,0:T(2,128)S(1)}, u32[]{:S(2)}, u32[]{:S(2)}) collective-permute-start(f32[2,64]{1,0:T(2,128)S(1)} %add.6), channel_id=1, source_target_pairs={{0,1},{1,0},{2,3},{3,2},{4,5},{5,4},{6,7},{7,6},{8,9},{9,8},{10,11... | collective-permute-start | bytes 1544 | tf_op jit(solution)/shard_map/ppermute | solution.py:22

commit v11 on v9

--- a/solution.py
+++ b/solution.py
@@ -95,41 +95,40 @@
     )(me, t, *(pltpu.with_memory_space_constraint(v, pltpu.HBM) for v in (ids_t, tokens)))
 
 
-CUT = 2 * MOST // 16 * 16
-
-
-def near_kernel(own_ref, next_ref, out_ref):
-    both = jnp.concatenate([own_ref[...].astype(F32), unfold(next_ref[...].astype(F32))], axis=0)
-    out_ref[...] = both[:CUT].astype(BF)
-
-
-def far_kernel(next_ref, third_ref, fourth_ref, out_ref):
-    rest = unfold(next_ref[...].astype(F32))[CUT - MOST:]
-    blocks = [rest] + [unfold(r[...].astype(F32)) for r in (third_ref, fourth_ref)]
-    out_ref[...] = jnp.concatenate(blocks, axis=0).astype(BF)
-
-
-def pack_near(own, following):
+CUT = 3 * MOST // 16 * 16
+
+
+def near_kernel(own_ref, *refs):
+    blocks = [own_ref[...].astype(F32)] + [unfold(r[...].astype(F32)) for r in refs[:2]]
+    refs[-1][...] = jnp.concatenate(blocks, axis=0)[:CUT].astype(BF)
+
+
+def far_kernel(third_ref, fourth_ref, out_ref):
+    rest = unfold(third_ref[...].astype(F32))[CUT - 2 * MOST:]
+    out_ref[...] = jnp.concatenate([rest, unfold(fourth_ref[...].astype(F32))], axis=0).astype(BF)
+
+
+def pack_near(own, second, third):
     return pl.pallas_call(
         near_kernel,
         out_shape=jax.ShapeDtypeStruct((CUT, own.shape[1]), BF),
-        in_specs=[VMEM] * 2,
+        in_specs=[VMEM] * 3,
         out_specs=VMEM,
         name="pack_near",
         **SMALL,
-    )(own, following)
-
-
-def pack_far(blocks, width):
+    )(own, second, third)
+
+
+def pack_far(third, fourth, width):
     return pl.pallas_call(
         far_kernel,
         out_shape=jax.ShapeDtypeStruct((EXPERTS * MOST - CUT, width), BF),
-        in_specs=[VMEM] * 3,
+        in_specs=[VMEM] * 2,
         out_specs=VMEM,
         name="pack_far",
         compiler_params=pltpu.CompilerParams(vmem_limit_bytes=SMALL_LIMIT),
         cost_estimate=pl.CostEstimate(flops=1_000_000_000, bytes_accessed=1000, transcendentals=0),
-    )(*blocks)
+    )(third, fourth)
 
 
 def hold(value, after):
@@ -318,13 +317,13 @@
     rows = select_rows(me, t_index, ids_t, tokens)
     starts = [sum(CHUNKS[:i]) for i in range(len(CHUNKS))]
     arrived = {k: swap(rows[k], "expert", k) for k in Z_ORDER}
-    near = pack_near(rows[0], arrived[1])
+    near = pack_near(rows[0], arrived[1], arrived[2])
     near_across = swap(near, "tensor", 2)
-    far = hold(pack_far([arrived[k] for k in (1, 2, 3)], tokens.shape[1]), [near_across])
+    far = pack_far(arrived[2], arrived[3], tokens.shape[1])
     far_across = swap(far, "tensor", 2)
-    sides = [swap(v, "tensor", 1) for v in (near, far, near_across)]
-    far_across = hold(far_across, sides)
-    xs = [near, far, sides[0], sides[1], near_across, far_across, sides[2], swap(far_across, "tensor", 1)]
+    near_across = hold(near_across, [far_across])
+    xs = [near, far, swap(near, "tensor", 1), swap(far, "tensor", 1), near_across, far_across]
+    xs += [swap(near_across, "tensor", 1), swap(far_across, "tensor", 1)]
 
     hits, routes, picks, grads = prepare(me, ids_t, probs_t, out_grad)
 

time: 53.9 us -> 53.6 us (level)
  no operation moved by 1% of the time
where the time goes in v11:
time: 53.6 us; the launch traced here: 53.4 us
  waiting for transfers between devices  20.5 us (38%)
  starting transfers between devices  20.2 us (38%)
  Pallas kernels  10 us (19%)
  local copies, waits for them, and re-layouts  1.22 us (2%)
  between operations  0.91 us (2%)
  other arithmetic  0.57 us (1%)
    ppermute x26, waiting for transfers between devices, swap(): return lax.ppermute(value, axis, [(i, i ^ bit) for i in range(size)])  20.5 us
    ppermute x26, starting transfers between devices, swap(): return lax.ppermute(value, axis, [(i, i ^ bit) for i in range(size)])  20.2 us
    pallas_call x4, Pallas kernels, hidden_part(): pl.pallas_call(functools.partial(hidden_kernel, joined, parts, start), ou...  4.6 us
    pallas_call x4, Pallas kernels, down_part(): pl.pallas_call(functools.partial(down_kernel, len(pieces), where, slab, h...  2.55 us
    pallas_call x1, Pallas kernels, select_rows(): pl.pallas_call(select_kernel, out_shape=[jax.ShapeDtypeStruct((MOST, widt...  1.3 us
    unnamed x26, local copies, waits for them, and re-layouts  1.22 us
  transfers between devices with their start and end apart: 26, of which 15 were waited for; matrix products, arithmetic and copies ran while one was open for 0% of the time, Pallas kernels for 14%

profile of v11, /device:TPU:0, one launch (start us, length us, event | category | flops | bytes accessed | tf_op | source)
XLA Modules:
  0.0 53.4 jit_solution(3815863600661020375)
XLA Ops:
  0.6 0.0 slice-start
  0.6 0.0 slice-start.1
  0.7 0.0 slice-start.2
  0.7 1.3 %select_rows.1 = (bf16[34,768]{1,0:T(8,128)(2,1)S(1)}, bf16[204,128]{1,0:T(8,128)(2,1)S(1)}, bf16[204,128]{1,0:T(8,128)(2,1)S(1)}, bf16[204,128]{1,0:T(8,128)(2,1)S(1)}) custom-call(s32[1]{0:T(128)} %bitcast.me_ref, s32[1]{0:T(128)} %bitcast.3.t_ref, s32[2,64]{1,0:T(2,128)} %bitcast.12, bf16[64,768]{1,0:T(8,128)(2,1)} %tokens_hbm.1), custom_call_target="tpu_custom_call" | custom-call | flops 8000000000 | bytes 1000 | tf_op jit(solution)/shard_map/select_rows/pallas_call | solution.py:82
  2.0 3.1 %collective-permute-start = (bf16[204,128]{1,0:T(8,128)(2,1)S(1)}, bf16[204,128]{1,0:T(8,128)(2,1)S(1)}, u32[]{:S(2)}, u32[]{:S(2)}) collective-permute-start(bf16[204,128]{1,0:T(8,128)(2,1)S(1)} %get-tuple-element.30), channel_id=1, source_target_pairs={{0,4},{4,0},{8,12},{12,8},{1,5},{5,1},{9,13},{13,9},{2,6},{6,2},{1... | collective-permute-start | bytes 156680 | tf_op jit(solution)/shard_map/ppermute | solution.py:22
  5.1 2.6 %collective-permute-start.1 = (bf16[204,128]{1,0:T(8,128)(2,1)S(1)}, bf16[204,128]{1,0:T(8,128)(2,1)S(1)}, u32[]{:S(2)}, u32[]{:S(2)}) collective-permute-start(bf16[204,128]{1,0:T(8,128)(2,1)S(1)} %get-tuple-element.31), channel_id=1, source_target_pairs={{0,8},{4,12},{8,0},{12,4},{1,9},{5,13},{9,1},{13,5},{2,10},{6,14},... | collective-permute-start | bytes 156680 | tf_op jit(solution)/shard_map/ppermute | solution.py:22
  7.7 0.0 collective-permute-start.2
  7.7 0.0 collective-permute-done.refs_0_
  7.7 3.5 %collective-permute-done.1.refs_1_.third_ref = bf16[204,128]{1,0:T(8,128)(2,1)S(1)} collective-permute-done((bf16[204,128]{1,0:T(8,128)(2,1)S(1)}, bf16[204,128]{1,0:T(8,128)(2,1)S(1)}, u32[]{:S(2)}, u32[]{:S(2)}) %collective-permute-start.1) | collective-permute-done | bytes 52256 | tf_op jit(solution)/shard_map/ppermute | solution.py:22
  11.2 1.6 %collective-permute-start.5 = (bf16[96,768]{1,0:T(8,128)(2,1)S(1)}, bf16[96,768]{1,0:T(8,128)(2,1)S(1)}, u32[]{:S(2)}, u32[]{:S(2)}) collective-permute-start(bf16[96,768]{1,0:T(8,128)(2,1)S(1)} %pack_near.1.refs_0_), channel_id=1, source_target_pairs={{0,2},{1,3},{2,0},{3,1},{4,6},{5,7},{6,4},{7,5},{8,10},{9,11},{10,... | collective-permute-start | bytes 442376 | tf_op jit(solution)/shard_map/ppermute | solution.py:22
  12.7 0.9 %collective-permute-done.2.fourth_ref = bf16[204,128]{1,0:T(8,128)(2,1)S(1)} collective-permute-done((bf16[204,128]{1,0:T(8,128)(2,1)S(1)}, bf16[204,128]{1,0:T(8,128)(2,1)S(1)}, u32[]{:S(2)}, u32[]{:S(2)}) %collective-permute-start.2) | collective-permute-done | bytes 52256 | tf_op jit(solution)/shard_map/ppermute | solution.py:22
  13.6 1.6 %collective-permute-start.6 = (bf16[40,768]{1,0:T(8,128)(2,1)S(1)}, bf16[40,768]{1,0:T(8,128)(2,1)S(1)}, u32[]{:S(2)}, u32[]{:S(2)}) collective-permute-start(bf16[40,768]{1,0:T(8,128)(2,1)S(1)} %pack_far.1.refs_1_), channel_id=1, source_target_pairs={{0,2},{1,3},{2,0},{3,1},{4,6},{5,7},{6,4},{7,5},{8,10},{9,11},{10,... | collective-permute-start | bytes 184328 | tf_op jit(solution)/shard_map/ppermute | solution.py:22
  15.2 0.0 collective-permute-start.3
  15.2 2.7 %collective-permute-done.6.refs_1_.refs_5_ = bf16[40,768]{1,0:T(8,128)(2,1)S(1)} collective-permute-done((bf16[40,768]{1,0:T(8,128)(2,1)S(1)}, bf16[40,768]{1,0:T(8,128)(2,1)S(1)}, u32[]{:S(2)}, u32[]{:S(2)}) %collective-permute-start.6) | collective-permute-done | bytes 61472 | tf_op jit(solution)/shard_map/ppermute | solution.py:22
  17.9 0.0 collective-permute-done.5.refs_0_
  17.9 0.5 collective-permute-start.4
  18.4 0.1 collective-permute-start.8
  18.5 0.9 %collective-permute-done.4.refs_3_ = bf16[40,768]{1,0:T(8,128)(2,1)S(1)} collective-permute-done((bf16[40,768]{1,0:T(8,128)(2,1)S(1)}, bf16[40,768]{1,0:T(8,128)(2,1)S(1)}, u32[]{:S(2)}, u32[]{:S(2)}) %collective-permute-start.4) | collective-permute-done | bytes 61472 | tf_op jit(solution)/shard_map/ppermute | solution.py:22
  19.4 0.3 collective-permute-done.8.refs_7_
  19.7 0.0 collective-permute-done.3.refs_2_
  19.7 0.0 collective-permute-done.7.refs_6_
  19.7 0.7 %hidden_part.4 = (bf16[136,256]{1,0:T(8,128)(2,1)S(1)}, bf16[4,136,768]{2,1,0:T(8,128)(2,1)S(1)}) custom-call(s32[1]{0:T(128)} %bitcast.3.t_ref, bf16[96,768]{1,0:T(8,128)(2,1)S(1)} %pack_near.1.refs_0_, bf16[40,768]{1,0:T(8,128)(2,1)S(1)} %pack_far.1.refs_1_, bf16[96,768]{1,0:T(8,128)(2,1)S(1)} %collective-permute-done.3.refs_2_, ...), custom_call_target="tpu_custom_call" | custom-call | flops 1000 | bytes 1000 | tf_op jit(solution)/shard_map/hidden_part/pallas_call | solution.py:177
  20.4 1.6 %collective-permute-start.12 = (bf16[136,256]{1,0:T(8,128)(2,1)S(1)}, bf16[136,256]{1,0:T(8,128)(2,1)S(1)}, u32[]{:S(2)}, u32[]{:S(2)}) collective-permute-start(bf16[136,256]{1,0:T(8,128)(2,1)S(1)} %get-tuple-element.34.refs_0_), channel_id=1, source_target_pairs={{0,2},{1,3},{2,0},{3,1},{4,6},{5,7},{6,4},{7,5},{8,10},{9,11},{10,... | collective-permute-start | bytes 208904 | tf_op jit(solution)/shard_map/ppermute | solution.py:22
  22.0 1.1 %hidden_part.5.refs_4_ = bf16[136,512]{1,0:T(8,128)(2,1)S(1)} custom-call(s32[1]{0:T(128)} %bitcast.3.t_ref, bf16[4,136,768]{2,1,0:T(8,128)(2,1)S(1)} %get-tuple-element.33.refs_0_, bf16[1,3072,2048]{2,1,0:T(8,128)(2,1)S(1)} %bitcast.7, bf16[1,3072,2048]{2,1,0:T(8,128)(2,1)S(1)} %copy-done), custom_call_target="tpu_custom_call" | custom-call | flops 1000 | bytes 1000 | tf_op jit(solution)/shard_map/hidden_part/pallas_call | solution.py:177
  23.1 0.6 %collective-permute-start.9 = (bf16[136,512]{1,0:T(8,128)(2,1)S(1)}, bf16[136,512]{1,0:T(8,128)(2,1)S(1)}, u32[]{:S(2)}, u32[]{:S(2)}) collective-permute-start(bf16[136,512]{1,0:T(8,128)(2,1)S(1)} %hidden_part.5.refs_4_), channel_id=1, source_target_pairs={{0,2},{1,3},{2,0},{3,1},{4,6},{5,7},{6,4},{7,5},{8,10},{9,11},{10,... | collective-permute-start | bytes 417800 | tf_op jit(solution)/shard_map/ppermute | solution.py:22
  23.7 1.1 %collective-permute-done.12.refs_3_.refs_2_ = bf16[136,256]{1,0:T(8,128)(2,1)S(1)} collective-permute-done((bf16[136,256]{1,0:T(8,128)(2,1)S(1)}, bf16[136,256]{1,0:T(8,128)(2,1)S(1)}, u32[]{:S(2)}, u32[]{:S(2)}) %collective-permute-start.12) | collective-permute-done | bytes 69664 | tf_op jit(solution)/shard_map/ppermute | solution.py:22
  24.8 1.6 %hidden_part.7.refs_2_ = bf16[136,768]{1,0:T(8,128)(2,1)S(1)} custom-call(s32[1]{0:T(128)} %bitcast.3.t_ref, bf16[4,136,768]{2,1,0:T(8,128)(2,1)S(1)} %get-tuple-element.33.refs_0_, bf16[1,3072,2048]{2,1,0:T(8,128)(2,1)S(1)} %bitcast.7, bf16[1,3072,2048]{2,1,0:T(8,128)(2,1)S(1)} %copy-done, bf16[136,256]{1,0:T(8,128)(2,1)S(1)} %collective-permute-done.12.refs_3_.refs_2_), custom_call_target="tpu_custom_call" | custom-call | flops 1000 | bytes 1000 | tf_op jit(solution)/shard_map/hidden_part/pallas_call | solution.py:177
  26.4 0.0 slice-start.5
  26.4 1.7 %collective-permute-start.18 = (bf16[136,768]{1,0:T(8,128)(2,1)S(1)}, bf16[136,768]{1,0:T(8,128)(2,1)S(1)}, u32[]{:S(2)}, u32[]{:S(2)}) collective-permute-start(bf16[136,768]{1,0:T(8,128)(2,1)S(1)} %hidden_part.7.refs_2_), channel_id=1, source_target_pairs={{0,2},{1,3},{2,0},{3,1},{4,6},{5,7},{6,4},{7,5},{8,10},{9,11},{10,... | collective-permute-start | bytes 626696 | tf_op jit(solution)/shard_map/ppermute | solution.py:22
  28.1 0.0 collective-permute-start.14
  28.1 0.5 collective-permute-start.16
  28.6 0.0 collective-permute-start.13
  28.7 0.7 %collective-permute-done.14.refs_1_ = bf16[136,256]{1,0:T(8,128)(2,1)S(1)} collective-permute-done((bf16[136,256]{1,0:T(8,128)(2,1)S(1)}, bf16[136,256]{1,0:T(8,128)(2,1)S(1)}, u32[]{:S(2)}, u32[]{:S(2)}) %collective-permute-start.14) | collective-permute-done | bytes 69664 | tf_op jit(solution)/shard_map/ppermute | solution.py:22
  29.4 0.2 collective-permute-start.15
  29.6 0.4 collective-permute-start.11
  29.9 1.2 %hidden_part.6.refs_2_ = bf16[136,512]{1,0:T(8,128)(2,1)S(1)} custom-call(s32[1]{0:T(128)} %bitcast.3.t_ref, bf16[4,136,768]{2,1,0:T(8,128)(2,1)S(1)} %get-tuple-element.33.refs_0_, bf16[1,3072,2048]{2,1,0:T(8,128)(2,1)S(1)} %bitcast.7, bf16[1,3072,2048]{2,1,0:T(8,128)(2,1)S(1)} %copy-done, bf16[136,512]{1,0:T(8,128)(2,1)S(1)} %collective-permute-done.9.refs_3_.refs_0_), custom_call_target="tpu_custom_call" | custom-call | flops 1000 | bytes 1000 | tf_op jit(solution)/shard_map/hidden_part/pallas_call | solution.py:177
  31.1 0.0 slice-start.8
  31.1 0.5 collective-permute-start.10
  31.6 0.6 %down_part.4.refs_5_.refs_1_ = f32[136,768]{1,0:T(8,128)S(1)} custom-call(s32[1]{0:T(128)} %bitcast.3.t_ref, bf16[136,256]{1,0:T(8,128)(2,1)S(1)} %get-tuple-element.34.refs_0_, bf16[136,256]{1,0:T(8,128)(2,1)S(1)} %collective-permute-done.14.refs_1_, bf16[136,256]{1,0:T(8,128)(2,1)S(1)} %collective-permute-done.12.refs_3_.refs_2_, ...), custom_call_target="tpu_custom_call" | custom-call | flops 427819008 | bytes 1000 | tf_op jit(solution)/shard_map/down_part/pallas_call | solution.py:215
  32.2 0.9 %collective-permute-done.18.refs_0_ = bf16[136,768]{1,0:T(8,128)(2,1)S(1)} collective-permute-done((bf16[136,768]{1,0:T(8,128)(2,1)S(1)}, bf16[136,768]{1,0:T(8,128)(2,1)S(1)}, u32[]{:S(2)}, u32[]{:S(2)}) %collective-permute-start.18) | collective-permute-done | bytes 208928 | tf_op jit(solution)/shard_map/ppermute | solution.py:22
  33.1 0.0 collective-permute-start.19
  33.1 0.5 collective-permute-start.20
  33.6 1.2 %slice-done.8 = s8[4194304]{0:T(1024)(128)(4,1)S(1)} async-done(((s8[12582912]{0:T(1024)(128)(4,1)}), s8[4194304]{0:T(1024)(128)(4,1)S(1)}, s32[]{:S(2)}) %slice-start.8) | async-done | bytes 4194328
  34.8 0.7 %down_part.5.refs_1_.refs_5_ = f32[136,768]{1,0:T(8,128)S(1)} custom-call(s32[1]{0:T(128)} %bitcast.3.t_ref, bf16[136,512]{1,0:T(8,128)(2,1)S(1)} %collective-permute-done.9.refs_3_.refs_0_, bf16[136,512]{1,0:T(8,128)(2,1)S(1)} %collective-permute-done.11.refs_1_, bf16[136,768]{1,0:T(8,128)(2,1)S(1)} %hidden_part.7.refs_2_, ...), custom_call_target="tpu_custom_call" | custom-call | flops 534773760 | bytes 1000 | tf_op jit(solution)/shard_map/down_part/pallas_call | solution.py:215
  35.6 1.4 %collective-permute-done.10.refs_0_ = bf16[136,512]{1,0:T(8,128)(2,1)S(1)} collective-permute-done((bf16[136,512]{1,0:T(8,128)(2,1)S(1)}, bf16[136,512]{1,0:T(8,128)(2,1)S(1)}, u32[]{:S(2)}, u32[]{:S(2)}) %collective-permute-start.10) | collective-permute-done | bytes 139296 | tf_op jit(solution)/shard_map/ppermute | solution.py:22
  36.9 0.1 collective-permute-start.17
  37.0 0.0 collective-permute-done.20.refs_3_
  37.0 0.0 collective-permute-done.19.refs_1_
  37.0 0.8 %down_part.6.refs_3_ = f32[136,768]{1,0:T(8,128)S(1)} custom-call(s32[1]{0:T(128)} %bitcast.3.t_ref, bf16[136,768]{1,0:T(8,128)(2,1)S(1)} %hold.6.refs_0_, bf16[136,768]{1,0:T(8,128)(2,1)S(1)} %collective-permute-done.19.refs_1_, bf16[136,512]{1,0:T(8,128)(2,1)S(1)} %hidden_part.6.refs_2_, bf16[136,512]{1,0:T(8,128)(2,1)S(1)} %collective-permute-done.20.refs_3_, ...), custom_call_target="tpu_custom_call" | custom-call | flops 534773760 | bytes 1000 | tf_op jit(solution)/shard_map/down_part/pallas_call | solution.py:215
  37.8 0.6 %collective-permute-done.17.refs_1_ = bf16[136,512]{1,0:T(8,128)(2,1)S(1)} collective-permute-done((bf16[136,512]{1,0:T(8,128)(2,1)S(1)}, bf16[136,512]{1,0:T(8,128)(2,1)S(1)}, u32[]{:S(2)}, u32[]{:S(2)}) %collective-permute-start.17) | collective-permute-done | bytes 139296 | tf_op jit(solution)/shard_map/ppermute | solution.py:22
  38.3 0.4 down_part.7
  38.8 0.1 collective-permute-start.21
  38.8 3.1 %collective-permute-start.22 = (bf16[204,128]{1,0:T(8,128)(2,1)S(1)}, bf16[204,128]{1,0:T(8,128)(2,1)S(1)}, u32[]{:S(2)}, u32[]{:S(2)}) collective-permute-start(bf16[204,128]{1,0:T(8,128)(2,1)S(1)} %get-tuple-element.37), channel_id=1, source_target_pairs={{0,8},{4,12},{8,0},{12,4},{1,9},{5,13},{9,1},{13,5},{2,10},{6,14},... | collective-permute-start | bytes 156680 | tf_op jit(solution)/shard_map/ppermute | solution.py:22
  41.9 1.3 %collective-permute-start.23 = (bf16[204,128]{1,0:T(8,128)(2,1)S(1)}, bf16[204,128]{1,0:T(8,128)(2,1)S(1)}, u32[]{:S(2)}, u32[]{:S(2)}) collective-permute-start(bf16[204,128]{1,0:T(8,128)(2,1)S(1)} %get-tuple-element.38), channel_id=1, source_target_pairs={{0,12},{4,8},{8,4},{12,0},{1,13},{5,9},{9,5},{13,1},{2,14},{6,10},... | collective-permute-start | bytes 156680 | tf_op jit(solution)/shard_map/ppermute | solution.py:22
  43.2 0.3 prepare.1
  43.6 0.2 collective-permute-done.21.refs_5_.refs_9_
  43.8 1.7 %collective-permute-done.22.refs_6_.refs_10_ = bf16[204,128]{1,0:T(8,128)(2,1)S(1)} collective-permute-done((bf16[204,128]{1,0:T(8,128)(2,1)S(1)}, bf16[204,128]{1,0:T(8,128)(2,1)S(1)}, u32[]{:S(2)}, u32[]{:S(2)}) %collective-permute-start.22) | collective-permute-done | bytes 52256 | tf_op jit(solution)/shard_map/ppermute | solution.py:22
  45.5 2.4 %collective-permute-done.23.refs_7_.refs_11_ = bf16[204,128]{1,0:T(8,128)(2,1)S(1)} collective-permute-done((bf16[204,128]{1,0:T(8,128)(2,1)S(1)}, bf16[204,128]{1,0:T(8,128)(2,1)S(1)}, u32[]{:S(2)}, u32[]{:S(2)}) %collective-permute-start.23) | collective-permute-done | bytes 52256 | tf_op jit(solution)/shard_map/ppermute | solution.py:22
  47.9 0.2 dots.1
  48.1 0.5 collective-permute-start.24
  48.6 0.9 %mix.1 = (bf16[64,768]{1,0:T(8,128)(2,1)}, f32[8,128]{1,0:T(8,128)S(1)}) custom-call(f32[64,128]{1,0:T(8,128)S(1)} %get-tuple-element.24.routes_ref, f32[204,64]{1,0:T(8,128)S(1)} %get-tuple-element.25.refs_0_, f32[204,64]{1,0:T(8,128)S(1)} %get-tuple-element.26.refs_1_, f32[204,64]{1,0:T(8,128)S(1)} %get-tuple-element.27.refs_2_, ...), custom_call_target="tpu_custom_call" | custom-call | flops 1000000000 | bytes 1000 | tf_op jit(solution)/shard_map/mix/pallas_call | solution.py:296
  49.5 2.2 %collective-permute-done.24.refs_0_ = f32[2,64]{1,0:T(2,128)S(1)} collective-permute-done((f32[2,64]{1,0:T(2,128)S(1)}, f32[2,64]{1,0:T(2,128)S(1)}, u32[]{:S(2)}, u32[]{:S(2)}) %collective-permute-start.24) | collective-permute-done | bytes 544 | tf_op jit(solution)/shard_map/ppermute | solution.py:22
  51.7 1.1 %collective-permute-done.25 = f32[2,64]{1,0:T(2,128)S(1)} collective-permute-done((f32[2,64]{1,0:T(2,128)S(1)}, f32[2,64]{1,0:T(2,128)S(1)}, u32[]{:S(2)}, u32[]{:S(2)}) %collective-permute-start.25) | collective-permute-done | bytes 544 | tf_op jit(solution)/shard_map/ppermute | solution.py:22
  52.9 0.6 %add_bitcast_fusion = f32[64,2]{0,1:T(2,128)} fusion(f32[2,64]{1,0:T(2,128)S(1)} %add.6, f32[2,64]{1,0:T(2,128)S(1)} %collective-permute-done.25), kind=kLoop, calls=%fused_computation | loop fusion | flops 128 | bytes 1536 | tf_op jit(solution)/shard_map/transpose | solution.py:355
  (37 shorter events, 0.1 us)
Async XLA Ops:
  0.6 19.1 %slice-start = ((s8[12582912]{0:T(1024)(128)(4,1)}), s8[4194304]{0:T(1024)(128)(4,1)S(1)}, s32[]{:S(2)}) async-start(s8[12582912]{0:T(1024)(128)(4,1)} %bitcast.6), calls=%async_computation | async-start | bytes 8388608
  0.6 19.1 %slice-start.1 = ((s8[12582912]{0:T(1024)(128)(4,1)}), s8[4194304]{0:T(1024)(128)(4,1)S(1)}, s32[]{:S(2)}) async-start(s8[12582912]{0:T(1024)(128)(4,1)} %bitcast.6), calls=%async_computation.1 | async-start | bytes 8388608
  0.7 19.1 %slice-start.2 = ((s8[12582912]{0:T(1024)(128)(4,1)}), s8[4194304]{0:T(1024)(128)(4,1)S(1)}, s32[]{:S(2)}) async-start(s8[12582912]{0:T(1024)(128)(4,1)} %bitcast.6), calls=%async_computation.2 | async-start | bytes 8388608
  0.7 19.1 %copy-start = (bf16[1,3072,2048]{2,1,0:T(8,128)(2,1)S(1)}, bf16[1,3072,2048]{2,1,0:T(8,128)(2,1)}, u32[]{:S(2)}) copy-start(bf16[1,3072,2048]{2,1,0:T(8,128)(2,1)} %refs_2_.6) | copy-start | bytes 37748740
  2.0 5.7 %collective-permute-start = (bf16[204,128]{1,0:T(8,128)(2,1)S(1)}, bf16[204,128]{1,0:T(8,128)(2,1)S(1)}, u32[]{:S(2)}, u32[]{:S(2)}) collective-permute-start(bf16[204,128]{1,0:T(8,128)(2,1)S(1)} %get-tuple-element.30), channel_id=1, source_target_pairs={{0,4},{4,0},{8,12},{12,8},{1,5},{5,1},{9,13},{13,9},{2,6},{6,2},{1... | collective-permute-start | bytes 156680 | tf_op jit(solution)/shard_map/ppermute | solution.py:22
  5.1 6.1 %collective-permute-start.1 = (bf16[204,128]{1,0:T(8,128)(2,1)S(1)}, bf16[204,128]{1,0:T(8,128)(2,1)S(1)}, u32[]{:S(2)}, u32[]{:S(2)}) collective-permute-start(bf16[204,128]{1,0:T(8,128)(2,1)S(1)} %get-tuple-element.31), channel_id=1, source_target_pairs={{0,8},{4,12},{8,0},{12,4},{1,9},{5,13},{9,1},{13,5},{2,10},{6,14},... | collective-permute-start | bytes 156680 | tf_op jit(solution)/shard_map/ppermute | solution.py:22
  7.7 5.9 %collective-permute-start.2 = (bf16[204,128]{1,0:T(8,128)(2,1)S(1)}, bf16[204,128]{1,0:T(8,128)(2,1)S(1)}, u32[]{:S(2)}, u32[]{:S(2)}) collective-permute-start(bf16[204,128]{1,0:T(8,128)(2,1)S(1)} %get-tuple-element.32), channel_id=1, source_target_pairs={{0,12},{4,8},{8,4},{12,0},{1,13},{5,9},{9,5},{13,1},{2,14},{6,10},... | collective-permute-start | bytes 156680 | tf_op jit(solution)/shard_map/ppermute | solution.py:22
  11.2 6.7 %collective-permute-start.5 = (bf16[96,768]{1,0:T(8,128)(2,1)S(1)}, bf16[96,768]{1,0:T(8,128)(2,1)S(1)}, u32[]{:S(2)}, u32[]{:S(2)}) collective-permute-start(bf16[96,768]{1,0:T(8,128)(2,1)S(1)} %pack_near.1.refs_0_), channel_id=1, source_target_pairs={{0,2},{1,3},{2,0},{3,1},{4,6},{5,7},{6,4},{7,5},{8,10},{9,11},{10,... | collective-permute-start | bytes 442376 | tf_op jit(solution)/shard_map/ppermute | solution.py:22
  13.6 4.3 %collective-permute-start.6 = (bf16[40,768]{1,0:T(8,128)(2,1)S(1)}, bf16[40,768]{1,0:T(8,128)(2,1)S(1)}, u32[]{:S(2)}, u32[]{:S(2)}) collective-permute-start(bf16[40,768]{1,0:T(8,128)(2,1)S(1)} %pack_far.1.refs_1_), channel_id=1, source_target_pairs={{0,2},{1,3},{2,0},{3,1},{4,6},{5,7},{6,4},{7,5},{8,10},{9,11},{10,... | collective-permute-start | bytes 184328 | tf_op jit(solution)/shard_map/ppermute | solution.py:22
  15.2 4.5 %collective-permute-start.3 = (bf16[96,768]{1,0:T(8,128)(2,1)S(1)}, bf16[96,768]{1,0:T(8,128)(2,1)S(1)}, u32[]{:S(2)}, u32[]{:S(2)}) collective-permute-start(bf16[96,768]{1,0:T(8,128)(2,1)S(1)} %pack_near.1.refs_0_), channel_id=1, source_target_pairs={{0,1},{1,0},{2,3},{3,2},{4,5},{5,4},{6,7},{7,6},{8,9},{9,8},{10,11... | collective-permute-start | bytes 442376 | tf_op jit(solution)/shard_map/ppermute | solution.py:22
  17.9 1.8 %collective-permute-start.7 = (bf16[96,768]{1,0:T(8,128)(2,1)S(1)}, bf16[96,768]{1,0:T(8,128)(2,1)S(1)}, u32[]{:S(2)}, u32[]{:S(2)}) collective-permute-start(bf16[96,768]{1,0:T(8,128)(2,1)S(1)} %hold.4.refs_4_), channel_id=1, source_target_pairs={{0,1},{1,0},{2,3},{3,2},{4,5},{5,4},{6,7},{7,6},{8,9},{9,8},{10,11... | collective-permute-start | bytes 442376 | tf_op jit(solution)/shard_map/ppermute | solution.py:22
  17.9 1.5 %collective-permute-start.4 = (bf16[40,768]{1,0:T(8,128)(2,1)S(1)}, bf16[40,768]{1,0:T(8,128)(2,1)S(1)}, u32[]{:S(2)}, u32[]{:S(2)}) collective-permute-start(bf16[40,768]{1,0:T(8,128)(2,1)S(1)} %pack_far.1.refs_1_), channel_id=1, source_target_pairs={{0,1},{1,0},{2,3},{3,2},{4,5},{5,4},{6,7},{7,6},{8,9},{9,8},{10,11... | collective-permute-start | bytes 184328 | tf_op jit(solution)/shard_map/ppermute | solution.py:22
  18.4 1.2 %collective-permute-start.8 = (bf16[40,768]{1,0:T(8,128)(2,1)S(1)}, bf16[40,768]{1,0:T(8,128)(2,1)S(1)}, u32[]{:S(2)}, u32[]{:S(2)}) collective-permute-start(bf16[40,768]{1,0:T(8,128)(2,1)S(1)} %collective-permute-done.6.refs_1_.refs_5_), channel_id=1, source_target_pairs={{0,1},{1,0},{2,3},{3,2},{4,5},{5,4},{6,7},{7,6},{8,9},{9,8},{10,11... | collective-permute-start | bytes 184328 | tf_op jit(solution)/shard_map/ppermute | solution.py:22
  20.4 4.4 %collective-permute-start.12 = (bf16[136,256]{1,0:T(8,128)(2,1)S(1)}, bf16[136,256]{1,0:T(8,128)(2,1)S(1)}, u32[]{:S(2)}, u32[]{:S(2)}) collective-permute-start(bf16[136,256]{1,0:T(8,128)(2,1)S(1)} %get-tuple-element.34.refs_0_), channel_id=1, source_target_pairs={{0,2},{1,3},{2,0},{3,1},{4,6},{5,7},{6,4},{7,5},{8,10},{9,11},{10,... | collective-permute-start | bytes 208904 | tf_op jit(solution)/shard_map/ppermute | solution.py:22
  23.1 6.5 %collective-permute-start.9 = (bf16[136,512]{1,0:T(8,128)(2,1)S(1)}, bf16[136,512]{1,0:T(8,128)(2,1)S(1)}, u32[]{:S(2)}, u32[]{:S(2)}) collective-permute-start(bf16[136,512]{1,0:T(8,128)(2,1)S(1)} %hidden_part.5.refs_4_), channel_id=1, source_target_pairs={{0,2},{1,3},{2,0},{3,1},{4,6},{5,7},{6,4},{7,5},{8,10},{9,11},{10,... | collective-permute-start | bytes 417800 | tf_op jit(solution)/shard_map/ppermute | solution.py:22
  24.8 6.8 %slice-start.3 = ((s8[12582912]{0:T(1024)(128)(4,1)}), s8[4194304]{0:T(1024)(128)(4,1)S(1)}, s32[]{:S(2)}) async-start(s8[12582912]{0:T(1024)(128)(4,1)} %bitcast.8), calls=%async_computation.3 | async-start | bytes 8388608
  24.8 6.8 %slice-start.4 = ((s8[12582912]{0:T(1024)(128)(4,1)}), s8[4194304]{0:T(1024)(128)(4,1)S(1)}, s32[]{:S(2)}) async-start(s8[12582912]{0:T(1024)(128)(4,1)} %bitcast.8), calls=%async_computation.4 | async-start | bytes 8388608
  26.4 5.1 %slice-start.5 = ((s8[12582912]{0:T(1024)(128)(4,1)}), s8[4194304]{0:T(1024)(128)(4,1)S(1)}, s32[]{:S(2)}) async-start(s8[12582912]{0:T(1024)(128)(4,1)} %bitcast.8), calls=%async_computation.5 | async-start | bytes 8388608
  26.4 6.7 %collective-permute-start.18 = (bf16[136,768]{1,0:T(8,128)(2,1)S(1)}, bf16[136,768]{1,0:T(8,128)(2,1)S(1)}, u32[]{:S(2)}, u32[]{:S(2)}) collective-permute-start(bf16[136,768]{1,0:T(8,128)(2,1)S(1)} %hidden_part.7.refs_2_), channel_id=1, source_target_pairs={{0,2},{1,3},{2,0},{3,1},{4,6},{5,7},{6,4},{7,5},{8,10},{9,11},{10,... | collective-permute-start | bytes 626696 | tf_op jit(solution)/shard_map/ppermute | solution.py:22
  28.1 1.3 %collective-permute-start.14 = (bf16[136,256]{1,0:T(8,128)(2,1)S(1)}, bf16[136,256]{1,0:T(8,128)(2,1)S(1)}, u32[]{:S(2)}, u32[]{:S(2)}) collective-permute-start(bf16[136,256]{1,0:T(8,128)(2,1)S(1)} %get-tuple-element.34.refs_0_), channel_id=1, source_target_pairs={{0,1},{1,0},{2,3},{3,2},{4,5},{5,4},{6,7},{7,6},{8,9},{9,8},{10,11... | collective-permute-start | bytes 208904 | tf_op jit(solution)/shard_map/ppermute | solution.py:22
  28.1 3.4 %collective-permute-start.16 = (bf16[136,512]{1,0:T(8,128)(2,1)S(1)}, bf16[136,512]{1,0:T(8,128)(2,1)S(1)}, u32[]{:S(2)}, u32[]{:S(2)}) collective-permute-start(bf16[136,512]{1,0:T(8,128)(2,1)S(1)} %hidden_part.5.refs_4_), channel_id=1, source_target_pairs={{0,1},{1,0},{2,3},{3,2},{4,5},{5,4},{6,7},{7,6},{8,9},{9,8},{10,11... | collective-permute-start | bytes 417800 | tf_op jit(solution)/shard_map/ppermute | solution.py:22
  28.6 5.0 %collective-permute-start.13 = (bf16[136,768]{1,0:T(8,128)(2,1)S(1)}, bf16[136,768]{1,0:T(8,128)(2,1)S(1)}, u32[]{:S(2)}, u32[]{:S(2)}) collective-permute-start(bf16[136,768]{1,0:T(8,128)(2,1)S(1)} %hidden_part.7.refs_2_), channel_id=1, source_target_pairs={{0,1},{1,0},{2,3},{3,2},{4,5},{5,4},{6,7},{7,6},{8,9},{9,8},{10,11... | collective-permute-start | bytes 626696 | tf_op jit(solution)/shard_map/ppermute | solution.py:22
  29.4 1.7 %collective-permute-start.15 = (bf16[136,256]{1,0:T(8,128)(2,1)S(1)}, bf16[136,256]{1,0:T(8,128)(2,1)S(1)}, u32[]{:S(2)}, u32[]{:S(2)}) collective-permute-start(bf16[136,256]{1,0:T(8,128)(2,1)S(1)} %collective-permute-done.12.refs_3_.refs_2_), channel_id=1, source_target_pairs={{0,1},{1,0},{2,3},{3,2},{4,5},{5,4},{6,7},{7,6},{8,9},{9,8},{10,11... | collective-permute-start | bytes 208904 | tf_op jit(solution)/shard_map/ppermute | solution.py:22
  29.6 4.1 %collective-permute-start.11 = (bf16[136,512]{1,0:T(8,128)(2,1)S(1)}, bf16[136,512]{1,0:T(8,128)(2,1)S(1)}, u32[]{:S(2)}, u32[]{:S(2)}) collective-permute-start(bf16[136,512]{1,0:T(8,128)(2,1)S(1)} %collective-permute-done.9.refs_3_.refs_0_), channel_id=1, source_target_pairs={{0,1},{1,0},{2,3},{3,2},{4,5},{5,4},{6,7},{7,6},{8,9},{9,8},{10,11... | collective-permute-start | bytes 417800 | tf_op jit(solution)/shard_map/ppermute | solution.py:22
  29.9 3.7 %slice-start.6 = ((s8[12582912]{0:T(1024)(128)(4,1)}), s8[4194304]{0:T(1024)(128)(4,1)S(1)}, s32[]{:S(2)}) async-start(s8[12582912]{0:T(1024)(128)(4,1)} %bitcast.10), calls=%async_computation.6 | async-start | bytes 8388608
  29.9 3.7 %slice-start.7 = ((s8[12582912]{0:T(1024)(128)(4,1)}), s8[4194304]{0:T(1024)(128)(4,1)S(1)}, s32[]{:S(2)}) async-start(s8[12582912]{0:T(1024)(128)(4,1)} %bitcast.10), calls=%async_computation.7 | async-start | bytes 8388608
  31.1 3.7 %slice-start.8 = ((s8[12582912]{0:T(1024)(128)(4,1)}), s8[4194304]{0:T(1024)(128)(4,1)S(1)}, s32[]{:S(2)}) async-start(s8[12582912]{0:T(1024)(128)(4,1)} %bitcast.10), calls=%async_computation.8 | async-start | bytes 8388608
  31.1 5.8 %collective-permute-start.10 = (bf16[136,512]{1,0:T(8,128)(2,1)S(1)}, bf16[136,512]{1,0:T(8,128)(2,1)S(1)}, u32[]{:S(2)}, u32[]{:S(2)}) collective-permute-start(bf16[136,512]{1,0:T(8,128)(2,1)S(1)} %hidden_part.6.refs_2_), channel_id=1, source_target_pairs={{0,2},{1,3},{2,0},{3,1},{4,6},{5,7},{6,4},{7,5},{8,10},{9,11},{10,... | collective-permute-start | bytes 417800 | tf_op jit(solution)/shard_map/ppermute | solution.py:22
  33.1 3.9 %collective-permute-start.19 = (bf16[136,768]{1,0:T(8,128)(2,1)S(1)}, bf16[136,768]{1,0:T(8,128)(2,1)S(1)}, u32[]{:S(2)}, u32[]{:S(2)}) collective-permute-start(bf16[136,768]{1,0:T(8,128)(2,1)S(1)} %hold.6.refs_0_), channel_id=1, source_target_pairs={{0,1},{1,0},{2,3},{3,2},{4,5},{5,4},{6,7},{7,6},{8,9},{9,8},{10,11... | collective-permute-start | bytes 626696 | tf_op jit(solution)/shard_map/ppermute | solution.py:22
  33.1 3.9 %collective-permute-start.20 = (bf16[136,512]{1,0:T(8,128)(2,1)S(1)}, bf16[136,512]{1,0:T(8,128)(2,1)S(1)}, u32[]{:S(2)}, u32[]{:S(2)}) collective-permute-start(bf16[136,512]{1,0:T(8,128)(2,1)S(1)} %hidden_part.6.refs_2_), channel_id=1, source_target_pairs={{0,1},{1,0},{2,3},{3,2},{4,5},{5,4},{6,7},{7,6},{8,9},{9,8},{10,11... | collective-permute-start | bytes 417800 | tf_op jit(solution)/shard_map/ppermute | solution.py:22
  36.9 6.3 %copy-start.1 = (bf16[64,768]{1,0:T(8,128)(2,1)S(1)}, bf16[64,768]{1,0:T(8,128)(2,1)}, u32[]{:S(2)}) copy-start(bf16[64,768]{1,0:T(8,128)(2,1)} %grad_ref.1) | copy-start | bytes 294916
  36.9 6.3 %copy-start.2 = (s32[64,2]{0,1:T(2,128)S(1)}, s32[64,2]{0,1:T(2,128)}, u32[]{:S(2)}) copy-start(s32[64,2]{0,1:T(2,128)} %param.8) | copy-start | bytes 1540
  36.9 6.3 %copy-start.3 = (f32[64,2]{0,1:T(2,128)S(1)}, f32[64,2]{0,1:T(2,128)}, u32[]{:S(2)}) copy-start(f32[64,2]{0,1:T(2,128)} %param.9) | copy-start | bytes 1540
  36.9 1.4 %collective-permute-start.17 = (bf16[136,512]{1,0:T(8,128)(2,1)S(1)}, bf16[136,512]{1,0:T(8,128)(2,1)S(1)}, u32[]{:S(2)}, u32[]{:S(2)}) collective-permute-start(bf16[136,512]{1,0:T(8,128)(2,1)S(1)} %hold.5.refs_0_), channel_id=1, source_target_pairs={{0,1},{1,0},{2,3},{3,2},{4,5},{5,4},{6,7},{7,6},{8,9},{9,8},{10,11... | collective-permute-start | bytes 417800 | tf_op jit(solution)/shard_map/ppermute | solution.py:22
  38.8 5.0 %collective-permute-start.21 = (bf16[204,128]{1,0:T(8,128)(2,1)S(1)}, bf16[204,128]{1,0:T(8,128)(2,1)S(1)}, u32[]{:S(2)}, u32[]{:S(2)}) collective-permute-start(bf16[204,128]{1,0:T(8,128)(2,1)S(1)} %get-tuple-element.36), channel_id=1, source_target_pairs={{0,4},{4,0},{8,12},{12,8},{1,5},{5,1},{9,13},{13,9},{2,6},{6,2},{1... | collective-permute-start | bytes 156680 | tf_op jit(solution)/shard_map/ppermute | solution.py:22
  38.8 6.7 %collective-permute-start.22 = (bf16[204,128]{1,0:T(8,128)(2,1)S(1)}, bf16[204,128]{1,0:T(8,128)(2,1)S(1)}, u32[]{:S(2)}, u32[]{:S(2)}) collective-permute-start(bf16[204,128]{1,0:T(8,128)(2,1)S(1)} %get-tuple-element.37), channel_id=1, source_target_pairs={{0,8},{4,12},{8,0},{12,4},{1,9},{5,13},{9,1},{13,5},{2,10},{6,14},... | collective-permute-start | bytes 156680 | tf_op jit(solution)/shard_map/ppermute | solution.py:22
  41.9 5.9 %collective-permute-start.23 = (bf16[204,128]{1,0:T(8,128)(2,1)S(1)}, bf16[204,128]{1,0:T(8,128)(2,1)S(1)}, u32[]{:S(2)}, u32[]{:S(2)}) collective-permute-start(bf16[204,128]{1,0:T(8,128)(2,1)S(1)} %get-tuple-element.38), channel_id=1, source_target_pairs={{0,12},{4,8},{8,4},{12,0},{1,13},{5,9},{9,5},{13,1},{2,14},{6,10},... | collective-permute-start | bytes 156680 | tf_op jit(solution)/shard_map/ppermute | solution.py:22
  48.1 3.6 %collective-permute-start.24 = (f32[2,64]{1,0:T(2,128)S(1)}, f32[2,64]{1,0:T(2,128)S(1)}, u32[]{:S(2)}, u32[]{:S(2)}) collective-permute-start(f32[2,64]{1,0:T(2,128)S(1)} %dots.1), channel_id=1, source_target_pairs={{0,2},{1,3},{2,0},{3,1},{4,6},{5,7},{6,4},{7,5},{8,10},{9,11},{10,... | collective-permute-start | bytes 1544 | tf_op jit(solution)/shard_map/ppermute | solution.py:22
  51.7 1.1 %collective-permute-start.25 = (f32[2,64]{1,0:T(2,128)S(1)}, f32[2,64]{1,0:T(2,128)S(1)}, u32[]{:S(2)}, u32[]{:S(2)}) collective-permute-start(f32[2,64]{1,0:T(2,128)S(1)} %add.6), channel_id=1, source_target_pairs={{0,1},{1,0},{2,3},{3,2},{4,5},{5,4},{6,7},{7,6},{8,9},{9,8},{10,11... | collective-permute-start | bytes 1544 | tf_op jit(solution)/shard_map/ppermute | solution.py:22

commit v12 on v11

--- a/solution.py
+++ b/solution.py
@@ -321,8 +321,9 @@
     near_across = swap(near, "tensor", 2)
     far = pack_far(arrived[2], arrived[3], tokens.shape[1])
     far_across = swap(far, "tensor", 2)
-    near_across = hold(near_across, [far_across])
-    xs = [near, far, swap(near, "tensor", 1), swap(far, "tensor", 1), near_across, far_across]
+    near_side, far_side = swap(near, "tensor", 1), swap(far, "tensor", 1)
+    near_across = hold(near_across, [far_across, near_side, far_side])
+    xs = [near, far, near_side, far_side, near_across, far_across]
     xs += [swap(near_across, "tensor", 1), swap(far_across, "tensor", 1)]
 
     hits, routes, picks, grads = prepare(me, ids_t, probs_t, out_grad)

time: 53.6 us -> 54 us (level)
  transfers between devices with their start and end apart: 26 -> 26, of which waited for: 15 -> 13; matrix products, arithmetic and copies ran while one was open for 0% -> 0% of each run, Pallas kernels for 14% -> 14%
where the time goes in v12:
time: 54 us; the launch traced here: 53.9 us
  waiting for transfers between devices  20.8 us (39%)
  starting transfers between devices  20.5 us (38%)
  Pallas kernels  10 us (19%)
  local copies, waits for them, and re-layouts  1.06 us (2%)
  between operations  0.92 us (2%)
  other arithmetic  0.57 us (1%)
    ppermute x26, waiting for transfers between devices, swap(): return lax.ppermute(value, axis, [(i, i ^ bit) for i in range(size)])  20.8 us
    ppermute x26, starting transfers between devices, swap(): return lax.ppermute(value, axis, [(i, i ^ bit) for i in range(size)])  20.5 us
    pallas_call x4, Pallas kernels, hidden_part(): pl.pallas_call(functools.partial(hidden_kernel, joined, parts, start), ou...  4.6 us
    pallas_call x4, Pallas kernels, down_part(): pl.pallas_call(functools.partial(down_kernel, len(pieces), where, slab, h...  2.55 us
    pallas_call x1, Pallas kernels, select_rows(): pl.pallas_call(select_kernel, out_shape=[jax.ShapeDtypeStruct((MOST, widt...  1.3 us
  transfers between devices with their start and end apart: 26, of which 13 were waited for; matrix products, arithmetic and copies ran while one was open for 0% of the time, Pallas kernels for 14%

profile of v12, /device:TPU:0, one launch (start us, length us, event | category | flops | bytes accessed | tf_op | source)
XLA Modules:
  0.0 53.9 jit_solution(2640723969041620376)
XLA Ops:
  0.6 0.0 slice-start
  0.6 0.0 slice-start.1
  0.7 0.0 slice-start.2
  0.7 1.3 %select_rows.1 = (bf16[34,768]{1,0:T(8,128)(2,1)S(1)}, bf16[204,128]{1,0:T(8,128)(2,1)S(1)}, bf16[204,128]{1,0:T(8,128)(2,1)S(1)}, bf16[204,128]{1,0:T(8,128)(2,1)S(1)}) custom-call(s32[1]{0:T(128)} %bitcast.me_ref, s32[1]{0:T(128)} %bitcast.3.t_ref, s32[2,64]{1,0:T(2,128)} %bitcast.12, bf16[64,768]{1,0:T(8,128)(2,1)} %tokens_hbm.1), custom_call_target="tpu_custom_call" | custom-call | flops 8000000000 | bytes 1000 | tf_op jit(solution)/shard_map/select_rows/pallas_call | solution.py:82
  2.0 3.1 %collective-permute-start = (bf16[204,128]{1,0:T(8,128)(2,1)S(1)}, bf16[204,128]{1,0:T(8,128)(2,1)S(1)}, u32[]{:S(2)}, u32[]{:S(2)}) collective-permute-start(bf16[204,128]{1,0:T(8,128)(2,1)S(1)} %get-tuple-element.30), channel_id=1, source_target_pairs={{0,4},{4,0},{8,12},{12,8},{1,5},{5,1},{9,13},{13,9},{2,6},{6,2},{1... | collective-permute-start | bytes 156680 | tf_op jit(solution)/shard_map/ppermute | solution.py:22
  5.1 2.6 %collective-permute-start.1 = (bf16[204,128]{1,0:T(8,128)(2,1)S(1)}, bf16[204,128]{1,0:T(8,128)(2,1)S(1)}, u32[]{:S(2)}, u32[]{:S(2)}) collective-permute-start(bf16[204,128]{1,0:T(8,128)(2,1)S(1)} %get-tuple-element.31), channel_id=1, source_target_pairs={{0,8},{4,12},{8,0},{12,4},{1,9},{5,13},{9,1},{13,5},{2,10},{6,14},... | collective-permute-start | bytes 156680 | tf_op jit(solution)/shard_map/ppermute | solution.py:22
  7.7 3.5 %collective-permute-done.1.refs_1_.third_ref = bf16[204,128]{1,0:T(8,128)(2,1)S(1)} collective-permute-done((bf16[204,128]{1,0:T(8,128)(2,1)S(1)}, bf16[204,128]{1,0:T(8,128)(2,1)S(1)}, u32[]{:S(2)}, u32[]{:S(2)}) %collective-permute-start.1) | collective-permute-done | bytes 52256 | tf_op jit(solution)/shard_map/ppermute | solution.py:22
  11.2 1.6 %collective-permute-start.5 = (bf16[96,768]{1,0:T(8,128)(2,1)S(1)}, bf16[96,768]{1,0:T(8,128)(2,1)S(1)}, u32[]{:S(2)}, u32[]{:S(2)}) collective-permute-start(bf16[96,768]{1,0:T(8,128)(2,1)S(1)} %pack_near.1.refs_0_), channel_id=1, source_target_pairs={{0,2},{1,3},{2,0},{3,1},{4,6},{5,7},{6,4},{7,5},{8,10},{9,11},{10,... | collective-permute-start | bytes 442376 | tf_op jit(solution)/shard_map/ppermute | solution.py:22
  12.7 0.0 collective-permute-start.3
  12.7 0.9 %collective-permute-done.2.fourth_ref = bf16[204,128]{1,0:T(8,128)(2,1)S(1)} collective-permute-done((bf16[204,128]{1,0:T(8,128)(2,1)S(1)}, bf16[204,128]{1,0:T(8,128)(2,1)S(1)}, u32[]{:S(2)}, u32[]{:S(2)}) %collective-permute-start.2) | collective-permute-done | bytes 52256 | tf_op jit(solution)/shard_map/ppermute | solution.py:22
  13.6 1.6 %collective-permute-start.6 = (bf16[40,768]{1,0:T(8,128)(2,1)S(1)}, bf16[40,768]{1,0:T(8,128)(2,1)S(1)}, u32[]{:S(2)}, u32[]{:S(2)}) collective-permute-start(bf16[40,768]{1,0:T(8,128)(2,1)S(1)} %pack_far.1.refs_1_), channel_id=1, source_target_pairs={{0,2},{1,3},{2,0},{3,1},{4,6},{5,7},{6,4},{7,5},{8,10},{9,11},{10,... | collective-permute-start | bytes 184328 | tf_op jit(solution)/shard_map/ppermute | solution.py:22
  15.2 0.0 collective-permute-start.4
  15.2 2.7 %collective-permute-done.6.refs_1_.refs_5_ = bf16[40,768]{1,0:T(8,128)(2,1)S(1)} collective-permute-done((bf16[40,768]{1,0:T(8,128)(2,1)S(1)}, bf16[40,768]{1,0:T(8,128)(2,1)S(1)}, u32[]{:S(2)}, u32[]{:S(2)}) %collective-permute-start.6) | collective-permute-done | bytes 61472 | tf_op jit(solution)/shard_map/ppermute | solution.py:22
  17.9 0.0 collective-permute-done.5.refs_0_
  17.9 0.0 collective-permute-done.3.refs_2_
  17.9 0.1 collective-permute-start.7
  18.0 0.5 collective-permute-start.8
  18.5 0.9 %collective-permute-done.8.refs_7_ = bf16[40,768]{1,0:T(8,128)(2,1)S(1)} collective-permute-done((bf16[40,768]{1,0:T(8,128)(2,1)S(1)}, bf16[40,768]{1,0:T(8,128)(2,1)S(1)}, u32[]{:S(2)}, u32[]{:S(2)}) %collective-permute-start.8) | collective-permute-done | bytes 61472 | tf_op jit(solution)/shard_map/ppermute | solution.py:22
  19.5 0.7 %hidden_part.4 = (bf16[136,256]{1,0:T(8,128)(2,1)S(1)}, bf16[4,136,768]{2,1,0:T(8,128)(2,1)S(1)}) custom-call(s32[1]{0:T(128)} %bitcast.3.t_ref, bf16[96,768]{1,0:T(8,128)(2,1)S(1)} %pack_near.1.refs_0_, bf16[40,768]{1,0:T(8,128)(2,1)S(1)} %pack_far.1.refs_1_, bf16[96,768]{1,0:T(8,128)(2,1)S(1)} %collective-permute-done.3.refs_2_, ...), custom_call_target="tpu_custom_call" | custom-call | flops 1000 | bytes 1000 | tf_op jit(solution)/shard_map/hidden_part/pallas_call | solution.py:177
  20.2 1.5 %collective-permute-start.12 = (bf16[136,256]{1,0:T(8,128)(2,1)S(1)}, bf16[136,256]{1,0:T(8,128)(2,1)S(1)}, u32[]{:S(2)}, u32[]{:S(2)}) collective-permute-start(bf16[136,256]{1,0:T(8,128)(2,1)S(1)} %get-tuple-element.34.refs_0_), channel_id=1, source_target_pairs={{0,2},{1,3},{2,0},{3,1},{4,6},{5,7},{6,4},{7,5},{8,10},{9,11},{10,... | collective-permute-start | bytes 208904 | tf_op jit(solution)/shard_map/ppermute | solution.py:22
  21.7 1.1 %hidden_part.5.refs_4_ = bf16[136,512]{1,0:T(8,128)(2,1)S(1)} custom-call(s32[1]{0:T(128)} %bitcast.3.t_ref, bf16[4,136,768]{2,1,0:T(8,128)(2,1)S(1)} %get-tuple-element.33.refs_0_, bf16[1,3072,2048]{2,1,0:T(8,128)(2,1)S(1)} %bitcast.7, bf16[1,3072,2048]{2,1,0:T(8,128)(2,1)S(1)} %copy-done), custom_call_target="tpu_custom_call" | custom-call | flops 1000 | bytes 1000 | tf_op jit(solution)/shard_map/hidden_part/pallas_call | solution.py:177
  22.9 0.6 %collective-permute-start.9 = (bf16[136,512]{1,0:T(8,128)(2,1)S(1)}, bf16[136,512]{1,0:T(8,128)(2,1)S(1)}, u32[]{:S(2)}, u32[]{:S(2)}) collective-permute-start(bf16[136,512]{1,0:T(8,128)(2,1)S(1)} %hidden_part.5.refs_4_), channel_id=1, source_target_pairs={{0,2},{1,3},{2,0},{3,1},{4,6},{5,7},{6,4},{7,5},{8,10},{9,11},{10,... | collective-permute-start | bytes 417800 | tf_op jit(solution)/shard_map/ppermute | solution.py:22
  23.5 1.1 %collective-permute-done.12.refs_3_.refs_2_ = bf16[136,256]{1,0:T(8,128)(2,1)S(1)} collective-permute-done((bf16[136,256]{1,0:T(8,128)(2,1)S(1)}, bf16[136,256]{1,0:T(8,128)(2,1)S(1)}, u32[]{:S(2)}, u32[]{:S(2)}) %collective-permute-start.12) | collective-permute-done | bytes 69664 | tf_op jit(solution)/shard_map/ppermute | solution.py:22
  24.6 1.6 %hidden_part.7.refs_2_ = bf16[136,768]{1,0:T(8,128)(2,1)S(1)} custom-call(s32[1]{0:T(128)} %bitcast.3.t_ref, bf16[4,136,768]{2,1,0:T(8,128)(2,1)S(1)} %get-tuple-element.33.refs_0_, bf16[1,3072,2048]{2,1,0:T(8,128)(2,1)S(1)} %bitcast.7, bf16[1,3072,2048]{2,1,0:T(8,128)(2,1)S(1)} %copy-done, bf16[136,256]{1,0:T(8,128)(2,1)S(1)} %collective-permute-done.12.refs_3_.refs_2_), custom_call_target="tpu_custom_call" | custom-call | flops 1000 | bytes 1000 | tf_op jit(solution)/shard_map/hidden_part/pallas_call | solution.py:177
  26.3 0.0 slice-start.5
  26.3 1.6 %collective-permute-start.18 = (bf16[136,768]{1,0:T(8,128)(2,1)S(1)}, bf16[136,768]{1,0:T(8,128)(2,1)S(1)}, u32[]{:S(2)}, u32[]{:S(2)}) collective-permute-start(bf16[136,768]{1,0:T(8,128)(2,1)S(1)} %hidden_part.7.refs_2_), channel_id=1, source_target_pairs={{0,2},{1,3},{2,0},{3,1},{4,6},{5,7},{6,4},{7,5},{8,10},{9,11},{10,... | collective-permute-start | bytes 626696 | tf_op jit(solution)/shard_map/ppermute | solution.py:22
  27.9 0.5 collective-permute-start.16
  28.4 0.0 collective-permute-start.13
  28.4 0.7 %collective-permute-done.14.refs_1_ = bf16[136,256]{1,0:T(8,128)(2,1)S(1)} collective-permute-done((bf16[136,256]{1,0:T(8,128)(2,1)S(1)}, bf16[136,256]{1,0:T(8,128)(2,1)S(1)}, u32[]{:S(2)}, u32[]{:S(2)}) %collective-permute-start.14) | collective-permute-done | bytes 69664 | tf_op jit(solution)/shard_map/ppermute | solution.py:22
  29.1 0.2 collective-permute-start.15
  29.3 0.0 collective-permute-done.9.refs_3_.refs_0_
  29.3 0.4 collective-permute-start.11
  29.7 1.2 %hidden_part.6.refs_2_ = bf16[136,512]{1,0:T(8,128)(2,1)S(1)} custom-call(s32[1]{0:T(128)} %bitcast.3.t_ref, bf16[4,136,768]{2,1,0:T(8,128)(2,1)S(1)} %get-tuple-element.33.refs_0_, bf16[1,3072,2048]{2,1,0:T(8,128)(2,1)S(1)} %bitcast.7, bf16[1,3072,2048]{2,1,0:T(8,128)(2,1)S(1)} %copy-done, bf16[136,512]{1,0:T(8,128)(2,1)S(1)} %collective-permute-done.9.refs_3_.refs_0_), custom_call_target="tpu_custom_call" | custom-call | flops 1000 | bytes 1000 | tf_op jit(solution)/shard_map/hidden_part/pallas_call | solution.py:177
  30.8 0.0 slice-start.8
  30.8 0.0 collective-permute-done.15.refs_3_
  30.8 0.6 %collective-permute-start.10 = (bf16[136,512]{1,0:T(8,128)(2,1)S(1)}, bf16[136,512]{1,0:T(8,128)(2,1)S(1)}, u32[]{:S(2)}, u32[]{:S(2)}) collective-permute-start(bf16[136,512]{1,0:T(8,128)(2,1)S(1)} %hidden_part.6.refs_2_), channel_id=1, source_target_pairs={{0,2},{1,3},{2,0},{3,1},{4,6},{5,7},{6,4},{7,5},{8,10},{9,11},{10,... | collective-permute-start | bytes 417800 | tf_op jit(solution)/shard_map/ppermute | solution.py:22
  31.4 0.6 %down_part.4.refs_5_.refs_1_ = f32[136,768]{1,0:T(8,128)S(1)} custom-call(s32[1]{0:T(128)} %bitcast.3.t_ref, bf16[136,256]{1,0:T(8,128)(2,1)S(1)} %get-tuple-element.34.refs_0_, bf16[136,256]{1,0:T(8,128)(2,1)S(1)} %collective-permute-done.14.refs_1_, bf16[136,256]{1,0:T(8,128)(2,1)S(1)} %collective-permute-done.12.refs_3_.refs_2_, ...), custom_call_target="tpu_custom_call" | custom-call | flops 427819008 | bytes 1000 | tf_op jit(solution)/shard_map/down_part/pallas_call | solution.py:215
  32.1 0.9 %collective-permute-done.18.refs_0_ = bf16[136,768]{1,0:T(8,128)(2,1)S(1)} collective-permute-done((bf16[136,768]{1,0:T(8,128)(2,1)S(1)}, bf16[136,768]{1,0:T(8,128)(2,1)S(1)}, u32[]{:S(2)}, u32[]{:S(2)}) %collective-permute-start.18) | collective-permute-done | bytes 208928 | tf_op jit(solution)/shard_map/ppermute | solution.py:22
  33.0 0.0 collective-permute-start.19
  33.0 0.5 collective-permute-start.20
  33.5 0.0 collective-permute-done.13.refs_3_
  33.5 1.0 %slice-done.8 = s8[4194304]{0:T(1024)(128)(4,1)S(1)} async-done(((s8[12582912]{0:T(1024)(128)(4,1)}), s8[4194304]{0:T(1024)(128)(4,1)S(1)}, s32[]{:S(2)}) %slice-start.8) | async-done | bytes 4194328
  34.5 0.7 %down_part.5.refs_1_.refs_5_ = f32[136,768]{1,0:T(8,128)S(1)} custom-call(s32[1]{0:T(128)} %bitcast.3.t_ref, bf16[136,512]{1,0:T(8,128)(2,1)S(1)} %collective-permute-done.9.refs_3_.refs_0_, bf16[136,512]{1,0:T(8,128)(2,1)S(1)} %collective-permute-done.11.refs_1_, bf16[136,768]{1,0:T(8,128)(2,1)S(1)} %hidden_part.7.refs_2_, ...), custom_call_target="tpu_custom_call" | custom-call | flops 534773760 | bytes 1000 | tf_op jit(solution)/shard_map/down_part/pallas_call | solution.py:215
  35.3 1.3 %collective-permute-done.10.refs_0_ = bf16[136,512]{1,0:T(8,128)(2,1)S(1)} collective-permute-done((bf16[136,512]{1,0:T(8,128)(2,1)S(1)}, bf16[136,512]{1,0:T(8,128)(2,1)S(1)}, u32[]{:S(2)}, u32[]{:S(2)}) %collective-permute-start.10) | collective-permute-done | bytes 139296 | tf_op jit(solution)/shard_map/ppermute | solution.py:22
  36.6 0.1 collective-permute-start.17
  36.7 0.0 collective-permute-done.20.refs_3_
  36.7 0.0 collective-permute-done.19.refs_1_
  36.7 0.8 %down_part.6.refs_3_ = f32[136,768]{1,0:T(8,128)S(1)} custom-call(s32[1]{0:T(128)} %bitcast.3.t_ref, bf16[136,768]{1,0:T(8,128)(2,1)S(1)} %hold.6.refs_0_, bf16[136,768]{1,0:T(8,128)(2,1)S(1)} %collective-permute-done.19.refs_1_, bf16[136,512]{1,0:T(8,128)(2,1)S(1)} %hidden_part.6.refs_2_, bf16[136,512]{1,0:T(8,128)(2,1)S(1)} %collective-permute-done.20.refs_3_, ...), custom_call_target="tpu_custom_call" | custom-call | flops 534773760 | bytes 1000 | tf_op jit(solution)/shard_map/down_part/pallas_call | solution.py:215
  37.5 0.6 %collective-permute-done.17.refs_1_ = bf16[136,512]{1,0:T(8,128)(2,1)S(1)} collective-permute-done((bf16[136,512]{1,0:T(8,128)(2,1)S(1)}, bf16[136,512]{1,0:T(8,128)(2,1)S(1)}, u32[]{:S(2)}, u32[]{:S(2)}) %collective-permute-start.17) | collective-permute-done | bytes 139296 | tf_op jit(solution)/shard_map/ppermute | solution.py:22
  38.1 0.4 down_part.7
  38.5 0.6 %collective-permute-start.21 = (bf16[204,128]{1,0:T(8,128)(2,1)S(1)}, bf16[204,128]{1,0:T(8,128)(2,1)S(1)}, u32[]{:S(2)}, u32[]{:S(2)}) collective-permute-start(bf16[204,128]{1,0:T(8,128)(2,1)S(1)} %get-tuple-element.36), channel_id=1, source_target_pairs={{0,4},{4,0},{8,12},{12,8},{1,5},{5,1},{9,13},{13,9},{2,6},{6,2},{1... | collective-permute-start | bytes 156680 | tf_op jit(solution)/shard_map/ppermute | solution.py:22
  39.1 3.3 %collective-permute-start.22 = (bf16[204,128]{1,0:T(8,128)(2,1)S(1)}, bf16[204,128]{1,0:T(8,128)(2,1)S(1)}, u32[]{:S(2)}, u32[]{:S(2)}) collective-permute-start(bf16[204,128]{1,0:T(8,128)(2,1)S(1)} %get-tuple-element.37), channel_id=1, source_target_pairs={{0,8},{4,12},{8,0},{12,4},{1,9},{5,13},{9,1},{13,5},{2,10},{6,14},... | collective-permute-start | bytes 156680 | tf_op jit(solution)/shard_map/ppermute | solution.py:22
  42.4 0.5 %collective-permute-start.23 = (bf16[204,128]{1,0:T(8,128)(2,1)S(1)}, bf16[204,128]{1,0:T(8,128)(2,1)S(1)}, u32[]{:S(2)}, u32[]{:S(2)}) collective-permute-start(bf16[204,128]{1,0:T(8,128)(2,1)S(1)} %get-tuple-element.38), channel_id=1, source_target_pairs={{0,12},{4,8},{8,4},{12,0},{1,13},{5,9},{9,5},{13,1},{2,14},{6,10},... | collective-permute-start | bytes 156680 | tf_op jit(solution)/shard_map/ppermute | solution.py:22
  42.9 0.3 prepare.1
  43.3 0.0 collective-permute-done.21.refs_5_.refs_9_
  43.3 2.5 %collective-permute-done.22.refs_6_.refs_10_ = bf16[204,128]{1,0:T(8,128)(2,1)S(1)} collective-permute-done((bf16[204,128]{1,0:T(8,128)(2,1)S(1)}, bf16[204,128]{1,0:T(8,128)(2,1)S(1)}, u32[]{:S(2)}, u32[]{:S(2)}) %collective-permute-start.22) | collective-permute-done | bytes 52256 | tf_op jit(solution)/shard_map/ppermute | solution.py:22
  45.8 2.6 %collective-permute-done.23.refs_7_.refs_11_ = bf16[204,128]{1,0:T(8,128)(2,1)S(1)} collective-permute-done((bf16[204,128]{1,0:T(8,128)(2,1)S(1)}, bf16[204,128]{1,0:T(8,128)(2,1)S(1)}, u32[]{:S(2)}, u32[]{:S(2)}) %collective-permute-start.23) | collective-permute-done | bytes 52256 | tf_op jit(solution)/shard_map/ppermute | solution.py:22
  48.3 0.2 dots.1
  48.5 0.8 %collective-permute-start.24 = (f32[2,64]{1,0:T(2,128)S(1)}, f32[2,64]{1,0:T(2,128)S(1)}, u32[]{:S(2)}, u32[]{:S(2)}) collective-permute-start(f32[2,64]{1,0:T(2,128)S(1)} %dots.1), channel_id=1, source_target_pairs={{0,2},{1,3},{2,0},{3,1},{4,6},{5,7},{6,4},{7,5},{8,10},{9,11},{10,... | collective-permute-start | bytes 1544 | tf_op jit(solution)/shard_map/ppermute | solution.py:22
  49.3 0.9 %mix.1 = (bf16[64,768]{1,0:T(8,128)(2,1)}, f32[8,128]{1,0:T(8,128)S(1)}) custom-call(f32[64,128]{1,0:T(8,128)S(1)} %get-tuple-element.24.routes_ref, f32[204,64]{1,0:T(8,128)S(1)} %get-tuple-element.25.refs_0_, f32[204,64]{1,0:T(8,128)S(1)} %get-tuple-element.26.refs_1_, f32[204,64]{1,0:T(8,128)S(1)} %get-tuple-element.27.refs_2_, ...), custom_call_target="tpu_custom_call" | custom-call | flops 1000000000 | bytes 1000 | tf_op jit(solution)/shard_map/mix/pallas_call | solution.py:296
  50.3 1.9 %collective-permute-done.24.refs_0_ = f32[2,64]{1,0:T(2,128)S(1)} collective-permute-done((f32[2,64]{1,0:T(2,128)S(1)}, f32[2,64]{1,0:T(2,128)S(1)}, u32[]{:S(2)}, u32[]{:S(2)}) %collective-permute-start.24) | collective-permute-done | bytes 544 | tf_op jit(solution)/shard_map/ppermute | solution.py:22
  52.2 0.0 collective-permute-start.25
  52.2 1.1 %collective-permute-done.25 = f32[2,64]{1,0:T(2,128)S(1)} collective-permute-done((f32[2,64]{1,0:T(2,128)S(1)}, f32[2,64]{1,0:T(2,128)S(1)}, u32[]{:S(2)}, u32[]{:S(2)}) %collective-permute-start.25) | collective-permute-done | bytes 544 | tf_op jit(solution)/shard_map/ppermute | solution.py:22
  53.3 0.6 %add_bitcast_fusion = f32[64,2]{0,1:T(2,128)} fusion(f32[2,64]{1,0:T(2,128)S(1)} %add.6, f32[2,64]{1,0:T(2,128)S(1)} %collective-permute-done.25), kind=kLoop, calls=%fused_computation | loop fusion | flops 128 | bytes 1536 | tf_op jit(solution)/shard_map/transpose | solution.py:356
  (37 shorter events, 0.1 us)
Async XLA Ops:
  0.6 18.8 %slice-start = ((s8[12582912]{0:T(1024)(128)(4,1)}), s8[4194304]{0:T(1024)(128)(4,1)S(1)}, s32[]{:S(2)}) async-start(s8[12582912]{0:T(1024)(128)(4,1)} %bitcast.6), calls=%async_computation | async-start | bytes 8388608
  0.6 18.8 %slice-start.1 = ((s8[12582912]{0:T(1024)(128)(4,1)}), s8[4194304]{0:T(1024)(128)(4,1)S(1)}, s32[]{:S(2)}) async-start(s8[12582912]{0:T(1024)(128)(4,1)} %bitcast.6), calls=%async_computation.1 | async-start | bytes 8388608
  0.7 18.8 %slice-start.2 = ((s8[12582912]{0:T(1024)(128)(4,1)}), s8[4194304]{0:T(1024)(128)(4,1)S(1)}, s32[]{:S(2)}) async-start(s8[12582912]{0:T(1024)(128)(4,1)} %bitcast.6), calls=%async_computation.2 | async-start | bytes 8388608
  0.7 18.8 %copy-start = (bf16[1,3072,2048]{2,1,0:T(8,128)(2,1)S(1)}, bf16[1,3072,2048]{2,1,0:T(8,128)(2,1)}, u32[]{:S(2)}) copy-start(bf16[1,3072,2048]{2,1,0:T(8,128)(2,1)} %refs_2_.6) | copy-start | bytes 37748740
  2.0 5.7 %collective-permute-start = (bf16[204,128]{1,0:T(8,128)(2,1)S(1)}, bf16[204,128]{1,0:T(8,128)(2,1)S(1)}, u32[]{:S(2)}, u32[]{:S(2)}) collective-permute-start(bf16[204,128]{1,0:T(8,128)(2,1)S(1)} %get-tuple-element.30), channel_id=1, source_target_pairs={{0,4},{4,0},{8,12},{12,8},{1,5},{5,1},{9,13},{13,9},{2,6},{6,2},{1... | collective-permute-start | bytes 156680 | tf_op jit(solution)/shard_map/ppermute | solution.py:22
  5.1 6.1 %collective-permute-start.1 = (bf16[204,128]{1,0:T(8,128)(2,1)S(1)}, bf16[204,128]{1,0:T(8,128)(2,1)S(1)}, u32[]{:S(2)}, u32[]{:S(2)}) collective-permute-start(bf16[204,128]{1,0:T(8,128)(2,1)S(1)} %get-tuple-element.31), channel_id=1, source_target_pairs={{0,8},{4,12},{8,0},{12,4},{1,9},{5,13},{9,1},{13,5},{2,10},{6,14},... | collective-permute-start | bytes 156680 | tf_op jit(solution)/shard_map/ppermute | solution.py:22
  7.7 5.9 %collective-permute-start.2 = (bf16[204,128]{1,0:T(8,128)(2,1)S(1)}, bf16[204,128]{1,0:T(8,128)(2,1)S(1)}, u32[]{:S(2)}, u32[]{:S(2)}) collective-permute-start(bf16[204,128]{1,0:T(8,128)(2,1)S(1)} %get-tuple-element.32), channel_id=1, source_target_pairs={{0,12},{4,8},{8,4},{12,0},{1,13},{5,9},{9,5},{13,1},{2,14},{6,10},... | collective-permute-start | bytes 156680 | tf_op jit(solution)/shard_map/ppermute | solution.py:22
  11.2 6.7 %collective-permute-start.5 = (bf16[96,768]{1,0:T(8,128)(2,1)S(1)}, bf16[96,768]{1,0:T(8,128)(2,1)S(1)}, u32[]{:S(2)}, u32[]{:S(2)}) collective-permute-start(bf16[96,768]{1,0:T(8,128)(2,1)S(1)} %pack_near.1.refs_0_), channel_id=1, source_target_pairs={{0,2},{1,3},{2,0},{3,1},{4,6},{5,7},{6,4},{7,5},{8,10},{9,11},{10,... | collective-permute-start | bytes 442376 | tf_op jit(solution)/shard_map/ppermute | solution.py:22
  12.7 5.2 %collective-permute-start.3 = (bf16[96,768]{1,0:T(8,128)(2,1)S(1)}, bf16[96,768]{1,0:T(8,128)(2,1)S(1)}, u32[]{:S(2)}, u32[]{:S(2)}) collective-permute-start(bf16[96,768]{1,0:T(8,128)(2,1)S(1)} %pack_near.1.refs_0_), channel_id=1, source_target_pairs={{0,1},{1,0},{2,3},{3,2},{4,5},{5,4},{6,7},{7,6},{8,9},{9,8},{10,11... | collective-permute-start | bytes 442376 | tf_op jit(solution)/shard_map/ppermute | solution.py:22
  13.6 4.3 %collective-permute-start.6 = (bf16[40,768]{1,0:T(8,128)(2,1)S(1)}, bf16[40,768]{1,0:T(8,128)(2,1)S(1)}, u32[]{:S(2)}, u32[]{:S(2)}) collective-permute-start(bf16[40,768]{1,0:T(8,128)(2,1)S(1)} %pack_far.1.refs_1_), channel_id=1, source_target_pairs={{0,2},{1,3},{2,0},{3,1},{4,6},{5,7},{6,4},{7,5},{8,10},{9,11},{10,... | collective-permute-start | bytes 184328 | tf_op jit(solution)/shard_map/ppermute | solution.py:22
  15.2 2.7 %collective-permute-start.4 = (bf16[40,768]{1,0:T(8,128)(2,1)S(1)}, bf16[40,768]{1,0:T(8,128)(2,1)S(1)}, u32[]{:S(2)}, u32[]{:S(2)}) collective-permute-start(bf16[40,768]{1,0:T(8,128)(2,1)S(1)} %pack_far.1.refs_1_), channel_id=1, source_target_pairs={{0,1},{1,0},{2,3},{3,2},{4,5},{5,4},{6,7},{7,6},{8,9},{9,8},{10,11... | collective-permute-start | bytes 184328 | tf_op jit(solution)/shard_map/ppermute | solution.py:22
  17.9 1.5 %collective-permute-start.7 = (bf16[96,768]{1,0:T(8,128)(2,1)S(1)}, bf16[96,768]{1,0:T(8,128)(2,1)S(1)}, u32[]{:S(2)}, u32[]{:S(2)}) collective-permute-start(bf16[96,768]{1,0:T(8,128)(2,1)S(1)} %hold.4.refs_4_), channel_id=1, source_target_pairs={{0,1},{1,0},{2,3},{3,2},{4,5},{5,4},{6,7},{7,6},{8,9},{9,8},{10,11... | collective-permute-start | bytes 442376 | tf_op jit(solution)/shard_map/ppermute | solution.py:22
  18.0 1.4 %collective-permute-start.8 = (bf16[40,768]{1,0:T(8,128)(2,1)S(1)}, bf16[40,768]{1,0:T(8,128)(2,1)S(1)}, u32[]{:S(2)}, u32[]{:S(2)}) collective-permute-start(bf16[40,768]{1,0:T(8,128)(2,1)S(1)} %collective-permute-done.6.refs_1_.refs_5_), channel_id=1, source_target_pairs={{0,1},{1,0},{2,3},{3,2},{4,5},{5,4},{6,7},{7,6},{8,9},{9,8},{10,11... | collective-permute-start | bytes 184328 | tf_op jit(solution)/shard_map/ppermute | solution.py:22
  20.2 4.5 %collective-permute-start.12 = (bf16[136,256]{1,0:T(8,128)(2,1)S(1)}, bf16[136,256]{1,0:T(8,128)(2,1)S(1)}, u32[]{:S(2)}, u32[]{:S(2)}) collective-permute-start(bf16[136,256]{1,0:T(8,128)(2,1)S(1)} %get-tuple-element.34.refs_0_), channel_id=1, source_target_pairs={{0,2},{1,3},{2,0},{3,1},{4,6},{5,7},{6,4},{7,5},{8,10},{9,11},{10,... | collective-permute-start | bytes 208904 | tf_op jit(solution)/shard_map/ppermute | solution.py:22
  22.9 6.4 %collective-permute-start.9 = (bf16[136,512]{1,0:T(8,128)(2,1)S(1)}, bf16[136,512]{1,0:T(8,128)(2,1)S(1)}, u32[]{:S(2)}, u32[]{:S(2)}) collective-permute-start(bf16[136,512]{1,0:T(8,128)(2,1)S(1)} %hidden_part.5.refs_4_), channel_id=1, source_target_pairs={{0,2},{1,3},{2,0},{3,1},{4,6},{5,7},{6,4},{7,5},{8,10},{9,11},{10,... | collective-permute-start | bytes 417800 | tf_op jit(solution)/shard_map/ppermute | solution.py:22
  24.6 6.8 %slice-start.3 = ((s8[12582912]{0:T(1024)(128)(4,1)}), s8[4194304]{0:T(1024)(128)(4,1)S(1)}, s32[]{:S(2)}) async-start(s8[12582912]{0:T(1024)(128)(4,1)} %bitcast.8), calls=%async_computation.3 | async-start | bytes 8388608
  24.6 6.8 %slice-start.4 = ((s8[12582912]{0:T(1024)(128)(4,1)}), s8[4194304]{0:T(1024)(128)(4,1)S(1)}, s32[]{:S(2)}) async-start(s8[12582912]{0:T(1024)(128)(4,1)} %bitcast.8), calls=%async_computation.4 | async-start | bytes 8388608
  26.3 5.1 %slice-start.5 = ((s8[12582912]{0:T(1024)(128)(4,1)}), s8[4194304]{0:T(1024)(128)(4,1)S(1)}, s32[]{:S(2)}) async-start(s8[12582912]{0:T(1024)(128)(4,1)} %bitcast.8), calls=%async_computation.5 | async-start | bytes 8388608
  26.3 6.7 %collective-permute-start.18 = (bf16[136,768]{1,0:T(8,128)(2,1)S(1)}, bf16[136,768]{1,0:T(8,128)(2,1)S(1)}, u32[]{:S(2)}, u32[]{:S(2)}) collective-permute-start(bf16[136,768]{1,0:T(8,128)(2,1)S(1)} %hidden_part.7.refs_2_), channel_id=1, source_target_pairs={{0,2},{1,3},{2,0},{3,1},{4,6},{5,7},{6,4},{7,5},{8,10},{9,11},{10,... | collective-permute-start | bytes 626696 | tf_op jit(solution)/shard_map/ppermute | solution.py:22
  27.9 1.3 %collective-permute-start.14 = (bf16[136,256]{1,0:T(8,128)(2,1)S(1)}, bf16[136,256]{1,0:T(8,128)(2,1)S(1)}, u32[]{:S(2)}, u32[]{:S(2)}) collective-permute-start(bf16[136,256]{1,0:T(8,128)(2,1)S(1)} %get-tuple-element.34.refs_0_), channel_id=1, source_target_pairs={{0,1},{1,0},{2,3},{3,2},{4,5},{5,4},{6,7},{7,6},{8,9},{9,8},{10,11... | collective-permute-start | bytes 208904 | tf_op jit(solution)/shard_map/ppermute | solution.py:22
  27.9 3.5 %collective-permute-start.16 = (bf16[136,512]{1,0:T(8,128)(2,1)S(1)}, bf16[136,512]{1,0:T(8,128)(2,1)S(1)}, u32[]{:S(2)}, u32[]{:S(2)}) collective-permute-start(bf16[136,512]{1,0:T(8,128)(2,1)S(1)} %hidden_part.5.refs_4_), channel_id=1, source_target_pairs={{0,1},{1,0},{2,3},{3,2},{4,5},{5,4},{6,7},{7,6},{8,9},{9,8},{10,11... | collective-permute-start | bytes 417800 | tf_op jit(solution)/shard_map/ppermute | solution.py:22
  28.4 5.1 %collective-permute-start.13 = (bf16[136,768]{1,0:T(8,128)(2,1)S(1)}, bf16[136,768]{1,0:T(8,128)(2,1)S(1)}, u32[]{:S(2)}, u32[]{:S(2)}) collective-permute-start(bf16[136,768]{1,0:T(8,128)(2,1)S(1)} %hidden_part.7.refs_2_), channel_id=1, source_target_pairs={{0,1},{1,0},{2,3},{3,2},{4,5},{5,4},{6,7},{7,6},{8,9},{9,8},{10,11... | collective-permute-start | bytes 626696 | tf_op jit(solution)/shard_map/ppermute | solution.py:22
  29.1 1.7 %collective-permute-start.15 = (bf16[136,256]{1,0:T(8,128)(2,1)S(1)}, bf16[136,256]{1,0:T(8,128)(2,1)S(1)}, u32[]{:S(2)}, u32[]{:S(2)}) collective-permute-start(bf16[136,256]{1,0:T(8,128)(2,1)S(1)} %collective-permute-done.12.refs_3_.refs_2_), channel_id=1, source_target_pairs={{0,1},{1,0},{2,3},{3,2},{4,5},{5,4},{6,7},{7,6},{8,9},{9,8},{10,11... | collective-permute-start | bytes 208904 | tf_op jit(solution)/shard_map/ppermute | solution.py:22
  29.3 4.2 %collective-permute-start.11 = (bf16[136,512]{1,0:T(8,128)(2,1)S(1)}, bf16[136,512]{1,0:T(8,128)(2,1)S(1)}, u32[]{:S(2)}, u32[]{:S(2)}) collective-permute-start(bf16[136,512]{1,0:T(8,128)(2,1)S(1)} %collective-permute-done.9.refs_3_.refs_0_), channel_id=1, source_target_pairs={{0,1},{1,0},{2,3},{3,2},{4,5},{5,4},{6,7},{7,6},{8,9},{9,8},{10,11... | collective-permute-start | bytes 417800 | tf_op jit(solution)/shard_map/ppermute | solution.py:22
  29.7 3.9 %slice-start.6 = ((s8[12582912]{0:T(1024)(128)(4,1)}), s8[4194304]{0:T(1024)(128)(4,1)S(1)}, s32[]{:S(2)}) async-start(s8[12582912]{0:T(1024)(128)(4,1)} %bitcast.10), calls=%async_computation.6 | async-start | bytes 8388608
  29.7 3.9 %slice-start.7 = ((s8[12582912]{0:T(1024)(128)(4,1)}), s8[4194304]{0:T(1024)(128)(4,1)S(1)}, s32[]{:S(2)}) async-start(s8[12582912]{0:T(1024)(128)(4,1)} %bitcast.10), calls=%async_computation.7 | async-start | bytes 8388608
  30.8 3.7 %slice-start.8 = ((s8[12582912]{0:T(1024)(128)(4,1)}), s8[4194304]{0:T(1024)(128)(4,1)S(1)}, s32[]{:S(2)}) async-start(s8[12582912]{0:T(1024)(128)(4,1)} %bitcast.10), calls=%async_computation.8 | async-start | bytes 8388608
  30.8 5.8 %collective-permute-start.10 = (bf16[136,512]{1,0:T(8,128)(2,1)S(1)}, bf16[136,512]{1,0:T(8,128)(2,1)S(1)}, u32[]{:S(2)}, u32[]{:S(2)}) collective-permute-start(bf16[136,512]{1,0:T(8,128)(2,1)S(1)} %hidden_part.6.refs_2_), channel_id=1, source_target_pairs={{0,2},{1,3},{2,0},{3,1},{4,6},{5,7},{6,4},{7,5},{8,10},{9,11},{10,... | collective-permute-start | bytes 417800 | tf_op jit(solution)/shard_map/ppermute | solution.py:22
  33.0 3.7 %collective-permute-start.19 = (bf16[136,768]{1,0:T(8,128)(2,1)S(1)}, bf16[136,768]{1,0:T(8,128)(2,1)S(1)}, u32[]{:S(2)}, u32[]{:S(2)}) collective-permute-start(bf16[136,768]{1,0:T(8,128)(2,1)S(1)} %hold.6.refs_0_), channel_id=1, source_target_pairs={{0,1},{1,0},{2,3},{3,2},{4,5},{5,4},{6,7},{7,6},{8,9},{9,8},{10,11... | collective-permute-start | bytes 626696 | tf_op jit(solution)/shard_map/ppermute | solution.py:22
  33.0 3.7 %collective-permute-start.20 = (bf16[136,512]{1,0:T(8,128)(2,1)S(1)}, bf16[136,512]{1,0:T(8,128)(2,1)S(1)}, u32[]{:S(2)}, u32[]{:S(2)}) collective-permute-start(bf16[136,512]{1,0:T(8,128)(2,1)S(1)} %hidden_part.6.refs_2_), channel_id=1, source_target_pairs={{0,1},{1,0},{2,3},{3,2},{4,5},{5,4},{6,7},{7,6},{8,9},{9,8},{10,11... | collective-permute-start | bytes 417800 | tf_op jit(solution)/shard_map/ppermute | solution.py:22
  36.6 6.3 %copy-start.1 = (bf16[64,768]{1,0:T(8,128)(2,1)S(1)}, bf16[64,768]{1,0:T(8,128)(2,1)}, u32[]{:S(2)}) copy-start(bf16[64,768]{1,0:T(8,128)(2,1)} %grad_ref.1) | copy-start | bytes 294916
  36.6 6.3 %copy-start.2 = (s32[64,2]{0,1:T(2,128)S(1)}, s32[64,2]{0,1:T(2,128)}, u32[]{:S(2)}) copy-start(s32[64,2]{0,1:T(2,128)} %param.8) | copy-start | bytes 1540
  36.6 6.3 %copy-start.3 = (f32[64,2]{0,1:T(2,128)S(1)}, f32[64,2]{0,1:T(2,128)}, u32[]{:S(2)}) copy-start(f32[64,2]{0,1:T(2,128)} %param.9) | copy-start | bytes 1540
  36.6 1.4 %collective-permute-start.17 = (bf16[136,512]{1,0:T(8,128)(2,1)S(1)}, bf16[136,512]{1,0:T(8,128)(2,1)S(1)}, u32[]{:S(2)}, u32[]{:S(2)}) collective-permute-start(bf16[136,512]{1,0:T(8,128)(2,1)S(1)} %hold.5.refs_0_), channel_id=1, source_target_pairs={{0,1},{1,0},{2,3},{3,2},{4,5},{5,4},{6,7},{7,6},{8,9},{9,8},{10,11... | collective-permute-start | bytes 417800 | tf_op jit(solution)/shard_map/ppermute | solution.py:22
  38.5 4.8 %collective-permute-start.21 = (bf16[204,128]{1,0:T(8,128)(2,1)S(1)}, bf16[204,128]{1,0:T(8,128)(2,1)S(1)}, u32[]{:S(2)}, u32[]{:S(2)}) collective-permute-start(bf16[204,128]{1,0:T(8,128)(2,1)S(1)} %get-tuple-element.36), channel_id=1, source_target_pairs={{0,4},{4,0},{8,12},{12,8},{1,5},{5,1},{9,13},{13,9},{2,6},{6,2},{1... | collective-permute-start | bytes 156680 | tf_op jit(solution)/shard_map/ppermute | solution.py:22
  39.1 6.7 %collective-permute-start.22 = (bf16[204,128]{1,0:T(8,128)(2,1)S(1)}, bf16[204,128]{1,0:T(8,128)(2,1)S(1)}, u32[]{:S(2)}, u32[]{:S(2)}) collective-permute-start(bf16[204,128]{1,0:T(8,128)(2,1)S(1)} %get-tuple-element.37), channel_id=1, source_target_pairs={{0,8},{4,12},{8,0},{12,4},{1,9},{5,13},{9,1},{13,5},{2,10},{6,14},... | collective-permute-start | bytes 156680 | tf_op jit(solution)/shard_map/ppermute | solution.py:22
  42.4 5.9 %collective-permute-start.23 = (bf16[204,128]{1,0:T(8,128)(2,1)S(1)}, bf16[204,128]{1,0:T(8,128)(2,1)S(1)}, u32[]{:S(2)}, u32[]{:S(2)}) collective-permute-start(bf16[204,128]{1,0:T(8,128)(2,1)S(1)} %get-tuple-element.38), channel_id=1, source_target_pairs={{0,12},{4,8},{8,4},{12,0},{1,13},{5,9},{9,5},{13,1},{2,14},{6,10},... | collective-permute-start | bytes 156680 | tf_op jit(solution)/shard_map/ppermute | solution.py:22
  48.5 3.6 %collective-permute-start.24 = (f32[2,64]{1,0:T(2,128)S(1)}, f32[2,64]{1,0:T(2,128)S(1)}, u32[]{:S(2)}, u32[]{:S(2)}) collective-permute-start(f32[2,64]{1,0:T(2,128)S(1)} %dots.1), channel_id=1, source_target_pairs={{0,2},{1,3},{2,0},{3,1},{4,6},{5,7},{6,4},{7,5},{8,10},{9,11},{10,... | collective-permute-start | bytes 1544 | tf_op jit(solution)/shard_map/ppermute | solution.py:22
  52.2 1.1 %collective-permute-start.25 = (f32[2,64]{1,0:T(2,128)S(1)}, f32[2,64]{1,0:T(2,128)S(1)}, u32[]{:S(2)}, u32[]{:S(2)}) collective-permute-start(f32[2,64]{1,0:T(2,128)S(1)} %add.6), channel_id=1, source_target_pairs={{0,1},{1,0},{2,3},{3,2},{4,5},{5,4},{6,7},{7,6},{8,9},{9,8},{10,11... | collective-permute-start | bytes 1544 | tf_op jit(solution)/shard_map/ppermute | solution.py:22

commit v13 on v11

--- a/solution.py
+++ b/solution.py
@@ -305,7 +305,7 @@
 
 
 Z_ORDER = (1, 2, 3)
-CHUNKS = (256, 512, 768, 512)
+CHUNKS = (512, 512, 512, 512)
 
 
 def per_device(tokens, expert_ids, gate_probs, out_grad, gate_weight, up_weight, down_weight):

time: 53.6 us -> 54.6 us (1.019)
  starting transfers between devices: 20.2 us -> 21.5 us
    ppermute x26, starting transfers between devices: 20.2 us -> 21.5 us  [swap(): return lax.ppermute(value, axis, [(i, i ^ bit) for i in range(size)])]
  transfers between devices with their start and end apart: 26 -> 26, of which waited for: 15 -> 13; matrix products, arithmetic and copies ran while one was open for 0% -> 0% of each run, Pallas kernels for 14% -> 13%
where the time goes in v13:
time: 54.6 us; the launch traced here: 54.4 us
  starting transfers between devices  21.5 us (39%)
  waiting for transfers between devices  20.3 us (37%)
  Pallas kernels  10.1 us (18%)
  local copies, waits for them, and re-layouts  1.08 us (2%)
  between operations  0.93 us (2%)
  other arithmetic  0.57 us (1%)
    ppermute x26, starting transfers between devices, swap(): return lax.ppermute(value, axis, [(i, i ^ bit) for i in range(size)])  21.5 us
    ppermute x26, waiting for transfers between devices, swap(): return lax.ppermute(value, axis, [(i, i ^ bit) for i in range(size)])  20.3 us
    pallas_call x4, Pallas kernels, hidden_part(): pl.pallas_call(functools.partial(hidden_kernel, joined, parts, start), ou...  4.71 us
    pallas_call x4, Pallas kernels, down_part(): pl.pallas_call(functools.partial(down_kernel, len(pieces), where, slab, h...  2.54 us
    pallas_call x1, Pallas kernels, select_rows(): pl.pallas_call(select_kernel, out_shape=[jax.ShapeDtypeStruct((MOST, widt...  1.3 us
  transfers between devices with their start and end apart: 26, of which 13 were waited for; matrix products, arithmetic and copies ran while one was open for 0% of the time, Pallas kernels for 13%

profile of v13, /device:TPU:0, one launch (start us, length us, event | category | flops | bytes accessed | tf_op | source)
XLA Modules:
  0.0 54.4 jit_solution(9765879900293771194)
XLA Ops:
  0.6 0.0 slice-start
  0.6 0.0 slice-start.1
  0.7 0.0 slice-start.2
  0.7 1.3 %select_rows.1 = (bf16[34,768]{1,0:T(8,128)(2,1)S(1)}, bf16[204,128]{1,0:T(8,128)(2,1)S(1)}, bf16[204,128]{1,0:T(8,128)(2,1)S(1)}, bf16[204,128]{1,0:T(8,128)(2,1)S(1)}) custom-call(s32[1]{0:T(128)} %bitcast.me_ref, s32[1]{0:T(128)} %bitcast.3.t_ref, s32[2,64]{1,0:T(2,128)} %bitcast.12, bf16[64,768]{1,0:T(8,128)(2,1)} %tokens_hbm.1), custom_call_target="tpu_custom_call" | custom-call | flops 8000000000 | bytes 1000 | tf_op jit(solution)/shard_map/select_rows/pallas_call | solution.py:82
  2.0 3.1 %collective-permute-start = (bf16[204,128]{1,0:T(8,128)(2,1)S(1)}, bf16[204,128]{1,0:T(8,128)(2,1)S(1)}, u32[]{:S(2)}, u32[]{:S(2)}) collective-permute-start(bf16[204,128]{1,0:T(8,128)(2,1)S(1)} %get-tuple-element.30), channel_id=1, source_target_pairs={{0,4},{4,0},{8,12},{12,8},{1,5},{5,1},{9,13},{13,9},{2,6},{6,2},{1... | collective-permute-start | bytes 156680 | tf_op jit(solution)/shard_map/ppermute | solution.py:22
  5.1 2.6 %collective-permute-start.1 = (bf16[204,128]{1,0:T(8,128)(2,1)S(1)}, bf16[204,128]{1,0:T(8,128)(2,1)S(1)}, u32[]{:S(2)}, u32[]{:S(2)}) collective-permute-start(bf16[204,128]{1,0:T(8,128)(2,1)S(1)} %get-tuple-element.31), channel_id=1, source_target_pairs={{0,8},{4,12},{8,0},{12,4},{1,9},{5,13},{9,1},{13,5},{2,10},{6,14},... | collective-permute-start | bytes 156680 | tf_op jit(solution)/shard_map/ppermute | solution.py:22
  7.7 0.0 collective-permute-start.2
  7.7 0.0 collective-permute-done.refs_0_
  7.7 3.5 %collective-permute-done.1.refs_1_.third_ref = bf16[204,128]{1,0:T(8,128)(2,1)S(1)} collective-permute-done((bf16[204,128]{1,0:T(8,128)(2,1)S(1)}, bf16[204,128]{1,0:T(8,128)(2,1)S(1)}, u32[]{:S(2)}, u32[]{:S(2)}) %collective-permute-start.1) | collective-permute-done | bytes 52256 | tf_op jit(solution)/shard_map/ppermute | solution.py:22
  11.2 1.6 %collective-permute-start.5 = (bf16[96,768]{1,0:T(8,128)(2,1)S(1)}, bf16[96,768]{1,0:T(8,128)(2,1)S(1)}, u32[]{:S(2)}, u32[]{:S(2)}) collective-permute-start(bf16[96,768]{1,0:T(8,128)(2,1)S(1)} %pack_near.1.refs_0_), channel_id=1, source_target_pairs={{0,2},{1,3},{2,0},{3,1},{4,6},{5,7},{6,4},{7,5},{8,10},{9,11},{10,... | collective-permute-start | bytes 442376 | tf_op jit(solution)/shard_map/ppermute | solution.py:22
  12.7 0.9 %collective-permute-done.2.fourth_ref = bf16[204,128]{1,0:T(8,128)(2,1)S(1)} collective-permute-done((bf16[204,128]{1,0:T(8,128)(2,1)S(1)}, bf16[204,128]{1,0:T(8,128)(2,1)S(1)}, u32[]{:S(2)}, u32[]{:S(2)}) %collective-permute-start.2) | collective-permute-done | bytes 52256 | tf_op jit(solution)/shard_map/ppermute | solution.py:22
  13.6 1.6 %collective-permute-start.6 = (bf16[40,768]{1,0:T(8,128)(2,1)S(1)}, bf16[40,768]{1,0:T(8,128)(2,1)S(1)}, u32[]{:S(2)}, u32[]{:S(2)}) collective-permute-start(bf16[40,768]{1,0:T(8,128)(2,1)S(1)} %pack_far.1.refs_1_), channel_id=1, source_target_pairs={{0,2},{1,3},{2,0},{3,1},{4,6},{5,7},{6,4},{7,5},{8,10},{9,11},{10,... | collective-permute-start | bytes 184328 | tf_op jit(solution)/shard_map/ppermute | solution.py:22
  15.2 0.0 collective-permute-start.3
  15.2 2.7 %collective-permute-done.6.refs_1_.refs_5_ = bf16[40,768]{1,0:T(8,128)(2,1)S(1)} collective-permute-done((bf16[40,768]{1,0:T(8,128)(2,1)S(1)}, bf16[40,768]{1,0:T(8,128)(2,1)S(1)}, u32[]{:S(2)}, u32[]{:S(2)}) %collective-permute-start.6) | collective-permute-done | bytes 61472 | tf_op jit(solution)/shard_map/ppermute | solution.py:22
  17.9 0.0 collective-permute-done.5.refs_0_
  17.9 0.0 collective-permute-start.7
  17.9 0.5 collective-permute-start.4
  18.4 0.1 collective-permute-start.8
  18.5 0.9 %collective-permute-done.4.refs_3_ = bf16[40,768]{1,0:T(8,128)(2,1)S(1)} collective-permute-done((bf16[40,768]{1,0:T(8,128)(2,1)S(1)}, bf16[40,768]{1,0:T(8,128)(2,1)S(1)}, u32[]{:S(2)}, u32[]{:S(2)}) %collective-permute-start.4) | collective-permute-done | bytes 61472 | tf_op jit(solution)/shard_map/ppermute | solution.py:22
  19.4 0.3 collective-permute-done.8.refs_7_
  19.7 0.0 collective-permute-done.3.refs_2_
  19.7 0.0 collective-permute-done.7.refs_6_
  19.7 1.2 %hidden_part.4 = (bf16[136,512]{1,0:T(8,128)(2,1)S(1)}, bf16[4,136,768]{2,1,0:T(8,128)(2,1)S(1)}) custom-call(s32[1]{0:T(128)} %bitcast.3.t_ref, bf16[96,768]{1,0:T(8,128)(2,1)S(1)} %pack_near.1.refs_0_, bf16[40,768]{1,0:T(8,128)(2,1)S(1)} %pack_far.1.refs_1_, bf16[96,768]{1,0:T(8,128)(2,1)S(1)} %collective-permute-done.3.refs_2_, ...), custom_call_target="tpu_custom_call" | custom-call | flops 1000 | bytes 1000 | tf_op jit(solution)/shard_map/hidden_part/pallas_call | solution.py:177
  20.9 1.6 %collective-permute-start.12 = (bf16[136,512]{1,0:T(8,128)(2,1)S(1)}, bf16[136,512]{1,0:T(8,128)(2,1)S(1)}, u32[]{:S(2)}, u32[]{:S(2)}) collective-permute-start(bf16[136,512]{1,0:T(8,128)(2,1)S(1)} %get-tuple-element.34.refs_0_), channel_id=1, source_target_pairs={{0,2},{1,3},{2,0},{3,1},{4,6},{5,7},{6,4},{7,5},{8,10},{9,11},{10,... | collective-permute-start | bytes 417800 | tf_op jit(solution)/shard_map/ppermute | solution.py:22
  22.5 1.2 %hidden_part.5.refs_4_ = bf16[136,512]{1,0:T(8,128)(2,1)S(1)} custom-call(s32[1]{0:T(128)} %bitcast.3.t_ref, bf16[4,136,768]{2,1,0:T(8,128)(2,1)S(1)} %get-tuple-element.33.refs_0_, bf16[1,3072,2048]{2,1,0:T(8,128)(2,1)S(1)} %bitcast.7, bf16[1,3072,2048]{2,1,0:T(8,128)(2,1)S(1)} %copy-done), custom_call_target="tpu_custom_call" | custom-call | flops 1000 | bytes 1000 | tf_op jit(solution)/shard_map/hidden_part/pallas_call | solution.py:177
  23.6 0.6 %collective-permute-start.9 = (bf16[136,512]{1,0:T(8,128)(2,1)S(1)}, bf16[136,512]{1,0:T(8,128)(2,1)S(1)}, u32[]{:S(2)}, u32[]{:S(2)}) collective-permute-start(bf16[136,512]{1,0:T(8,128)(2,1)S(1)} %hidden_part.5.refs_4_), channel_id=1, source_target_pairs={{0,2},{1,3},{2,0},{3,1},{4,6},{5,7},{6,4},{7,5},{8,10},{9,11},{10,... | collective-permute-start | bytes 417800 | tf_op jit(solution)/shard_map/ppermute | solution.py:22
  24.3 0.0 collective-permute-start.16
  24.3 0.5 collective-permute-start.14
  24.8 2.4 %collective-permute-done.12.refs_3_.refs_2_ = bf16[136,512]{1,0:T(8,128)(2,1)S(1)} collective-permute-done((bf16[136,512]{1,0:T(8,128)(2,1)S(1)}, bf16[136,512]{1,0:T(8,128)(2,1)S(1)}, u32[]{:S(2)}, u32[]{:S(2)}) %collective-permute-start.12) | collective-permute-done | bytes 139296 | tf_op jit(solution)/shard_map/ppermute | solution.py:22
  27.2 1.2 %hidden_part.7.refs_2_ = bf16[136,512]{1,0:T(8,128)(2,1)S(1)} custom-call(s32[1]{0:T(128)} %bitcast.3.t_ref, bf16[4,136,768]{2,1,0:T(8,128)(2,1)S(1)} %get-tuple-element.33.refs_0_, bf16[1,3072,2048]{2,1,0:T(8,128)(2,1)S(1)} %bitcast.7, bf16[1,3072,2048]{2,1,0:T(8,128)(2,1)S(1)} %copy-done, bf16[136,512]{1,0:T(8,128)(2,1)S(1)} %collective-permute-done.12.refs_3_.refs_2_), custom_call_target="tpu_custom_call" | custom-call | flops 1000 | bytes 1000 | tf_op jit(solution)/shard_map/hidden_part/pallas_call | solution.py:177
  28.4 0.0 slice-start.5
  28.4 1.9 %collective-permute-start.18 = (bf16[136,512]{1,0:T(8,128)(2,1)S(1)}, bf16[136,512]{1,0:T(8,128)(2,1)S(1)}, u32[]{:S(2)}, u32[]{:S(2)}) collective-permute-start(bf16[136,512]{1,0:T(8,128)(2,1)S(1)} %hidden_part.7.refs_2_), channel_id=1, source_target_pairs={{0,2},{1,3},{2,0},{3,1},{4,6},{5,7},{6,4},{7,5},{8,10},{9,11},{10,... | collective-permute-start | bytes 417800 | tf_op jit(solution)/shard_map/ppermute | solution.py:22
  30.2 0.0 collective-permute-done.9.refs_3_.refs_0_
  30.3 0.2 collective-permute-start.11
  30.5 0.3 collective-permute-start.13
  30.8 1.2 %hidden_part.6.refs_2_ = bf16[136,512]{1,0:T(8,128)(2,1)S(1)} custom-call(s32[1]{0:T(128)} %bitcast.3.t_ref, bf16[4,136,768]{2,1,0:T(8,128)(2,1)S(1)} %get-tuple-element.33.refs_0_, bf16[1,3072,2048]{2,1,0:T(8,128)(2,1)S(1)} %bitcast.7, bf16[1,3072,2048]{2,1,0:T(8,128)(2,1)S(1)} %copy-done, bf16[136,512]{1,0:T(8,128)(2,1)S(1)} %collective-permute-done.9.refs_3_.refs_0_), custom_call_target="tpu_custom_call" | custom-call | flops 1000 | bytes 1000 | tf_op jit(solution)/shard_map/hidden_part/pallas_call | solution.py:177
  32.0 0.0 slice-start.8
  32.0 0.0 collective-permute-done.14.refs_1_
  32.0 1.0 %collective-permute-start.10 = (bf16[136,512]{1,0:T(8,128)(2,1)S(1)}, bf16[136,512]{1,0:T(8,128)(2,1)S(1)}, u32[]{:S(2)}, u32[]{:S(2)}) collective-permute-start(bf16[136,512]{1,0:T(8,128)(2,1)S(1)} %hidden_part.6.refs_2_), channel_id=1, source_target_pairs={{0,2},{1,3},{2,0},{3,1},{4,6},{5,7},{6,4},{7,5},{8,10},{9,11},{10,... | collective-permute-start | bytes 417800 | tf_op jit(solution)/shard_map/ppermute | solution.py:22
  33.0 0.9 %down_part.4.refs_5_.refs_1_ = f32[136,768]{1,0:T(8,128)S(1)} custom-call(s32[1]{0:T(128)} %bitcast.3.t_ref, bf16[136,512]{1,0:T(8,128)(2,1)S(1)} %get-tuple-element.34.refs_0_, bf16[136,512]{1,0:T(8,128)(2,1)S(1)} %collective-permute-done.14.refs_1_, bf16[136,512]{1,0:T(8,128)(2,1)S(1)} %collective-permute-done.12.refs_3_.refs_2_, ...), custom_call_target="tpu_custom_call" | custom-call | flops 641728512 | bytes 1000 | tf_op jit(solution)/shard_map/down_part/pallas_call | solution.py:215
  33.9 0.7 %collective-permute-done.18.refs_0_ = bf16[136,512]{1,0:T(8,128)(2,1)S(1)} collective-permute-done((bf16[136,512]{1,0:T(8,128)(2,1)S(1)}, bf16[136,512]{1,0:T(8,128)(2,1)S(1)}, u32[]{:S(2)}, u32[]{:S(2)}) %collective-permute-start.18) | collective-permute-done | bytes 139296 | tf_op jit(solution)/shard_map/ppermute | solution.py:22
  34.6 0.0 collective-permute-done.11.refs_1_
  34.6 0.0 collective-permute-done.13.refs_3_
  34.6 1.0 %slice-done.8 = s8[4194304]{0:T(1024)(128)(4,1)S(1)} async-done(((s8[12582912]{0:T(1024)(128)(4,1)}), s8[4194304]{0:T(1024)(128)(4,1)S(1)}, s32[]{:S(2)}) %slice-start.8) | async-done | bytes 4194328
  35.6 0.6 %down_part.5.refs_1_.refs_5_ = f32[136,768]{1,0:T(8,128)S(1)} custom-call(s32[1]{0:T(128)} %bitcast.3.t_ref, bf16[136,512]{1,0:T(8,128)(2,1)S(1)} %collective-permute-done.9.refs_3_.refs_0_, bf16[136,512]{1,0:T(8,128)(2,1)S(1)} %collective-permute-done.11.refs_1_, bf16[136,512]{1,0:T(8,128)(2,1)S(1)} %hidden_part.7.refs_2_, ...), custom_call_target="tpu_custom_call" | custom-call | flops 427819008 | bytes 1000 | tf_op jit(solution)/shard_map/down_part/pallas_call | solution.py:215
  36.3 1.6 %collective-permute-done.10.refs_0_ = bf16[136,512]{1,0:T(8,128)(2,1)S(1)} collective-permute-done((bf16[136,512]{1,0:T(8,128)(2,1)S(1)}, bf16[136,512]{1,0:T(8,128)(2,1)S(1)}, u32[]{:S(2)}, u32[]{:S(2)}) %collective-permute-start.10) | collective-permute-done | bytes 139296 | tf_op jit(solution)/shard_map/ppermute | solution.py:22
  37.9 0.1 collective-permute-start.17
  37.9 0.0 collective-permute-done.20.refs_3_
  38.0 0.6 %down_part.6.refs_3_ = f32[136,768]{1,0:T(8,128)S(1)} custom-call(s32[1]{0:T(128)} %bitcast.3.t_ref, bf16[136,512]{1,0:T(8,128)(2,1)S(1)} %hold.6.refs_0_, bf16[136,512]{1,0:T(8,128)(2,1)S(1)} %collective-permute-done.19.refs_1_, bf16[136,512]{1,0:T(8,128)(2,1)S(1)} %hidden_part.6.refs_2_, bf16[136,512]{1,0:T(8,128)(2,1)S(1)} %collective-permute-done.20.refs_3_, ...), custom_call_target="tpu_custom_call" | custom-call | flops 427819008 | bytes 1000 | tf_op jit(solution)/shard_map/down_part/pallas_call | solution.py:215
  38.6 0.7 %collective-permute-done.17.refs_1_ = bf16[136,512]{1,0:T(8,128)(2,1)S(1)} collective-permute-done((bf16[136,512]{1,0:T(8,128)(2,1)S(1)}, bf16[136,512]{1,0:T(8,128)(2,1)S(1)}, u32[]{:S(2)}, u32[]{:S(2)}) %collective-permute-start.17) | collective-permute-done | bytes 139296 | tf_op jit(solution)/shard_map/ppermute | solution.py:22
  39.3 0.4 down_part.7
  39.7 0.1 collective-permute-start.21
  39.8 3.1 %collective-permute-start.22 = (bf16[204,128]{1,0:T(8,128)(2,1)S(1)}, bf16[204,128]{1,0:T(8,128)(2,1)S(1)}, u32[]{:S(2)}, u32[]{:S(2)}) collective-permute-start(bf16[204,128]{1,0:T(8,128)(2,1)S(1)} %get-tuple-element.37), channel_id=1, source_target_pairs={{0,8},{4,12},{8,0},{12,4},{1,9},{5,13},{9,1},{13,5},{2,10},{6,14},... | collective-permute-start | bytes 156680 | tf_op jit(solution)/shard_map/ppermute | solution.py:22
  42.9 1.2 %collective-permute-start.23 = (bf16[204,128]{1,0:T(8,128)(2,1)S(1)}, bf16[204,128]{1,0:T(8,128)(2,1)S(1)}, u32[]{:S(2)}, u32[]{:S(2)}) collective-permute-start(bf16[204,128]{1,0:T(8,128)(2,1)S(1)} %get-tuple-element.38), channel_id=1, source_target_pairs={{0,12},{4,8},{8,4},{12,0},{1,13},{5,9},{9,5},{13,1},{2,14},{6,10},... | collective-permute-start | bytes 156680 | tf_op jit(solution)/shard_map/ppermute | solution.py:22
  44.2 0.3 prepare.1
  44.5 2.0 %collective-permute-done.22.refs_6_.refs_10_ = bf16[204,128]{1,0:T(8,128)(2,1)S(1)} collective-permute-done((bf16[204,128]{1,0:T(8,128)(2,1)S(1)}, bf16[204,128]{1,0:T(8,128)(2,1)S(1)}, u32[]{:S(2)}, u32[]{:S(2)}) %collective-permute-start.22) | collective-permute-done | bytes 52256 | tf_op jit(solution)/shard_map/ppermute | solution.py:22
  46.5 2.3 %collective-permute-done.23.refs_7_.refs_11_ = bf16[204,128]{1,0:T(8,128)(2,1)S(1)} collective-permute-done((bf16[204,128]{1,0:T(8,128)(2,1)S(1)}, bf16[204,128]{1,0:T(8,128)(2,1)S(1)}, u32[]{:S(2)}, u32[]{:S(2)}) %collective-permute-start.23) | collective-permute-done | bytes 52256 | tf_op jit(solution)/shard_map/ppermute | solution.py:22
  48.9 0.2 dots.1
  49.1 1.5 %collective-permute-start.24 = (f32[2,64]{1,0:T(2,128)S(1)}, f32[2,64]{1,0:T(2,128)S(1)}, u32[]{:S(2)}, u32[]{:S(2)}) collective-permute-start(f32[2,64]{1,0:T(2,128)S(1)} %dots.1), channel_id=1, source_target_pairs={{0,2},{1,3},{2,0},{3,1},{4,6},{5,7},{6,4},{7,5},{8,10},{9,11},{10,... | collective-permute-start | bytes 1544 | tf_op jit(solution)/shard_map/ppermute | solution.py:22
  50.6 0.9 %mix.1 = (bf16[64,768]{1,0:T(8,128)(2,1)}, f32[8,128]{1,0:T(8,128)S(1)}) custom-call(f32[64,128]{1,0:T(8,128)S(1)} %get-tuple-element.24.routes_ref, f32[204,64]{1,0:T(8,128)S(1)} %get-tuple-element.25.refs_0_, f32[204,64]{1,0:T(8,128)S(1)} %get-tuple-element.26.refs_1_, f32[204,64]{1,0:T(8,128)S(1)} %get-tuple-element.27.refs_2_, ...), custom_call_target="tpu_custom_call" | custom-call | flops 1000000000 | bytes 1000 | tf_op jit(solution)/shard_map/mix/pallas_call | solution.py:296
  51.5 1.2 %collective-permute-done.24.refs_0_ = f32[2,64]{1,0:T(2,128)S(1)} collective-permute-done((f32[2,64]{1,0:T(2,128)S(1)}, f32[2,64]{1,0:T(2,128)S(1)}, u32[]{:S(2)}, u32[]{:S(2)}) %collective-permute-start.24) | collective-permute-done | bytes 544 | tf_op jit(solution)/shard_map/ppermute | solution.py:22
  52.7 0.0 collective-permute-start.25
  52.7 1.1 %collective-permute-done.25 = f32[2,64]{1,0:T(2,128)S(1)} collective-permute-done((f32[2,64]{1,0:T(2,128)S(1)}, f32[2,64]{1,0:T(2,128)S(1)}, u32[]{:S(2)}, u32[]{:S(2)}) %collective-permute-start.25) | collective-permute-done | bytes 544 | tf_op jit(solution)/shard_map/ppermute | solution.py:22
  53.8 0.6 %add_bitcast_fusion = f32[64,2]{0,1:T(2,128)} fusion(f32[2,64]{1,0:T(2,128)S(1)} %add.6, f32[2,64]{1,0:T(2,128)S(1)} %collective-permute-done.25), kind=kLoop, calls=%fused_computation | loop fusion | flops 128 | bytes 1536 | tf_op jit(solution)/shard_map/transpose | solution.py:355
  (37 shorter events, 0.1 us)
Async XLA Ops:
  0.6 19.1 %slice-start = ((s8[12582912]{0:T(1024)(128)(4,1)}), s8[4194304]{0:T(1024)(128)(4,1)S(1)}, s32[]{:S(2)}) async-start(s8[12582912]{0:T(1024)(128)(4,1)} %bitcast.6), calls=%async_computation | async-start | bytes 8388608
  0.6 19.1 %slice-start.1 = ((s8[12582912]{0:T(1024)(128)(4,1)}), s8[4194304]{0:T(1024)(128)(4,1)S(1)}, s32[]{:S(2)}) async-start(s8[12582912]{0:T(1024)(128)(4,1)} %bitcast.6), calls=%async_computation.1 | async-start | bytes 8388608
  0.7 19.1 %slice-start.2 = ((s8[12582912]{0:T(1024)(128)(4,1)}), s8[4194304]{0:T(1024)(128)(4,1)S(1)}, s32[]{:S(2)}) async-start(s8[12582912]{0:T(1024)(128)(4,1)} %bitcast.6), calls=%async_computation.2 | async-start | bytes 8388608
  0.7 19.1 %copy-start = (bf16[1,3072,2048]{2,1,0:T(8,128)(2,1)S(1)}, bf16[1,3072,2048]{2,1,0:T(8,128)(2,1)}, u32[]{:S(2)}) copy-start(bf16[1,3072,2048]{2,1,0:T(8,128)(2,1)} %refs_2_.6) | copy-start | bytes 37748740
  2.0 5.7 %collective-permute-start = (bf16[204,128]{1,0:T(8,128)(2,1)S(1)}, bf16[204,128]{1,0:T(8,128)(2,1)S(1)}, u32[]{:S(2)}, u32[]{:S(2)}) collective-permute-start(bf16[204,128]{1,0:T(8,128)(2,1)S(1)} %get-tuple-element.30), channel_id=1, source_target_pairs={{0,4},{4,0},{8,12},{12,8},{1,5},{5,1},{9,13},{13,9},{2,6},{6,2},{1... | collective-permute-start | bytes 156680 | tf_op jit(solution)/shard_map/ppermute | solution.py:22
  5.1 6.1 %collective-permute-start.1 = (bf16[204,128]{1,0:T(8,128)(2,1)S(1)}, bf16[204,128]{1,0:T(8,128)(2,1)S(1)}, u32[]{:S(2)}, u32[]{:S(2)}) collective-permute-start(bf16[204,128]{1,0:T(8,128)(2,1)S(1)} %get-tuple-element.31), channel_id=1, source_target_pairs={{0,8},{4,12},{8,0},{12,4},{1,9},{5,13},{9,1},{13,5},{2,10},{6,14},... | collective-permute-start | bytes 156680 | tf_op jit(solution)/shard_map/ppermute | solution.py:22
  7.7 5.9 %collective-permute-start.2 = (bf16[204,128]{1,0:T(8,128)(2,1)S(1)}, bf16[204,128]{1,0:T(8,128)(2,1)S(1)}, u32[]{:S(2)}, u32[]{:S(2)}) collective-permute-start(bf16[204,128]{1,0:T(8,128)(2,1)S(1)} %get-tuple-element.32), channel_id=1, source_target_pairs={{0,12},{4,8},{8,4},{12,0},{1,13},{5,9},{9,5},{13,1},{2,14},{6,10},... | collective-permute-start | bytes 156680 | tf_op jit(solution)/shard_map/ppermute | solution.py:22
  11.2 6.7 %collective-permute-start.5 = (bf16[96,768]{1,0:T(8,128)(2,1)S(1)}, bf16[96,768]{1,0:T(8,128)(2,1)S(1)}, u32[]{:S(2)}, u32[]{:S(2)}) collective-permute-start(bf16[96,768]{1,0:T(8,128)(2,1)S(1)} %pack_near.1.refs_0_), channel_id=1, source_target_pairs={{0,2},{1,3},{2,0},{3,1},{4,6},{5,7},{6,4},{7,5},{8,10},{9,11},{10,... | collective-permute-start | bytes 442376 | tf_op jit(solution)/shard_map/ppermute | solution.py:22
  13.6 4.3 %collective-permute-start.6 = (bf16[40,768]{1,0:T(8,128)(2,1)S(1)}, bf16[40,768]{1,0:T(8,128)(2,1)S(1)}, u32[]{:S(2)}, u32[]{:S(2)}) collective-permute-start(bf16[40,768]{1,0:T(8,128)(2,1)S(1)} %pack_far.1.refs_1_), channel_id=1, source_target_pairs={{0,2},{1,3},{2,0},{3,1},{4,6},{5,7},{6,4},{7,5},{8,10},{9,11},{10,... | collective-permute-start | bytes 184328 | tf_op jit(solution)/shard_map/ppermute | solution.py:22
  15.2 4.5 %collective-permute-start.3 = (bf16[96,768]{1,0:T(8,128)(2,1)S(1)}, bf16[96,768]{1,0:T(8,128)(2,1)S(1)}, u32[]{:S(2)}, u32[]{:S(2)}) collective-permute-start(bf16[96,768]{1,0:T(8,128)(2,1)S(1)} %pack_near.1.refs_0_), channel_id=1, source_target_pairs={{0,1},{1,0},{2,3},{3,2},{4,5},{5,4},{6,7},{7,6},{8,9},{9,8},{10,11... | collective-permute-start | bytes 442376 | tf_op jit(solution)/shard_map/ppermute | solution.py:22
  17.9 1.8 %collective-permute-start.7 = (bf16[96,768]{1,0:T(8,128)(2,1)S(1)}, bf16[96,768]{1,0:T(8,128)(2,1)S(1)}, u32[]{:S(2)}, u32[]{:S(2)}) collective-permute-start(bf16[96,768]{1,0:T(8,128)(2,1)S(1)} %hold.4.refs_4_), channel_id=1, source_target_pairs={{0,1},{1,0},{2,3},{3,2},{4,5},{5,4},{6,7},{7,6},{8,9},{9,8},{10,11... | collective-permute-start | bytes 442376 | tf_op jit(solution)/shard_map/ppermute | solution.py:22
  17.9 1.5 %collective-permute-start.4 = (bf16[40,768]{1,0:T(8,128)(2,1)S(1)}, bf16[40,768]{1,0:T(8,128)(2,1)S(1)}, u32[]{:S(2)}, u32[]{:S(2)}) collective-permute-start(bf16[40,768]{1,0:T(8,128)(2,1)S(1)} %pack_far.1.refs_1_), channel_id=1, source_target_pairs={{0,1},{1,0},{2,3},{3,2},{4,5},{5,4},{6,7},{7,6},{8,9},{9,8},{10,11... | collective-permute-start | bytes 184328 | tf_op jit(solution)/shard_map/ppermute | solution.py:22
  18.4 1.2 %collective-permute-start.8 = (bf16[40,768]{1,0:T(8,128)(2,1)S(1)}, bf16[40,768]{1,0:T(8,128)(2,1)S(1)}, u32[]{:S(2)}, u32[]{:S(2)}) collective-permute-start(bf16[40,768]{1,0:T(8,128)(2,1)S(1)} %collective-permute-done.6.refs_1_.refs_5_), channel_id=1, source_target_pairs={{0,1},{1,0},{2,3},{3,2},{4,5},{5,4},{6,7},{7,6},{8,9},{9,8},{10,11... | collective-permute-start | bytes 184328 | tf_op jit(solution)/shard_map/ppermute | solution.py:22
  20.9 6.3 %collective-permute-start.12 = (bf16[136,512]{1,0:T(8,128)(2,1)S(1)}, bf16[136,512]{1,0:T(8,128)(2,1)S(1)}, u32[]{:S(2)}, u32[]{:S(2)}) collective-permute-start(bf16[136,512]{1,0:T(8,128)(2,1)S(1)} %get-tuple-element.34.refs_0_), channel_id=1, source_target_pairs={{0,2},{1,3},{2,0},{3,1},{4,6},{5,7},{6,4},{7,5},{8,10},{9,11},{10,... | collective-permute-start | bytes 417800 | tf_op jit(solution)/shard_map/ppermute | solution.py:22
  23.6 6.6 %collective-permute-start.9 = (bf16[136,512]{1,0:T(8,128)(2,1)S(1)}, bf16[136,512]{1,0:T(8,128)(2,1)S(1)}, u32[]{:S(2)}, u32[]{:S(2)}) collective-permute-start(bf16[136,512]{1,0:T(8,128)(2,1)S(1)} %hidden_part.5.refs_4_), channel_id=1, source_target_pairs={{0,2},{1,3},{2,0},{3,1},{4,6},{5,7},{6,4},{7,5},{8,10},{9,11},{10,... | collective-permute-start | bytes 417800 | tf_op jit(solution)/shard_map/ppermute | solution.py:22
  24.3 6.2 %collective-permute-start.16 = (bf16[136,512]{1,0:T(8,128)(2,1)S(1)}, bf16[136,512]{1,0:T(8,128)(2,1)S(1)}, u32[]{:S(2)}, u32[]{:S(2)}) collective-permute-start(bf16[136,512]{1,0:T(8,128)(2,1)S(1)} %hidden_part.5.refs_4_), channel_id=1, source_target_pairs={{0,1},{1,0},{2,3},{3,2},{4,5},{5,4},{6,7},{7,6},{8,9},{9,8},{10,11... | collective-permute-start | bytes 417800 | tf_op jit(solution)/shard_map/ppermute | solution.py:22
  24.3 7.7 %collective-permute-start.14 = (bf16[136,512]{1,0:T(8,128)(2,1)S(1)}, bf16[136,512]{1,0:T(8,128)(2,1)S(1)}, u32[]{:S(2)}, u32[]{:S(2)}) collective-permute-start(bf16[136,512]{1,0:T(8,128)(2,1)S(1)} %get-tuple-element.34.refs_0_), channel_id=1, source_target_pairs={{0,1},{1,0},{2,3},{3,2},{4,5},{5,4},{6,7},{7,6},{8,9},{9,8},{10,11... | collective-permute-start | bytes 417800 | tf_op jit(solution)/shard_map/ppermute | solution.py:22
  27.2 5.8 %collective-permute-start.15 = (bf16[136,512]{1,0:T(8,128)(2,1)S(1)}, bf16[136,512]{1,0:T(8,128)(2,1)S(1)}, u32[]{:S(2)}, u32[]{:S(2)}) collective-permute-start(bf16[136,512]{1,0:T(8,128)(2,1)S(1)} %collective-permute-done.12.refs_3_.refs_2_), channel_id=1, source_target_pairs={{0,1},{1,0},{2,3},{3,2},{4,5},{5,4},{6,7},{7,6},{8,9},{9,8},{10,11... | collective-permute-start | bytes 417800 | tf_op jit(solution)/shard_map/ppermute | solution.py:22
  27.2 5.8 %slice-start.3 = ((s8[12582912]{0:T(1024)(128)(4,1)}), s8[4194304]{0:T(1024)(128)(4,1)S(1)}, s32[]{:S(2)}) async-start(s8[12582912]{0:T(1024)(128)(4,1)} %bitcast.8), calls=%async_computation.3 | async-start | bytes 8388608
  27.2 5.8 %slice-start.4 = ((s8[12582912]{0:T(1024)(128)(4,1)}), s8[4194304]{0:T(1024)(128)(4,1)S(1)}, s32[]{:S(2)}) async-start(s8[12582912]{0:T(1024)(128)(4,1)} %bitcast.8), calls=%async_computation.4 | async-start | bytes 8388608
  28.4 4.6 %slice-start.5 = ((s8[12582912]{0:T(1024)(128)(4,1)}), s8[4194304]{0:T(1024)(128)(4,1)S(1)}, s32[]{:S(2)}) async-start(s8[12582912]{0:T(1024)(128)(4,1)} %bitcast.8), calls=%async_computation.5 | async-start | bytes 8388608
  28.4 6.2 %collective-permute-start.18 = (bf16[136,512]{1,0:T(8,128)(2,1)S(1)}, bf16[136,512]{1,0:T(8,128)(2,1)S(1)}, u32[]{:S(2)}, u32[]{:S(2)}) collective-permute-start(bf16[136,512]{1,0:T(8,128)(2,1)S(1)} %hidden_part.7.refs_2_), channel_id=1, source_target_pairs={{0,2},{1,3},{2,0},{3,1},{4,6},{5,7},{6,4},{7,5},{8,10},{9,11},{10,... | collective-permute-start | bytes 417800 | tf_op jit(solution)/shard_map/ppermute | solution.py:22
  30.3 4.3 %collective-permute-start.11 = (bf16[136,512]{1,0:T(8,128)(2,1)S(1)}, bf16[136,512]{1,0:T(8,128)(2,1)S(1)}, u32[]{:S(2)}, u32[]{:S(2)}) collective-permute-start(bf16[136,512]{1,0:T(8,128)(2,1)S(1)} %collective-permute-done.9.refs_3_.refs_0_), channel_id=1, source_target_pairs={{0,1},{1,0},{2,3},{3,2},{4,5},{5,4},{6,7},{7,6},{8,9},{9,8},{10,11... | collective-permute-start | bytes 417800 | tf_op jit(solution)/shard_map/ppermute | solution.py:22
  30.5 4.1 %collective-permute-start.13 = (bf16[136,512]{1,0:T(8,128)(2,1)S(1)}, bf16[136,512]{1,0:T(8,128)(2,1)S(1)}, u32[]{:S(2)}, u32[]{:S(2)}) collective-permute-start(bf16[136,512]{1,0:T(8,128)(2,1)S(1)} %hidden_part.7.refs_2_), channel_id=1, source_target_pairs={{0,1},{1,0},{2,3},{3,2},{4,5},{5,4},{6,7},{7,6},{8,9},{9,8},{10,11... | collective-permute-start | bytes 417800 | tf_op jit(solution)/shard_map/ppermute | solution.py:22
  30.8 3.8 %slice-start.6 = ((s8[12582912]{0:T(1024)(128)(4,1)}), s8[4194304]{0:T(1024)(128)(4,1)S(1)}, s32[]{:S(2)}) async-start(s8[12582912]{0:T(1024)(128)(4,1)} %bitcast.10), calls=%async_computation.6 | async-start | bytes 8388608
  30.8 3.8 %slice-start.7 = ((s8[12582912]{0:T(1024)(128)(4,1)}), s8[4194304]{0:T(1024)(128)(4,1)S(1)}, s32[]{:S(2)}) async-start(s8[12582912]{0:T(1024)(128)(4,1)} %bitcast.10), calls=%async_computation.7 | async-start | bytes 8388608
  32.0 3.7 %slice-start.8 = ((s8[12582912]{0:T(1024)(128)(4,1)}), s8[4194304]{0:T(1024)(128)(4,1)S(1)}, s32[]{:S(2)}) async-start(s8[12582912]{0:T(1024)(128)(4,1)} %bitcast.10), calls=%async_computation.8 | async-start | bytes 8388608
  32.0 5.9 %collective-permute-start.10 = (bf16[136,512]{1,0:T(8,128)(2,1)S(1)}, bf16[136,512]{1,0:T(8,128)(2,1)S(1)}, u32[]{:S(2)}, u32[]{:S(2)}) collective-permute-start(bf16[136,512]{1,0:T(8,128)(2,1)S(1)} %hidden_part.6.refs_2_), channel_id=1, source_target_pairs={{0,2},{1,3},{2,0},{3,1},{4,6},{5,7},{6,4},{7,5},{8,10},{9,11},{10,... | collective-permute-start | bytes 417800 | tf_op jit(solution)/shard_map/ppermute | solution.py:22
  33.0 5.0 %collective-permute-start.20 = (bf16[136,512]{1,0:T(8,128)(2,1)S(1)}, bf16[136,512]{1,0:T(8,128)(2,1)S(1)}, u32[]{:S(2)}, u32[]{:S(2)}) collective-permute-start(bf16[136,512]{1,0:T(8,128)(2,1)S(1)} %hidden_part.6.refs_2_), channel_id=1, source_target_pairs={{0,1},{1,0},{2,3},{3,2},{4,5},{5,4},{6,7},{7,6},{8,9},{9,8},{10,11... | collective-permute-start | bytes 417800 | tf_op jit(solution)/shard_map/ppermute | solution.py:22
  34.6 3.4 %collective-permute-start.19 = (bf16[136,512]{1,0:T(8,128)(2,1)S(1)}, bf16[136,512]{1,0:T(8,128)(2,1)S(1)}, u32[]{:S(2)}, u32[]{:S(2)}) collective-permute-start(bf16[136,512]{1,0:T(8,128)(2,1)S(1)} %hold.6.refs_0_), channel_id=1, source_target_pairs={{0,1},{1,0},{2,3},{3,2},{4,5},{5,4},{6,7},{7,6},{8,9},{9,8},{10,11... | collective-permute-start | bytes 417800 | tf_op jit(solution)/shard_map/ppermute | solution.py:22
  37.9 6.3 %copy-start.1 = (bf16[64,768]{1,0:T(8,128)(2,1)S(1)}, bf16[64,768]{1,0:T(8,128)(2,1)}, u32[]{:S(2)}) copy-start(bf16[64,768]{1,0:T(8,128)(2,1)} %grad_ref.1) | copy-start | bytes 294916
  37.9 6.3 %copy-start.2 = (s32[64,2]{0,1:T(2,128)S(1)}, s32[64,2]{0,1:T(2,128)}, u32[]{:S(2)}) copy-start(s32[64,2]{0,1:T(2,128)} %param.8) | copy-start | bytes 1540
  37.9 6.3 %copy-start.3 = (f32[64,2]{0,1:T(2,128)S(1)}, f32[64,2]{0,1:T(2,128)}, u32[]{:S(2)}) copy-start(f32[64,2]{0,1:T(2,128)} %param.9) | copy-start | bytes 1540
  37.9 1.4 %collective-permute-start.17 = (bf16[136,512]{1,0:T(8,128)(2,1)S(1)}, bf16[136,512]{1,0:T(8,128)(2,1)S(1)}, u32[]{:S(2)}, u32[]{:S(2)}) collective-permute-start(bf16[136,512]{1,0:T(8,128)(2,1)S(1)} %hold.5.refs_0_), channel_id=1, source_target_pairs={{0,1},{1,0},{2,3},{3,2},{4,5},{5,4},{6,7},{7,6},{8,9},{9,8},{10,11... | collective-permute-start | bytes 417800 | tf_op jit(solution)/shard_map/ppermute | solution.py:22
  39.7 4.8 %collective-permute-start.21 = (bf16[204,128]{1,0:T(8,128)(2,1)S(1)}, bf16[204,128]{1,0:T(8,128)(2,1)S(1)}, u32[]{:S(2)}, u32[]{:S(2)}) collective-permute-start(bf16[204,128]{1,0:T(8,128)(2,1)S(1)} %get-tuple-element.36), channel_id=1, source_target_pairs={{0,4},{4,0},{8,12},{12,8},{1,5},{5,1},{9,13},{13,9},{2,6},{6,2},{1... | collective-permute-start | bytes 156680 | tf_op jit(solution)/shard_map/ppermute | solution.py:22
  39.8 6.7 %collective-permute-start.22 = (bf16[204,128]{1,0:T(8,128)(2,1)S(1)}, bf16[204,128]{1,0:T(8,128)(2,1)S(1)}, u32[]{:S(2)}, u32[]{:S(2)}) collective-permute-start(bf16[204,128]{1,0:T(8,128)(2,1)S(1)} %get-tuple-element.37), channel_id=1, source_target_pairs={{0,8},{4,12},{8,0},{12,4},{1,9},{5,13},{9,1},{13,5},{2,10},{6,14},... | collective-permute-start | bytes 156680 | tf_op jit(solution)/shard_map/ppermute | solution.py:22
  42.9 5.9 %collective-permute-start.23 = (bf16[204,128]{1,0:T(8,128)(2,1)S(1)}, bf16[204,128]{1,0:T(8,128)(2,1)S(1)}, u32[]{:S(2)}, u32[]{:S(2)}) collective-permute-start(bf16[204,128]{1,0:T(8,128)(2,1)S(1)} %get-tuple-element.38), channel_id=1, source_target_pairs={{0,12},{4,8},{8,4},{12,0},{1,13},{5,9},{9,5},{13,1},{2,14},{6,10},... | collective-permute-start | bytes 156680 | tf_op jit(solution)/shard_map/ppermute | solution.py:22
  49.1 3.6 %collective-permute-start.24 = (f32[2,64]{1,0:T(2,128)S(1)}, f32[2,64]{1,0:T(2,128)S(1)}, u32[]{:S(2)}, u32[]{:S(2)}) collective-permute-start(f32[2,64]{1,0:T(2,128)S(1)} %dots.1), channel_id=1, source_target_pairs={{0,2},{1,3},{2,0},{3,1},{4,6},{5,7},{6,4},{7,5},{8,10},{9,11},{10,... | collective-permute-start | bytes 1544 | tf_op jit(solution)/shard_map/ppermute | solution.py:22
  52.7 1.1 %collective-permute-start.25 = (f32[2,64]{1,0:T(2,128)S(1)}, f32[2,64]{1,0:T(2,128)S(1)}, u32[]{:S(2)}, u32[]{:S(2)}) collective-permute-start(f32[2,64]{1,0:T(2,128)S(1)} %add.6), channel_id=1, source_target_pairs={{0,1},{1,0},{2,3},{3,2},{4,5},{5,4},{6,7},{7,6},{8,9},{9,8},{10,11... | collective-permute-start | bytes 1544 | tf_op jit(solution)/shard_map/ppermute | solution.py:22

commit v14 on v11

--- a/solution.py
+++ b/solution.py
@@ -350,8 +350,8 @@
     back = [result[0]] + [swap(result[k], "expert", k) for k in (1, 2, 3)]
     gate_grad = take_dots(hits, picks, grads, back)
     mixed, done = mix(routes, picks, back, tokens.shape[1])
-    gate_grad = gate_grad + hold(swap(gate_grad, "tensor", 2), [done])
-    gate_grad = gate_grad + swap(gate_grad, "tensor", 1)
+    across, beside, both = (swap(gate_grad, "tensor", bit) for bit in (2, 1, 3))
+    gate_grad = (gate_grad + hold(across, [done])) + (beside + hold(both, [done]))
     return mixed, gate_grad.T
 
 

time: 53.6 us -> 53 us (0.989)
  waiting for transfers between devices: 20.5 us -> 18.2 us
  starting transfers between devices: 20.2 us -> 21.9 us
    ppermute x26 -> x27, waiting for transfers between devices: 20.5 us -> 18.2 us  [swap(): return lax.ppermute(value, axis, [(i, i ^ bit) for i in range(size)])]
    ppermute x26 -> x27, starting transfers between devices: 20.2 us -> 21.9 us  [swap(): return lax.ppermute(value, axis, [(i, i ^ bit) for i in range(size)])]
  transfers between devices with their start and end apart: 26 -> 27, of which waited for: 15 -> 14; matrix products, arithmetic and copies ran while one was open for 0% -> 0% of each run, Pallas kernels for 14% -> 14%
where the time goes in v14:
time: 53 us; the launch traced here: 52.9 us
  starting transfers between devices  21.9 us (41%)
  waiting for transfers between devices  18.2 us (34%)
  Pallas kernels  10 us (19%)
  local copies, waits for them, and re-layouts  1.22 us (2%)
  between operations  0.92 us (2%)
  other arithmetic  0.57 us (1%)
    ppermute x27, starting transfers between devices, swap(): return lax.ppermute(value, axis, [(i, i ^ bit) for i in range(size)])  21.9 us
    ppermute x27, waiting for transfers between devices, swap(): return lax.ppermute(value, axis, [(i, i ^ bit) for i in range(size)])  18.2 us
    pallas_call x4, Pallas kernels, hidden_part(): pl.pallas_call(functools.partial(hidden_kernel, joined, parts, start), ou...  4.6 us
    pallas_call x4, Pallas kernels, down_part(): pl.pallas_call(functools.partial(down_kernel, len(pieces), where, slab, h...  2.55 us
    pallas_call x1, Pallas kernels, select_rows(): pl.pallas_call(select_kernel, out_shape=[jax.ShapeDtypeStruct((MOST, widt...  1.3 us
    unnamed x26, local copies, waits for them, and re-layouts  1.22 us
  transfers between devices with their start and end apart: 27, of which 14 were waited for; matrix products, arithmetic and copies ran while one was open for 0% of the time, Pallas kernels for 14%

profile of v14, /device:TPU:0, one launch (start us, length us, event | category | flops | bytes accessed | tf_op | source)
XLA Modules:
  0.0 52.9 jit_solution(17895546795638688490)
XLA Ops:
  0.6 0.0 slice-start
  0.7 0.0 slice-start.2
  0.7 1.3 %select_rows.1 = (bf16[34,768]{1,0:T(8,128)(2,1)S(1)}, bf16[204,128]{1,0:T(8,128)(2,1)S(1)}, bf16[204,128]{1,0:T(8,128)(2,1)S(1)}, bf16[204,128]{1,0:T(8,128)(2,1)S(1)}) custom-call(s32[1]{0:T(128)} %bitcast.me_ref, s32[1]{0:T(128)} %bitcast.3.t_ref, s32[2,64]{1,0:T(2,128)} %bitcast.12, bf16[64,768]{1,0:T(8,128)(2,1)} %tokens_hbm.1), custom_call_target="tpu_custom_call" | custom-call | flops 8000000000 | bytes 1000 | tf_op jit(solution)/shard_map/select_rows/pallas_call | solution.py:82
  2.0 3.1 %collective-permute-start = (bf16[204,128]{1,0:T(8,128)(2,1)S(1)}, bf16[204,128]{1,0:T(8,128)(2,1)S(1)}, u32[]{:S(2)}, u32[]{:S(2)}) collective-permute-start(bf16[204,128]{1,0:T(8,128)(2,1)S(1)} %get-tuple-element.30), channel_id=1, source_target_pairs={{0,4},{4,0},{8,12},{12,8},{1,5},{5,1},{9,13},{13,9},{2,6},{6,2},{1... | collective-permute-start | bytes 156680 | tf_op jit(solution)/shard_map/ppermute | solution.py:22
  5.1 2.6 %collective-permute-start.1 = (bf16[204,128]{1,0:T(8,128)(2,1)S(1)}, bf16[204,128]{1,0:T(8,128)(2,1)S(1)}, u32[]{:S(2)}, u32[]{:S(2)}) collective-permute-start(bf16[204,128]{1,0:T(8,128)(2,1)S(1)} %get-tuple-element.31), channel_id=1, source_target_pairs={{0,8},{4,12},{8,0},{12,4},{1,9},{5,13},{9,1},{13,5},{2,10},{6,14},... | collective-permute-start | bytes 156680 | tf_op jit(solution)/shard_map/ppermute | solution.py:22
  7.7 0.0 collective-permute-done.refs_0_
  7.7 3.5 %collective-permute-done.1.refs_1_.third_ref = bf16[204,128]{1,0:T(8,128)(2,1)S(1)} collective-permute-done((bf16[204,128]{1,0:T(8,128)(2,1)S(1)}, bf16[204,128]{1,0:T(8,128)(2,1)S(1)}, u32[]{:S(2)}, u32[]{:S(2)}) %collective-permute-start.1) | collective-permute-done | bytes 52256 | tf_op jit(solution)/shard_map/ppermute | solution.py:22
  11.2 1.6 %collective-permute-start.5 = (bf16[96,768]{1,0:T(8,128)(2,1)S(1)}, bf16[96,768]{1,0:T(8,128)(2,1)S(1)}, u32[]{:S(2)}, u32[]{:S(2)}) collective-permute-start(bf16[96,768]{1,0:T(8,128)(2,1)S(1)} %pack_near.1.refs_0_), channel_id=1, source_target_pairs={{0,2},{1,3},{2,0},{3,1},{4,6},{5,7},{6,4},{7,5},{8,10},{9,11},{10,... | collective-permute-start | bytes 442376 | tf_op jit(solution)/shard_map/ppermute | solution.py:22
  12.7 0.9 %collective-permute-done.2.fourth_ref = bf16[204,128]{1,0:T(8,128)(2,1)S(1)} collective-permute-done((bf16[204,128]{1,0:T(8,128)(2,1)S(1)}, bf16[204,128]{1,0:T(8,128)(2,1)S(1)}, u32[]{:S(2)}, u32[]{:S(2)}) %collective-permute-start.2) | collective-permute-done | bytes 52256 | tf_op jit(solution)/shard_map/ppermute | solution.py:22
  13.6 1.6 %collective-permute-start.6 = (bf16[40,768]{1,0:T(8,128)(2,1)S(1)}, bf16[40,768]{1,0:T(8,128)(2,1)S(1)}, u32[]{:S(2)}, u32[]{:S(2)}) collective-permute-start(bf16[40,768]{1,0:T(8,128)(2,1)S(1)} %pack_far.1.refs_1_), channel_id=1, source_target_pairs={{0,2},{1,3},{2,0},{3,1},{4,6},{5,7},{6,4},{7,5},{8,10},{9,11},{10,... | collective-permute-start | bytes 184328 | tf_op jit(solution)/shard_map/ppermute | solution.py:22
  15.2 0.0 collective-permute-start.3
  15.2 2.7 %collective-permute-done.6.refs_1_.refs_5_ = bf16[40,768]{1,0:T(8,128)(2,1)S(1)} collective-permute-done((bf16[40,768]{1,0:T(8,128)(2,1)S(1)}, bf16[40,768]{1,0:T(8,128)(2,1)S(1)}, u32[]{:S(2)}, u32[]{:S(2)}) %collective-permute-start.6) | collective-permute-done | bytes 61472 | tf_op jit(solution)/shard_map/ppermute | solution.py:22
  17.9 0.0 collective-permute-done.5.refs_0_
  17.9 0.5 collective-permute-start.4
  18.4 0.1 collective-permute-start.8
  18.5 0.9 %collective-permute-done.4.refs_3_ = bf16[40,768]{1,0:T(8,128)(2,1)S(1)} collective-permute-done((bf16[40,768]{1,0:T(8,128)(2,1)S(1)}, bf16[40,768]{1,0:T(8,128)(2,1)S(1)}, u32[]{:S(2)}, u32[]{:S(2)}) %collective-permute-start.4) | collective-permute-done | bytes 61472 | tf_op jit(solution)/shard_map/ppermute | solution.py:22
  19.4 0.3 collective-permute-done.8.refs_7_
  19.7 0.0 collective-permute-done.3.refs_2_
  19.7 0.0 collective-permute-done.7.refs_6_
  19.7 0.7 %hidden_part.4 = (bf16[136,256]{1,0:T(8,128)(2,1)S(1)}, bf16[4,136,768]{2,1,0:T(8,128)(2,1)S(1)}) custom-call(s32[1]{0:T(128)} %bitcast.3.t_ref, bf16[96,768]{1,0:T(8,128)(2,1)S(1)} %pack_near.1.refs_0_, bf16[40,768]{1,0:T(8,128)(2,1)S(1)} %pack_far.1.refs_1_, bf16[96,768]{1,0:T(8,128)(2,1)S(1)} %collective-permute-done.3.refs_2_, ...), custom_call_target="tpu_custom_call" | custom-call | flops 1000 | bytes 1000 | tf_op jit(solution)/shard_map/hidden_part/pallas_call | solution.py:177
  20.4 1.6 %collective-permute-start.12 = (bf16[136,256]{1,0:T(8,128)(2,1)S(1)}, bf16[136,256]{1,0:T(8,128)(2,1)S(1)}, u32[]{:S(2)}, u32[]{:S(2)}) collective-permute-start(bf16[136,256]{1,0:T(8,128)(2,1)S(1)} %get-tuple-element.34.refs_0_), channel_id=1, source_target_pairs={{0,2},{1,3},{2,0},{3,1},{4,6},{5,7},{6,4},{7,5},{8,10},{9,11},{10,... | collective-permute-start | bytes 208904 | tf_op jit(solution)/shard_map/ppermute | solution.py:22
  22.0 1.1 %hidden_part.5.refs_4_ = bf16[136,512]{1,0:T(8,128)(2,1)S(1)} custom-call(s32[1]{0:T(128)} %bitcast.3.t_ref, bf16[4,136,768]{2,1,0:T(8,128)(2,1)S(1)} %get-tuple-element.33.refs_0_, bf16[1,3072,2048]{2,1,0:T(8,128)(2,1)S(1)} %bitcast.7, bf16[1,3072,2048]{2,1,0:T(8,128)(2,1)S(1)} %copy-done), custom_call_target="tpu_custom_call" | custom-call | flops 1000 | bytes 1000 | tf_op jit(solution)/shard_map/hidden_part/pallas_call | solution.py:177
  23.1 0.6 %collective-permute-start.9 = (bf16[136,512]{1,0:T(8,128)(2,1)S(1)}, bf16[136,512]{1,0:T(8,128)(2,1)S(1)}, u32[]{:S(2)}, u32[]{:S(2)}) collective-permute-start(bf16[136,512]{1,0:T(8,128)(2,1)S(1)} %hidden_part.5.refs_4_), channel_id=1, source_target_pairs={{0,2},{1,3},{2,0},{3,1},{4,6},{5,7},{6,4},{7,5},{8,10},{9,11},{10,... | collective-permute-start | bytes 417800 | tf_op jit(solution)/shard_map/ppermute | solution.py:22
  23.7 1.1 %collective-permute-done.12.refs_3_.refs_2_ = bf16[136,256]{1,0:T(8,128)(2,1)S(1)} collective-permute-done((bf16[136,256]{1,0:T(8,128)(2,1)S(1)}, bf16[136,256]{1,0:T(8,128)(2,1)S(1)}, u32[]{:S(2)}, u32[]{:S(2)}) %collective-permute-start.12) | collective-permute-done | bytes 69664 | tf_op jit(solution)/shard_map/ppermute | solution.py:22
  24.8 1.6 %hidden_part.7.refs_2_ = bf16[136,768]{1,0:T(8,128)(2,1)S(1)} custom-call(s32[1]{0:T(128)} %bitcast.3.t_ref, bf16[4,136,768]{2,1,0:T(8,128)(2,1)S(1)} %get-tuple-element.33.refs_0_, bf16[1,3072,2048]{2,1,0:T(8,128)(2,1)S(1)} %bitcast.7, bf16[1,3072,2048]{2,1,0:T(8,128)(2,1)S(1)} %copy-done, bf16[136,256]{1,0:T(8,128)(2,1)S(1)} %collective-permute-done.12.refs_3_.refs_2_), custom_call_target="tpu_custom_call" | custom-call | flops 1000 | bytes 1000 | tf_op jit(solution)/shard_map/hidden_part/pallas_call | solution.py:177
  26.4 0.0 slice-start.5
  26.4 1.7 %collective-permute-start.18 = (bf16[136,768]{1,0:T(8,128)(2,1)S(1)}, bf16[136,768]{1,0:T(8,128)(2,1)S(1)}, u32[]{:S(2)}, u32[]{:S(2)}) collective-permute-start(bf16[136,768]{1,0:T(8,128)(2,1)S(1)} %hidden_part.7.refs_2_), channel_id=1, source_target_pairs={{0,2},{1,3},{2,0},{3,1},{4,6},{5,7},{6,4},{7,5},{8,10},{9,11},{10,... | collective-permute-start | bytes 626696 | tf_op jit(solution)/shard_map/ppermute | solution.py:22
  28.1 0.0 collective-permute-start.14
  28.1 0.5 collective-permute-start.16
  28.6 0.0 collective-permute-start.13
  28.7 0.7 %collective-permute-done.14.refs_1_ = bf16[136,256]{1,0:T(8,128)(2,1)S(1)} collective-permute-done((bf16[136,256]{1,0:T(8,128)(2,1)S(1)}, bf16[136,256]{1,0:T(8,128)(2,1)S(1)}, u32[]{:S(2)}, u32[]{:S(2)}) %collective-permute-start.14) | collective-permute-done | bytes 69664 | tf_op jit(solution)/shard_map/ppermute | solution.py:22
  29.4 0.2 collective-permute-start.15
  29.6 0.4 collective-permute-start.11
  29.9 1.2 %hidden_part.6.refs_2_ = bf16[136,512]{1,0:T(8,128)(2,1)S(1)} custom-call(s32[1]{0:T(128)} %bitcast.3.t_ref, bf16[4,136,768]{2,1,0:T(8,128)(2,1)S(1)} %get-tuple-element.33.refs_0_, bf16[1,3072,2048]{2,1,0:T(8,128)(2,1)S(1)} %bitcast.7, bf16[1,3072,2048]{2,1,0:T(8,128)(2,1)S(1)} %copy-done, bf16[136,512]{1,0:T(8,128)(2,1)S(1)} %collective-permute-done.9.refs_3_.refs_0_), custom_call_target="tpu_custom_call" | custom-call | flops 1000 | bytes 1000 | tf_op jit(solution)/shard_map/hidden_part/pallas_call | solution.py:177
  31.1 0.0 slice-start.8
  31.1 0.5 collective-permute-start.10
  31.6 0.6 %down_part.4.refs_5_.refs_1_ = f32[136,768]{1,0:T(8,128)S(1)} custom-call(s32[1]{0:T(128)} %bitcast.3.t_ref, bf16[136,256]{1,0:T(8,128)(2,1)S(1)} %get-tuple-element.34.refs_0_, bf16[136,256]{1,0:T(8,128)(2,1)S(1)} %collective-permute-done.14.refs_1_, bf16[136,256]{1,0:T(8,128)(2,1)S(1)} %collective-permute-done.12.refs_3_.refs_2_, ...), custom_call_target="tpu_custom_call" | custom-call | flops 427819008 | bytes 1000 | tf_op jit(solution)/shard_map/down_part/pallas_call | solution.py:215
  32.2 0.9 %collective-permute-done.18.refs_0_ = bf16[136,768]{1,0:T(8,128)(2,1)S(1)} collective-permute-done((bf16[136,768]{1,0:T(8,128)(2,1)S(1)}, bf16[136,768]{1,0:T(8,128)(2,1)S(1)}, u32[]{:S(2)}, u32[]{:S(2)}) %collective-permute-start.18) | collective-permute-done | bytes 208928 | tf_op jit(solution)/shard_map/ppermute | solution.py:22
  33.1 0.0 collective-permute-start.19
  33.1 0.5 collective-permute-start.20
  33.6 1.2 %slice-done.8 = s8[4194304]{0:T(1024)(128)(4,1)S(1)} async-done(((s8[12582912]{0:T(1024)(128)(4,1)}), s8[4194304]{0:T(1024)(128)(4,1)S(1)}, s32[]{:S(2)}) %slice-start.8) | async-done | bytes 4194328
  34.8 0.7 %down_part.5.refs_1_.refs_5_ = f32[136,768]{1,0:T(8,128)S(1)} custom-call(s32[1]{0:T(128)} %bitcast.3.t_ref, bf16[136,512]{1,0:T(8,128)(2,1)S(1)} %collective-permute-done.9.refs_3_.refs_0_, bf16[136,512]{1,0:T(8,128)(2,1)S(1)} %collective-permute-done.11.refs_1_, bf16[136,768]{1,0:T(8,128)(2,1)S(1)} %hidden_part.7.refs_2_, ...), custom_call_target="tpu_custom_call" | custom-call | flops 534773760 | bytes 1000 | tf_op jit(solution)/shard_map/down_part/pallas_call | solution.py:215
  35.6 1.4 %collective-permute-done.10.refs_0_ = bf16[136,512]{1,0:T(8,128)(2,1)S(1)} collective-permute-done((bf16[136,512]{1,0:T(8,128)(2,1)S(1)}, bf16[136,512]{1,0:T(8,128)(2,1)S(1)}, u32[]{:S(2)}, u32[]{:S(2)}) %collective-permute-start.10) | collective-permute-done | bytes 139296 | tf_op jit(solution)/shard_map/ppermute | solution.py:22
  36.9 0.1 collective-permute-start.17
  37.0 0.0 collective-permute-done.20.refs_3_
  37.0 0.0 collective-permute-done.19.refs_1_
  37.0 0.8 %down_part.6.refs_3_ = f32[136,768]{1,0:T(8,128)S(1)} custom-call(s32[1]{0:T(128)} %bitcast.3.t_ref, bf16[136,768]{1,0:T(8,128)(2,1)S(1)} %hold.7.refs_0_, bf16[136,768]{1,0:T(8,128)(2,1)S(1)} %collective-permute-done.19.refs_1_, bf16[136,512]{1,0:T(8,128)(2,1)S(1)} %hidden_part.6.refs_2_, bf16[136,512]{1,0:T(8,128)(2,1)S(1)} %collective-permute-done.20.refs_3_, ...), custom_call_target="tpu_custom_call" | custom-call | flops 534773760 | bytes 1000 | tf_op jit(solution)/shard_map/down_part/pallas_call | solution.py:215
  37.8 0.6 %collective-permute-done.17.refs_1_ = bf16[136,512]{1,0:T(8,128)(2,1)S(1)} collective-permute-done((bf16[136,512]{1,0:T(8,128)(2,1)S(1)}, bf16[136,512]{1,0:T(8,128)(2,1)S(1)}, u32[]{:S(2)}, u32[]{:S(2)}) %collective-permute-start.17) | collective-permute-done | bytes 139296 | tf_op jit(solution)/shard_map/ppermute | solution.py:22
  38.3 0.4 down_part.7
  38.8 0.1 collective-permute-start.21
  38.8 3.1 %collective-permute-start.22 = (bf16[204,128]{1,0:T(8,128)(2,1)S(1)}, bf16[204,128]{1,0:T(8,128)(2,1)S(1)}, u32[]{:S(2)}, u32[]{:S(2)}) collective-permute-start(bf16[204,128]{1,0:T(8,128)(2,1)S(1)} %get-tuple-element.37), channel_id=1, source_target_pairs={{0,8},{4,12},{8,0},{12,4},{1,9},{5,13},{9,1},{13,5},{2,10},{6,14},... | collective-permute-start | bytes 156680 | tf_op jit(solution)/shard_map/ppermute | solution.py:22
  41.9 1.3 %collective-permute-start.23 = (bf16[204,128]{1,0:T(8,128)(2,1)S(1)}, bf16[204,128]{1,0:T(8,128)(2,1)S(1)}, u32[]{:S(2)}, u32[]{:S(2)}) collective-permute-start(bf16[204,128]{1,0:T(8,128)(2,1)S(1)} %get-tuple-element.38), channel_id=1, source_target_pairs={{0,12},{4,8},{8,4},{12,0},{1,13},{5,9},{9,5},{13,1},{2,14},{6,10},... | collective-permute-start | bytes 156680 | tf_op jit(solution)/shard_map/ppermute | solution.py:22
  43.2 0.3 prepare.1
  43.6 0.2 collective-permute-done.21.refs_5_.refs_9_
  43.8 1.7 %collective-permute-done.22.refs_6_.refs_10_ = bf16[204,128]{1,0:T(8,128)(2,1)S(1)} collective-permute-done((bf16[204,128]{1,0:T(8,128)(2,1)S(1)}, bf16[204,128]{1,0:T(8,128)(2,1)S(1)}, u32[]{:S(2)}, u32[]{:S(2)}) %collective-permute-start.22) | collective-permute-done | bytes 52256 | tf_op jit(solution)/shard_map/ppermute | solution.py:22
  45.5 2.4 %collective-permute-done.23.refs_7_.refs_11_ = bf16[204,128]{1,0:T(8,128)(2,1)S(1)} collective-permute-done((bf16[204,128]{1,0:T(8,128)(2,1)S(1)}, bf16[204,128]{1,0:T(8,128)(2,1)S(1)}, u32[]{:S(2)}, u32[]{:S(2)}) %collective-permute-start.23) | collective-permute-done | bytes 52256 | tf_op jit(solution)/shard_map/ppermute | solution.py:22
  47.9 0.2 dots.1
  48.1 0.1 collective-permute-start.26
  48.2 0.6 %collective-permute-start.25 = (f32[2,64]{1,0:T(2,128)S(1)}, f32[2,64]{1,0:T(2,128)S(1)}, u32[]{:S(2)}, u32[]{:S(2)}) collective-permute-start(f32[2,64]{1,0:T(2,128)S(1)} %dots.1), channel_id=1, source_target_pairs={{0,1},{1,0},{2,3},{3,2},{4,5},{5,4},{6,7},{7,6},{8,9},{9,8},{10,11... | collective-permute-start | bytes 1544 | tf_op jit(solution)/shard_map/ppermute | solution.py:22
  48.7 1.6 %collective-permute-start.24 = (f32[2,64]{1,0:T(2,128)S(1)}, f32[2,64]{1,0:T(2,128)S(1)}, u32[]{:S(2)}, u32[]{:S(2)}) collective-permute-start(f32[2,64]{1,0:T(2,128)S(1)} %dots.1), channel_id=1, source_target_pairs={{0,2},{1,3},{2,0},{3,1},{4,6},{5,7},{6,4},{7,5},{8,10},{9,11},{10,... | collective-permute-start | bytes 1544 | tf_op jit(solution)/shard_map/ppermute | solution.py:22
  50.3 0.9 %mix.1 = (bf16[64,768]{1,0:T(8,128)(2,1)}, f32[8,128]{1,0:T(8,128)S(1)}) custom-call(f32[64,128]{1,0:T(8,128)S(1)} %get-tuple-element.24.routes_ref, f32[204,64]{1,0:T(8,128)S(1)} %get-tuple-element.25.refs_0_, f32[204,64]{1,0:T(8,128)S(1)} %get-tuple-element.26.refs_1_, f32[204,64]{1,0:T(8,128)S(1)} %get-tuple-element.27.refs_2_, ...), custom_call_target="tpu_custom_call" | custom-call | flops 1000000000 | bytes 1000 | tf_op jit(solution)/shard_map/mix/pallas_call | solution.py:296
  51.2 0.0 collective-permute-done.26.refs_0_
  51.2 1.1 %collective-permute-done.24.refs_0_ = f32[2,64]{1,0:T(2,128)S(1)} collective-permute-done((f32[2,64]{1,0:T(2,128)S(1)}, f32[2,64]{1,0:T(2,128)S(1)}, u32[]{:S(2)}, u32[]{:S(2)}) %collective-permute-start.24) | collective-permute-done | bytes 544 | tf_op jit(solution)/shard_map/ppermute | solution.py:22
  52.3 0.6 %add_bitcast_fusion = f32[64,2]{0,1:T(2,128)} fusion(f32[2,64]{1,0:T(2,128)S(1)} %collective-permute-done.25, f32[2,64]{1,0:T(2,128)S(1)} %hold.9, f32[2,64]{1,0:T(2,128)S(1)} %dots.1, f32[2,64]{1,0:T(2,128)S(1)} %hold.8), kind=kLoop, calls=%fused_computation | loop fusion | flops 384 | bytes 2560 | tf_op jit(solution)/shard_map/transpose | solution.py:355
  (39 shorter events, 0.1 us)
Async XLA Ops:
  0.6 19.1 %slice-start = ((s8[12582912]{0:T(1024)(128)(4,1)}), s8[4194304]{0:T(1024)(128)(4,1)S(1)}, s32[]{:S(2)}) async-start(s8[12582912]{0:T(1024)(128)(4,1)} %bitcast.6), calls=%async_computation | async-start | bytes 8388608
  0.6 19.1 %slice-start.1 = ((s8[12582912]{0:T(1024)(128)(4,1)}), s8[4194304]{0:T(1024)(128)(4,1)S(1)}, s32[]{:S(2)}) async-start(s8[12582912]{0:T(1024)(128)(4,1)} %bitcast.6), calls=%async_computation.1 | async-start | bytes 8388608
  0.7 19.1 %slice-start.2 = ((s8[12582912]{0:T(1024)(128)(4,1)}), s8[4194304]{0:T(1024)(128)(4,1)S(1)}, s32[]{:S(2)}) async-start(s8[12582912]{0:T(1024)(128)(4,1)} %bitcast.6), calls=%async_computation.2 | async-start | bytes 8388608
  0.7 19.1 %copy-start = (bf16[1,3072,2048]{2,1,0:T(8,128)(2,1)S(1)}, bf16[1,3072,2048]{2,1,0:T(8,128)(2,1)}, u32[]{:S(2)}) copy-start(bf16[1,3072,2048]{2,1,0:T(8,128)(2,1)} %refs_2_.6) | copy-start | bytes 37748740
  2.0 5.7 %collective-permute-start = (bf16[204,128]{1,0:T(8,128)(2,1)S(1)}, bf16[204,128]{1,0:T(8,128)(2,1)S(1)}, u32[]{:S(2)}, u32[]{:S(2)}) collective-permute-start(bf16[204,128]{1,0:T(8,128)(2,1)S(1)} %get-tuple-element.30), channel_id=1, source_target_pairs={{0,4},{4,0},{8,12},{12,8},{1,5},{5,1},{9,13},{13,9},{2,6},{6,2},{1... | collective-permute-start | bytes 156680 | tf_op jit(solution)/shard_map/ppermute | solution.py:22
  5.1 6.1 %collective-permute-start.1 = (bf16[204,128]{1,0:T(8,128)(2,1)S(1)}, bf16[204,128]{1,0:T(8,128)(2,1)S(1)}, u32[]{:S(2)}, u32[]{:S(2)}) collective-permute-start(bf16[204,128]{1,0:T(8,128)(2,1)S(1)} %get-tuple-element.31), channel_id=1, source_target_pairs={{0,8},{4,12},{8,0},{12,4},{1,9},{5,13},{9,1},{13,5},{2,10},{6,14},... | collective-permute-start | bytes 156680 | tf_op jit(solution)/shard_map/ppermute | solution.py:22
  7.7 5.9 %collective-permute-start.2 = (bf16[204,128]{1,0:T(8,128)(2,1)S(1)}, bf16[204,128]{1,0:T(8,128)(2,1)S(1)}, u32[]{:S(2)}, u32[]{:S(2)}) collective-permute-start(bf16[204,128]{1,0:T(8,128)(2,1)S(1)} %get-tuple-element.32), channel_id=1, source_target_pairs={{0,12},{4,8},{8,4},{12,0},{1,13},{5,9},{9,5},{13,1},{2,14},{6,10},... | collective-permute-start | bytes 156680 | tf_op jit(solution)/shard_map/ppermute | solution.py:22
  11.2 6.7 %collective-permute-start.5 = (bf16[96,768]{1,0:T(8,128)(2,1)S(1)}, bf16[96,768]{1,0:T(8,128)(2,1)S(1)}, u32[]{:S(2)}, u32[]{:S(2)}) collective-permute-start(bf16[96,768]{1,0:T(8,128)(2,1)S(1)} %pack_near.1.refs_0_), channel_id=1, source_target_pairs={{0,2},{1,3},{2,0},{3,1},{4,6},{5,7},{6,4},{7,5},{8,10},{9,11},{10,... | collective-permute-start | bytes 442376 | tf_op jit(solution)/shard_map/ppermute | solution.py:22
  13.6 4.3 %collective-permute-start.6 = (bf16[40,768]{1,0:T(8,128)(2,1)S(1)}, bf16[40,768]{1,0:T(8,128)(2,1)S(1)}, u32[]{:S(2)}, u32[]{:S(2)}) collective-permute-start(bf16[40,768]{1,0:T(8,128)(2,1)S(1)} %pack_far.1.refs_1_), channel_id=1, source_target_pairs={{0,2},{1,3},{2,0},{3,1},{4,6},{5,7},{6,4},{7,5},{8,10},{9,11},{10,... | collective-permute-start | bytes 184328 | tf_op jit(solution)/shard_map/ppermute | solution.py:22
  15.2 4.5 %collective-permute-start.3 = (bf16[96,768]{1,0:T(8,128)(2,1)S(1)}, bf16[96,768]{1,0:T(8,128)(2,1)S(1)}, u32[]{:S(2)}, u32[]{:S(2)}) collective-permute-start(bf16[96,768]{1,0:T(8,128)(2,1)S(1)} %pack_near.1.refs_0_), channel_id=1, source_target_pairs={{0,1},{1,0},{2,3},{3,2},{4,5},{5,4},{6,7},{7,6},{8,9},{9,8},{10,11... | collective-permute-start | bytes 442376 | tf_op jit(solution)/shard_map/ppermute | solution.py:22
  17.9 1.8 %collective-permute-start.7 = (bf16[96,768]{1,0:T(8,128)(2,1)S(1)}, bf16[96,768]{1,0:T(8,128)(2,1)S(1)}, u32[]{:S(2)}, u32[]{:S(2)}) collective-permute-start(bf16[96,768]{1,0:T(8,128)(2,1)S(1)} %hold.5.refs_4_), channel_id=1, source_target_pairs={{0,1},{1,0},{2,3},{3,2},{4,5},{5,4},{6,7},{7,6},{8,9},{9,8},{10,11... | collective-permute-start | bytes 442376 | tf_op jit(solution)/shard_map/ppermute | solution.py:22
  17.9 1.5 %collective-permute-start.4 = (bf16[40,768]{1,0:T(8,128)(2,1)S(1)}, bf16[40,768]{1,0:T(8,128)(2,1)S(1)}, u32[]{:S(2)}, u32[]{:S(2)}) collective-permute-start(bf16[40,768]{1,0:T(8,128)(2,1)S(1)} %pack_far.1.refs_1_), channel_id=1, source_target_pairs={{0,1},{1,0},{2,3},{3,2},{4,5},{5,4},{6,7},{7,6},{8,9},{9,8},{10,11... | collective-permute-start | bytes 184328 | tf_op jit(solution)/shard_map/ppermute | solution.py:22
  18.4 1.2 %collective-permute-start.8 = (bf16[40,768]{1,0:T(8,128)(2,1)S(1)}, bf16[40,768]{1,0:T(8,128)(2,1)S(1)}, u32[]{:S(2)}, u32[]{:S(2)}) collective-permute-start(bf16[40,768]{1,0:T(8,128)(2,1)S(1)} %collective-permute-done.6.refs_1_.refs_5_), channel_id=1, source_target_pairs={{0,1},{1,0},{2,3},{3,2},{4,5},{5,4},{6,7},{7,6},{8,9},{9,8},{10,11... | collective-permute-start | bytes 184328 | tf_op jit(solution)/shard_map/ppermute | solution.py:22
  20.4 4.4 %collective-permute-start.12 = (bf16[136,256]{1,0:T(8,128)(2,1)S(1)}, bf16[136,256]{1,0:T(8,128)(2,1)S(1)}, u32[]{:S(2)}, u32[]{:S(2)}) collective-permute-start(bf16[136,256]{1,0:T(8,128)(2,1)S(1)} %get-tuple-element.34.refs_0_), channel_id=1, source_target_pairs={{0,2},{1,3},{2,0},{3,1},{4,6},{5,7},{6,4},{7,5},{8,10},{9,11},{10,... | collective-permute-start | bytes 208904 | tf_op jit(solution)/shard_map/ppermute | solution.py:22
  23.1 6.5 %collective-permute-start.9 = (bf16[136,512]{1,0:T(8,128)(2,1)S(1)}, bf16[136,512]{1,0:T(8,128)(2,1)S(1)}, u32[]{:S(2)}, u32[]{:S(2)}) collective-permute-start(bf16[136,512]{1,0:T(8,128)(2,1)S(1)} %hidden_part.5.refs_4_), channel_id=1, source_target_pairs={{0,2},{1,3},{2,0},{3,1},{4,6},{5,7},{6,4},{7,5},{8,10},{9,11},{10,... | collective-permute-start | bytes 417800 | tf_op jit(solution)/shard_map/ppermute | solution.py:22
  24.8 6.8 %slice-start.3 = ((s8[12582912]{0:T(1024)(128)(4,1)}), s8[4194304]{0:T(1024)(128)(4,1)S(1)}, s32[]{:S(2)}) async-start(s8[12582912]{0:T(1024)(128)(4,1)} %bitcast.8), calls=%async_computation.3 | async-start | bytes 8388608
  24.8 6.8 %slice-start.4 = ((s8[12582912]{0:T(1024)(128)(4,1)}), s8[4194304]{0:T(1024)(128)(4,1)S(1)}, s32[]{:S(2)}) async-start(s8[12582912]{0:T(1024)(128)(4,1)} %bitcast.8), calls=%async_computation.4 | async-start | bytes 8388608
  26.4 5.1 %slice-start.5 = ((s8[12582912]{0:T(1024)(128)(4,1)}), s8[4194304]{0:T(1024)(128)(4,1)S(1)}, s32[]{:S(2)}) async-start(s8[12582912]{0:T(1024)(128)(4,1)} %bitcast.8), calls=%async_computation.5 | async-start | bytes 8388608
  26.4 6.7 %collective-permute-start.18 = (bf16[136,768]{1,0:T(8,128)(2,1)S(1)}, bf16[136,768]{1,0:T(8,128)(2,1)S(1)}, u32[]{:S(2)}, u32[]{:S(2)}) collective-permute-start(bf16[136,768]{1,0:T(8,128)(2,1)S(1)} %hidden_part.7.refs_2_), channel_id=1, source_target_pairs={{0,2},{1,3},{2,0},{3,1},{4,6},{5,7},{6,4},{7,5},{8,10},{9,11},{10,... | collective-permute-start | bytes 626696 | tf_op jit(solution)/shard_map/ppermute | solution.py:22
  28.1 1.3 %collective-permute-start.14 = (bf16[136,256]{1,0:T(8,128)(2,1)S(1)}, bf16[136,256]{1,0:T(8,128)(2,1)S(1)}, u32[]{:S(2)}, u32[]{:S(2)}) collective-permute-start(bf16[136,256]{1,0:T(8,128)(2,1)S(1)} %get-tuple-element.34.refs_0_), channel_id=1, source_target_pairs={{0,1},{1,0},{2,3},{3,2},{4,5},{5,4},{6,7},{7,6},{8,9},{9,8},{10,11... | collective-permute-start | bytes 208904 | tf_op jit(solution)/shard_map/ppermute | solution.py:22
  28.1 3.4 %collective-permute-start.16 = (bf16[136,512]{1,0:T(8,128)(2,1)S(1)}, bf16[136,512]{1,0:T(8,128)(2,1)S(1)}, u32[]{:S(2)}, u32[]{:S(2)}) collective-permute-start(bf16[136,512]{1,0:T(8,128)(2,1)S(1)} %hidden_part.5.refs_4_), channel_id=1, source_target_pairs={{0,1},{1,0},{2,3},{3,2},{4,5},{5,4},{6,7},{7,6},{8,9},{9,8},{10,11... | collective-permute-start | bytes 417800 | tf_op jit(solution)/shard_map/ppermute | solution.py:22
  28.6 5.0 %collective-permute-start.13 = (bf16[136,768]{1,0:T(8,128)(2,1)S(1)}, bf16[136,768]{1,0:T(8,128)(2,1)S(1)}, u32[]{:S(2)}, u32[]{:S(2)}) collective-permute-start(bf16[136,768]{1,0:T(8,128)(2,1)S(1)} %hidden_part.7.refs_2_), channel_id=1, source_target_pairs={{0,1},{1,0},{2,3},{3,2},{4,5},{5,4},{6,7},{7,6},{8,9},{9,8},{10,11... | collective-permute-start | bytes 626696 | tf_op jit(solution)/shard_map/ppermute | solution.py:22
  29.4 1.7 %collective-permute-start.15 = (bf16[136,256]{1,0:T(8,128)(2,1)S(1)}, bf16[136,256]{1,0:T(8,128)(2,1)S(1)}, u32[]{:S(2)}, u32[]{:S(2)}) collective-permute-start(bf16[136,256]{1,0:T(8,128)(2,1)S(1)} %collective-permute-done.12.refs_3_.refs_2_), channel_id=1, source_target_pairs={{0,1},{1,0},{2,3},{3,2},{4,5},{5,4},{6,7},{7,6},{8,9},{9,8},{10,11... | collective-permute-start | bytes 208904 | tf_op jit(solution)/shard_map/ppermute | solution.py:22
  29.6 4.1 %collective-permute-start.11 = (bf16[136,512]{1,0:T(8,128)(2,1)S(1)}, bf16[136,512]{1,0:T(8,128)(2,1)S(1)}, u32[]{:S(2)}, u32[]{:S(2)}) collective-permute-start(bf16[136,512]{1,0:T(8,128)(2,1)S(1)} %collective-permute-done.9.refs_3_.refs_0_), channel_id=1, source_target_pairs={{0,1},{1,0},{2,3},{3,2},{4,5},{5,4},{6,7},{7,6},{8,9},{9,8},{10,11... | collective-permute-start | bytes 417800 | tf_op jit(solution)/shard_map/ppermute | solution.py:22
  29.9 3.7 %slice-start.6 = ((s8[12582912]{0:T(1024)(128)(4,1)}), s8[4194304]{0:T(1024)(128)(4,1)S(1)}, s32[]{:S(2)}) async-start(s8[12582912]{0:T(1024)(128)(4,1)} %bitcast.10), calls=%async_computation.6 | async-start | bytes 8388608
  29.9 3.7 %slice-start.7 = ((s8[12582912]{0:T(1024)(128)(4,1)}), s8[4194304]{0:T(1024)(128)(4,1)S(1)}, s32[]{:S(2)}) async-start(s8[12582912]{0:T(1024)(128)(4,1)} %bitcast.10), calls=%async_computation.7 | async-start | bytes 8388608
  31.1 3.7 %slice-start.8 = ((s8[12582912]{0:T(1024)(128)(4,1)}), s8[4194304]{0:T(1024)(128)(4,1)S(1)}, s32[]{:S(2)}) async-start(s8[12582912]{0:T(1024)(128)(4,1)} %bitcast.10), calls=%async_computation.8 | async-start | bytes 8388608
  31.1 5.8 %collective-permute-start.10 = (bf16[136,512]{1,0:T(8,128)(2,1)S(1)}, bf16[136,512]{1,0:T(8,128)(2,1)S(1)}, u32[]{:S(2)}, u32[]{:S(2)}) collective-permute-start(bf16[136,512]{1,0:T(8,128)(2,1)S(1)} %hidden_part.6.refs_2_), channel_id=1, source_target_pairs={{0,2},{1,3},{2,0},{3,1},{4,6},{5,7},{6,4},{7,5},{8,10},{9,11},{10,... | collective-permute-start | bytes 417800 | tf_op jit(solution)/shard_map/ppermute | solution.py:22
  33.1 3.9 %collective-permute-start.19 = (bf16[136,768]{1,0:T(8,128)(2,1)S(1)}, bf16[136,768]{1,0:T(8,128)(2,1)S(1)}, u32[]{:S(2)}, u32[]{:S(2)}) collective-permute-start(bf16[136,768]{1,0:T(8,128)(2,1)S(1)} %hold.7.refs_0_), channel_id=1, source_target_pairs={{0,1},{1,0},{2,3},{3,2},{4,5},{5,4},{6,7},{7,6},{8,9},{9,8},{10,11... | collective-permute-start | bytes 626696 | tf_op jit(solution)/shard_map/ppermute | solution.py:22
  33.1 3.9 %collective-permute-start.20 = (bf16[136,512]{1,0:T(8,128)(2,1)S(1)}, bf16[136,512]{1,0:T(8,128)(2,1)S(1)}, u32[]{:S(2)}, u32[]{:S(2)}) collective-permute-start(bf16[136,512]{1,0:T(8,128)(2,1)S(1)} %hidden_part.6.refs_2_), channel_id=1, source_target_pairs={{0,1},{1,0},{2,3},{3,2},{4,5},{5,4},{6,7},{7,6},{8,9},{9,8},{10,11... | collective-permute-start | bytes 417800 | tf_op jit(solution)/shard_map/ppermute | solution.py:22
  36.9 6.3 %copy-start.1 = (bf16[64,768]{1,0:T(8,128)(2,1)S(1)}, bf16[64,768]{1,0:T(8,128)(2,1)}, u32[]{:S(2)}) copy-start(bf16[64,768]{1,0:T(8,128)(2,1)} %grad_ref.1) | copy-start | bytes 294916
  36.9 6.3 %copy-start.2 = (s32[64,2]{0,1:T(2,128)S(1)}, s32[64,2]{0,1:T(2,128)}, u32[]{:S(2)}) copy-start(s32[64,2]{0,1:T(2,128)} %param.8) | copy-start | bytes 1540
  36.9 6.3 %copy-start.3 = (f32[64,2]{0,1:T(2,128)S(1)}, f32[64,2]{0,1:T(2,128)}, u32[]{:S(2)}) copy-start(f32[64,2]{0,1:T(2,128)} %param.9) | copy-start | bytes 1540
  36.9 1.4 %collective-permute-start.17 = (bf16[136,512]{1,0:T(8,128)(2,1)S(1)}, bf16[136,512]{1,0:T(8,128)(2,1)S(1)}, u32[]{:S(2)}, u32[]{:S(2)}) collective-permute-start(bf16[136,512]{1,0:T(8,128)(2,1)S(1)} %hold.6.refs_0_), channel_id=1, source_target_pairs={{0,1},{1,0},{2,3},{3,2},{4,5},{5,4},{6,7},{7,6},{8,9},{9,8},{10,11... | collective-permute-start | bytes 417800 | tf_op jit(solution)/shard_map/ppermute | solution.py:22
  38.8 5.0 %collective-permute-start.21 = (bf16[204,128]{1,0:T(8,128)(2,1)S(1)}, bf16[204,128]{1,0:T(8,128)(2,1)S(1)}, u32[]{:S(2)}, u32[]{:S(2)}) collective-permute-start(bf16[204,128]{1,0:T(8,128)(2,1)S(1)} %get-tuple-element.36), channel_id=1, source_target_pairs={{0,4},{4,0},{8,12},{12,8},{1,5},{5,1},{9,13},{13,9},{2,6},{6,2},{1... | collective-permute-start | bytes 156680 | tf_op jit(solution)/shard_map/ppermute | solution.py:22
  38.8 6.7 %collective-permute-start.22 = (bf16[204,128]{1,0:T(8,128)(2,1)S(1)}, bf16[204,128]{1,0:T(8,128)(2,1)S(1)}, u32[]{:S(2)}, u32[]{:S(2)}) collective-permute-start(bf16[204,128]{1,0:T(8,128)(2,1)S(1)} %get-tuple-element.37), channel_id=1, source_target_pairs={{0,8},{4,12},{8,0},{12,4},{1,9},{5,13},{9,1},{13,5},{2,10},{6,14},... | collective-permute-start | bytes 156680 | tf_op jit(solution)/shard_map/ppermute | solution.py:22
  41.9 5.9 %collective-permute-start.23 = (bf16[204,128]{1,0:T(8,128)(2,1)S(1)}, bf16[204,128]{1,0:T(8,128)(2,1)S(1)}, u32[]{:S(2)}, u32[]{:S(2)}) collective-permute-start(bf16[204,128]{1,0:T(8,128)(2,1)S(1)} %get-tuple-element.38), channel_id=1, source_target_pairs={{0,12},{4,8},{8,4},{12,0},{1,13},{5,9},{9,5},{13,1},{2,14},{6,10},... | collective-permute-start | bytes 156680 | tf_op jit(solution)/shard_map/ppermute | solution.py:22
  48.1 3.1 %collective-permute-start.26 = (f32[2,64]{1,0:T(2,128)S(1)}, f32[2,64]{1,0:T(2,128)S(1)}, u32[]{:S(2)}, u32[]{:S(2)}) collective-permute-start(f32[2,64]{1,0:T(2,128)S(1)} %dots.1), channel_id=1, source_target_pairs={{0,3},{1,2},{2,1},{3,0},{4,7},{5,6},{6,5},{7,4},{8,11},{9,10},{10,... | collective-permute-start | bytes 1544 | tf_op jit(solution)/shard_map/ppermute | solution.py:22
  48.2 4.1 %collective-permute-start.25 = (f32[2,64]{1,0:T(2,128)S(1)}, f32[2,64]{1,0:T(2,128)S(1)}, u32[]{:S(2)}, u32[]{:S(2)}) collective-permute-start(f32[2,64]{1,0:T(2,128)S(1)} %dots.1), channel_id=1, source_target_pairs={{0,1},{1,0},{2,3},{3,2},{4,5},{5,4},{6,7},{7,6},{8,9},{9,8},{10,11... | collective-permute-start | bytes 1544 | tf_op jit(solution)/shard_map/ppermute | solution.py:22
  48.7 3.6 %collective-permute-start.24 = (f32[2,64]{1,0:T(2,128)S(1)}, f32[2,64]{1,0:T(2,128)S(1)}, u32[]{:S(2)}, u32[]{:S(2)}) collective-permute-start(f32[2,64]{1,0:T(2,128)S(1)} %dots.1), channel_id=1, source_target_pairs={{0,2},{1,3},{2,0},{3,1},{4,6},{5,7},{6,4},{7,5},{8,10},{9,11},{10,... | collective-permute-start | bytes 1544 | tf_op jit(solution)/shard_map/ppermute | solution.py:22

commit v15 on v12

--- a/solution.py
+++ b/solution.py
@@ -351,8 +351,8 @@
     back = [result[0]] + [swap(result[k], "expert", k) for k in (1, 2, 3)]
     gate_grad = take_dots(hits, picks, grads, back)
     mixed, done = mix(routes, picks, back, tokens.shape[1])
-    gate_grad = gate_grad + hold(swap(gate_grad, "tensor", 2), [done])
-    gate_grad = gate_grad + swap(gate_grad, "tensor", 1)
+    across, beside, both = (swap(gate_grad, "tensor", bit) for bit in (2, 1, 3))
+    gate_grad = (gate_grad + hold(across, [done])) + (beside + hold(both, [done]))
     return mixed, gate_grad.T
 
 

time: 54 us -> 53.7 us (level)
  waiting for transfers between devices: 20.8 us -> 19.1 us
  starting transfers between devices: 20.5 us -> 21.9 us
    ppermute x26 -> x27, waiting for transfers between devices: 20.8 us -> 19.1 us  [swap(): return lax.ppermute(value, axis, [(i, i ^ bit) for i in range(size)])]
    ppermute x26 -> x27, starting transfers between devices: 20.5 us -> 21.9 us  [swap(): return lax.ppermute(value, axis, [(i, i ^ bit) for i in range(size)])]
  transfers between devices with their start and end apart: 26 -> 27, of which waited for: 13 -> 12; matrix products, arithmetic and copies ran while one was open for 0% -> 0% of each run, Pallas kernels for 14% -> 14%
where the time goes in v15:
time: 53.7 us; the launch traced here: 53.6 us
  starting transfers between devices  21.9 us (41%)
  waiting for transfers between devices  19.1 us (36%)
  Pallas kernels  10 us (19%)
  local copies, waits for them, and re-layouts  1.06 us (2%)
  between operations  0.93 us (2%)
  other arithmetic  0.57 us (1%)
    ppermute x27, starting transfers between devices, swap(): return lax.ppermute(value, axis, [(i, i ^ bit) for i in range(size)])  21.9 us
    ppermute x27, waiting for transfers between devices, swap(): return lax.ppermute(value, axis, [(i, i ^ bit) for i in range(size)])  19.1 us
    pallas_call x4, Pallas kernels, hidden_part(): pl.pallas_call(functools.partial(hidden_kernel, joined, parts, start), ou...  4.6 us
    pallas_call x4, Pallas kernels, down_part(): pl.pallas_call(functools.partial(down_kernel, len(pieces), where, slab, h...  2.55 us
    pallas_call x1, Pallas kernels, select_rows(): pl.pallas_call(select_kernel, out_shape=[jax.ShapeDtypeStruct((MOST, widt...  1.3 us
  transfers between devices with their start and end apart: 27, of which 12 were waited for; matrix products, arithmetic and copies ran while one was open for 0% of the time, Pallas kernels for 14%

profile of v15, /device:TPU:0, one launch (start us, length us, event | category | flops | bytes accessed | tf_op | source)
XLA Modules:
  0.0 53.6 jit_solution(6749492012191069125)
XLA Ops:
  0.6 0.0 slice-start
  0.6 0.0 slice-start.1
  0.7 0.0 slice-start.2
  0.7 1.3 %select_rows.1 = (bf16[34,768]{1,0:T(8,128)(2,1)S(1)}, bf16[204,128]{1,0:T(8,128)(2,1)S(1)}, bf16[204,128]{1,0:T(8,128)(2,1)S(1)}, bf16[204,128]{1,0:T(8,128)(2,1)S(1)}) custom-call(s32[1]{0:T(128)} %bitcast.me_ref, s32[1]{0:T(128)} %bitcast.3.t_ref, s32[2,64]{1,0:T(2,128)} %bitcast.12, bf16[64,768]{1,0:T(8,128)(2,1)} %tokens_hbm.1), custom_call_target="tpu_custom_call" | custom-call | flops 8000000000 | bytes 1000 | tf_op jit(solution)/shard_map/select_rows/pallas_call | solution.py:82
  2.0 3.1 %collective-permute-start = (bf16[204,128]{1,0:T(8,128)(2,1)S(1)}, bf16[204,128]{1,0:T(8,128)(2,1)S(1)}, u32[]{:S(2)}, u32[]{:S(2)}) collective-permute-start(bf16[204,128]{1,0:T(8,128)(2,1)S(1)} %get-tuple-element.30), channel_id=1, source_target_pairs={{0,4},{4,0},{8,12},{12,8},{1,5},{5,1},{9,13},{13,9},{2,6},{6,2},{1... | collective-permute-start | bytes 156680 | tf_op jit(solution)/shard_map/ppermute | solution.py:22
  5.1 2.6 %collective-permute-start.1 = (bf16[204,128]{1,0:T(8,128)(2,1)S(1)}, bf16[204,128]{1,0:T(8,128)(2,1)S(1)}, u32[]{:S(2)}, u32[]{:S(2)}) collective-permute-start(bf16[204,128]{1,0:T(8,128)(2,1)S(1)} %get-tuple-element.31), channel_id=1, source_target_pairs={{0,8},{4,12},{8,0},{12,4},{1,9},{5,13},{9,1},{13,5},{2,10},{6,14},... | collective-permute-start | bytes 156680 | tf_op jit(solution)/shard_map/ppermute | solution.py:22
  7.7 0.0 collective-permute-start.2
  7.7 0.0 collective-permute-done.refs_0_
  7.7 3.5 %collective-permute-done.1.refs_1_.third_ref = bf16[204,128]{1,0:T(8,128)(2,1)S(1)} collective-permute-done((bf16[204,128]{1,0:T(8,128)(2,1)S(1)}, bf16[204,128]{1,0:T(8,128)(2,1)S(1)}, u32[]{:S(2)}, u32[]{:S(2)}) %collective-permute-start.1) | collective-permute-done | bytes 52256 | tf_op jit(solution)/shard_map/ppermute | solution.py:22
  11.2 1.6 %collective-permute-start.5 = (bf16[96,768]{1,0:T(8,128)(2,1)S(1)}, bf16[96,768]{1,0:T(8,128)(2,1)S(1)}, u32[]{:S(2)}, u32[]{:S(2)}) collective-permute-start(bf16[96,768]{1,0:T(8,128)(2,1)S(1)} %pack_near.1.refs_0_), channel_id=1, source_target_pairs={{0,2},{1,3},{2,0},{3,1},{4,6},{5,7},{6,4},{7,5},{8,10},{9,11},{10,... | collective-permute-start | bytes 442376 | tf_op jit(solution)/shard_map/ppermute | solution.py:22
  12.7 0.0 collective-permute-start.3
  12.7 0.9 %collective-permute-done.2.fourth_ref = bf16[204,128]{1,0:T(8,128)(2,1)S(1)} collective-permute-done((bf16[204,128]{1,0:T(8,128)(2,1)S(1)}, bf16[204,128]{1,0:T(8,128)(2,1)S(1)}, u32[]{:S(2)}, u32[]{:S(2)}) %collective-permute-start.2) | collective-permute-done | bytes 52256 | tf_op jit(solution)/shard_map/ppermute | solution.py:22
  13.6 1.6 %collective-permute-start.6 = (bf16[40,768]{1,0:T(8,128)(2,1)S(1)}, bf16[40,768]{1,0:T(8,128)(2,1)S(1)}, u32[]{:S(2)}, u32[]{:S(2)}) collective-permute-start(bf16[40,768]{1,0:T(8,128)(2,1)S(1)} %pack_far.1.refs_1_), channel_id=1, source_target_pairs={{0,2},{1,3},{2,0},{3,1},{4,6},{5,7},{6,4},{7,5},{8,10},{9,11},{10,... | collective-permute-start | bytes 184328 | tf_op jit(solution)/shard_map/ppermute | solution.py:22
  15.2 0.0 collective-permute-start.4
  15.2 2.7 %collective-permute-done.6.refs_1_.refs_5_ = bf16[40,768]{1,0:T(8,128)(2,1)S(1)} collective-permute-done((bf16[40,768]{1,0:T(8,128)(2,1)S(1)}, bf16[40,768]{1,0:T(8,128)(2,1)S(1)}, u32[]{:S(2)}, u32[]{:S(2)}) %collective-permute-start.6) | collective-permute-done | bytes 61472 | tf_op jit(solution)/shard_map/ppermute | solution.py:22
  17.9 0.1 collective-permute-start.7
  18.0 0.5 collective-permute-start.8
  18.5 0.9 %collective-permute-done.8.refs_7_ = bf16[40,768]{1,0:T(8,128)(2,1)S(1)} collective-permute-done((bf16[40,768]{1,0:T(8,128)(2,1)S(1)}, bf16[40,768]{1,0:T(8,128)(2,1)S(1)}, u32[]{:S(2)}, u32[]{:S(2)}) %collective-permute-start.8) | collective-permute-done | bytes 61472 | tf_op jit(solution)/shard_map/ppermute | solution.py:22
  19.5 0.7 %hidden_part.4 = (bf16[136,256]{1,0:T(8,128)(2,1)S(1)}, bf16[4,136,768]{2,1,0:T(8,128)(2,1)S(1)}) custom-call(s32[1]{0:T(128)} %bitcast.3.t_ref, bf16[96,768]{1,0:T(8,128)(2,1)S(1)} %pack_near.1.refs_0_, bf16[40,768]{1,0:T(8,128)(2,1)S(1)} %pack_far.1.refs_1_, bf16[96,768]{1,0:T(8,128)(2,1)S(1)} %collective-permute-done.3.refs_2_, ...), custom_call_target="tpu_custom_call" | custom-call | flops 1000 | bytes 1000 | tf_op jit(solution)/shard_map/hidden_part/pallas_call | solution.py:177
  20.2 1.5 %collective-permute-start.12 = (bf16[136,256]{1,0:T(8,128)(2,1)S(1)}, bf16[136,256]{1,0:T(8,128)(2,1)S(1)}, u32[]{:S(2)}, u32[]{:S(2)}) collective-permute-start(bf16[136,256]{1,0:T(8,128)(2,1)S(1)} %get-tuple-element.34.refs_0_), channel_id=1, source_target_pairs={{0,2},{1,3},{2,0},{3,1},{4,6},{5,7},{6,4},{7,5},{8,10},{9,11},{10,... | collective-permute-start | bytes 208904 | tf_op jit(solution)/shard_map/ppermute | solution.py:22
  21.7 1.1 %hidden_part.5.refs_4_ = bf16[136,512]{1,0:T(8,128)(2,1)S(1)} custom-call(s32[1]{0:T(128)} %bitcast.3.t_ref, bf16[4,136,768]{2,1,0:T(8,128)(2,1)S(1)} %get-tuple-element.33.refs_0_, bf16[1,3072,2048]{2,1,0:T(8,128)(2,1)S(1)} %bitcast.7, bf16[1,3072,2048]{2,1,0:T(8,128)(2,1)S(1)} %copy-done), custom_call_target="tpu_custom_call" | custom-call | flops 1000 | bytes 1000 | tf_op jit(solution)/shard_map/hidden_part/pallas_call | solution.py:177
  22.9 0.6 %collective-permute-start.9 = (bf16[136,512]{1,0:T(8,128)(2,1)S(1)}, bf16[136,512]{1,0:T(8,128)(2,1)S(1)}, u32[]{:S(2)}, u32[]{:S(2)}) collective-permute-start(bf16[136,512]{1,0:T(8,128)(2,1)S(1)} %hidden_part.5.refs_4_), channel_id=1, source_target_pairs={{0,2},{1,3},{2,0},{3,1},{4,6},{5,7},{6,4},{7,5},{8,10},{9,11},{10,... | collective-permute-start | bytes 417800 | tf_op jit(solution)/shard_map/ppermute | solution.py:22
  23.5 1.1 %collective-permute-done.12.refs_3_.refs_2_ = bf16[136,256]{1,0:T(8,128)(2,1)S(1)} collective-permute-done((bf16[136,256]{1,0:T(8,128)(2,1)S(1)}, bf16[136,256]{1,0:T(8,128)(2,1)S(1)}, u32[]{:S(2)}, u32[]{:S(2)}) %collective-permute-start.12) | collective-permute-done | bytes 69664 | tf_op jit(solution)/shard_map/ppermute | solution.py:22
  24.6 1.6 %hidden_part.7.refs_2_ = bf16[136,768]{1,0:T(8,128)(2,1)S(1)} custom-call(s32[1]{0:T(128)} %bitcast.3.t_ref, bf16[4,136,768]{2,1,0:T(8,128)(2,1)S(1)} %get-tuple-element.33.refs_0_, bf16[1,3072,2048]{2,1,0:T(8,128)(2,1)S(1)} %bitcast.7, bf16[1,3072,2048]{2,1,0:T(8,128)(2,1)S(1)} %copy-done, bf16[136,256]{1,0:T(8,128)(2,1)S(1)} %collective-permute-done.12.refs_3_.refs_2_), custom_call_target="tpu_custom_call" | custom-call | flops 1000 | bytes 1000 | tf_op jit(solution)/shard_map/hidden_part/pallas_call | solution.py:177
  26.3 0.0 slice-start.5
  26.3 1.6 %collective-permute-start.18 = (bf16[136,768]{1,0:T(8,128)(2,1)S(1)}, bf16[136,768]{1,0:T(8,128)(2,1)S(1)}, u32[]{:S(2)}, u32[]{:S(2)}) collective-permute-start(bf16[136,768]{1,0:T(8,128)(2,1)S(1)} %hidden_part.7.refs_2_), channel_id=1, source_target_pairs={{0,2},{1,3},{2,0},{3,1},{4,6},{5,7},{6,4},{7,5},{8,10},{9,11},{10,... | collective-permute-start | bytes 626696 | tf_op jit(solution)/shard_map/ppermute | solution.py:22
  27.9 0.0 collective-permute-start.14
  27.9 0.5 collective-permute-start.16
  28.4 0.0 collective-permute-start.13
  28.4 0.7 %collective-permute-done.14.refs_1_ = bf16[136,256]{1,0:T(8,128)(2,1)S(1)} collective-permute-done((bf16[136,256]{1,0:T(8,128)(2,1)S(1)}, bf16[136,256]{1,0:T(8,128)(2,1)S(1)}, u32[]{:S(2)}, u32[]{:S(2)}) %collective-permute-start.14) | collective-permute-done | bytes 69664 | tf_op jit(solution)/shard_map/ppermute | solution.py:22
  29.1 0.2 collective-permute-start.15
  29.3 0.4 collective-permute-start.11
  29.7 1.2 %hidden_part.6.refs_2_ = bf16[136,512]{1,0:T(8,128)(2,1)S(1)} custom-call(s32[1]{0:T(128)} %bitcast.3.t_ref, bf16[4,136,768]{2,1,0:T(8,128)(2,1)S(1)} %get-tuple-element.33.refs_0_, bf16[1,3072,2048]{2,1,0:T(8,128)(2,1)S(1)} %bitcast.7, bf16[1,3072,2048]{2,1,0:T(8,128)(2,1)S(1)} %copy-done, bf16[136,512]{1,0:T(8,128)(2,1)S(1)} %collective-permute-done.9.refs_3_.refs_0_), custom_call_target="tpu_custom_call" | custom-call | flops 1000 | bytes 1000 | tf_op jit(solution)/shard_map/hidden_part/pallas_call | solution.py:177
  30.8 0.0 slice-start.8
  30.8 0.6 %collective-permute-start.10 = (bf16[136,512]{1,0:T(8,128)(2,1)S(1)}, bf16[136,512]{1,0:T(8,128)(2,1)S(1)}, u32[]{:S(2)}, u32[]{:S(2)}) collective-permute-start(bf16[136,512]{1,0:T(8,128)(2,1)S(1)} %hidden_part.6.refs_2_), channel_id=1, source_target_pairs={{0,2},{1,3},{2,0},{3,1},{4,6},{5,7},{6,4},{7,5},{8,10},{9,11},{10,... | collective-permute-start | bytes 417800 | tf_op jit(solution)/shard_map/ppermute | solution.py:22
  31.4 0.0 collective-permute-done.16.refs_5_
  31.4 0.6 %down_part.4.refs_5_.refs_1_ = f32[136,768]{1,0:T(8,128)S(1)} custom-call(s32[1]{0:T(128)} %bitcast.3.t_ref, bf16[136,256]{1,0:T(8,128)(2,1)S(1)} %get-tuple-element.34.refs_0_, bf16[136,256]{1,0:T(8,128)(2,1)S(1)} %collective-permute-done.14.refs_1_, bf16[136,256]{1,0:T(8,128)(2,1)S(1)} %collective-permute-done.12.refs_3_.refs_2_, ...), custom_call_target="tpu_custom_call" | custom-call | flops 427819008 | bytes 1000 | tf_op jit(solution)/shard_map/down_part/pallas_call | solution.py:215
  32.1 0.9 %collective-permute-done.18.refs_0_ = bf16[136,768]{1,0:T(8,128)(2,1)S(1)} collective-permute-done((bf16[136,768]{1,0:T(8,128)(2,1)S(1)}, bf16[136,768]{1,0:T(8,128)(2,1)S(1)}, u32[]{:S(2)}, u32[]{:S(2)}) %collective-permute-start.18) | collective-permute-done | bytes 208928 | tf_op jit(solution)/shard_map/ppermute | solution.py:22
  33.0 0.5 collective-permute-start.20
  33.5 0.0 collective-permute-done.13.refs_3_
  33.5 0.0 collective-permute-done.11.refs_1_
  33.5 1.0 %slice-done.8 = s8[4194304]{0:T(1024)(128)(4,1)S(1)} async-done(((s8[12582912]{0:T(1024)(128)(4,1)}), s8[4194304]{0:T(1024)(128)(4,1)S(1)}, s32[]{:S(2)}) %slice-start.8) | async-done | bytes 4194328
  34.5 0.7 %down_part.5.refs_1_.refs_5_ = f32[136,768]{1,0:T(8,128)S(1)} custom-call(s32[1]{0:T(128)} %bitcast.3.t_ref, bf16[136,512]{1,0:T(8,128)(2,1)S(1)} %collective-permute-done.9.refs_3_.refs_0_, bf16[136,512]{1,0:T(8,128)(2,1)S(1)} %collective-permute-done.11.refs_1_, bf16[136,768]{1,0:T(8,128)(2,1)S(1)} %hidden_part.7.refs_2_, ...), custom_call_target="tpu_custom_call" | custom-call | flops 534773760 | bytes 1000 | tf_op jit(solution)/shard_map/down_part/pallas_call | solution.py:215
  35.3 1.3 %collective-permute-done.10.refs_0_ = bf16[136,512]{1,0:T(8,128)(2,1)S(1)} collective-permute-done((bf16[136,512]{1,0:T(8,128)(2,1)S(1)}, bf16[136,512]{1,0:T(8,128)(2,1)S(1)}, u32[]{:S(2)}, u32[]{:S(2)}) %collective-permute-start.10) | collective-permute-done | bytes 139296 | tf_op jit(solution)/shard_map/ppermute | solution.py:22
  36.6 0.1 collective-permute-start.17
  36.7 0.0 collective-permute-done.20.refs_3_
  36.7 0.8 %down_part.6.refs_3_ = f32[136,768]{1,0:T(8,128)S(1)} custom-call(s32[1]{0:T(128)} %bitcast.3.t_ref, bf16[136,768]{1,0:T(8,128)(2,1)S(1)} %hold.7.refs_0_, bf16[136,768]{1,0:T(8,128)(2,1)S(1)} %collective-permute-done.19.refs_1_, bf16[136,512]{1,0:T(8,128)(2,1)S(1)} %hidden_part.6.refs_2_, bf16[136,512]{1,0:T(8,128)(2,1)S(1)} %collective-permute-done.20.refs_3_, ...), custom_call_target="tpu_custom_call" | custom-call | flops 534773760 | bytes 1000 | tf_op jit(solution)/shard_map/down_part/pallas_call | solution.py:215
  37.5 0.6 %collective-permute-done.17.refs_1_ = bf16[136,512]{1,0:T(8,128)(2,1)S(1)} collective-permute-done((bf16[136,512]{1,0:T(8,128)(2,1)S(1)}, bf16[136,512]{1,0:T(8,128)(2,1)S(1)}, u32[]{:S(2)}, u32[]{:S(2)}) %collective-permute-start.17) | collective-permute-done | bytes 139296 | tf_op jit(solution)/shard_map/ppermute | solution.py:22
  38.1 0.4 down_part.7
  38.5 0.6 %collective-permute-start.21 = (bf16[204,128]{1,0:T(8,128)(2,1)S(1)}, bf16[204,128]{1,0:T(8,128)(2,1)S(1)}, u32[]{:S(2)}, u32[]{:S(2)}) collective-permute-start(bf16[204,128]{1,0:T(8,128)(2,1)S(1)} %get-tuple-element.36), channel_id=1, source_target_pairs={{0,4},{4,0},{8,12},{12,8},{1,5},{5,1},{9,13},{13,9},{2,6},{6,2},{1... | collective-permute-start | bytes 156680 | tf_op jit(solution)/shard_map/ppermute | solution.py:22
  39.1 3.3 %collective-permute-start.22 = (bf16[204,128]{1,0:T(8,128)(2,1)S(1)}, bf16[204,128]{1,0:T(8,128)(2,1)S(1)}, u32[]{:S(2)}, u32[]{:S(2)}) collective-permute-start(bf16[204,128]{1,0:T(8,128)(2,1)S(1)} %get-tuple-element.37), channel_id=1, source_target_pairs={{0,8},{4,12},{8,0},{12,4},{1,9},{5,13},{9,1},{13,5},{2,10},{6,14},... | collective-permute-start | bytes 156680 | tf_op jit(solution)/shard_map/ppermute | solution.py:22
  42.4 0.5 %collective-permute-start.23 = (bf16[204,128]{1,0:T(8,128)(2,1)S(1)}, bf16[204,128]{1,0:T(8,128)(2,1)S(1)}, u32[]{:S(2)}, u32[]{:S(2)}) collective-permute-start(bf16[204,128]{1,0:T(8,128)(2,1)S(1)} %get-tuple-element.38), channel_id=1, source_target_pairs={{0,12},{4,8},{8,4},{12,0},{1,13},{5,9},{9,5},{13,1},{2,14},{6,10},... | collective-permute-start | bytes 156680 | tf_op jit(solution)/shard_map/ppermute | solution.py:22
  42.9 0.3 prepare.1
  43.3 0.0 collective-permute-done.21.refs_5_.refs_9_
  43.3 2.5 %collective-permute-done.22.refs_6_.refs_10_ = bf16[204,128]{1,0:T(8,128)(2,1)S(1)} collective-permute-done((bf16[204,128]{1,0:T(8,128)(2,1)S(1)}, bf16[204,128]{1,0:T(8,128)(2,1)S(1)}, u32[]{:S(2)}, u32[]{:S(2)}) %collective-permute-start.22) | collective-permute-done | bytes 52256 | tf_op jit(solution)/shard_map/ppermute | solution.py:22
  45.8 2.6 %collective-permute-done.23.refs_7_.refs_11_ = bf16[204,128]{1,0:T(8,128)(2,1)S(1)} collective-permute-done((bf16[204,128]{1,0:T(8,128)(2,1)S(1)}, bf16[204,128]{1,0:T(8,128)(2,1)S(1)}, u32[]{:S(2)}, u32[]{:S(2)}) %collective-permute-start.23) | collective-permute-done | bytes 52256 | tf_op jit(solution)/shard_map/ppermute | solution.py:22
  48.3 0.2 dots.1
  48.5 0.1 collective-permute-start.26
  48.6 0.8 %collective-permute-start.25 = (f32[2,64]{1,0:T(2,128)S(1)}, f32[2,64]{1,0:T(2,128)S(1)}, u32[]{:S(2)}, u32[]{:S(2)}) collective-permute-start(f32[2,64]{1,0:T(2,128)S(1)} %dots.1), channel_id=1, source_target_pairs={{0,1},{1,0},{2,3},{3,2},{4,5},{5,4},{6,7},{7,6},{8,9},{9,8},{10,11... | collective-permute-start | bytes 1544 | tf_op jit(solution)/shard_map/ppermute | solution.py:22
  49.4 1.3 %collective-permute-start.24 = (f32[2,64]{1,0:T(2,128)S(1)}, f32[2,64]{1,0:T(2,128)S(1)}, u32[]{:S(2)}, u32[]{:S(2)}) collective-permute-start(f32[2,64]{1,0:T(2,128)S(1)} %dots.1), channel_id=1, source_target_pairs={{0,2},{1,3},{2,0},{3,1},{4,6},{5,7},{6,4},{7,5},{8,10},{9,11},{10,... | collective-permute-start | bytes 1544 | tf_op jit(solution)/shard_map/ppermute | solution.py:22
  50.8 0.9 %mix.1 = (bf16[64,768]{1,0:T(8,128)(2,1)}, f32[8,128]{1,0:T(8,128)S(1)}) custom-call(f32[64,128]{1,0:T(8,128)S(1)} %get-tuple-element.24.routes_ref, f32[204,64]{1,0:T(8,128)S(1)} %get-tuple-element.25.refs_0_, f32[204,64]{1,0:T(8,128)S(1)} %get-tuple-element.26.refs_1_, f32[204,64]{1,0:T(8,128)S(1)} %get-tuple-element.27.refs_2_, ...), custom_call_target="tpu_custom_call" | custom-call | flops 1000000000 | bytes 1000 | tf_op jit(solution)/shard_map/mix/pallas_call | solution.py:296
  51.7 1.3 %collective-permute-done.24.refs_0_ = f32[2,64]{1,0:T(2,128)S(1)} collective-permute-done((f32[2,64]{1,0:T(2,128)S(1)}, f32[2,64]{1,0:T(2,128)S(1)}, u32[]{:S(2)}, u32[]{:S(2)}) %collective-permute-start.24) | collective-permute-done | bytes 544 | tf_op jit(solution)/shard_map/ppermute | solution.py:22
  53.0 0.0 collective-permute-done.25
  53.0 0.6 %add_bitcast_fusion = f32[64,2]{0,1:T(2,128)} fusion(f32[2,64]{1,0:T(2,128)S(1)} %collective-permute-done.25, f32[2,64]{1,0:T(2,128)S(1)} %hold.9, f32[2,64]{1,0:T(2,128)S(1)} %dots.1, f32[2,64]{1,0:T(2,128)S(1)} %hold.8), kind=kLoop, calls=%fused_computation | loop fusion | flops 384 | bytes 2560 | tf_op jit(solution)/shard_map/transpose | solution.py:356
  (39 shorter events, 0.1 us)
Async XLA Ops:
  0.6 18.8 %slice-start = ((s8[12582912]{0:T(1024)(128)(4,1)}), s8[4194304]{0:T(1024)(128)(4,1)S(1)}, s32[]{:S(2)}) async-start(s8[12582912]{0:T(1024)(128)(4,1)} %bitcast.6), calls=%async_computation | async-start | bytes 8388608
  0.6 18.8 %slice-start.1 = ((s8[12582912]{0:T(1024)(128)(4,1)}), s8[4194304]{0:T(1024)(128)(4,1)S(1)}, s32[]{:S(2)}) async-start(s8[12582912]{0:T(1024)(128)(4,1)} %bitcast.6), calls=%async_computation.1 | async-start | bytes 8388608
  0.7 18.8 %slice-start.2 = ((s8[12582912]{0:T(1024)(128)(4,1)}), s8[4194304]{0:T(1024)(128)(4,1)S(1)}, s32[]{:S(2)}) async-start(s8[12582912]{0:T(1024)(128)(4,1)} %bitcast.6), calls=%async_computation.2 | async-start | bytes 8388608
  0.7 18.8 %copy-start = (bf16[1,3072,2048]{2,1,0:T(8,128)(2,1)S(1)}, bf16[1,3072,2048]{2,1,0:T(8,128)(2,1)}, u32[]{:S(2)}) copy-start(bf16[1,3072,2048]{2,1,0:T(8,128)(2,1)} %refs_2_.6) | copy-start | bytes 37748740
  2.0 5.7 %collective-permute-start = (bf16[204,128]{1,0:T(8,128)(2,1)S(1)}, bf16[204,128]{1,0:T(8,128)(2,1)S(1)}, u32[]{:S(2)}, u32[]{:S(2)}) collective-permute-start(bf16[204,128]{1,0:T(8,128)(2,1)S(1)} %get-tuple-element.30), channel_id=1, source_target_pairs={{0,4},{4,0},{8,12},{12,8},{1,5},{5,1},{9,13},{13,9},{2,6},{6,2},{1... | collective-permute-start | bytes 156680 | tf_op jit(solution)/shard_map/ppermute | solution.py:22
  5.1 6.1 %collective-permute-start.1 = (bf16[204,128]{1,0:T(8,128)(2,1)S(1)}, bf16[204,128]{1,0:T(8,128)(2,1)S(1)}, u32[]{:S(2)}, u32[]{:S(2)}) collective-permute-start(bf16[204,128]{1,0:T(8,128)(2,1)S(1)} %get-tuple-element.31), channel_id=1, source_target_pairs={{0,8},{4,12},{8,0},{12,4},{1,9},{5,13},{9,1},{13,5},{2,10},{6,14},... | collective-permute-start | bytes 156680 | tf_op jit(solution)/shard_map/ppermute | solution.py:22
  7.7 5.9 %collective-permute-start.2 = (bf16[204,128]{1,0:T(8,128)(2,1)S(1)}, bf16[204,128]{1,0:T(8,128)(2,1)S(1)}, u32[]{:S(2)}, u32[]{:S(2)}) collective-permute-start(bf16[204,128]{1,0:T(8,128)(2,1)S(1)} %get-tuple-element.32), channel_id=1, source_target_pairs={{0,12},{4,8},{8,4},{12,0},{1,13},{5,9},{9,5},{13,1},{2,14},{6,10},... | collective-permute-start | bytes 156680 | tf_op jit(solution)/shard_map/ppermute | solution.py:22
  11.2 6.7 %collective-permute-start.5 = (bf16[96,768]{1,0:T(8,128)(2,1)S(1)}, bf16[96,768]{1,0:T(8,128)(2,1)S(1)}, u32[]{:S(2)}, u32[]{:S(2)}) collective-permute-start(bf16[96,768]{1,0:T(8,128)(2,1)S(1)} %pack_near.1.refs_0_), channel_id=1, source_target_pairs={{0,2},{1,3},{2,0},{3,1},{4,6},{5,7},{6,4},{7,5},{8,10},{9,11},{10,... | collective-permute-start | bytes 442376 | tf_op jit(solution)/shard_map/ppermute | solution.py:22
  12.7 5.2 %collective-permute-start.3 = (bf16[96,768]{1,0:T(8,128)(2,1)S(1)}, bf16[96,768]{1,0:T(8,128)(2,1)S(1)}, u32[]{:S(2)}, u32[]{:S(2)}) collective-permute-start(bf16[96,768]{1,0:T(8,128)(2,1)S(1)} %pack_near.1.refs_0_), channel_id=1, source_target_pairs={{0,1},{1,0},{2,3},{3,2},{4,5},{5,4},{6,7},{7,6},{8,9},{9,8},{10,11... | collective-permute-start | bytes 442376 | tf_op jit(solution)/shard_map/ppermute | solution.py:22
  13.6 4.3 %collective-permute-start.6 = (bf16[40,768]{1,0:T(8,128)(2,1)S(1)}, bf16[40,768]{1,0:T(8,128)(2,1)S(1)}, u32[]{:S(2)}, u32[]{:S(2)}) collective-permute-start(bf16[40,768]{1,0:T(8,128)(2,1)S(1)} %pack_far.1.refs_1_), channel_id=1, source_target_pairs={{0,2},{1,3},{2,0},{3,1},{4,6},{5,7},{6,4},{7,5},{8,10},{9,11},{10,... | collective-permute-start | bytes 184328 | tf_op jit(solution)/shard_map/ppermute | solution.py:22
  15.2 2.7 %collective-permute-start.4 = (bf16[40,768]{1,0:T(8,128)(2,1)S(1)}, bf16[40,768]{1,0:T(8,128)(2,1)S(1)}, u32[]{:S(2)}, u32[]{:S(2)}) collective-permute-start(bf16[40,768]{1,0:T(8,128)(2,1)S(1)} %pack_far.1.refs_1_), channel_id=1, source_target_pairs={{0,1},{1,0},{2,3},{3,2},{4,5},{5,4},{6,7},{7,6},{8,9},{9,8},{10,11... | collective-permute-start | bytes 184328 | tf_op jit(solution)/shard_map/ppermute | solution.py:22
  17.9 1.5 %collective-permute-start.7 = (bf16[96,768]{1,0:T(8,128)(2,1)S(1)}, bf16[96,768]{1,0:T(8,128)(2,1)S(1)}, u32[]{:S(2)}, u32[]{:S(2)}) collective-permute-start(bf16[96,768]{1,0:T(8,128)(2,1)S(1)} %hold.5.refs_4_), channel_id=1, source_target_pairs={{0,1},{1,0},{2,3},{3,2},{4,5},{5,4},{6,7},{7,6},{8,9},{9,8},{10,11... | collective-permute-start | bytes 442376 | tf_op jit(solution)/shard_map/ppermute | solution.py:22
  18.0 1.4 %collective-permute-start.8 = (bf16[40,768]{1,0:T(8,128)(2,1)S(1)}, bf16[40,768]{1,0:T(8,128)(2,1)S(1)}, u32[]{:S(2)}, u32[]{:S(2)}) collective-permute-start(bf16[40,768]{1,0:T(8,128)(2,1)S(1)} %collective-permute-done.6.refs_1_.refs_5_), channel_id=1, source_target_pairs={{0,1},{1,0},{2,3},{3,2},{4,5},{5,4},{6,7},{7,6},{8,9},{9,8},{10,11... | collective-permute-start | bytes 184328 | tf_op jit(solution)/shard_map/ppermute | solution.py:22
  20.2 4.5 %collective-permute-start.12 = (bf16[136,256]{1,0:T(8,128)(2,1)S(1)}, bf16[136,256]{1,0:T(8,128)(2,1)S(1)}, u32[]{:S(2)}, u32[]{:S(2)}) collective-permute-start(bf16[136,256]{1,0:T(8,128)(2,1)S(1)} %get-tuple-element.34.refs_0_), channel_id=1, source_target_pairs={{0,2},{1,3},{2,0},{3,1},{4,6},{5,7},{6,4},{7,5},{8,10},{9,11},{10,... | collective-permute-start | bytes 208904 | tf_op jit(solution)/shard_map/ppermute | solution.py:22
  22.9 6.4 %collective-permute-start.9 = (bf16[136,512]{1,0:T(8,128)(2,1)S(1)}, bf16[136,512]{1,0:T(8,128)(2,1)S(1)}, u32[]{:S(2)}, u32[]{:S(2)}) collective-permute-start(bf16[136,512]{1,0:T(8,128)(2,1)S(1)} %hidden_part.5.refs_4_), channel_id=1, source_target_pairs={{0,2},{1,3},{2,0},{3,1},{4,6},{5,7},{6,4},{7,5},{8,10},{9,11},{10,... | collective-permute-start | bytes 417800 | tf_op jit(solution)/shard_map/ppermute | solution.py:22
  24.6 6.8 %slice-start.3 = ((s8[12582912]{0:T(1024)(128)(4,1)}), s8[4194304]{0:T(1024)(128)(4,1)S(1)}, s32[]{:S(2)}) async-start(s8[12582912]{0:T(1024)(128)(4,1)} %bitcast.8), calls=%async_computation.3 | async-start | bytes 8388608
  24.6 6.8 %slice-start.4 = ((s8[12582912]{0:T(1024)(128)(4,1)}), s8[4194304]{0:T(1024)(128)(4,1)S(1)}, s32[]{:S(2)}) async-start(s8[12582912]{0:T(1024)(128)(4,1)} %bitcast.8), calls=%async_computation.4 | async-start | bytes 8388608
  26.3 5.1 %slice-start.5 = ((s8[12582912]{0:T(1024)(128)(4,1)}), s8[4194304]{0:T(1024)(128)(4,1)S(1)}, s32[]{:S(2)}) async-start(s8[12582912]{0:T(1024)(128)(4,1)} %bitcast.8), calls=%async_computation.5 | async-start | bytes 8388608
  26.3 6.7 %collective-permute-start.18 = (bf16[136,768]{1,0:T(8,128)(2,1)S(1)}, bf16[136,768]{1,0:T(8,128)(2,1)S(1)}, u32[]{:S(2)}, u32[]{:S(2)}) collective-permute-start(bf16[136,768]{1,0:T(8,128)(2,1)S(1)} %hidden_part.7.refs_2_), channel_id=1, source_target_pairs={{0,2},{1,3},{2,0},{3,1},{4,6},{5,7},{6,4},{7,5},{8,10},{9,11},{10,... | collective-permute-start | bytes 626696 | tf_op jit(solution)/shard_map/ppermute | solution.py:22
  27.9 1.3 %collective-permute-start.14 = (bf16[136,256]{1,0:T(8,128)(2,1)S(1)}, bf16[136,256]{1,0:T(8,128)(2,1)S(1)}, u32[]{:S(2)}, u32[]{:S(2)}) collective-permute-start(bf16[136,256]{1,0:T(8,128)(2,1)S(1)} %get-tuple-element.34.refs_0_), channel_id=1, source_target_pairs={{0,1},{1,0},{2,3},{3,2},{4,5},{5,4},{6,7},{7,6},{8,9},{9,8},{10,11... | collective-permute-start | bytes 208904 | tf_op jit(solution)/shard_map/ppermute | solution.py:22
  27.9 3.5 %collective-permute-start.16 = (bf16[136,512]{1,0:T(8,128)(2,1)S(1)}, bf16[136,512]{1,0:T(8,128)(2,1)S(1)}, u32[]{:S(2)}, u32[]{:S(2)}) collective-permute-start(bf16[136,512]{1,0:T(8,128)(2,1)S(1)} %hidden_part.5.refs_4_), channel_id=1, source_target_pairs={{0,1},{1,0},{2,3},{3,2},{4,5},{5,4},{6,7},{7,6},{8,9},{9,8},{10,11... | collective-permute-start | bytes 417800 | tf_op jit(solution)/shard_map/ppermute | solution.py:22
  28.4 5.1 %collective-permute-start.13 = (bf16[136,768]{1,0:T(8,128)(2,1)S(1)}, bf16[136,768]{1,0:T(8,128)(2,1)S(1)}, u32[]{:S(2)}, u32[]{:S(2)}) collective-permute-start(bf16[136,768]{1,0:T(8,128)(2,1)S(1)} %hidden_part.7.refs_2_), channel_id=1, source_target_pairs={{0,1},{1,0},{2,3},{3,2},{4,5},{5,4},{6,7},{7,6},{8,9},{9,8},{10,11... | collective-permute-start | bytes 626696 | tf_op jit(solution)/shard_map/ppermute | solution.py:22
  29.1 1.7 %collective-permute-start.15 = (bf16[136,256]{1,0:T(8,128)(2,1)S(1)}, bf16[136,256]{1,0:T(8,128)(2,1)S(1)}, u32[]{:S(2)}, u32[]{:S(2)}) collective-permute-start(bf16[136,256]{1,0:T(8,128)(2,1)S(1)} %collective-permute-done.12.refs_3_.refs_2_), channel_id=1, source_target_pairs={{0,1},{1,0},{2,3},{3,2},{4,5},{5,4},{6,7},{7,6},{8,9},{9,8},{10,11... | collective-permute-start | bytes 208904 | tf_op jit(solution)/shard_map/ppermute | solution.py:22
  29.3 4.2 %collective-permute-start.11 = (bf16[136,512]{1,0:T(8,128)(2,1)S(1)}, bf16[136,512]{1,0:T(8,128)(2,1)S(1)}, u32[]{:S(2)}, u32[]{:S(2)}) collective-permute-start(bf16[136,512]{1,0:T(8,128)(2,1)S(1)} %collective-permute-done.9.refs_3_.refs_0_), channel_id=1, source_target_pairs={{0,1},{1,0},{2,3},{3,2},{4,5},{5,4},{6,7},{7,6},{8,9},{9,8},{10,11... | collective-permute-start | bytes 417800 | tf_op jit(solution)/shard_map/ppermute | solution.py:22
  29.7 3.9 %slice-start.6 = ((s8[12582912]{0:T(1024)(128)(4,1)}), s8[4194304]{0:T(1024)(128)(4,1)S(1)}, s32[]{:S(2)}) async-start(s8[12582912]{0:T(1024)(128)(4,1)} %bitcast.10), calls=%async_computation.6 | async-start | bytes 8388608
  29.7 3.9 %slice-start.7 = ((s8[12582912]{0:T(1024)(128)(4,1)}), s8[4194304]{0:T(1024)(128)(4,1)S(1)}, s32[]{:S(2)}) async-start(s8[12582912]{0:T(1024)(128)(4,1)} %bitcast.10), calls=%async_computation.7 | async-start | bytes 8388608
  30.8 3.7 %slice-start.8 = ((s8[12582912]{0:T(1024)(128)(4,1)}), s8[4194304]{0:T(1024)(128)(4,1)S(1)}, s32[]{:S(2)}) async-start(s8[12582912]{0:T(1024)(128)(4,1)} %bitcast.10), calls=%async_computation.8 | async-start | bytes 8388608
  30.8 5.8 %collective-permute-start.10 = (bf16[136,512]{1,0:T(8,128)(2,1)S(1)}, bf16[136,512]{1,0:T(8,128)(2,1)S(1)}, u32[]{:S(2)}, u32[]{:S(2)}) collective-permute-start(bf16[136,512]{1,0:T(8,128)(2,1)S(1)} %hidden_part.6.refs_2_), channel_id=1, source_target_pairs={{0,2},{1,3},{2,0},{3,1},{4,6},{5,7},{6,4},{7,5},{8,10},{9,11},{10,... | collective-permute-start | bytes 417800 | tf_op jit(solution)/shard_map/ppermute | solution.py:22
  33.0 3.7 %collective-permute-start.19 = (bf16[136,768]{1,0:T(8,128)(2,1)S(1)}, bf16[136,768]{1,0:T(8,128)(2,1)S(1)}, u32[]{:S(2)}, u32[]{:S(2)}) collective-permute-start(bf16[136,768]{1,0:T(8,128)(2,1)S(1)} %hold.7.refs_0_), channel_id=1, source_target_pairs={{0,1},{1,0},{2,3},{3,2},{4,5},{5,4},{6,7},{7,6},{8,9},{9,8},{10,11... | collective-permute-start | bytes 626696 | tf_op jit(solution)/shard_map/ppermute | solution.py:22
  33.0 3.7 %collective-permute-start.20 = (bf16[136,512]{1,0:T(8,128)(2,1)S(1)}, bf16[136,512]{1,0:T(8,128)(2,1)S(1)}, u32[]{:S(2)}, u32[]{:S(2)}) collective-permute-start(bf16[136,512]{1,0:T(8,128)(2,1)S(1)} %hidden_part.6.refs_2_), channel_id=1, source_target_pairs={{0,1},{1,0},{2,3},{3,2},{4,5},{5,4},{6,7},{7,6},{8,9},{9,8},{10,11... | collective-permute-start | bytes 417800 | tf_op jit(solution)/shard_map/ppermute | solution.py:22
  36.6 6.3 %copy-start.1 = (bf16[64,768]{1,0:T(8,128)(2,1)S(1)}, bf16[64,768]{1,0:T(8,128)(2,1)}, u32[]{:S(2)}) copy-start(bf16[64,768]{1,0:T(8,128)(2,1)} %grad_ref.1) | copy-start | bytes 294916
  36.6 6.3 %copy-start.2 = (s32[64,2]{0,1:T(2,128)S(1)}, s32[64,2]{0,1:T(2,128)}, u32[]{:S(2)}) copy-start(s32[64,2]{0,1:T(2,128)} %param.8) | copy-start | bytes 1540
  36.6 6.3 %copy-start.3 = (f32[64,2]{0,1:T(2,128)S(1)}, f32[64,2]{0,1:T(2,128)}, u32[]{:S(2)}) copy-start(f32[64,2]{0,1:T(2,128)} %param.9) | copy-start | bytes 1540
  36.6 1.4 %collective-permute-start.17 = (bf16[136,512]{1,0:T(8,128)(2,1)S(1)}, bf16[136,512]{1,0:T(8,128)(2,1)S(1)}, u32[]{:S(2)}, u32[]{:S(2)}) collective-permute-start(bf16[136,512]{1,0:T(8,128)(2,1)S(1)} %hold.6.refs_0_), channel_id=1, source_target_pairs={{0,1},{1,0},{2,3},{3,2},{4,5},{5,4},{6,7},{7,6},{8,9},{9,8},{10,11... | collective-permute-start | bytes 417800 | tf_op jit(solution)/shard_map/ppermute | solution.py:22
  38.5 4.8 %collective-permute-start.21 = (bf16[204,128]{1,0:T(8,128)(2,1)S(1)}, bf16[204,128]{1,0:T(8,128)(2,1)S(1)}, u32[]{:S(2)}, u32[]{:S(2)}) collective-permute-start(bf16[204,128]{1,0:T(8,128)(2,1)S(1)} %get-tuple-element.36), channel_id=1, source_target_pairs={{0,4},{4,0},{8,12},{12,8},{1,5},{5,1},{9,13},{13,9},{2,6},{6,2},{1... | collective-permute-start | bytes 156680 | tf_op jit(solution)/shard_map/ppermute | solution.py:22
  39.1 6.7 %collective-permute-start.22 = (bf16[204,128]{1,0:T(8,128)(2,1)S(1)}, bf16[204,128]{1,0:T(8,128)(2,1)S(1)}, u32[]{:S(2)}, u32[]{:S(2)}) collective-permute-start(bf16[204,128]{1,0:T(8,128)(2,1)S(1)} %get-tuple-element.37), channel_id=1, source_target_pairs={{0,8},{4,12},{8,0},{12,4},{1,9},{5,13},{9,1},{13,5},{2,10},{6,14},... | collective-permute-start | bytes 156680 | tf_op jit(solution)/shard_map/ppermute | solution.py:22
  42.4 5.9 %collective-permute-start.23 = (bf16[204,128]{1,0:T(8,128)(2,1)S(1)}, bf16[204,128]{1,0:T(8,128)(2,1)S(1)}, u32[]{:S(2)}, u32[]{:S(2)}) collective-permute-start(bf16[204,128]{1,0:T(8,128)(2,1)S(1)} %get-tuple-element.38), channel_id=1, source_target_pairs={{0,12},{4,8},{8,4},{12,0},{1,13},{5,9},{9,5},{13,1},{2,14},{6,10},... | collective-permute-start | bytes 156680 | tf_op jit(solution)/shard_map/ppermute | solution.py:22
  48.5 3.1 %collective-permute-start.26 = (f32[2,64]{1,0:T(2,128)S(1)}, f32[2,64]{1,0:T(2,128)S(1)}, u32[]{:S(2)}, u32[]{:S(2)}) collective-permute-start(f32[2,64]{1,0:T(2,128)S(1)} %dots.1), channel_id=1, source_target_pairs={{0,3},{1,2},{2,1},{3,0},{4,7},{5,6},{6,5},{7,4},{8,11},{9,10},{10,... | collective-permute-start | bytes 1544 | tf_op jit(solution)/shard_map/ppermute | solution.py:22
  48.6 4.4 %collective-permute-start.25 = (f32[2,64]{1,0:T(2,128)S(1)}, f32[2,64]{1,0:T(2,128)S(1)}, u32[]{:S(2)}, u32[]{:S(2)}) collective-permute-start(f32[2,64]{1,0:T(2,128)S(1)} %dots.1), channel_id=1, source_target_pairs={{0,1},{1,0},{2,3},{3,2},{4,5},{5,4},{6,7},{7,6},{8,9},{9,8},{10,11... | collective-permute-start | bytes 1544 | tf_op jit(solution)/shard_map/ppermute | solution.py:22
  49.4 3.6 %collective-permute-start.24 = (f32[2,64]{1,0:T(2,128)S(1)}, f32[2,64]{1,0:T(2,128)S(1)}, u32[]{:S(2)}, u32[]{:S(2)}) collective-permute-start(f32[2,64]{1,0:T(2,128)S(1)} %dots.1), channel_id=1, source_target_pairs={{0,2},{1,3},{2,0},{3,1},{4,6},{5,7},{6,4},{7,5},{8,10},{9,11},{10,... | collective-permute-start | bytes 1544 | tf_op jit(solution)/shard_map/ppermute | solution.py:22

commit v16 on v14

--- a/solution.py
+++ b/solution.py
@@ -323,7 +323,7 @@
     far_across = swap(far, "tensor", 2)
     near_across = hold(near_across, [far_across])
     xs = [near, far, swap(near, "tensor", 1), swap(far, "tensor", 1), near_across, far_across]
-    xs += [swap(near_across, "tensor", 1), swap(far_across, "tensor", 1)]
+    xs += [swap(near_across, "tensor", 1), swap(far, "tensor", 3)]
 
     hits, routes, picks, grads = prepare(me, ids_t, probs_t, out_grad)
 

time: 53 us -> 55.6 us (1.049)
  waiting for transfers between devices: 18.2 us -> 20 us
  starting transfers between devices: 21.9 us -> 23 us
    ppermute x27, waiting for transfers between devices: 18.2 us -> 20 us  [swap(): return lax.ppermute(value, axis, [(i, i ^ bit) for i in range(size)])]
    ppermute x27, starting transfers between devices: 21.9 us -> 23 us  [swap(): return lax.ppermute(value, axis, [(i, i ^ bit) for i in range(size)])]
  transfers between devices with their start and end apart: 27 -> 27, of which waited for: 14 -> 13; matrix products, arithmetic and copies ran while one was open for 0% -> 0% of each run, Pallas kernels for 14% -> 13%
where the time goes in v16:
time: 55.6 us; the launch traced here: 55.5 us
  starting transfers between devices  23 us (41%)
  waiting for transfers between devices  20 us (36%)
  Pallas kernels  10 us (18%)
  local copies, waits for them, and re-layouts  1 us (2%)
  between operations  0.92 us (2%)
  other arithmetic  0.57 us (1%)
    ppermute x27, starting transfers between devices, swap(): return lax.ppermute(value, axis, [(i, i ^ bit) for i in range(size)])  23 us
    ppermute x27, waiting for transfers between devices, swap(): return lax.ppermute(value, axis, [(i, i ^ bit) for i in range(size)])  20 us
    pallas_call x4, Pallas kernels, hidden_part(): pl.pallas_call(functools.partial(hidden_kernel, joined, parts, start), ou...  4.6 us
    pallas_call x4, Pallas kernels, down_part(): pl.pallas_call(functools.partial(down_kernel, len(pieces), where, slab, h...  2.56 us
    pallas_call x1, Pallas kernels, select_rows(): pl.pallas_call(select_kernel, out_shape=[jax.ShapeDtypeStruct((MOST, widt...  1.3 us
  transfers between devices with their start and end apart: 27, of which 13 were waited for; matrix products, arithmetic and copies ran while one was open for 0% of the time, Pallas kernels for 13%

profile of v16, /device:TPU:0, one launch (start us, length us, event | category | flops | bytes accessed | tf_op | source)
XLA Modules:
  0.0 55.5 jit_solution(947578741756342836)
XLA Ops:
  0.6 0.0 slice-start
  0.6 0.0 slice-start.1
  0.7 0.0 slice-start.2
  0.7 1.3 %select_rows.1 = (bf16[34,768]{1,0:T(8,128)(2,1)S(1)}, bf16[204,128]{1,0:T(8,128)(2,1)S(1)}, bf16[204,128]{1,0:T(8,128)(2,1)S(1)}, bf16[204,128]{1,0:T(8,128)(2,1)S(1)}) custom-call(s32[1]{0:T(128)} %bitcast.me_ref, s32[1]{0:T(128)} %bitcast.3.t_ref, s32[2,64]{1,0:T(2,128)} %bitcast.12, bf16[64,768]{1,0:T(8,128)(2,1)} %tokens_hbm.1), custom_call_target="tpu_custom_call" | custom-call | flops 8000000000 | bytes 1000 | tf_op jit(solution)/shard_map/select_rows/pallas_call | solution.py:82
  2.0 3.1 %collective-permute-start = (bf16[204,128]{1,0:T(8,128)(2,1)S(1)}, bf16[204,128]{1,0:T(8,128)(2,1)S(1)}, u32[]{:S(2)}, u32[]{:S(2)}) collective-permute-start(bf16[204,128]{1,0:T(8,128)(2,1)S(1)} %get-tuple-element.30), channel_id=1, source_target_pairs={{0,4},{4,0},{8,12},{12,8},{1,5},{5,1},{9,13},{13,9},{2,6},{6,2},{1... | collective-permute-start | bytes 156680 | tf_op jit(solution)/shard_map/ppermute | solution.py:22
  5.1 2.6 %collective-permute-start.1 = (bf16[204,128]{1,0:T(8,128)(2,1)S(1)}, bf16[204,128]{1,0:T(8,128)(2,1)S(1)}, u32[]{:S(2)}, u32[]{:S(2)}) collective-permute-start(bf16[204,128]{1,0:T(8,128)(2,1)S(1)} %get-tuple-element.31), channel_id=1, source_target_pairs={{0,8},{4,12},{8,0},{12,4},{1,9},{5,13},{9,1},{13,5},{2,10},{6,14},... | collective-permute-start | bytes 156680 | tf_op jit(solution)/shard_map/ppermute | solution.py:22
  7.7 0.0 collective-permute-start.2
  7.7 0.0 collective-permute-done.refs_0_
  7.7 3.5 %collective-permute-done.1.refs_1_.third_ref = bf16[204,128]{1,0:T(8,128)(2,1)S(1)} collective-permute-done((bf16[204,128]{1,0:T(8,128)(2,1)S(1)}, bf16[204,128]{1,0:T(8,128)(2,1)S(1)}, u32[]{:S(2)}, u32[]{:S(2)}) %collective-permute-start.1) | collective-permute-done | bytes 52256 | tf_op jit(solution)/shard_map/ppermute | solution.py:22
  11.2 1.6 %collective-permute-start.5 = (bf16[96,768]{1,0:T(8,128)(2,1)S(1)}, bf16[96,768]{1,0:T(8,128)(2,1)S(1)}, u32[]{:S(2)}, u32[]{:S(2)}) collective-permute-start(bf16[96,768]{1,0:T(8,128)(2,1)S(1)} %pack_near.1.refs_0_), channel_id=1, source_target_pairs={{0,2},{1,3},{2,0},{3,1},{4,6},{5,7},{6,4},{7,5},{8,10},{9,11},{10,... | collective-permute-start | bytes 442376 | tf_op jit(solution)/shard_map/ppermute | solution.py:22
  12.7 0.9 %collective-permute-done.2.fourth_ref = bf16[204,128]{1,0:T(8,128)(2,1)S(1)} collective-permute-done((bf16[204,128]{1,0:T(8,128)(2,1)S(1)}, bf16[204,128]{1,0:T(8,128)(2,1)S(1)}, u32[]{:S(2)}, u32[]{:S(2)}) %collective-permute-start.2) | collective-permute-done | bytes 52256 | tf_op jit(solution)/shard_map/ppermute | solution.py:22
  13.6 1.6 %collective-permute-start.6 = (bf16[40,768]{1,0:T(8,128)(2,1)S(1)}, bf16[40,768]{1,0:T(8,128)(2,1)S(1)}, u32[]{:S(2)}, u32[]{:S(2)}) collective-permute-start(bf16[40,768]{1,0:T(8,128)(2,1)S(1)} %pack_far.1.refs_1_), channel_id=1, source_target_pairs={{0,2},{1,3},{2,0},{3,1},{4,6},{5,7},{6,4},{7,5},{8,10},{9,11},{10,... | collective-permute-start | bytes 184328 | tf_op jit(solution)/shard_map/ppermute | solution.py:22
  15.2 0.0 collective-permute-start.3
  15.2 2.7 %collective-permute-done.6.refs_1_.refs_5_ = bf16[40,768]{1,0:T(8,128)(2,1)S(1)} collective-permute-done((bf16[40,768]{1,0:T(8,128)(2,1)S(1)}, bf16[40,768]{1,0:T(8,128)(2,1)S(1)}, u32[]{:S(2)}, u32[]{:S(2)}) %collective-permute-start.6) | collective-permute-done | bytes 61472 | tf_op jit(solution)/shard_map/ppermute | solution.py:22
  17.9 0.0 collective-permute-done.5.refs_0_
  17.9 1.6 %collective-permute-start.8 = (bf16[40,768]{1,0:T(8,128)(2,1)S(1)}, bf16[40,768]{1,0:T(8,128)(2,1)S(1)}, u32[]{:S(2)}, u32[]{:S(2)}) collective-permute-start(bf16[40,768]{1,0:T(8,128)(2,1)S(1)} %pack_far.1.refs_1_), channel_id=1, source_target_pairs={{0,3},{1,2},{2,1},{3,0},{4,7},{5,6},{6,5},{7,4},{8,11},{9,10},{10,... | collective-permute-start | bytes 184328 | tf_op jit(solution)/shard_map/ppermute | solution.py:22
  19.5 0.1 collective-permute-start.4
  19.6 2.1 %collective-permute-done.8.refs_7_ = bf16[40,768]{1,0:T(8,128)(2,1)S(1)} collective-permute-done((bf16[40,768]{1,0:T(8,128)(2,1)S(1)}, bf16[40,768]{1,0:T(8,128)(2,1)S(1)}, u32[]{:S(2)}, u32[]{:S(2)}) %collective-permute-start.8) | collective-permute-done | bytes 61472 | tf_op jit(solution)/shard_map/ppermute | solution.py:22
  21.7 0.0 collective-permute-done.4.refs_3_
  21.8 0.7 %hidden_part.4 = (bf16[136,256]{1,0:T(8,128)(2,1)S(1)}, bf16[4,136,768]{2,1,0:T(8,128)(2,1)S(1)}) custom-call(s32[1]{0:T(128)} %bitcast.3.t_ref, bf16[96,768]{1,0:T(8,128)(2,1)S(1)} %pack_near.1.refs_0_, bf16[40,768]{1,0:T(8,128)(2,1)S(1)} %pack_far.1.refs_1_, bf16[96,768]{1,0:T(8,128)(2,1)S(1)} %collective-permute-done.3.refs_2_, ...), custom_call_target="tpu_custom_call" | custom-call | flops 1000 | bytes 1000 | tf_op jit(solution)/shard_map/hidden_part/pallas_call | solution.py:177
  22.5 1.5 %collective-permute-start.12 = (bf16[136,256]{1,0:T(8,128)(2,1)S(1)}, bf16[136,256]{1,0:T(8,128)(2,1)S(1)}, u32[]{:S(2)}, u32[]{:S(2)}) collective-permute-start(bf16[136,256]{1,0:T(8,128)(2,1)S(1)} %get-tuple-element.34.refs_0_), channel_id=1, source_target_pairs={{0,2},{1,3},{2,0},{3,1},{4,6},{5,7},{6,4},{7,5},{8,10},{9,11},{10,... | collective-permute-start | bytes 208904 | tf_op jit(solution)/shard_map/ppermute | solution.py:22
  24.0 1.1 %hidden_part.5.refs_4_ = bf16[136,512]{1,0:T(8,128)(2,1)S(1)} custom-call(s32[1]{0:T(128)} %bitcast.3.t_ref, bf16[4,136,768]{2,1,0:T(8,128)(2,1)S(1)} %get-tuple-element.33.refs_0_, bf16[1,3072,2048]{2,1,0:T(8,128)(2,1)S(1)} %bitcast.7, bf16[1,3072,2048]{2,1,0:T(8,128)(2,1)S(1)} %copy-done), custom_call_target="tpu_custom_call" | custom-call | flops 1000 | bytes 1000 | tf_op jit(solution)/shard_map/hidden_part/pallas_call | solution.py:177
  25.2 0.6 %collective-permute-start.9 = (bf16[136,512]{1,0:T(8,128)(2,1)S(1)}, bf16[136,512]{1,0:T(8,128)(2,1)S(1)}, u32[]{:S(2)}, u32[]{:S(2)}) collective-permute-start(bf16[136,512]{1,0:T(8,128)(2,1)S(1)} %hidden_part.5.refs_4_), channel_id=1, source_target_pairs={{0,2},{1,3},{2,0},{3,1},{4,6},{5,7},{6,4},{7,5},{8,10},{9,11},{10,... | collective-permute-start | bytes 417800 | tf_op jit(solution)/shard_map/ppermute | solution.py:22
  25.8 1.3 %collective-permute-done.12.refs_3_.refs_2_ = bf16[136,256]{1,0:T(8,128)(2,1)S(1)} collective-permute-done((bf16[136,256]{1,0:T(8,128)(2,1)S(1)}, bf16[136,256]{1,0:T(8,128)(2,1)S(1)}, u32[]{:S(2)}, u32[]{:S(2)}) %collective-permute-start.12) | collective-permute-done | bytes 69664 | tf_op jit(solution)/shard_map/ppermute | solution.py:22
  27.0 1.6 %hidden_part.7.refs_2_ = bf16[136,768]{1,0:T(8,128)(2,1)S(1)} custom-call(s32[1]{0:T(128)} %bitcast.3.t_ref, bf16[4,136,768]{2,1,0:T(8,128)(2,1)S(1)} %get-tuple-element.33.refs_0_, bf16[1,3072,2048]{2,1,0:T(8,128)(2,1)S(1)} %bitcast.7, bf16[1,3072,2048]{2,1,0:T(8,128)(2,1)S(1)} %copy-done, bf16[136,256]{1,0:T(8,128)(2,1)S(1)} %collective-permute-done.12.refs_3_.refs_2_), custom_call_target="tpu_custom_call" | custom-call | flops 1000 | bytes 1000 | tf_op jit(solution)/shard_map/hidden_part/pallas_call | solution.py:177
  28.7 0.0 slice-start.5
  28.7 1.6 %collective-permute-start.18 = (bf16[136,768]{1,0:T(8,128)(2,1)S(1)}, bf16[136,768]{1,0:T(8,128)(2,1)S(1)}, u32[]{:S(2)}, u32[]{:S(2)}) collective-permute-start(bf16[136,768]{1,0:T(8,128)(2,1)S(1)} %hidden_part.7.refs_2_), channel_id=1, source_target_pairs={{0,2},{1,3},{2,0},{3,1},{4,6},{5,7},{6,4},{7,5},{8,10},{9,11},{10,... | collective-permute-start | bytes 626696 | tf_op jit(solution)/shard_map/ppermute | solution.py:22
  30.3 0.0 collective-permute-start.14
  30.3 0.5 collective-permute-start.16
  30.8 0.0 collective-permute-start.13
  30.8 0.7 %collective-permute-done.14.refs_1_ = bf16[136,256]{1,0:T(8,128)(2,1)S(1)} collective-permute-done((bf16[136,256]{1,0:T(8,128)(2,1)S(1)}, bf16[136,256]{1,0:T(8,128)(2,1)S(1)}, u32[]{:S(2)}, u32[]{:S(2)}) %collective-permute-start.14) | collective-permute-done | bytes 69664 | tf_op jit(solution)/shard_map/ppermute | solution.py:22
  31.5 0.2 collective-permute-start.15
  31.7 0.4 collective-permute-start.11
  32.1 1.2 %hidden_part.6.refs_2_ = bf16[136,512]{1,0:T(8,128)(2,1)S(1)} custom-call(s32[1]{0:T(128)} %bitcast.3.t_ref, bf16[4,136,768]{2,1,0:T(8,128)(2,1)S(1)} %get-tuple-element.33.refs_0_, bf16[1,3072,2048]{2,1,0:T(8,128)(2,1)S(1)} %bitcast.7, bf16[1,3072,2048]{2,1,0:T(8,128)(2,1)S(1)} %copy-done, bf16[136,512]{1,0:T(8,128)(2,1)S(1)} %collective-permute-done.9.refs_3_.refs_0_), custom_call_target="tpu_custom_call" | custom-call | flops 1000 | bytes 1000 | tf_op jit(solution)/shard_map/hidden_part/pallas_call | solution.py:177
  33.2 0.0 slice-start.8
  33.2 0.6 %collective-permute-start.10 = (bf16[136,512]{1,0:T(8,128)(2,1)S(1)}, bf16[136,512]{1,0:T(8,128)(2,1)S(1)}, u32[]{:S(2)}, u32[]{:S(2)}) collective-permute-start(bf16[136,512]{1,0:T(8,128)(2,1)S(1)} %hidden_part.6.refs_2_), channel_id=1, source_target_pairs={{0,2},{1,3},{2,0},{3,1},{4,6},{5,7},{6,4},{7,5},{8,10},{9,11},{10,... | collective-permute-start | bytes 417800 | tf_op jit(solution)/shard_map/ppermute | solution.py:22
  33.8 0.6 %down_part.4.refs_5_.refs_1_ = f32[136,768]{1,0:T(8,128)S(1)} custom-call(s32[1]{0:T(128)} %bitcast.3.t_ref, bf16[136,256]{1,0:T(8,128)(2,1)S(1)} %get-tuple-element.34.refs_0_, bf16[136,256]{1,0:T(8,128)(2,1)S(1)} %collective-permute-done.14.refs_1_, bf16[136,256]{1,0:T(8,128)(2,1)S(1)} %collective-permute-done.12.refs_3_.refs_2_, ...), custom_call_target="tpu_custom_call" | custom-call | flops 427819008 | bytes 1000 | tf_op jit(solution)/shard_map/down_part/pallas_call | solution.py:215
  34.5 1.0 %collective-permute-done.18.refs_0_ = bf16[136,768]{1,0:T(8,128)(2,1)S(1)} collective-permute-done((bf16[136,768]{1,0:T(8,128)(2,1)S(1)}, bf16[136,768]{1,0:T(8,128)(2,1)S(1)}, u32[]{:S(2)}, u32[]{:S(2)}) %collective-permute-start.18) | collective-permute-done | bytes 208928 | tf_op jit(solution)/shard_map/ppermute | solution.py:22
  35.5 0.5 collective-permute-start.20
  36.0 0.0 collective-permute-done.13.refs_3_
  36.0 0.0 collective-permute-done.11.refs_1_
  36.0 0.9 %slice-done.8 = s8[4194304]{0:T(1024)(128)(4,1)S(1)} async-done(((s8[12582912]{0:T(1024)(128)(4,1)}), s8[4194304]{0:T(1024)(128)(4,1)S(1)}, s32[]{:S(2)}) %slice-start.8) | async-done | bytes 4194328
  36.9 0.7 %down_part.5.refs_1_.refs_5_ = f32[136,768]{1,0:T(8,128)S(1)} custom-call(s32[1]{0:T(128)} %bitcast.3.t_ref, bf16[136,512]{1,0:T(8,128)(2,1)S(1)} %collective-permute-done.9.refs_3_.refs_0_, bf16[136,512]{1,0:T(8,128)(2,1)S(1)} %collective-permute-done.11.refs_1_, bf16[136,768]{1,0:T(8,128)(2,1)S(1)} %hidden_part.7.refs_2_, ...), custom_call_target="tpu_custom_call" | custom-call | flops 534773760 | bytes 1000 | tf_op jit(solution)/shard_map/down_part/pallas_call | solution.py:215
  37.7 1.3 %collective-permute-done.10.refs_0_ = bf16[136,512]{1,0:T(8,128)(2,1)S(1)} collective-permute-done((bf16[136,512]{1,0:T(8,128)(2,1)S(1)}, bf16[136,512]{1,0:T(8,128)(2,1)S(1)}, u32[]{:S(2)}, u32[]{:S(2)}) %collective-permute-start.10) | collective-permute-done | bytes 139296 | tf_op jit(solution)/shard_map/ppermute | solution.py:22
  39.1 0.1 collective-permute-start.17
  39.1 0.0 collective-permute-done.20.refs_3_
  39.2 0.8 %down_part.6.refs_3_ = f32[136,768]{1,0:T(8,128)S(1)} custom-call(s32[1]{0:T(128)} %bitcast.3.t_ref, bf16[136,768]{1,0:T(8,128)(2,1)S(1)} %hold.7.refs_0_, bf16[136,768]{1,0:T(8,128)(2,1)S(1)} %collective-permute-done.19.refs_1_, bf16[136,512]{1,0:T(8,128)(2,1)S(1)} %hidden_part.6.refs_2_, bf16[136,512]{1,0:T(8,128)(2,1)S(1)} %collective-permute-done.20.refs_3_, ...), custom_call_target="tpu_custom_call" | custom-call | flops 534773760 | bytes 1000 | tf_op jit(solution)/shard_map/down_part/pallas_call | solution.py:215
  39.9 0.6 %collective-permute-done.17.refs_1_ = bf16[136,512]{1,0:T(8,128)(2,1)S(1)} collective-permute-done((bf16[136,512]{1,0:T(8,128)(2,1)S(1)}, bf16[136,512]{1,0:T(8,128)(2,1)S(1)}, u32[]{:S(2)}, u32[]{:S(2)}) %collective-permute-start.17) | collective-permute-done | bytes 139296 | tf_op jit(solution)/shard_map/ppermute | solution.py:22
  40.5 0.4 down_part.7
  40.9 0.1 collective-permute-start.21
  41.0 3.1 %collective-permute-start.22 = (bf16[204,128]{1,0:T(8,128)(2,1)S(1)}, bf16[204,128]{1,0:T(8,128)(2,1)S(1)}, u32[]{:S(2)}, u32[]{:S(2)}) collective-permute-start(bf16[204,128]{1,0:T(8,128)(2,1)S(1)} %get-tuple-element.37), channel_id=1, source_target_pairs={{0,8},{4,12},{8,0},{12,4},{1,9},{5,13},{9,1},{13,5},{2,10},{6,14},... | collective-permute-start | bytes 156680 | tf_op jit(solution)/shard_map/ppermute | solution.py:22
  44.1 1.2 %collective-permute-start.23 = (bf16[204,128]{1,0:T(8,128)(2,1)S(1)}, bf16[204,128]{1,0:T(8,128)(2,1)S(1)}, u32[]{:S(2)}, u32[]{:S(2)}) collective-permute-start(bf16[204,128]{1,0:T(8,128)(2,1)S(1)} %get-tuple-element.38), channel_id=1, source_target_pairs={{0,12},{4,8},{8,4},{12,0},{1,13},{5,9},{9,5},{13,1},{2,14},{6,10},... | collective-permute-start | bytes 156680 | tf_op jit(solution)/shard_map/ppermute | solution.py:22
  45.4 0.3 prepare.1
  45.7 0.1 collective-permute-done.21.refs_5_.refs_9_
  45.8 1.9 %collective-permute-done.22.refs_6_.refs_10_ = bf16[204,128]{1,0:T(8,128)(2,1)S(1)} collective-permute-done((bf16[204,128]{1,0:T(8,128)(2,1)S(1)}, bf16[204,128]{1,0:T(8,128)(2,1)S(1)}, u32[]{:S(2)}, u32[]{:S(2)}) %collective-permute-start.22) | collective-permute-done | bytes 52256 | tf_op jit(solution)/shard_map/ppermute | solution.py:22
  47.7 2.4 %collective-permute-done.23.refs_7_.refs_11_ = bf16[204,128]{1,0:T(8,128)(2,1)S(1)} collective-permute-done((bf16[204,128]{1,0:T(8,128)(2,1)S(1)}, bf16[204,128]{1,0:T(8,128)(2,1)S(1)}, u32[]{:S(2)}, u32[]{:S(2)}) %collective-permute-start.23) | collective-permute-done | bytes 52256 | tf_op jit(solution)/shard_map/ppermute | solution.py:22
  50.0 0.2 dots.1
  50.2 0.1 collective-permute-start.26
  50.3 1.0 %collective-permute-start.25 = (f32[2,64]{1,0:T(2,128)S(1)}, f32[2,64]{1,0:T(2,128)S(1)}, u32[]{:S(2)}, u32[]{:S(2)}) collective-permute-start(f32[2,64]{1,0:T(2,128)S(1)} %dots.1), channel_id=1, source_target_pairs={{0,1},{1,0},{2,3},{3,2},{4,5},{5,4},{6,7},{7,6},{8,9},{9,8},{10,11... | collective-permute-start | bytes 1544 | tf_op jit(solution)/shard_map/ppermute | solution.py:22
  51.4 1.1 %collective-permute-start.24 = (f32[2,64]{1,0:T(2,128)S(1)}, f32[2,64]{1,0:T(2,128)S(1)}, u32[]{:S(2)}, u32[]{:S(2)}) collective-permute-start(f32[2,64]{1,0:T(2,128)S(1)} %dots.1), channel_id=1, source_target_pairs={{0,2},{1,3},{2,0},{3,1},{4,6},{5,7},{6,4},{7,5},{8,10},{9,11},{10,... | collective-permute-start | bytes 1544 | tf_op jit(solution)/shard_map/ppermute | solution.py:22
  52.5 0.9 %mix.1 = (bf16[64,768]{1,0:T(8,128)(2,1)}, f32[8,128]{1,0:T(8,128)S(1)}) custom-call(f32[64,128]{1,0:T(8,128)S(1)} %get-tuple-element.24.routes_ref, f32[204,64]{1,0:T(8,128)S(1)} %get-tuple-element.25.refs_0_, f32[204,64]{1,0:T(8,128)S(1)} %get-tuple-element.26.refs_1_, f32[204,64]{1,0:T(8,128)S(1)} %get-tuple-element.27.refs_2_, ...), custom_call_target="tpu_custom_call" | custom-call | flops 1000000000 | bytes 1000 | tf_op jit(solution)/shard_map/mix/pallas_call | solution.py:296
  53.4 0.0 collective-permute-done.26.refs_0_
  53.4 1.5 %collective-permute-done.24.refs_0_ = f32[2,64]{1,0:T(2,128)S(1)} collective-permute-done((f32[2,64]{1,0:T(2,128)S(1)}, f32[2,64]{1,0:T(2,128)S(1)}, u32[]{:S(2)}, u32[]{:S(2)}) %collective-permute-start.24) | collective-permute-done | bytes 544 | tf_op jit(solution)/shard_map/ppermute | solution.py:22
  54.9 0.6 %add_bitcast_fusion = f32[64,2]{0,1:T(2,128)} fusion(f32[2,64]{1,0:T(2,128)S(1)} %collective-permute-done.25, f32[2,64]{1,0:T(2,128)S(1)} %hold.9, f32[2,64]{1,0:T(2,128)S(1)} %dots.1, f32[2,64]{1,0:T(2,128)S(1)} %hold.8), kind=kLoop, calls=%fused_computation | loop fusion | flops 384 | bytes 2560 | tf_op jit(solution)/shard_map/transpose | solution.py:355
  (39 shorter events, 0.1 us)
Async XLA Ops:
  0.6 21.1 %slice-start = ((s8[12582912]{0:T(1024)(128)(4,1)}), s8[4194304]{0:T(1024)(128)(4,1)S(1)}, s32[]{:S(2)}) async-start(s8[12582912]{0:T(1024)(128)(4,1)} %bitcast.6), calls=%async_computation | async-start | bytes 8388608
  0.6 21.1 %slice-start.1 = ((s8[12582912]{0:T(1024)(128)(4,1)}), s8[4194304]{0:T(1024)(128)(4,1)S(1)}, s32[]{:S(2)}) async-start(s8[12582912]{0:T(1024)(128)(4,1)} %bitcast.6), calls=%async_computation.1 | async-start | bytes 8388608
  0.7 21.1 %slice-start.2 = ((s8[12582912]{0:T(1024)(128)(4,1)}), s8[4194304]{0:T(1024)(128)(4,1)S(1)}, s32[]{:S(2)}) async-start(s8[12582912]{0:T(1024)(128)(4,1)} %bitcast.6), calls=%async_computation.2 | async-start | bytes 8388608
  0.7 21.1 %copy-start = (bf16[1,3072,2048]{2,1,0:T(8,128)(2,1)S(1)}, bf16[1,3072,2048]{2,1,0:T(8,128)(2,1)}, u32[]{:S(2)}) copy-start(bf16[1,3072,2048]{2,1,0:T(8,128)(2,1)} %refs_2_.6) | copy-start | bytes 37748740
  2.0 5.7 %collective-permute-start = (bf16[204,128]{1,0:T(8,128)(2,1)S(1)}, bf16[204,128]{1,0:T(8,128)(2,1)S(1)}, u32[]{:S(2)}, u32[]{:S(2)}) collective-permute-start(bf16[204,128]{1,0:T(8,128)(2,1)S(1)} %get-tuple-element.30), channel_id=1, source_target_pairs={{0,4},{4,0},{8,12},{12,8},{1,5},{5,1},{9,13},{13,9},{2,6},{6,2},{1... | collective-permute-start | bytes 156680 | tf_op jit(solution)/shard_map/ppermute | solution.py:22
  5.1 6.1 %collective-permute-start.1 = (bf16[204,128]{1,0:T(8,128)(2,1)S(1)}, bf16[204,128]{1,0:T(8,128)(2,1)S(1)}, u32[]{:S(2)}, u32[]{:S(2)}) collective-permute-start(bf16[204,128]{1,0:T(8,128)(2,1)S(1)} %get-tuple-element.31), channel_id=1, source_target_pairs={{0,8},{4,12},{8,0},{12,4},{1,9},{5,13},{9,1},{13,5},{2,10},{6,14},... | collective-permute-start | bytes 156680 | tf_op jit(solution)/shard_map/ppermute | solution.py:22
  7.7 5.9 %collective-permute-start.2 = (bf16[204,128]{1,0:T(8,128)(2,1)S(1)}, bf16[204,128]{1,0:T(8,128)(2,1)S(1)}, u32[]{:S(2)}, u32[]{:S(2)}) collective-permute-start(bf16[204,128]{1,0:T(8,128)(2,1)S(1)} %get-tuple-element.32), channel_id=1, source_target_pairs={{0,12},{4,8},{8,4},{12,0},{1,13},{5,9},{9,5},{13,1},{2,14},{6,10},... | collective-permute-start | bytes 156680 | tf_op jit(solution)/shard_map/ppermute | solution.py:22
  11.2 6.7 %collective-permute-start.5 = (bf16[96,768]{1,0:T(8,128)(2,1)S(1)}, bf16[96,768]{1,0:T(8,128)(2,1)S(1)}, u32[]{:S(2)}, u32[]{:S(2)}) collective-permute-start(bf16[96,768]{1,0:T(8,128)(2,1)S(1)} %pack_near.1.refs_0_), channel_id=1, source_target_pairs={{0,2},{1,3},{2,0},{3,1},{4,6},{5,7},{6,4},{7,5},{8,10},{9,11},{10,... | collective-permute-start | bytes 442376 | tf_op jit(solution)/shard_map/ppermute | solution.py:22
  13.6 4.3 %collective-permute-start.6 = (bf16[40,768]{1,0:T(8,128)(2,1)S(1)}, bf16[40,768]{1,0:T(8,128)(2,1)S(1)}, u32[]{:S(2)}, u32[]{:S(2)}) collective-permute-start(bf16[40,768]{1,0:T(8,128)(2,1)S(1)} %pack_far.1.refs_1_), channel_id=1, source_target_pairs={{0,2},{1,3},{2,0},{3,1},{4,6},{5,7},{6,4},{7,5},{8,10},{9,11},{10,... | collective-permute-start | bytes 184328 | tf_op jit(solution)/shard_map/ppermute | solution.py:22
  15.2 6.5 %collective-permute-start.3 = (bf16[96,768]{1,0:T(8,128)(2,1)S(1)}, bf16[96,768]{1,0:T(8,128)(2,1)S(1)}, u32[]{:S(2)}, u32[]{:S(2)}) collective-permute-start(bf16[96,768]{1,0:T(8,128)(2,1)S(1)} %pack_near.1.refs_0_), channel_id=1, source_target_pairs={{0,1},{1,0},{2,3},{3,2},{4,5},{5,4},{6,7},{7,6},{8,9},{9,8},{10,11... | collective-permute-start | bytes 442376 | tf_op jit(solution)/shard_map/ppermute | solution.py:22
  17.9 3.8 %collective-permute-start.7 = (bf16[96,768]{1,0:T(8,128)(2,1)S(1)}, bf16[96,768]{1,0:T(8,128)(2,1)S(1)}, u32[]{:S(2)}, u32[]{:S(2)}) collective-permute-start(bf16[96,768]{1,0:T(8,128)(2,1)S(1)} %hold.5.refs_4_), channel_id=1, source_target_pairs={{0,1},{1,0},{2,3},{3,2},{4,5},{5,4},{6,7},{7,6},{8,9},{9,8},{10,11... | collective-permute-start | bytes 442376 | tf_op jit(solution)/shard_map/ppermute | solution.py:22
  17.9 3.8 %collective-permute-start.8 = (bf16[40,768]{1,0:T(8,128)(2,1)S(1)}, bf16[40,768]{1,0:T(8,128)(2,1)S(1)}, u32[]{:S(2)}, u32[]{:S(2)}) collective-permute-start(bf16[40,768]{1,0:T(8,128)(2,1)S(1)} %pack_far.1.refs_1_), channel_id=1, source_target_pairs={{0,3},{1,2},{2,1},{3,0},{4,7},{5,6},{6,5},{7,4},{8,11},{9,10},{10,... | collective-permute-start | bytes 184328 | tf_op jit(solution)/shard_map/ppermute | solution.py:22
  19.5 2.2 %collective-permute-start.4 = (bf16[40,768]{1,0:T(8,128)(2,1)S(1)}, bf16[40,768]{1,0:T(8,128)(2,1)S(1)}, u32[]{:S(2)}, u32[]{:S(2)}) collective-permute-start(bf16[40,768]{1,0:T(8,128)(2,1)S(1)} %pack_far.1.refs_1_), channel_id=1, source_target_pairs={{0,1},{1,0},{2,3},{3,2},{4,5},{5,4},{6,7},{7,6},{8,9},{9,8},{10,11... | collective-permute-start | bytes 184328 | tf_op jit(solution)/shard_map/ppermute | solution.py:22
  22.5 4.6 %collective-permute-start.12 = (bf16[136,256]{1,0:T(8,128)(2,1)S(1)}, bf16[136,256]{1,0:T(8,128)(2,1)S(1)}, u32[]{:S(2)}, u32[]{:S(2)}) collective-permute-start(bf16[136,256]{1,0:T(8,128)(2,1)S(1)} %get-tuple-element.34.refs_0_), channel_id=1, source_target_pairs={{0,2},{1,3},{2,0},{3,1},{4,6},{5,7},{6,4},{7,5},{8,10},{9,11},{10,... | collective-permute-start | bytes 208904 | tf_op jit(solution)/shard_map/ppermute | solution.py:22
  25.2 6.5 %collective-permute-start.9 = (bf16[136,512]{1,0:T(8,128)(2,1)S(1)}, bf16[136,512]{1,0:T(8,128)(2,1)S(1)}, u32[]{:S(2)}, u32[]{:S(2)}) collective-permute-start(bf16[136,512]{1,0:T(8,128)(2,1)S(1)} %hidden_part.5.refs_4_), channel_id=1, source_target_pairs={{0,2},{1,3},{2,0},{3,1},{4,6},{5,7},{6,4},{7,5},{8,10},{9,11},{10,... | collective-permute-start | bytes 417800 | tf_op jit(solution)/shard_map/ppermute | solution.py:22
  27.0 6.8 %slice-start.3 = ((s8[12582912]{0:T(1024)(128)(4,1)}), s8[4194304]{0:T(1024)(128)(4,1)S(1)}, s32[]{:S(2)}) async-start(s8[12582912]{0:T(1024)(128)(4,1)} %bitcast.8), calls=%async_computation.3 | async-start | bytes 8388608
  27.0 6.8 %slice-start.4 = ((s8[12582912]{0:T(1024)(128)(4,1)}), s8[4194304]{0:T(1024)(128)(4,1)S(1)}, s32[]{:S(2)}) async-start(s8[12582912]{0:T(1024)(128)(4,1)} %bitcast.8), calls=%async_computation.4 | async-start | bytes 8388608
  28.7 5.2 %slice-start.5 = ((s8[12582912]{0:T(1024)(128)(4,1)}), s8[4194304]{0:T(1024)(128)(4,1)S(1)}, s32[]{:S(2)}) async-start(s8[12582912]{0:T(1024)(128)(4,1)} %bitcast.8), calls=%async_computation.5 | async-start | bytes 8388608
  28.7 6.8 %collective-permute-start.18 = (bf16[136,768]{1,0:T(8,128)(2,1)S(1)}, bf16[136,768]{1,0:T(8,128)(2,1)S(1)}, u32[]{:S(2)}, u32[]{:S(2)}) collective-permute-start(bf16[136,768]{1,0:T(8,128)(2,1)S(1)} %hidden_part.7.refs_2_), channel_id=1, source_target_pairs={{0,2},{1,3},{2,0},{3,1},{4,6},{5,7},{6,4},{7,5},{8,10},{9,11},{10,... | collective-permute-start | bytes 626696 | tf_op jit(solution)/shard_map/ppermute | solution.py:22
  30.3 1.3 %collective-permute-start.14 = (bf16[136,256]{1,0:T(8,128)(2,1)S(1)}, bf16[136,256]{1,0:T(8,128)(2,1)S(1)}, u32[]{:S(2)}, u32[]{:S(2)}) collective-permute-start(bf16[136,256]{1,0:T(8,128)(2,1)S(1)} %get-tuple-element.34.refs_0_), channel_id=1, source_target_pairs={{0,1},{1,0},{2,3},{3,2},{4,5},{5,4},{6,7},{7,6},{8,9},{9,8},{10,11... | collective-permute-start | bytes 208904 | tf_op jit(solution)/shard_map/ppermute | solution.py:22
  30.3 3.5 %collective-permute-start.16 = (bf16[136,512]{1,0:T(8,128)(2,1)S(1)}, bf16[136,512]{1,0:T(8,128)(2,1)S(1)}, u32[]{:S(2)}, u32[]{:S(2)}) collective-permute-start(bf16[136,512]{1,0:T(8,128)(2,1)S(1)} %hidden_part.5.refs_4_), channel_id=1, source_target_pairs={{0,1},{1,0},{2,3},{3,2},{4,5},{5,4},{6,7},{7,6},{8,9},{9,8},{10,11... | collective-permute-start | bytes 417800 | tf_op jit(solution)/shard_map/ppermute | solution.py:22
  30.8 5.2 %collective-permute-start.13 = (bf16[136,768]{1,0:T(8,128)(2,1)S(1)}, bf16[136,768]{1,0:T(8,128)(2,1)S(1)}, u32[]{:S(2)}, u32[]{:S(2)}) collective-permute-start(bf16[136,768]{1,0:T(8,128)(2,1)S(1)} %hidden_part.7.refs_2_), channel_id=1, source_target_pairs={{0,1},{1,0},{2,3},{3,2},{4,5},{5,4},{6,7},{7,6},{8,9},{9,8},{10,11... | collective-permute-start | bytes 626696 | tf_op jit(solution)/shard_map/ppermute | solution.py:22
  31.5 1.7 %collective-permute-start.15 = (bf16[136,256]{1,0:T(8,128)(2,1)S(1)}, bf16[136,256]{1,0:T(8,128)(2,1)S(1)}, u32[]{:S(2)}, u32[]{:S(2)}) collective-permute-start(bf16[136,256]{1,0:T(8,128)(2,1)S(1)} %collective-permute-done.12.refs_3_.refs_2_), channel_id=1, source_target_pairs={{0,1},{1,0},{2,3},{3,2},{4,5},{5,4},{6,7},{7,6},{8,9},{9,8},{10,11... | collective-permute-start | bytes 208904 | tf_op jit(solution)/shard_map/ppermute | solution.py:22
  31.7 4.3 %collective-permute-start.11 = (bf16[136,512]{1,0:T(8,128)(2,1)S(1)}, bf16[136,512]{1,0:T(8,128)(2,1)S(1)}, u32[]{:S(2)}, u32[]{:S(2)}) collective-permute-start(bf16[136,512]{1,0:T(8,128)(2,1)S(1)} %collective-permute-done.9.refs_3_.refs_0_), channel_id=1, source_target_pairs={{0,1},{1,0},{2,3},{3,2},{4,5},{5,4},{6,7},{7,6},{8,9},{9,8},{10,11... | collective-permute-start | bytes 417800 | tf_op jit(solution)/shard_map/ppermute | solution.py:22
  32.1 3.9 %slice-start.6 = ((s8[12582912]{0:T(1024)(128)(4,1)}), s8[4194304]{0:T(1024)(128)(4,1)S(1)}, s32[]{:S(2)}) async-start(s8[12582912]{0:T(1024)(128)(4,1)} %bitcast.10), calls=%async_computation.6 | async-start | bytes 8388608
  32.1 3.9 %slice-start.7 = ((s8[12582912]{0:T(1024)(128)(4,1)}), s8[4194304]{0:T(1024)(128)(4,1)S(1)}, s32[]{:S(2)}) async-start(s8[12582912]{0:T(1024)(128)(4,1)} %bitcast.10), calls=%async_computation.7 | async-start | bytes 8388608
  33.2 3.7 %slice-start.8 = ((s8[12582912]{0:T(1024)(128)(4,1)}), s8[4194304]{0:T(1024)(128)(4,1)S(1)}, s32[]{:S(2)}) async-start(s8[12582912]{0:T(1024)(128)(4,1)} %bitcast.10), calls=%async_computation.8 | async-start | bytes 8388608
  33.2 5.8 %collective-permute-start.10 = (bf16[136,512]{1,0:T(8,128)(2,1)S(1)}, bf16[136,512]{1,0:T(8,128)(2,1)S(1)}, u32[]{:S(2)}, u32[]{:S(2)}) collective-permute-start(bf16[136,512]{1,0:T(8,128)(2,1)S(1)} %hidden_part.6.refs_2_), channel_id=1, source_target_pairs={{0,2},{1,3},{2,0},{3,1},{4,6},{5,7},{6,4},{7,5},{8,10},{9,11},{10,... | collective-permute-start | bytes 417800 | tf_op jit(solution)/shard_map/ppermute | solution.py:22
  35.5 3.7 %collective-permute-start.19 = (bf16[136,768]{1,0:T(8,128)(2,1)S(1)}, bf16[136,768]{1,0:T(8,128)(2,1)S(1)}, u32[]{:S(2)}, u32[]{:S(2)}) collective-permute-start(bf16[136,768]{1,0:T(8,128)(2,1)S(1)} %hold.7.refs_0_), channel_id=1, source_target_pairs={{0,1},{1,0},{2,3},{3,2},{4,5},{5,4},{6,7},{7,6},{8,9},{9,8},{10,11... | collective-permute-start | bytes 626696 | tf_op jit(solution)/shard_map/ppermute | solution.py:22
  35.5 3.7 %collective-permute-start.20 = (bf16[136,512]{1,0:T(8,128)(2,1)S(1)}, bf16[136,512]{1,0:T(8,128)(2,1)S(1)}, u32[]{:S(2)}, u32[]{:S(2)}) collective-permute-start(bf16[136,512]{1,0:T(8,128)(2,1)S(1)} %hidden_part.6.refs_2_), channel_id=1, source_target_pairs={{0,1},{1,0},{2,3},{3,2},{4,5},{5,4},{6,7},{7,6},{8,9},{9,8},{10,11... | collective-permute-start | bytes 417800 | tf_op jit(solution)/shard_map/ppermute | solution.py:22
  39.0 6.3 %copy-start.1 = (bf16[64,768]{1,0:T(8,128)(2,1)S(1)}, bf16[64,768]{1,0:T(8,128)(2,1)}, u32[]{:S(2)}) copy-start(bf16[64,768]{1,0:T(8,128)(2,1)} %grad_ref.1) | copy-start | bytes 294916
  39.1 6.3 %copy-start.2 = (s32[64,2]{0,1:T(2,128)S(1)}, s32[64,2]{0,1:T(2,128)}, u32[]{:S(2)}) copy-start(s32[64,2]{0,1:T(2,128)} %param.8) | copy-start | bytes 1540
  39.1 6.3 %copy-start.3 = (f32[64,2]{0,1:T(2,128)S(1)}, f32[64,2]{0,1:T(2,128)}, u32[]{:S(2)}) copy-start(f32[64,2]{0,1:T(2,128)} %param.9) | copy-start | bytes 1540
  39.1 1.4 %collective-permute-start.17 = (bf16[136,512]{1,0:T(8,128)(2,1)S(1)}, bf16[136,512]{1,0:T(8,128)(2,1)S(1)}, u32[]{:S(2)}, u32[]{:S(2)}) collective-permute-start(bf16[136,512]{1,0:T(8,128)(2,1)S(1)} %hold.6.refs_0_), channel_id=1, source_target_pairs={{0,1},{1,0},{2,3},{3,2},{4,5},{5,4},{6,7},{7,6},{8,9},{9,8},{10,11... | collective-permute-start | bytes 417800 | tf_op jit(solution)/shard_map/ppermute | solution.py:22
  40.9 4.9 %collective-permute-start.21 = (bf16[204,128]{1,0:T(8,128)(2,1)S(1)}, bf16[204,128]{1,0:T(8,128)(2,1)S(1)}, u32[]{:S(2)}, u32[]{:S(2)}) collective-permute-start(bf16[204,128]{1,0:T(8,128)(2,1)S(1)} %get-tuple-element.36), channel_id=1, source_target_pairs={{0,4},{4,0},{8,12},{12,8},{1,5},{5,1},{9,13},{13,9},{2,6},{6,2},{1... | collective-permute-start | bytes 156680 | tf_op jit(solution)/shard_map/ppermute | solution.py:22
  41.0 6.7 %collective-permute-start.22 = (bf16[204,128]{1,0:T(8,128)(2,1)S(1)}, bf16[204,128]{1,0:T(8,128)(2,1)S(1)}, u32[]{:S(2)}, u32[]{:S(2)}) collective-permute-start(bf16[204,128]{1,0:T(8,128)(2,1)S(1)} %get-tuple-element.37), channel_id=1, source_target_pairs={{0,8},{4,12},{8,0},{12,4},{1,9},{5,13},{9,1},{13,5},{2,10},{6,14},... | collective-permute-start | bytes 156680 | tf_op jit(solution)/shard_map/ppermute | solution.py:22
  44.1 5.9 %collective-permute-start.23 = (bf16[204,128]{1,0:T(8,128)(2,1)S(1)}, bf16[204,128]{1,0:T(8,128)(2,1)S(1)}, u32[]{:S(2)}, u32[]{:S(2)}) collective-permute-start(bf16[204,128]{1,0:T(8,128)(2,1)S(1)} %get-tuple-element.38), channel_id=1, source_target_pairs={{0,12},{4,8},{8,4},{12,0},{1,13},{5,9},{9,5},{13,1},{2,14},{6,10},... | collective-permute-start | bytes 156680 | tf_op jit(solution)/shard_map/ppermute | solution.py:22
  50.2 3.1 %collective-permute-start.26 = (f32[2,64]{1,0:T(2,128)S(1)}, f32[2,64]{1,0:T(2,128)S(1)}, u32[]{:S(2)}, u32[]{:S(2)}) collective-permute-start(f32[2,64]{1,0:T(2,128)S(1)} %dots.1), channel_id=1, source_target_pairs={{0,3},{1,2},{2,1},{3,0},{4,7},{5,6},{6,5},{7,4},{8,11},{9,10},{10,... | collective-permute-start | bytes 1544 | tf_op jit(solution)/shard_map/ppermute | solution.py:22
  50.3 4.6 %collective-permute-start.25 = (f32[2,64]{1,0:T(2,128)S(1)}, f32[2,64]{1,0:T(2,128)S(1)}, u32[]{:S(2)}, u32[]{:S(2)}) collective-permute-start(f32[2,64]{1,0:T(2,128)S(1)} %dots.1), channel_id=1, source_target_pairs={{0,1},{1,0},{2,3},{3,2},{4,5},{5,4},{6,7},{7,6},{8,9},{9,8},{10,11... | collective-permute-start | bytes 1544 | tf_op jit(solution)/shard_map/ppermute | solution.py:22
  51.4 3.6 %collective-permute-start.24 = (f32[2,64]{1,0:T(2,128)S(1)}, f32[2,64]{1,0:T(2,128)S(1)}, u32[]{:S(2)}, u32[]{:S(2)}) collective-permute-start(f32[2,64]{1,0:T(2,128)S(1)} %dots.1), channel_id=1, source_target_pairs={{0,2},{1,3},{2,0},{3,1},{4,6},{5,7},{6,4},{7,5},{8,10},{9,11},{10,... | collective-permute-start | bytes 1544 | tf_op jit(solution)/shard_map/ppermute | solution.py:22
